TPU v7x, 32 devices: a whole 2x2x4 slice. The times are simulated.
32 devices in a mesh: dp: 4 (over y, x), seq: 8 (over z, core).
Axes of the slice: x: 2, y: 2, z: 4, core: 2. Of those that a mesh axis runs over, the one named last changes fastest.
Arguments:
- inputs: bfloat16 [4, 1280, 1152], P('dp', 'seq'), may hold values from -6 to 6
- skipped: bfloat16 [4, 1280, 1152], P('dp', 'seq'), may hold values from -6 to 6
- item_lengths: int32 [4, 5], P('dp'), may hold values from 0 to 1026, as said below
- skip_w: bfloat16 [2304, 1152], P(('dp', 'seq')), may hold values from -0.125 to 0.125
- qkv_w: bfloat16 [1152, 3456], P(('dp', 'seq')), may hold values from -0.25 to 0.25
- proj_w: bfloat16 [1152, 1152], P(('dp', 'seq')), may hold values from -1 to 1
- fc1_w: bfloat16 [1152, 4608], P(('dp', 'seq')), may hold values from -0.1875 to 0.1875
- fc2_w: bfloat16 [4608, 1152], P(('dp', 'seq')), may hold values from -0.09375 to 0.09375
- skip_b: bfloat16 [1152], P(('dp', 'seq')), may hold values from -3 to 3
- ln1_g: bfloat16 [1152], P(('dp', 'seq')), may hold values from 0.25 to 1.75
- ln1_b: bfloat16 [1152], P(('dp', 'seq')), may hold values from -3 to 3
- proj_b: bfloat16 [1152], P(('dp', 'seq')), may hold values from -3 to 3
- ln2_g: bfloat16 [1152], P(('dp', 'seq')), may hold values from 0.25 to 1.75
- ln2_b: bfloat16 [1152], P(('dp', 'seq')), may hold values from -3 to 3
- fc1_b: bfloat16 [4608], P(('dp', 'seq')), may hold values from -3 to 3
- fc2_b: bfloat16 [1152], P(('dp', 'seq')), may hold values from -3 to 3
- cotangent: bfloat16 [4, 1280, 1152], P('dp', 'seq'), may hold values from -6 to 6
Outputs:
- output: bfloat16 [4, 1280, 1152], P('dp', 'seq')
- input_grad: float32 [4, 1280, 1152], P('dp', 'seq')
- skip_grad: float32 [4, 1280, 1152], P('dp', 'seq')
- skip_w_grad: float32 [2304, 1152], P(('dp', 'seq'))
- qkv_w_grad: float32 [1152, 3456], P(('dp', 'seq'))
- proj_w_grad: float32 [1152, 1152], P(('dp', 'seq'))
- fc1_w_grad: float32 [1152, 4608], P(('dp', 'seq'))
- fc2_w_grad: float32 [4608, 1152], P(('dp', 'seq'))
- skip_b_grad: float32 [1152], P(('dp', 'seq'))
- ln1_g_grad: float32 [1152], P(('dp', 'seq'))
- ln1_b_grad: float32 [1152], P(('dp', 'seq'))
- proj_b_grad: float32 [1152], P(('dp', 'seq'))
- ln2_g_grad: float32 [1152], P(('dp', 'seq'))
- ln2_b_grad: float32 [1152], P(('dp', 'seq'))
- fc1_b_grad: float32 [4608], P(('dp', 'seq'))
- fc2_b_grad: float32 [1152], P(('dp', 'seq'))
Inputs may be any that keep to these rules, and one draw needn't show every extreme that they name: `item_lengths`: in each row the nonzero lengths, each 258 or 1026, stand first and sum to at most 1280; the first is 1026; later slots are 0.
All inputs are finite; a program needn't handle non-finite values.
Results may differ from a plain program's by a relative error of at most 0.024.
Values may be sent and summed in bfloat16 or wider, within the bound.
No kernel may reach another device: no remote copies, remote signals or barrier semaphores. Data moves between devices by JAX's collectives and lax.ppermute only.
A program may use at most 256 MiB of HBM per device.

v0:
```python
from functools import partial
import math

import jax
import jax.numpy as jnp
from jax import lax
from jax.sharding import PartitionSpec as P

HEADS = 16
HEAD_DIM = 72


EPSILON = 1e-05
NEGATIVE = -1e30


def norm_forward_pieces(hvals, gain_factor, shift_bias):
    centered_rows = hvals - jnp.mean(hvals, axis=-1, keepdims=True)
    inverse_deviation = lax.rsqrt(
        jnp.mean(centered_rows * centered_rows, axis=-1, keepdims=True) + EPSILON
    )
    standardized_input = centered_rows * inverse_deviation
    return (standardized_input * gain_factor + shift_bias, standardized_input, inverse_deviation)


def norm_backward_rows(incoming_gradient, standardized_input, inverse_deviation, gain_factor):
    scaled_rows = incoming_gradient * gain_factor
    passed_through = inverse_deviation * (
        scaled_rows
        - jnp.mean(scaled_rows, axis=-1, keepdims=True)
        - standardized_input * jnp.mean(scaled_rows * standardized_input, axis=-1, keepdims=True)
    )
    return (
        passed_through,
        jnp.sum(incoming_gradient * standardized_input, axis=0),
        jnp.sum(incoming_gradient, axis=0),
    )


def segment_of(lengths, places):
    ends = jnp.cumsum(lengths, axis=1)
    return jnp.sum((ends[:, None, :] <= places[None, :, None]).astype(jnp.int32), axis=2)


def inner(left, right):
    return lax.dot_general(
        left, right, (((0,), (0,)), ((), ())), preferred_element_type=jnp.float32
    )


def times_transposed(left, right):
    return lax.dot_general(
        left, right, (((1,), (1,)), ((), ())), preferred_element_type=jnp.float32
    )


def key_blocks(step_fn, carry, piece):
    count = jax.tree.leaves(piece)[0].shape[1]
    block_len = math.gcd(count, 512)

    def advance(index, state):
        block = jax.tree.map(
            lambda part_array: lax.dynamic_slice_in_dim(
                part_array, index * block_len, block_len, 1
            ),
            piece,
        )
        return step_fn(state, block, index * block_len)

    return lax.fori_loop(0, count // block_len, advance, carry)


def on_device(
    inputs,
    skipped,
    item_lengths,
    skip_w,
    qkv_w,
    proj_w,
    fc1_w,
    fc2_w,
    skip_b,
    ln1_g,
    ln1_b,
    proj_b,
    ln2_g,
    ln2_b,
    fc1_b,
    fc2_b,
    cotangent,
):
    row_count, local_len, features = inputs.shape
    head_count = HEADS
    head_size = HEAD_DIM
    token_count = row_count * local_len
    scale = head_size ** (-0.5)
    single_precision = jnp.float32
    bf16 = jnp.bfloat16
    full = (
        lax.all_gather(skip_w, ("dp", "seq"), axis=0, tiled=True),
        lax.all_gather(qkv_w, ("dp", "seq"), axis=0, tiled=True),
        lax.all_gather(proj_w, ("dp", "seq"), axis=0, tiled=True),
        lax.all_gather(fc1_w, ("dp", "seq"), axis=0, tiled=True),
        lax.all_gather(fc2_w, ("dp", "seq"), axis=0, tiled=True),
        lax.all_gather(skip_b, ("dp", "seq"), axis=0, tiled=True),
        lax.all_gather(ln1_g, ("dp", "seq"), axis=0, tiled=True),
        lax.all_gather(ln1_b, ("dp", "seq"), axis=0, tiled=True),
        lax.all_gather(proj_b, ("dp", "seq"), axis=0, tiled=True),
        lax.all_gather(ln2_g, ("dp", "seq"), axis=0, tiled=True),
        lax.all_gather(ln2_b, ("dp", "seq"), axis=0, tiled=True),
        lax.all_gather(fc1_b, ("dp", "seq"), axis=0, tiled=True),
        lax.all_gather(fc2_b, ("dp", "seq"), axis=0, tiled=True),
    )
    (
        w_skip,
        w_qkv,
        w_proj,
        w_up,
        w_down,
        b_skip,
        first_norm_gain,
        first_norm_bias,
        b_proj,
        second_norm_gain,
        second_norm_bias,
        b_up,
        b_down,
    ) = full
    joined = jnp.concatenate([inputs, skipped], axis=2).reshape(token_count, 2 * features)
    first_output = jnp.dot(joined, w_skip, preferred_element_type=single_precision) + b_skip.astype(
        single_precision
    )
    first_normalized, first_standardized, first_inverse_deviation = norm_forward_pieces(
        first_output,
        first_norm_gain.astype(single_precision),
        first_norm_bias.astype(single_precision),
    )
    first_normalized = first_normalized.astype(bf16)
    triple = jnp.dot(first_normalized, w_qkv, preferred_element_type=single_precision).astype(bf16)
    queries = triple[:, :features].reshape(row_count, local_len, head_count, head_size)
    pairs = triple[:, features:].reshape(row_count, local_len, 2 * features)
    own_keys = pairs[:, :, :features].reshape(row_count, local_len, head_count, head_size)
    own_values = pairs[:, :, features:].reshape(row_count, local_len, head_count, head_size)
    offset = lax.axis_index("seq") * local_len
    query_segs = segment_of(item_lengths, offset + jnp.arange(local_len, dtype=jnp.int32))

    def scores_for(block, start):
        count = block.shape[1]
        keys = block[:, :, :features].reshape(row_count, count, head_count, head_size)
        values = block[:, :, features:].reshape(row_count, count, head_count, head_size)
        key_segs = segment_of(item_lengths, start + jnp.arange(count, dtype=jnp.int32))
        allowed = query_segs[:, None, :, None] == key_segs[:, None, None, :]
        raw = jnp.einsum("rqhd,rkhd->rhqk", queries, keys, preferred_element_type=single_precision)
        return (raw * scale, allowed, keys, values)

    def forward_block(carry, block, start):
        top, total, accum = carry
        logits, allowed, keys, values = scores_for(block, start)
        logits = jnp.where(allowed, logits, NEGATIVE)
        new_top = jnp.maximum(top, jnp.max(logits, axis=3))
        weights = jnp.where(allowed, jnp.exp(logits - new_top[..., None]), 0.0)
        decay = jnp.exp(top - new_top)
        total = total * decay + jnp.sum(weights, axis=3)
        update = jnp.einsum(
            "rhqk,rkhd->rqhd", weights.astype(bf16), values, preferred_element_type=single_precision
        )
        accum = accum * jnp.swapaxes(decay, 1, 2)[..., None] + update
        return (new_top, total, accum)

    start_state = (
        jnp.full((row_count, head_count, local_len), NEGATIVE, single_precision),
        jnp.zeros((row_count, head_count, local_len), single_precision),
        jnp.zeros((row_count, local_len, head_count, head_size), single_precision),
    )
    top, total, accum = key_blocks(
        forward_block, start_state, lax.all_gather(pairs, "seq", axis=1, tiled=True)
    )
    attended = accum / jnp.swapaxes(total, 1, 2)[..., None]
    log_total = top + jnp.log(total)
    attended_low = attended.reshape(token_count, features).astype(bf16)
    second_output = (
        first_output
        + jnp.dot(attended_low, w_proj, preferred_element_type=single_precision)
        + b_proj.astype(single_precision)
    )
    second_normalized, second_standardized, second_inverse_deviation = norm_forward_pieces(
        second_output,
        second_norm_gain.astype(single_precision),
        second_norm_bias.astype(single_precision),
    )
    second_normalized = second_normalized.astype(bf16)
    pre = jnp.dot(second_normalized, w_up, preferred_element_type=single_precision) + b_up.astype(
        single_precision
    )
    hidden = jax.nn.gelu(pre, approximate=False).astype(bf16)
    final = (
        second_output
        + jnp.dot(hidden, w_down, preferred_element_type=single_precision)
        + b_down.astype(single_precision)
    )
    output = final.astype(bf16).reshape(row_count, local_len, features)
    back = (
        lax.all_gather(skip_w, ("dp", "seq"), axis=0, tiled=True),
        lax.all_gather(qkv_w, ("dp", "seq"), axis=0, tiled=True),
        lax.all_gather(proj_w, ("dp", "seq"), axis=0, tiled=True),
        lax.all_gather(fc1_w, ("dp", "seq"), axis=0, tiled=True),
        lax.all_gather(fc2_w, ("dp", "seq"), axis=0, tiled=True),
        lax.all_gather(ln1_g, ("dp", "seq"), axis=0, tiled=True),
        lax.all_gather(ln2_g, ("dp", "seq"), axis=0, tiled=True),
    )
    k_skip, k_qkv, k_proj, k_up, k_down, first_gain_again, second_gain_again = back
    grad_out = cotangent.reshape(token_count, features)
    fc2_w_grad = inner(hidden, grad_out)
    fc2_b_grad = jnp.sum(grad_out.astype(single_precision), axis=0)
    hidden_grad = times_transposed(grad_out, k_down)
    gelu_value, gelu_pull = jax.vjp(partial(jax.nn.gelu, approximate=False), pre)
    pre_grad = gelu_pull(hidden_grad)[0]
    fc1_b_grad = jnp.sum(pre_grad, axis=0)
    pre_low = pre_grad.astype(bf16)
    fc1_w_grad = inner(second_normalized, pre_low)
    second_normalized_gradient = times_transposed(pre_low, k_up)
    through_two, ln2_g_grad, ln2_b_grad = norm_backward_rows(
        second_normalized_gradient,
        second_standardized,
        second_inverse_deviation,
        second_gain_again.astype(single_precision),
    )
    second_grad = grad_out.astype(single_precision) + through_two
    proj_b_grad = jnp.sum(second_grad, axis=0)
    second_low = second_grad.astype(bf16)
    proj_w_grad = inner(attended_low, second_low)
    attended_grad = (
        times_transposed(second_low, k_proj)
        .astype(bf16)
        .reshape(row_count, local_len, head_count, head_size)
    )
    delta = jnp.swapaxes(jnp.sum(attended_grad.astype(single_precision) * attended, axis=3), 1, 2)

    def query_terms(block, start):
        logits, allowed, keys, values = scores_for(block, start)
        probs = jnp.where(allowed, jnp.exp(logits - log_total[..., None]), 0.0)
        prob_grad = jnp.einsum(
            "rqhd,rkhd->rhqk", attended_grad, values, preferred_element_type=single_precision
        )
        logit_grad = (probs * (prob_grad - delta[..., None]) * scale).astype(bf16)
        return (probs, logit_grad, keys)

    def query_block(carry, block, start):
        probs, logit_grad, keys = query_terms(block, start)
        return carry + jnp.einsum(
            "rhqk,rkhd->rqhd", logit_grad, keys, preferred_element_type=single_precision
        )

    query_grad = key_blocks(
        query_block,
        jnp.zeros((row_count, local_len, head_count, head_size), single_precision),
        lax.all_gather(pairs, "seq", axis=1, tiled=True),
    )
    row_lse, row_delta = (
        lax.all_gather(jnp.swapaxes(log_total, 1, 2), "seq", axis=1, tiled=True),
        lax.all_gather(jnp.swapaxes(delta, 1, 2), "seq", axis=1, tiled=True),
    )

    def key_block(carry, piece, start):
        key_total, value_total = carry
        far_queries, far_grads = piece
        count = far_queries.shape[1]
        far_segs = segment_of(item_lengths, start + jnp.arange(count, dtype=jnp.int32))
        allowed = far_segs[:, None, :, None] == query_segs[:, None, None, :]
        lse_piece = jnp.swapaxes(lax.dynamic_slice_in_dim(row_lse, start, count, 1), 1, 2)
        delta_piece = jnp.swapaxes(lax.dynamic_slice_in_dim(row_delta, start, count, 1), 1, 2)
        logits = (
            jnp.einsum(
                "rqhd,rkhd->rhqk", far_queries, own_keys, preferred_element_type=single_precision
            )
            * scale
        )
        probs = jnp.where(allowed, jnp.exp(logits - lse_piece[..., None]), 0.0)
        value_total = value_total + jnp.einsum(
            "rhqk,rqhd->rkhd",
            probs.astype(bf16),
            far_grads,
            preferred_element_type=single_precision,
        )
        prob_grad = jnp.einsum(
            "rqhd,rkhd->rhqk", far_grads, own_values, preferred_element_type=single_precision
        )
        logit_grad = (probs * (prob_grad - delta_piece[..., None]) * scale).astype(bf16)
        key_total = key_total + jnp.einsum(
            "rhqk,rqhd->rkhd", logit_grad, far_queries, preferred_element_type=single_precision
        )
        return (key_total, value_total)

    zero_side = jnp.zeros((row_count, local_len, head_count, head_size), single_precision)
    key_total, value_total = key_blocks(
        key_block,
        (zero_side, zero_side),
        (
            lax.all_gather(queries, "seq", axis=1, tiled=True),
            lax.all_gather(attended_grad, "seq", axis=1, tiled=True),
        ),
    )
    own_pair_grad = jnp.concatenate(
        [
            key_total.reshape(row_count, local_len, features),
            value_total.reshape(row_count, local_len, features),
        ],
        axis=2,
    )
    triple_grad = jnp.concatenate(
        [
            query_grad.reshape(token_count, features),
            own_pair_grad.reshape(token_count, 2 * features),
        ],
        axis=1,
    ).astype(bf16)
    qkv_w_grad = inner(first_normalized, triple_grad)
    first_normalized_gradient = times_transposed(triple_grad, k_qkv)
    through_one, ln1_g_grad, ln1_b_grad = norm_backward_rows(
        first_normalized_gradient,
        first_standardized,
        first_inverse_deviation,
        first_gain_again.astype(single_precision),
    )
    first_grad = second_grad + through_one
    skip_b_grad = jnp.sum(first_grad, axis=0)
    first_low = first_grad.astype(bf16)
    skip_w_grad = inner(joined, first_low)
    joined_grad = times_transposed(first_low, k_skip)
    input_grad = joined_grad[:, :features].reshape(row_count, local_len, features)
    skip_grad = joined_grad[:, features:].reshape(row_count, local_len, features)
    owned_grads = (
        lax.psum_scatter(skip_w_grad, ("dp", "seq"), scatter_dimension=0, tiled=True),
        lax.psum_scatter(qkv_w_grad, ("dp", "seq"), scatter_dimension=0, tiled=True),
        lax.psum_scatter(proj_w_grad, ("dp", "seq"), scatter_dimension=0, tiled=True),
        lax.psum_scatter(fc1_w_grad, ("dp", "seq"), scatter_dimension=0, tiled=True),
        lax.psum_scatter(fc2_w_grad, ("dp", "seq"), scatter_dimension=0, tiled=True),
        lax.psum_scatter(skip_b_grad, ("dp", "seq"), scatter_dimension=0, tiled=True),
        lax.psum_scatter(ln1_g_grad, ("dp", "seq"), scatter_dimension=0, tiled=True),
        lax.psum_scatter(ln1_b_grad, ("dp", "seq"), scatter_dimension=0, tiled=True),
        lax.psum_scatter(proj_b_grad, ("dp", "seq"), scatter_dimension=0, tiled=True),
        lax.psum_scatter(ln2_g_grad, ("dp", "seq"), scatter_dimension=0, tiled=True),
        lax.psum_scatter(ln2_b_grad, ("dp", "seq"), scatter_dimension=0, tiled=True),
        lax.psum_scatter(fc1_b_grad, ("dp", "seq"), scatter_dimension=0, tiled=True),
        lax.psum_scatter(fc2_b_grad, ("dp", "seq"), scatter_dimension=0, tiled=True),
    )
    return (output, input_grad, skip_grad) + tuple(owned_grads)


def solution(mesh):
    in_specs = (
        P("dp", "seq", None),
        P("dp", "seq", None),
        P("dp", None),
        P(("dp", "seq"), None),
        P(("dp", "seq"), None),
        P(("dp", "seq"), None),
        P(("dp", "seq"), None),
        P(("dp", "seq"), None),
        P(("dp", "seq")),
        P(("dp", "seq")),
        P(("dp", "seq")),
        P(("dp", "seq")),
        P(("dp", "seq")),
        P(("dp", "seq")),
        P(("dp", "seq")),
        P(("dp", "seq")),
        P("dp", "seq", None),
    )
    out_specs = (
        P("dp", "seq", None),
        P("dp", "seq", None),
        P("dp", "seq", None),
        P(("dp", "seq"), None),
        P(("dp", "seq"), None),
        P(("dp", "seq"), None),
        P(("dp", "seq"), None),
        P(("dp", "seq"), None),
        P(("dp", "seq")),
        P(("dp", "seq")),
        P(("dp", "seq")),
        P(("dp", "seq")),
        P(("dp", "seq")),
        P(("dp", "seq")),
        P(("dp", "seq")),
        P(("dp", "seq")),
    )
    return jax.shard_map(
        on_device, mesh=mesh, in_specs=in_specs, out_specs=out_specs, check_vma=False
    )
```

profile of v0, /device:TPU:0, one launch (start us, length us, event | category | flops | bytes accessed | tf_op | source)
XLA Modules:
  0.0 1782.7 jit_solution(11025282727169540492)
XLA Ops:
  16.8 43.5 %all-reduce.24 = (bf16[1152]{0:T(1024)(128)(2,1)S(1)}, bf16[1152]{0:T(1024)(128)(2,1)S(1)}, bf16[1152]{0:T(1024)(128)(2,1)S(1)}, bf16[1152]{0:T(1024)(128)(2,1)S...) all-reduce(bf16[1152]{0:T(1024)(128)(2,1)S(1)} %dynamic-update-slic, ...), channel_id=1, replica_groups=mesh['dp'=4,'seq'=8] {'dp','seq'}, use_global_device_ids=true, to_apply=%add | all-reduce | flops 12672 | bytes 50688
  60.3 19.0 %all-gather.15.cloned.1.call-done = bf16[2304,1152]{1,0:T(8,128)(2,1)} async-done(((bf16[72,1152]{1,0:T(8,128)(2,1)}), bf16[2304,1152]{1,0:T(8,128)(2,1)}) %all-gather.15.cloned.1.call-update) | async-done | bytes 5308432 | tf_op jit(solution)/shard_map/all_gather | solution.py:100
  83.5 77.2 %all-gather.25.cloned.1.call-done = bf16[32,36,3456]{2,1,0:T(8,128)(2,1)} async-done(((bf16[1,36,3456]{2,1,0:T(8,128)(2,1)}), bf16[32,36,3456]{2,1,0:T(8,128)(2,1)}) %all-gather.25.cloned.1.call-update) | async-done | bytes 7962640 | tf_op jit(solution)/shard_map/all_gather | solution.py:101
  160.7 12.5 reshape.802
  182.9 38.2 %all-gather.27.cloned.1.call-done = bf16[32,36,1152]{2,1,0:T(8,128)(2,1)} async-done(((bf16[1,36,1152]{2,1,0:T(8,128)(2,1)}), bf16[32,36,1152]{2,1,0:T(8,128)(2,1)}) %all-gather.27.cloned.1.call-update) | async-done | bytes 2654224 | tf_op jit(solution)/shard_map/all_gather | solution.py:102
  232.4 82.7 %all-gather.29.cloned.1.call-done = bf16[32,36,4608]{2,1,0:T(8,128)(2,1)} async-done(((bf16[1,36,4608]{2,1,0:T(8,128)(2,1)}), bf16[32,36,4608]{2,1,0:T(8,128)(2,1)}) %all-gather.29.cloned.1.call-update) | async-done | bytes 10616848 | tf_op jit(solution)/shard_map/all_gather | solution.py:103
  315.1 14.3 reshape.806
  329.4 42.2 %all-gather.19.cloned.1.call-done = bf16[1,1280,16,72]{3,2,0,1:T(8,128)(2,1)} async-done(((bf16[1,160,16,72]{3,2,0,1:T(8,128)(2,1)}), bf16[1,1280,16,72]{3,2,0,1:T(8,128)(2,1)}) %all-gather.19.cloned.1.call-update) | async-done | bytes 2949136 | tf_op jit(solution)/shard_map/all_gather | solution.py:299
  379.5 54.4 %all-gather.23.cloned.1.call-done = bf16[1280,2304]{1,0:T(8,128)(2,1)} async-done(((bf16[160,2304]{1,0:T(8,128)(2,1)}), bf16[1280,2304]{1,0:T(8,128)(2,1)}) %all-gather.23.cloned.1.call-update) | async-done | bytes 5898256 | tf_op jit(solution)/shard_map/all_gather | solution.py:176
  442.8 30.4 %while.54 = (s32[]{:T(128)}, f32[1,16,160]{2,1,0:T(8,128)S(1)}, f32[1,16,160]{2,1,0:T(8,128)S(1)}, f32[1,160,16,72]{1,3,2,0:T(8,128)}, s32[1,160]{1,0:T(1,128)S(...) while((s32[]{:T(128)}, f32[1,16,160]{2,1,0:T(8,128)S(1)}, ...), condition=%wide.region_8.9_spmd.clone, body=%wide.region_4.8_spmd.clone.sunk | while | flops 197876480 | bytes 19477412 | solution.py:70
  493.3 29.8 %all-gather.17.cloned.1.call-done = bf16[4608,1152]{1,0:T(8,128)(2,1)} async-done(((bf16[144,1152]{1,0:T(8,128)(2,1)}), bf16[4608,1152]{1,0:T(8,128)(2,1)}) %all-gather.17.cloned.1.call-update) | async-done | bytes 10616848 | tf_op jit(solution)/shard_map/all_gather | solution.py:104
  523.1 12.5 fusion.117
  554.3 15.0 all_gather.77
  569.9 14.4 all-gather.5
  584.4 40.4 %while.55 = (s32[]{:T(128)}, f32[1,160,16,72]{1,3,2,0:T(8,128)}, bf16[1,1280,2304]{1,2,0:T(8,128)(2,1)}, s32[1,160]{1,0:T(1,128)S(1)}, s32[1,1,5]{2,1,0:T(1,128)...) while((s32[]{:T(128)}, f32[1,160,16,72]{1,3,2,0:T(8,128)}, ...), condition=%wide.region_16.17_spmd.clone, body=%wide.region_14.16_spmd.clone.sunk | while | flops 288116480 | bytes 14050189 | solution.py:70
  635.0 46.0 %while.56 = (s32[]{:T(128)}, f32[1,160,16,72]{1,3,2,0:T(8,128)}, f32[1,160,16,72]{1,3,2,0:T(8,128)}, bf16[1,1280,16,72]{1,3,2,0:T(8,128)(2,1)}, s32[1,1,5]{2,1,0...) while((s32[]{:T(128)}, f32[1,160,16,72]{1,3,2,0:T(8,128)}, ...), condition=%wide.region_19.20_spmd.clone, body=%wide.region_17.19_spmd.clone.sunk | while | flops 385478400 | bytes 15260017 | solution.py:70
  699.2 15.3 fusion.94
  737.4 696.7 %fusion.111 = (f32[48,3456]{1,0:T(8,128)S(1)}, f32[48,1152]{1,0:T(8,128)S(1)}, f32[40,4608]{1,0:T(8,128)S(1)}) fusion(f32[1152,3456]{1,0:T(8,128)} %fusion.86, f32[1152,1152]{1,0:T(8,128)} %fusion.103, f32[1152,4608]{1,0:T(8,128)} %fusion.88), kind=kCustom, calls=%all-reduce-scatter.3 | all-reduce-scatter fusion | flops 12976130 | bytes 44089344
  1447.1 17.1 collective-permute-done.15
  1543.2 37.0 %collective-permute-start.17 = (f32[40,4608]{1,0:T(8,128)S(1)}, f32[40,4608]{1,0:T(8,128)S(1)}, u32[]{:S(2)}, u32[]{:S(2)}) collective-permute-start(f32[40,4608]{1,0:T(8,128)S(1)} %get-tuple-element.1000), channel_id=1, source_target_pairs={{0,2},{1,3},{2,4},{3,5},{4,6},{5,7},{6,8},{7,9},{8,10},{9,11},{10,... | collective-permute-start | bytes 2211848
  1580.2 26.5 %collective-permute-start.16 = (f32[40,4608]{1,0:T(8,128)S(1)}, f32[40,4608]{1,0:T(8,128)}, u32[]{:S(2)}, u32[]{:S(2)}) collective-permute-start(f32[40,4608]{1,0:T(8,128)S(1)} %get-tuple-element.1000), channel_id=1, source_target_pairs={{0,1},{1,2},{2,3},{3,4},{4,5},{5,6},{6,7},{7,8},{8,9},{9,10},{10,1... | collective-permute-start | bytes 2211848
  1608.6 84.1 %all-reduce.23 = (f32[1152]{0:T(1024)}, f32[1152]{0:T(1024)}, f32[1152]{0:T(1024)}, f32[1152]{0:T(1024)}, f32[1152]{0:T(1024)}, /*index=5*/f32[1152]{0:T(1024)}, f32[4608]{0:T(1024)}, f32[1152]{0:T(1024)}) all-reduce(f32[1152]{0:T(1024)} %get-tuple-element.1005, ...), channel_id=9, replica_groups=mesh['dp'=4,'seq'=8] {'dp','seq'}, use_global_device_ids=true, to_apply=%region_28.29.clone | all-reduce | flops 12672 | bytes 101376
  1702.9 14.7 concatenate.15
  1721.9 36.8 %concatenate.14 = f32[420,3456]{1,0:T(8,128)} concatenate(f32[36,3456]{1,0:T(8,128)} %copy-done.26, f32[48,3456]{1,0:T(8,128)} %copy-done.21, f32[48,3456]{1,0:T(8,128)} %copy-done.22, f32[48,3456]{1,0:T(8,128)} %copy-done.23, f32[48,3456]{1,0:T(8,128)} %copy-done.24, f32[48,3456]{1,0:T(8,128)} %copy-done.25, f32[48,3456]{1,0:T(8,128)} %collective-permute-done.1, ...), dimensions={0} | concatenate | bytes 11612160
  (390 shorter events, 382.9 us)
Async XLA Ops:
  7.2 72.1 %all-gather.15.cloned.1.call-start = ((), (), s32[]{:S(2)}) async-start(), calls=%async_computation.2 | async-start | bytes 5474304 | tf_op jit(solution)/shard_map/all_gather | solution.py:100
  7.9 152.8 %all-gather.25.cloned.1.call-start = ((), (), s32[]{:S(2)}) async-start(), calls=%async_computation.8 | async-start | bytes 9123840 | tf_op jit(solution)/shard_map/all_gather | solution.py:101
  8.7 212.5 %all-gather.27.cloned.1.call-start = ((), (), s32[]{:S(2)}) async-start(), calls=%async_computation.9 | async-start | bytes 3041280 | tf_op jit(solution)/shard_map/all_gather | solution.py:102
  9.4 305.7 %all-gather.29.cloned.1.call-start = ((), (), s32[]{:S(2)}) async-start(), calls=%async_computation.10 | async-start | bytes 12165120 | tf_op jit(solution)/shard_map/all_gather | solution.py:103
  10.0 361.6 %all-gather.19.cloned.1.call-start = ((), (), s32[]{:S(2)}) async-start(), calls=%async_computation.4 | async-start | bytes 5898240 | tf_op jit(solution)/shard_map/all_gather | solution.py:299
  180.2 253.7 %all-gather.23.cloned.1.call-start = ((), (), s32[]{:S(2)}) async-start(), calls=%async_computation.7 | async-start | bytes 6635520 | tf_op jit(solution)/shard_map/all_gather | solution.py:176
  181.5 341.6 %all-gather.17.cloned.1.call-start = ((), (), s32[]{:S(2)}) async-start(), calls=%async_computation.3 | async-start | bytes 10948608 | tf_op jit(solution)/shard_map/all_gather | solution.py:104
  182.2 444.7 %all-gather.21.cloned.1.call-start = ((), (), s32[]{:S(2)}) async-start(), calls=%async_computation.5 | async-start | bytes 5898240 | tf_op jit(solution)/shard_map/all_gather | solution.py:300
  569.7 1205.7 %reduce-scatter.13.cloned.1.call-start = ((), (), s32[]{:S(2)}) async-start(), calls=%async_computation.11 | async-start | bytes 10948608
  698.2 1077.2 %reduce-scatter.11.cloned.1.call-start = ((), (), s32[]{:S(2)}) async-start(), calls=%async_computation.6 | async-start | bytes 21897216 | tf_op jit(solution)/shard_map/reduce_scatter | solution.py:337
  1434.2 73.4 %collective-permute-start.7 = (f32[36,3456]{1,0:T(8,128)S(1)}, f32[36,3456]{1,0:T(8,128)S(1)}, u32[]{:S(2)}, u32[]{:S(2)}) collective-permute-start(f32[36,3456]{1,0:T(8,128)S(1)} %slice.70), channel_id=1, source_target_pairs={{0,8},{1,9},{2,10},{3,11},{4,12},{5,13},{6,14},{7,15},{8,16},{9,17... | collective-permute-start | bytes 1493000
  1438.2 32.0 %collective-permute-start.13 = (f32[48,1152]{1,0:T(8,128)S(1)}, f32[48,1152]{1,0:T(8,128)S(1)}, u32[]{:S(2)}, u32[]{:S(2)}) collective-permute-start(f32[48,1152]{1,0:T(8,128)S(1)} %get-tuple-element.999), channel_id=1, source_target_pairs={{0,6},{1,7},{2,8},{3,9},{4,10},{5,11},{6,12},{7,13},{8,14},{9,15},... | collective-permute-start | bytes 663560
  1441.6 38.0 %collective-permute-start.12 = (f32[48,1152]{1,0:T(8,128)S(1)}, f32[48,1152]{1,0:T(8,128)S(1)}, u32[]{:S(2)}, u32[]{:S(2)}) collective-permute-start(f32[48,1152]{1,0:T(8,128)S(1)} %get-tuple-element.999), channel_id=1, source_target_pairs={{0,5},{1,6},{2,7},{3,8},{4,9},{5,10},{6,11},{7,12},{8,13},{9,14},{... | collective-permute-start | bytes 663560
  1481.7 43.3 %collective-permute-start.6 = (f32[48,3456]{1,0:T(8,128)S(1)}, f32[48,3456]{1,0:T(8,128)S(1)}, u32[]{:S(2)}, u32[]{:S(2)}) collective-permute-start(f32[48,3456]{1,0:T(8,128)S(1)} %get-tuple-element.998), channel_id=1, source_target_pairs={{0,7},{1,8},{2,9},{3,10},{4,11},{5,12},{6,13},{7,14},{8,15},{9,16}... | collective-permute-start | bytes 1990664
  1487.4 42.2 %collective-permute-start.5 = (f32[48,3456]{1,0:T(8,128)S(1)}, f32[48,3456]{1,0:T(8,128)S(1)}, u32[]{:S(2)}, u32[]{:S(2)}) collective-permute-start(f32[48,3456]{1,0:T(8,128)S(1)} %get-tuple-element.998), channel_id=1, source_target_pairs={{0,6},{1,7},{2,8},{3,9},{4,10},{5,11},{6,12},{7,13},{8,14},{9,15},... | collective-permute-start | bytes 1990664
  1499.4 41.3 %collective-permute-start.4 = (f32[48,3456]{1,0:T(8,128)S(1)}, f32[48,3456]{1,0:T(8,128)S(1)}, u32[]{:S(2)}, u32[]{:S(2)}) collective-permute-start(f32[48,3456]{1,0:T(8,128)S(1)} %get-tuple-element.998), channel_id=1, source_target_pairs={{0,5},{1,6},{2,7},{3,8},{4,9},{5,10},{6,11},{7,12},{8,13},{9,14},{... | collective-permute-start | bytes 1990664
  1500.7 42.5 %collective-permute-start.3 = (f32[48,3456]{1,0:T(8,128)S(1)}, f32[48,3456]{1,0:T(8,128)S(1)}, u32[]{:S(2)}, u32[]{:S(2)}) collective-permute-start(f32[48,3456]{1,0:T(8,128)S(1)} %get-tuple-element.998), channel_id=1, source_target_pairs={{0,4},{1,5},{2,6},{3,7},{4,8},{5,9},{6,10},{7,11},{8,12},{9,13},{1... | collective-permute-start | bytes 1990664
  1507.7 72.5 %collective-permute-start.2 = (f32[48,3456]{1,0:T(8,128)S(1)}, f32[48,3456]{1,0:T(8,128)S(1)}, u32[]{:S(2)}, u32[]{:S(2)}) collective-permute-start(f32[48,3456]{1,0:T(8,128)S(1)} %get-tuple-element.998), channel_id=1, source_target_pairs={{0,3},{1,4},{2,5},{3,6},{4,7},{5,8},{6,9},{7,10},{8,11},{9,12},{10... | collective-permute-start | bytes 1990664
  1525.0 194.3 %collective-permute-start.1 = (f32[48,3456]{1,0:T(8,128)S(1)}, f32[48,3456]{1,0:T(8,128)}, u32[]{:S(2)}, u32[]{:S(2)}) collective-permute-start(f32[48,3456]{1,0:T(8,128)S(1)} %get-tuple-element.998), channel_id=1, source_target_pairs={{0,2},{1,3},{2,4},{3,5},{4,6},{5,7},{6,8},{7,9},{8,10},{9,11},{10,... | collective-permute-start | bytes 1990664
  1529.5 192.4 %collective-permute-start = (f32[48,3456]{1,0:T(8,128)S(1)}, f32[48,3456]{1,0:T(8,128)}, u32[]{:S(2)}, u32[]{:S(2)}) collective-permute-start(f32[48,3456]{1,0:T(8,128)S(1)} %get-tuple-element.998), channel_id=1, source_target_pairs={{0,1},{1,2},{2,3},{3,4},{4,5},{5,6},{6,7},{7,8},{8,9},{9,10},{10,1... | collective-permute-start | bytes 1990664
  1540.7 220.0 %collective-permute-start.18 = (f32[40,4608]{1,0:T(8,128)S(1)}, f32[40,4608]{1,0:T(8,128)S(1)}, u32[]{:S(2)}, u32[]{:S(2)}) collective-permute-start(f32[40,4608]{1,0:T(8,128)S(1)} %get-tuple-element.1000), channel_id=1, source_target_pairs={{0,3},{1,4},{2,5},{3,6},{4,7},{5,8},{6,9},{7,10},{8,11},{9,12},{10... | collective-permute-start | bytes 2211848
  1543.2 217.5 %collective-permute-start.17 = (f32[40,4608]{1,0:T(8,128)S(1)}, f32[40,4608]{1,0:T(8,128)S(1)}, u32[]{:S(2)}, u32[]{:S(2)}) collective-permute-start(f32[40,4608]{1,0:T(8,128)S(1)} %get-tuple-element.1000), channel_id=1, source_target_pairs={{0,2},{1,3},{2,4},{3,5},{4,6},{5,7},{6,8},{7,9},{8,10},{9,11},{10,... | collective-permute-start | bytes 2211848
  1580.2 182.2 %collective-permute-start.16 = (f32[40,4608]{1,0:T(8,128)S(1)}, f32[40,4608]{1,0:T(8,128)}, u32[]{:S(2)}, u32[]{:S(2)}) collective-permute-start(f32[40,4608]{1,0:T(8,128)S(1)} %get-tuple-element.1000), channel_id=1, source_target_pairs={{0,1},{1,2},{2,3},{3,4},{4,5},{5,6},{6,7},{7,8},{8,9},{9,10},{10,1... | collective-permute-start | bytes 2211848
  1719.3 41.4 %collective-permute-start.19 = (f32[4,4608]{1,0:T(4,128)}, f32[4,4608]{1,0:T(4,128)S(1)}, u32[]{:S(2)}, u32[]{:S(2)}) collective-permute-start(f32[4,4608]{1,0:T(4,128)} %slice.72), channel_id=1, source_target_pairs={{0,4},{1,5},{2,6},{3,7},{4,8},{5,9},{6,10},{7,11},{8,12},{9,13},{1... | collective-permute-start | bytes 221192
  (61 other events, 2349.8 us)
Sparse Core Ops, SparseCore 0:
  10.9 68.3 all-gather.14
  82.1 78.4 all-gather.24
  163.5 57.5 all-gather.26
  224.0 91.0 all-gather.28
  317.2 54.3 all-gather.18
  373.6 60.2 all-gather.22
  437.0 86.0 all-gather.16
  569.8 54.8 all-gather.20
  698.3 184.8 reduce-scatter.12
  890.1 329.2 reduce-scatter.10
where the time goes:
time: 1790 us; the launch traced here: 1780 us
  blocking collectives  854 us (48%)
  waiting for transfers between devices  365 us (20%)
  local copies, waits for them, and re-layouts  195 us (11%)
  matrix products  189 us (11%)
  starting transfers between devices  141 us (8%)
  other arithmetic  23 us (1%)
    unnamed x3, blocking collectives  824 us
    unnamed x126, local copies, waits for them, and re-layouts  153 us
    unnamed x21, starting transfers between devices  141 us
    all_gather x1, waiting for transfers between devices, on_device(): lax.all_gather(fc1_w, ('dp', 'seq'), axis=0, tiled=True)  82.7 us
    all_gather x1, waiting for transfers between devices, on_device(): lax.all_gather(qkv_w, ('dp', 'seq'), axis=0, tiled=True)  77.2 us
    all_gather x1, waiting for transfers between devices, on_device(): lax.all_gather(pairs, 'seq', axis=1, tiled=True)  54.4 us
    dot_general x5, matrix products, inner(): lax.dot_general(left, right, (((0,), (0,)), ((), ())), preferred_element_...  43.8 us
    all_gather x1, waiting for transfers between devices, on_device(): lax.all_gather(queries, 'seq', axis=1, tiled=True)  42.2 us
  transfers between devices with their start and end apart: 30, of which 9 were waited for; matrix products, arithmetic and copies ran while one was open for 55% of the time, Pallas kernels for 0%

commit v1 on v0

--- a/solution.py
+++ b/solution.py
@@ -38,8 +38,12 @@
 
 
 def segment_of(lengths, places):
-    ends = jnp.cumsum(lengths, axis=1)
-    return jnp.sum((ends[:, None, :] <= places[None, :, None]).astype(jnp.int32), axis=2)
+    running = jnp.zeros_like(lengths[:, :1])
+    passed = jnp.zeros((lengths.shape[0], places.shape[0]), jnp.int32)
+    for slot in range(lengths.shape[1]):
+        running = running + lengths[:, slot : slot + 1]
+        passed = passed + (running <= places[None, :]).astype(jnp.int32)
+    return passed
 
 
 def inner(left, right):

time: 1790 us -> 1800 us (level)
  transfers between devices with their start and end apart: 30 -> 30, of which waited for: 9 -> 9; matrix products, arithmetic and copies ran while one was open for 55% -> 56% of each run, Pallas kernels for 0% -> 0%
where the time goes in v1:
time: 1800 us; the launch traced here: 1790 us
  blocking collectives  865 us (48%)
  waiting for transfers between devices  358 us (20%)
  local copies, waits for them, and re-layouts  195 us (11%)
  matrix products  188 us (10%)
  starting transfers between devices  131 us (7%)
  other arithmetic  31.8 us (2%)
  between operations  18.6 us (1%)
    unnamed x3, blocking collectives  836 us
    unnamed x126, local copies, waits for them, and re-layouts  153 us
    unnamed x21, starting transfers between devices  130 us
    all_gather x1, waiting for transfers between devices, on_device(): lax.all_gather(fc1_w, ('dp', 'seq'), axis=0, tiled=True)  82.7 us
    all_gather x1, waiting for transfers between devices, on_device(): lax.all_gather(qkv_w, ('dp', 'seq'), axis=0, tiled=True)  77.2 us
    all_gather x1, waiting for transfers between devices, on_device(): lax.all_gather(pairs, 'seq', axis=1, tiled=True)  54.4 us
    dot_general x5, matrix products, inner(): lax.dot_general(left, right, (((0,), (0,)), ((), ())), preferred_element_...  43.9 us
    all_gather x1, waiting for transfers between devices, on_device(): lax.all_gather(queries, 'seq', axis=1, tiled=True)  42.2 us
  transfers between devices with their start and end apart: 30, of which 9 were waited for; matrix products, arithmetic and copies ran while one was open for 56% of the time, Pallas kernels for 0%

profile of v1, /device:TPU:0, one launch (start us, length us, event | category | flops | bytes accessed | tf_op | source)
XLA Modules:
  0.0 1789.7 jit_solution(16507711431853596058)
XLA Ops:
  16.8 43.5 %all-reduce.24 = (bf16[1152]{0:T(1024)(128)(2,1)S(1)}, bf16[1152]{0:T(1024)(128)(2,1)S(1)}, bf16[1152]{0:T(1024)(128)(2,1)S(1)}, bf16[1152]{0:T(1024)(128)(2,1)S...) all-reduce(bf16[1152]{0:T(1024)(128)(2,1)S(1)} %dynamic-update-slic, ...), channel_id=1, replica_groups=mesh['dp'=4,'seq'=8] {'dp','seq'}, use_global_device_ids=true, to_apply=%add | all-reduce | flops 12672 | bytes 50688
  60.4 18.9 %all-gather.15.cloned.1.call-done = bf16[2304,1152]{1,0:T(8,128)(2,1)} async-done(((bf16[72,1152]{1,0:T(8,128)(2,1)}), bf16[2304,1152]{1,0:T(8,128)(2,1)}) %all-gather.15.cloned.1.call-update) | async-done | bytes 5308432 | tf_op jit(solution)/shard_map/all_gather | solution.py:104
  83.5 77.2 %all-gather.25.cloned.1.call-done = bf16[32,36,3456]{2,1,0:T(8,128)(2,1)} async-done(((bf16[1,36,3456]{2,1,0:T(8,128)(2,1)}), bf16[32,36,3456]{2,1,0:T(8,128)(2,1)}) %all-gather.25.cloned.1.call-update) | async-done | bytes 7962640 | tf_op jit(solution)/shard_map/all_gather | solution.py:105
  160.7 12.5 reshape.751
  186.5 34.6 %all-gather.27.cloned.1.call-done = bf16[32,36,1152]{2,1,0:T(8,128)(2,1)} async-done(((bf16[1,36,1152]{2,1,0:T(8,128)(2,1)}), bf16[32,36,1152]{2,1,0:T(8,128)(2,1)}) %all-gather.27.cloned.1.call-update) | async-done | bytes 2654224 | tf_op jit(solution)/shard_map/all_gather | solution.py:106
  232.4 82.7 %all-gather.29.cloned.1.call-done = bf16[32,36,4608]{2,1,0:T(8,128)(2,1)} async-done(((bf16[1,36,4608]{2,1,0:T(8,128)(2,1)}), bf16[32,36,4608]{2,1,0:T(8,128)(2,1)}) %all-gather.29.cloned.1.call-update) | async-done | bytes 10616848 | tf_op jit(solution)/shard_map/all_gather | solution.py:107
  315.1 14.3 reshape.755
  329.4 42.2 %all-gather.19.cloned.1.call-done = bf16[1,1280,16,72]{3,2,0,1:T(8,128)(2,1)} async-done(((bf16[1,160,16,72]{3,2,0,1:T(8,128)(2,1)}), bf16[1,1280,16,72]{3,2,0,1:T(8,128)(2,1)}) %all-gather.19.cloned.1.call-update) | async-done | bytes 2949136 | tf_op jit(solution)/shard_map/all_gather | solution.py:303
  379.5 54.4 %all-gather.23.cloned.1.call-done = bf16[1280,2304]{1,0:T(8,128)(2,1)} async-done(((bf16[160,2304]{1,0:T(8,128)(2,1)}), bf16[1280,2304]{1,0:T(8,128)(2,1)}) %all-gather.23.cloned.1.call-update) | async-done | bytes 5898256 | tf_op jit(solution)/shard_map/all_gather | solution.py:180
  442.9 33.4 %while.51 = (s32[]{:T(128)}, f32[1,16,160]{2,1,0:T(8,128)S(1)}, f32[1,16,160]{2,1,0:T(8,128)S(1)}, f32[1,160,16,72]{1,3,2,0:T(8,128)}, s32[1,5]{1,0:T(1,128)S(1)...) while((s32[]{:T(128)}, f32[1,16,160]{2,1,0:T(8,128)S(1)}, ...), condition=%wide.region_5.6_spmd.clone, body=%wide.region_2.5_spmd.clone.sunk | while | flops 197878880 | bytes 19476100 | solution.py:74
  495.7 27.4 %all-gather.17.cloned.1.call-done = bf16[4608,1152]{1,0:T(8,128)(2,1)} async-done(((bf16[144,1152]{1,0:T(8,128)(2,1)}), bf16[4608,1152]{1,0:T(8,128)(2,1)}) %all-gather.17.cloned.1.call-update) | async-done | bytes 10616848 | tf_op jit(solution)/shard_map/all_gather | solution.py:108
  523.1 12.5 fusion.144
  554.3 15.0 all_gather.77
  569.8 14.3 all-gather.5
  584.4 43.3 %while.52 = (s32[]{:T(128)}, f32[1,160,16,72]{1,3,2,0:T(8,128)}, bf16[1,1280,2304]{1,2,0:T(8,128)(2,1)}, s32[1,5]{1,0:T(1,128)S(1)}, s32[1,1]{1,0:T(1,128)}, /*i...) while((s32[]{:T(128)}, f32[1,160,16,72]{1,3,2,0:T(8,128)}, ...), condition=%wide.region_12.13_spmd.clone, body=%wide.region_11.12_spmd.clone.sunk | while | flops 288118880 | bytes 14048877 | solution.py:74
  637.8 49.4 %while.53 = (s32[]{:T(128)}, f32[1,160,16,72]{1,3,2,0:T(8,128)}, f32[1,160,16,72]{1,3,2,0:T(8,128)}, bf16[1,1280,16,72]{1,3,2,0:T(8,128)(2,1)}, s32[1,5]{1,0:T(1...) while((s32[]{:T(128)}, f32[1,160,16,72]{1,3,2,0:T(8,128)}, ...), condition=%wide.region_14.15_spmd.clone, body=%wide.region_13.14_spmd.clone.sunk | while | flops 385480800 | bytes 15258705 | solution.py:74
  705.5 15.3 fusion.121
  743.8 696.7 %fusion.137 = (f32[48,3456]{1,0:T(8,128)S(1)}, f32[48,1152]{1,0:T(8,128)S(1)}, f32[40,4608]{1,0:T(8,128)S(1)}) fusion(f32[1152,3456]{1,0:T(8,128)} %fusion.113, f32[1152,1152]{1,0:T(8,128)} %fusion.130, f32[1152,4608]{1,0:T(8,128)} %fusion.115), kind=kCustom, calls=%all-reduce-scatter.3 | all-reduce-scatter fusion | flops 12976130 | bytes 44089344
  1453.4 16.2 collective-permute-done.15
  1490.1 12.2 collective-permute-start.5
  1545.4 49.2 %collective-permute-start.17 = (f32[40,4608]{1,0:T(8,128)S(1)}, f32[40,4608]{1,0:T(8,128)S(1)}, u32[]{:S(2)}, u32[]{:S(2)}) collective-permute-start(f32[40,4608]{1,0:T(8,128)S(1)} %get-tuple-element.1213), channel_id=1, source_target_pairs={{0,2},{1,3},{2,4},{3,5},{4,6},{5,7},{6,8},{7,9},{8,10},{9,11},{10,... | collective-permute-start | bytes 2211848
  1604.0 95.8 %all-reduce.23 = (f32[1152]{0:T(1024)}, f32[1152]{0:T(1024)}, f32[1152]{0:T(1024)}, f32[1152]{0:T(1024)}, f32[1152]{0:T(1024)}, /*index=5*/f32[1152]{0:T(1024)}, f32[4608]{0:T(1024)}, f32[1152]{0:T(1024)}) all-reduce(f32[1152]{0:T(1024)} %get-tuple-element.1218, ...), channel_id=9, replica_groups=mesh['dp'=4,'seq'=8] {'dp','seq'}, use_global_device_ids=true, to_apply=%region_23.24.clone | all-reduce | flops 12672 | bytes 101376
  1710.1 14.6 concatenate.15
  1729.0 36.8 %concatenate.14 = f32[420,3456]{1,0:T(8,128)} concatenate(f32[36,3456]{1,0:T(8,128)} %copy-done.26, f32[48,3456]{1,0:T(8,128)} %copy-done.21, f32[48,3456]{1,0:T(8,128)} %copy-done.22, f32[48,3456]{1,0:T(8,128)} %copy-done.23, f32[48,3456]{1,0:T(8,128)} %copy-done.24, f32[48,3456]{1,0:T(8,128)} %copy-done.25, f32[48,3456]{1,0:T(8,128)} %collective-permute-done.1, ...), dimensions={0} | concatenate | bytes 11612160
  (388 shorter events, 383.9 us)
Async XLA Ops:
  7.2 72.1 %all-gather.15.cloned.1.call-start = ((), (), s32[]{:S(2)}) async-start(), calls=%async_computation.2 | async-start | bytes 5474304 | tf_op jit(solution)/shard_map/all_gather | solution.py:104
  7.9 152.8 %all-gather.25.cloned.1.call-start = ((), (), s32[]{:S(2)}) async-start(), calls=%async_computation.8 | async-start | bytes 9123840 | tf_op jit(solution)/shard_map/all_gather | solution.py:105
  8.7 212.4 %all-gather.27.cloned.1.call-start = ((), (), s32[]{:S(2)}) async-start(), calls=%async_computation.9 | async-start | bytes 3041280 | tf_op jit(solution)/shard_map/all_gather | solution.py:106
  9.4 305.7 %all-gather.29.cloned.1.call-start = ((), (), s32[]{:S(2)}) async-start(), calls=%async_computation.10 | async-start | bytes 12165120 | tf_op jit(solution)/shard_map/all_gather | solution.py:107
  10.0 361.6 %all-gather.19.cloned.1.call-start = ((), (), s32[]{:S(2)}) async-start(), calls=%async_computation.4 | async-start | bytes 5898240 | tf_op jit(solution)/shard_map/all_gather | solution.py:303
  180.2 253.7 %all-gather.23.cloned.1.call-start = ((), (), s32[]{:S(2)}) async-start(), calls=%async_computation.7 | async-start | bytes 6635520 | tf_op jit(solution)/shard_map/all_gather | solution.py:180
  181.5 341.6 %all-gather.17.cloned.1.call-start = ((), (), s32[]{:S(2)}) async-start(), calls=%async_computation.3 | async-start | bytes 10948608 | tf_op jit(solution)/shard_map/all_gather | solution.py:108
  182.3 447.6 %all-gather.21.cloned.1.call-start = ((), (), s32[]{:S(2)}) async-start(), calls=%async_computation.5 | async-start | bytes 5898240 | tf_op jit(solution)/shard_map/all_gather | solution.py:304
  569.7 1212.7 %reduce-scatter.13.cloned.1.call-start = ((), (), s32[]{:S(2)}) async-start(), calls=%async_computation.11 | async-start | bytes 10948608
  704.5 1077.9 %reduce-scatter.11.cloned.1.call-start = ((), (), s32[]{:S(2)}) async-start(), calls=%async_computation.6 | async-start | bytes 21897216 | tf_op jit(solution)/shard_map/reduce_scatter | solution.py:341
  1440.6 73.6 %collective-permute-start.7 = (f32[36,3456]{1,0:T(8,128)S(1)}, f32[36,3456]{1,0:T(8,128)S(1)}, u32[]{:S(2)}, u32[]{:S(2)}) collective-permute-start(f32[36,3456]{1,0:T(8,128)S(1)} %slice.200), channel_id=1, source_target_pairs={{0,8},{1,9},{2,10},{3,11},{4,12},{5,13},{6,14},{7,15},{8,16},{9,17... | collective-permute-start | bytes 1493000
  1444.7 30.0 %collective-permute-start.13 = (f32[48,1152]{1,0:T(8,128)S(1)}, f32[48,1152]{1,0:T(8,128)S(1)}, u32[]{:S(2)}, u32[]{:S(2)}) collective-permute-start(f32[48,1152]{1,0:T(8,128)S(1)} %get-tuple-element.1212), channel_id=1, source_target_pairs={{0,6},{1,7},{2,8},{3,9},{4,10},{5,11},{6,12},{7,13},{8,14},{9,15},... | collective-permute-start | bytes 663560
  1447.9 31.8 %collective-permute-start.12 = (f32[48,1152]{1,0:T(8,128)S(1)}, f32[48,1152]{1,0:T(8,128)S(1)}, u32[]{:S(2)}, u32[]{:S(2)}) collective-permute-start(f32[48,1152]{1,0:T(8,128)S(1)} %get-tuple-element.1212), channel_id=1, source_target_pairs={{0,5},{1,6},{2,7},{3,8},{4,9},{5,10},{6,11},{7,12},{8,13},{9,14},{... | collective-permute-start | bytes 663560
  1484.3 47.2 %collective-permute-start.6 = (f32[48,3456]{1,0:T(8,128)S(1)}, f32[48,3456]{1,0:T(8,128)S(1)}, u32[]{:S(2)}, u32[]{:S(2)}) collective-permute-start(f32[48,3456]{1,0:T(8,128)S(1)} %get-tuple-element.1211), channel_id=1, source_target_pairs={{0,7},{1,8},{2,9},{3,10},{4,11},{5,12},{6,13},{7,14},{8,15},{9,16}... | collective-permute-start | bytes 1990664
  1490.1 45.4 %collective-permute-start.5 = (f32[48,3456]{1,0:T(8,128)S(1)}, f32[48,3456]{1,0:T(8,128)S(1)}, u32[]{:S(2)}, u32[]{:S(2)}) collective-permute-start(f32[48,3456]{1,0:T(8,128)S(1)} %get-tuple-element.1211), channel_id=1, source_target_pairs={{0,6},{1,7},{2,8},{3,9},{4,10},{5,11},{6,12},{7,13},{8,14},{9,15},... | collective-permute-start | bytes 1990664
  1502.3 40.4 %collective-permute-start.4 = (f32[48,3456]{1,0:T(8,128)S(1)}, f32[48,3456]{1,0:T(8,128)S(1)}, u32[]{:S(2)}, u32[]{:S(2)}) collective-permute-start(f32[48,3456]{1,0:T(8,128)S(1)} %get-tuple-element.1211), channel_id=1, source_target_pairs={{0,5},{1,6},{2,7},{3,8},{4,9},{5,10},{6,11},{7,12},{8,13},{9,14},{... | collective-permute-start | bytes 1990664
  1506.2 39.2 %collective-permute-start.3 = (f32[48,3456]{1,0:T(8,128)S(1)}, f32[48,3456]{1,0:T(8,128)S(1)}, u32[]{:S(2)}, u32[]{:S(2)}) collective-permute-start(f32[48,3456]{1,0:T(8,128)S(1)} %get-tuple-element.1211), channel_id=1, source_target_pairs={{0,4},{1,5},{2,6},{3,7},{4,8},{5,9},{6,10},{7,11},{8,12},{9,13},{1... | collective-permute-start | bytes 1990664
  1514.2 80.3 %collective-permute-start.2 = (f32[48,3456]{1,0:T(8,128)S(1)}, f32[48,3456]{1,0:T(8,128)S(1)}, u32[]{:S(2)}, u32[]{:S(2)}) collective-permute-start(f32[48,3456]{1,0:T(8,128)S(1)} %get-tuple-element.1211), channel_id=1, source_target_pairs={{0,3},{1,4},{2,5},{3,6},{4,7},{5,8},{6,9},{7,10},{8,11},{9,12},{10... | collective-permute-start | bytes 1990664
  1531.5 194.8 %collective-permute-start.1 = (f32[48,3456]{1,0:T(8,128)S(1)}, f32[48,3456]{1,0:T(8,128)}, u32[]{:S(2)}, u32[]{:S(2)}) collective-permute-start(f32[48,3456]{1,0:T(8,128)S(1)} %get-tuple-element.1211), channel_id=1, source_target_pairs={{0,2},{1,3},{2,4},{3,5},{4,6},{5,7},{6,8},{7,9},{8,10},{9,11},{10,... | collective-permute-start | bytes 1990664
  1535.6 193.4 %collective-permute-start = (f32[48,3456]{1,0:T(8,128)S(1)}, f32[48,3456]{1,0:T(8,128)}, u32[]{:S(2)}, u32[]{:S(2)}) collective-permute-start(f32[48,3456]{1,0:T(8,128)S(1)} %get-tuple-element.1211), channel_id=1, source_target_pairs={{0,1},{1,2},{2,3},{3,4},{4,5},{5,6},{6,7},{7,8},{8,9},{9,10},{10,1... | collective-permute-start | bytes 1990664
  1542.7 225.0 %collective-permute-start.18 = (f32[40,4608]{1,0:T(8,128)S(1)}, f32[40,4608]{1,0:T(8,128)S(1)}, u32[]{:S(2)}, u32[]{:S(2)}) collective-permute-start(f32[40,4608]{1,0:T(8,128)S(1)} %get-tuple-element.1213), channel_id=1, source_target_pairs={{0,3},{1,4},{2,5},{3,6},{4,7},{5,8},{6,9},{7,10},{8,11},{9,12},{10... | collective-permute-start | bytes 2211848
  1545.4 222.4 %collective-permute-start.17 = (f32[40,4608]{1,0:T(8,128)S(1)}, f32[40,4608]{1,0:T(8,128)S(1)}, u32[]{:S(2)}, u32[]{:S(2)}) collective-permute-start(f32[40,4608]{1,0:T(8,128)S(1)} %get-tuple-element.1213), channel_id=1, source_target_pairs={{0,2},{1,3},{2,4},{3,5},{4,6},{5,7},{6,8},{7,9},{8,10},{9,11},{10,... | collective-permute-start | bytes 2211848
  1594.5 174.9 %collective-permute-start.16 = (f32[40,4608]{1,0:T(8,128)S(1)}, f32[40,4608]{1,0:T(8,128)}, u32[]{:S(2)}, u32[]{:S(2)}) collective-permute-start(f32[40,4608]{1,0:T(8,128)S(1)} %get-tuple-element.1213), channel_id=1, source_target_pairs={{0,1},{1,2},{2,3},{3,4},{4,5},{5,6},{6,7},{7,8},{8,9},{9,10},{10,1... | collective-permute-start | bytes 2211848
  1726.4 41.3 %collective-permute-start.19 = (f32[4,4608]{1,0:T(4,128)}, f32[4,4608]{1,0:T(4,128)S(1)}, u32[]{:S(2)}, u32[]{:S(2)}) collective-permute-start(f32[4,4608]{1,0:T(4,128)} %slice.202), channel_id=1, source_target_pairs={{0,4},{1,5},{2,6},{3,7},{4,8},{5,9},{6,10},{7,11},{8,12},{9,13},{1... | collective-permute-start | bytes 221192
  (61 other events, 2252.9 us)
Sparse Core Ops, SparseCore 0:
  10.9 68.3 all-gather.14
  82.1 78.4 all-gather.24
  163.5 57.5 all-gather.26
  224.0 91.0 all-gather.28
  317.2 54.3 all-gather.18
  373.6 60.2 all-gather.22
  437.0 86.0 all-gather.16
  569.8 55.0 all-gather.20
  704.7 184.8 reduce-scatter.12
  896.4 329.2 reduce-scatter.10

commit v2 on v0

v2 whole, which is shorter than its diff:
```python
from functools import partial

import jax
import jax.numpy as jnp
from jax import lax
from jax.sharding import PartitionSpec as P

HEADS = 16
HEAD_DIM = 72
EPSILON = 1e-05
NEGATIVE = -1e30
F32 = jnp.float32
BF16 = jnp.bfloat16


def norm_pieces(hvals):
    centered = hvals - jnp.mean(hvals, axis=-1, keepdims=True)
    inverse = lax.rsqrt(jnp.mean(centered * centered, axis=-1, keepdims=True) + EPSILON)
    return centered * inverse, inverse


def norm_back(incoming, standardized, inverse, gain):
    scaled = incoming * gain
    passed = inverse * (
        scaled
        - jnp.mean(scaled, axis=-1, keepdims=True)
        - standardized * jnp.mean(scaled * standardized, axis=-1, keepdims=True)
    )
    return passed, jnp.sum(incoming * standardized, axis=0), jnp.sum(incoming, axis=0)


def segment_of(lengths, places):
    running = jnp.zeros((), jnp.int32)
    passed = jnp.zeros(places.shape, jnp.int32)
    for slot in range(lengths.shape[1]):
        running = running + lengths[0, slot]
        passed = passed + (running <= places).astype(jnp.int32)
    return passed


def dot(left, right):
    return jnp.dot(left, right, preferred_element_type=F32)


def inner(left, right):
    return lax.dot_general(left, right, (((0,), (0,)), ((), ())), preferred_element_type=F32)


def times_transposed(left, right):
    return lax.dot_general(left, right, (((1,), (1,)), ((), ())), preferred_element_type=F32)


def on_device(
    nd, ns,
    inputs, skipped, item_lengths,
    skip_w, qkv_w, proj_w, fc1_w, fc2_w,
    skip_b, ln1_g, ln1_b, proj_b, ln2_g, ln2_b, fc1_b, fc2_b,
    cotangent,
):
    _, local, features = inputs.shape
    hidden_units = fc1_w.shape[1]
    n = nd * ns
    row_len = local * ns
    heads = HEADS // ns
    head_cols = heads * HEAD_DIM
    scale = HEAD_DIM ** (-0.5)
    dp_at = lax.axis_index("dp")
    hidden_part = hidden_units // nd
    joined_part = 2 * features // nd

    def swap(v, k):
        return lax.ppermute(v, "dp", [(i, i ^ k) for i in range(nd)])

    def gather_rows(v):
        return jnp.concatenate([v] + [swap(v, k) for k in range(1, nd)], axis=0)

    def add_rows(partial_sums):
        own = partial_sums[:local]
        low = partial_sums.astype(BF16)
        for k in range(1, nd):
            own = own + swap(low[k * local : (k + 1) * local], k).astype(F32)
        return own

    def seq_exchange(v):
        return lax.all_to_all(v, "seq", 0, 0, tiled=True)

    skip_part = lax.all_gather(skip_w, "seq", axis=0, tiled=True)

    own_vectors = (skip_b, ln1_g, ln1_b, proj_b, ln2_g, ln2_b, fc2_b, fc1_b)
    packed = jnp.concatenate(own_vectors)
    own_size = packed.shape[0]
    padded = -(-own_size // 1024) * 1024
    packed = jnp.pad(packed, (0, padded - own_size)).reshape(padded // 128, 128)
    vectors = lax.all_gather(packed, ("dp", "seq"), axis=0, tiled=True).reshape(n, padded)
    vectors = vectors.astype(F32)
    small = features // n

    def vector(index):
        return vectors[:, index * small : (index + 1) * small].reshape(features)

    b_skip, g_one, b_one, b_proj, g_two, b_two, b_down = (vector(i) for i in range(7))
    up_bias = lax.dynamic_slice_in_dim(vectors[:, 7 * small : own_size], dp_at * ns, ns, 0)
    up_bias = up_bias.reshape(hidden_part)

    joined = jnp.concatenate([inputs[0], skipped[0]], axis=1)
    joined_slices = jnp.swapaxes(joined.reshape(local, nd, joined_part), 0, 1)
    joined_blocks = []
    for k in range(nd):
        away = lax.dynamic_index_in_dim(joined_slices, dp_at ^ k, 0, keepdims=False)
        joined_blocks.append(away if k == 0 else swap(away, k))
    joined_here = jnp.concatenate(joined_blocks, axis=0)
    first = add_rows(dot(joined_here, skip_part)) + b_skip
    xhat_one, inverse_one = norm_pieces(first)
    normed_one = (xhat_one * g_one + b_one).astype(BF16)

    qkv_mine = seq_exchange(
        qkv_w.reshape(features // n, 3, ns, head_cols).transpose(2, 0, 1, 3)
        .reshape(ns, features // n, 3 * head_cols)
    )
    qkv_mine = lax.all_gather(
        qkv_mine.reshape(features // nd, 3 * head_cols), "dp", axis=0, tiled=True
    )
    normed_one_row = lax.all_gather(normed_one, "seq", axis=0, tiled=True)
    triple = dot(normed_one_row, qkv_mine).astype(BF16)
    queries, keys, values = (
        jnp.swapaxes(
            triple[:, i * head_cols : (i + 1) * head_cols].reshape(row_len, heads, HEAD_DIM), 0, 1
        )
        for i in range(3)
    )
    segments = segment_of(item_lengths, jnp.arange(row_len, dtype=jnp.int32))
    allowed = (segments[:, None] == segments[None, :])[None]

    def head_dot(spec, left, right):
        return jnp.einsum(spec, left, right, preferred_element_type=F32)

    logits = jnp.where(allowed, head_dot("hqd,hkd->hqk", queries, keys) * scale, NEGATIVE)
    top = jnp.max(logits, axis=2, keepdims=True)
    total = jnp.sum(jnp.exp(logits - top), axis=2, keepdims=True)
    lse = top + jnp.log(total)
    probs_low = jnp.exp(logits - lse).astype(BF16)
    attended_heads = head_dot("hqk,hkd->hqd", probs_low, values)

    def heads_to_tokens(v):
        v = jnp.swapaxes(v.astype(BF16), 0, 1).reshape(ns, local, head_cols)
        return jnp.swapaxes(seq_exchange(v), 0, 1).reshape(local, features)

    def tokens_to_heads(v):
        v = seq_exchange(jnp.swapaxes(v.reshape(local, ns, head_cols), 0, 1))
        return jnp.swapaxes(v.reshape(row_len, heads, HEAD_DIM), 0, 1)

    attended_low = heads_to_tokens(attended_heads)
    w_proj = lax.all_gather(proj_w, ("dp", "seq"), axis=0, tiled=True)
    second = first + dot(attended_low, w_proj) + b_proj
    xhat_two, inverse_two = norm_pieces(second)
    normed_two = (xhat_two * g_two + b_two).astype(BF16)

    up_slices = jnp.swapaxes(fc1_w.reshape(features // n, nd, hidden_part), 0, 1)
    up_part = lax.all_gather(
        lax.all_to_all(up_slices, "dp", 0, 0, tiled=True), "seq", axis=0, tiled=False
    )
    up_part = jnp.swapaxes(up_part, 0, 1).reshape(features, hidden_part)
    down_part = lax.all_gather(fc2_w, "seq", axis=0, tiled=True)
    grad_out = cotangent[0]
    grad_out_rows = gather_rows(grad_out)
    normed_two_rows = gather_rows(normed_two)
    pre = dot(normed_two_rows, up_part) + up_bias
    gelu_value, gelu_pull = jax.vjp(partial(jax.nn.gelu, approximate=False), pre)
    hidden = gelu_value.astype(BF16)
    output = second + add_rows(dot(hidden, down_part)) + b_down
    output = output.astype(BF16)[None]

    pre_grad = gelu_pull(times_transposed(grad_out_rows, down_part))[0]
    pre_low = pre_grad.astype(BF16)
    normed_two_grad = add_rows(times_transposed(pre_low, up_part))
    fc2_w_grad = lax.psum_scatter(
        inner(hidden, grad_out_rows).astype(BF16), "seq", scatter_dimension=0, tiled=True
    ).astype(F32)

    def by_seq(grad):
        grad = grad.reshape(nd, ns, features // n, grad.shape[1]).astype(BF16)
        grad = jnp.swapaxes(grad, 0, 1).reshape(features, grad.shape[3])
        grad = lax.psum_scatter(grad, "seq", scatter_dimension=0, tiled=True)
        return lax.all_to_all(
            grad.reshape(nd, features // n, grad.shape[1]), "dp", 0, 0, tiled=True
        )

    fc1_w_grad = jnp.swapaxes(by_seq(inner(normed_two_rows, pre_low)), 0, 1)
    fc1_w_grad = fc1_w_grad.reshape(features // n, hidden_units).astype(F32)
    through_two, ln2_g_grad, ln2_b_grad = norm_back(normed_two_grad, xhat_two, inverse_two, g_two)
    second_grad = grad_out.astype(F32) + through_two
    second_low = second_grad.astype(BF16)
    proj_w_grad = jnp.sum(by_seq(inner(attended_low, second_low)).astype(F32), axis=0)
    attended_grad = tokens_to_heads(times_transposed(second_low, w_proj).astype(BF16))
    delta = jnp.sum(attended_grad.astype(F32) * attended_heads, axis=2, keepdims=True)
    probs = jnp.exp(logits - lse)
    prob_grad = head_dot("hqd,hkd->hqk", attended_grad, values)
    logit_grad = (probs * (prob_grad - delta) * scale).astype(BF16)
    triple_grad = jnp.concatenate(
        [
            jnp.swapaxes(v, 0, 1).reshape(row_len, head_cols).astype(BF16)
            for v in (
                head_dot("hqk,hkd->hqd", logit_grad, keys),
                head_dot("hqk,hqd->hkd", logit_grad, queries),
                head_dot("hqk,hqd->hkd", probs.astype(BF16), attended_grad),
            )
        ],
        axis=1,
    )
    normed_one_grad = lax.psum_scatter(
        times_transposed(triple_grad, qkv_mine).astype(BF16), "seq", scatter_dimension=0, tiled=True
    ).astype(F32)
    qkv_terms = inner(normed_one_row, triple_grad).astype(BF16)
    qkv_terms = lax.all_to_all(
        qkv_terms.reshape(nd, features // nd, 3 * head_cols), "dp", 0, 0, tiled=True
    )
    qkv_terms = jnp.sum(qkv_terms.astype(F32), axis=0).astype(BF16)
    qkv_w_grad = seq_exchange(qkv_terms.reshape(ns, features // n, 3 * head_cols))
    qkv_w_grad = (
        qkv_w_grad.reshape(ns, features // n, 3, head_cols)
        .transpose(1, 2, 0, 3).reshape(features // n, 3 * features).astype(F32)
    )
    through_one, ln1_g_grad, ln1_b_grad = norm_back(normed_one_grad, xhat_one, inverse_one, g_one)
    first_grad = second_grad + through_one
    first_low_rows = gather_rows(first_grad.astype(BF16))
    skip_w_grad = lax.psum_scatter(
        inner(joined_here, first_low_rows).astype(BF16), "seq", scatter_dimension=0, tiled=True
    ).astype(F32)
    joined_grad_part = times_transposed(first_low_rows, skip_part).astype(BF16)
    away = []
    for k in range(nd):
        block = joined_grad_part[k * local : (k + 1) * local]
        away.append(block if k == 0 else swap(block, k))
    away = jnp.stack(away, axis=0)
    joined_grad = jnp.concatenate(
        [lax.dynamic_index_in_dim(away, dp_at ^ k, 0, keepdims=False) for k in range(nd)], axis=1
    ).astype(F32)
    input_grad = joined_grad[None, :, :features]
    skip_grad = joined_grad[None, :, features:]

    vector_grads = jnp.stack(
        [
            jnp.sum(first_grad, axis=0),
            ln1_g_grad,
            ln1_b_grad,
            jnp.sum(second_grad, axis=0),
            ln2_g_grad,
            ln2_b_grad,
            jnp.sum(grad_out.astype(F32), axis=0),
        ]
    )
    vector_grads = jnp.swapaxes(vector_grads.reshape(7, n, small), 0, 1).reshape(n, 7 * small)
    up_grads = jnp.sum(pre_grad, axis=0).reshape(ns, hidden_units // n)
    up_grads = lax.dynamic_update_slice_in_dim(
        jnp.zeros((n, hidden_units // n), F32), up_grads, dp_at * ns, 0
    )
    vector_grads = jnp.concatenate([vector_grads, up_grads], axis=1)
    vector_grads = jnp.pad(vector_grads, ((0, 0), (0, padded - own_size)))
    vector_grads = lax.all_to_all(
        vector_grads.reshape(n, padded // 128, 128), ("dp", "seq"), 0, 0, tiled=True
    )
    vector_grads = jnp.sum(vector_grads, axis=0).reshape(padded)
    skip_b_grad, ln1_g_grad, ln1_b_grad, proj_b_grad, ln2_g_grad, ln2_b_grad, fc2_b_grad = (
        vector_grads[i * small : (i + 1) * small] for i in range(7)
    )
    fc1_b_grad = vector_grads[7 * small : own_size]
    return (
        output, input_grad, skip_grad,
        skip_w_grad, qkv_w_grad, proj_w_grad, fc1_w_grad, fc2_w_grad,
        skip_b_grad, ln1_g_grad, ln1_b_grad, proj_b_grad, ln2_g_grad, ln2_b_grad,
        fc1_b_grad, fc2_b_grad,
    )


def solution(mesh):
    tokens = P("dp", "seq", None)
    matrix = P(("dp", "seq"), None)
    flat = P(("dp", "seq"))
    in_specs = (tokens, tokens, P("dp", None)) + (matrix,) * 5 + (flat,) * 8 + (tokens,)
    out_specs = (tokens,) * 3 + (matrix,) * 5 + (flat,) * 8
    return jax.shard_map(
        partial(on_device, mesh.shape["dp"], mesh.shape["seq"]),
        mesh=mesh, in_specs=in_specs, out_specs=out_specs, check_vma=False,
    )
```

time: 1790 us -> 577 us (0.32)
  blocking collectives: 854 us -> 105 us
  waiting for transfers between devices: 365 us -> 206 us
  local copies, waits for them, and re-layouts: 195 us -> 69.1 us
  matrix products: 189 us -> 85.9 us
  starting transfers between devices: 141 us -> 54 us
    unnamed x3 -> x0, blocking collectives: 824 us -> none
    all_gather x8 -> x5, waiting for transfers between devices: 344 us -> 61.9 us  [the longest x1 27 us: on_device(): w_proj = lax.all_gather(proj_w, ('dp', 'seq'), axis=0, tiled=True)]
    unnamed x126, local copies, waits for them, and re-layouts: 153 us -> 10.8 us
    unnamed x21 -> x1, starting transfers between devices: 141 us -> 0.01 us
    reduce_scatter x1 -> x4, waiting for transfers between devices: 0.01 us -> 73.8 us  [the longest x2 51.3 us: by_seq(): grad = lax.psum_scatter(grad, 'seq', scatter_dimension=0, tiled=True)]
    dot_general x40 -> x11, matrix products: 111 us -> 49.8 us  [the longest x5 24.9 us: dot(): return jnp.dot(left, right, preferred_element_type=F32)]
    all_to_all x0 -> x3, blocking collectives: none -> 49.6 us  [the longest x1 19.5 us: seq_exchange(): return lax.all_to_all(v, 'seq', 0, 0, tiled=True)]
    ppermute x0 -> x24, waiting for transfers between devices: none -> 46 us  [swap(): return lax.ppermute(v, 'dp', [(i, i ^ k) for i in range(nd)])]
  transfers between devices with their start and end apart: 30 -> 40, of which waited for: 9 -> 17; matrix products, arithmetic and copies ran while one was open for 55% -> 23% of each run, Pallas kernels for 0% -> 0%
where the time goes in v2:
time: 577 us; the launch traced here: 567 us
  waiting for transfers between devices  206 us (36%)
  blocking collectives  105 us (18%)
  matrix products  85.9 us (15%)
  local copies, waits for them, and re-layouts  69.1 us (12%)
  starting transfers between devices  54 us (9%)
  other arithmetic  28.1 us (5%)
  between operations  19.2 us (3%)
    reduce_scatter x2, waiting for transfers between devices, by_seq(): grad = lax.psum_scatter(grad, 'seq', scatter_dimension=0, tiled=True)  51.3 us
    ppermute x24, waiting for transfers between devices, swap(): return lax.ppermute(v, 'dp', [(i, i ^ k) for i in range(nd)])  46 us
    all_gather x1, blocking collectives, on_device(): lax.all_gather(packed, ('dp', 'seq'), axis=0, tiled=True).reshape(n, padded)  40.5 us
    ppermute x24, starting transfers between devices, swap(): return lax.ppermute(v, 'dp', [(i, i ^ k) for i in range(nd)])  31.1 us
    all_gather x1, waiting for transfers between devices, on_device(): w_proj = lax.all_gather(proj_w, ('dp', 'seq'), axis=0, tiled=True)  27 us
    dot_general x5, matrix products, dot(): return jnp.dot(left, right, preferred_element_type=F32)  24.9 us
    dot_general x6, matrix products, head_dot(): return jnp.einsum(spec, left, right, preferred_element_type=F32)  24.9 us
    all_gather x1, waiting for transfers between devices, on_device(): lax.all_gather(lax.all_to_all(up_slices, 'dp', 0, 0, tiled=True), 'seq',...  23 us
  transfers between devices with their start and end apart: 40, of which 17 were waited for; matrix products, arithmetic and copies ran while one was open for 23% of the time, Pallas kernels for 0%

profile of v2, /device:TPU:0, one launch (start us, length us, event | category | flops | bytes accessed | tf_op | source)
XLA Modules:
  0.0 567.4 jit_solution(14905473138180888491)
XLA Ops:
  10.9 8.2 %fusion.38 = (bf16[160,1,576]{2,1,0:T(2,128)(2,1)S(1)}, bf16[160,1,576]{2,1,0:T(2,128)(2,1)S(1)}, bf16[160,1,576]{2,1,0:T(2,128)(2,1)S(1)}, bf16[160,1,576]{2,1,0:T(2,128)(2,1)S(1)}) fusion(s32[]{:T(128)S(6)} %select_n.25, bf16[160,2,576]{2,1,0:T(2,128)(2,1)S(1)} %concatenate.33, bf16[160,2,576]{2,1,0:T(2,128)(2,1)S(1)} %concatenate.34, s32[]{:T(128)S(6)} %select_n.26, ...), kind=kLoop, calls=%fused_computation.104 | loop fusion | flops 1474560 | bytes 1474576 | tf_op jit(solution)/shard_map/concatenate | solution.py:105
  44.0 40.5 %all_gather.25 = bf16[256,128]{1,0:T(8,128)(2,1)S(1)} all-gather(bf16[8,128]{1,0:T(8,128)(2,1)S(1)} %pad_bitcast_fusion), channel_id=1, replica_groups=mesh['dp'=4,'seq'=8] {'dp','seq'}, dimensions={0}, use_global_device_ids=true | all-gather | bytes 67584 | tf_op jit(solution)/shard_map/all_gather | solution.py:94
  89.1 10.8 %all_to_all.45 = bf16[4,36,1152]{2,1,0:T(8,128)(2,1)} all-to-all(bf16[4,36,1152]{2,1,0:T(8,128)(2,1)S(1)} %copy.157), channel_id=1, replica_groups=mesh['dp'=4,'seq'=8] {'dp'}, dimensions={0} | all-to-all | bytes 663552 | tf_op jit(solution)/shard_map/all_to_all | solution.py:160
  112.7 12.7 %all-to-all-done = bf16[8,36,432]{2,1,0:T(8,128)(2,1)S(1)} async-done(((bf16[8,36,432]{2,1,0:T(8,128)(2,1)}), bf16[8,36,432]{2,1,0:T(8,128)(2,1)S(1)}, u32[]{:S(2)}, u32[]{:S(2)}) %all-to-all-start) | async-done | bytes 248864 | tf_op jit(solution)/shard_map/all_to_all | solution.py:85
  125.4 15.1 %all_gather.27 = bf16[1152,432]{1,0:T(8,128)(2,1)S(1)} all-gather(bf16[288,432]{1,0:T(8,128)(2,1)S(1)} %reshape.281), channel_id=1, replica_groups=mesh['dp'=4,'seq'=8] {'dp'}, dimensions={0}, use_global_device_ids=true | all-gather | bytes 1244160 | tf_op jit(solution)/shard_map/all_gather | solution.py:120
  163.5 27.0 %all-gather.16.cloned.1.call-done = bf16[32,36,1152]{2,1,0:T(8,128)(2,1)} async-done(((bf16[1,36,1152]{2,1,0:T(8,128)(2,1)}), bf16[32,36,1152]{2,1,0:T(8,128)(2,1)}) %all-gather.16.cloned.1.call-update) | async-done | bytes 2654224 | tf_op jit(solution)/shard_map/all_gather | solution.py:153
  204.3 23.0 %all-gather.14.cloned.1.call-done = bf16[32,36,1152]{2,1,0:T(8,128)(2,1)} async-done(((bf16[4,36,1152]{2,1,0:T(8,128)(2,1)}), bf16[32,36,1152]{2,1,0:T(8,128)(2,1)}) %all-gather.14.cloned.1.call-update) | async-done | bytes 2654224 | tf_op jit(solution)/shard_map/all_gather | solution.py:159
  232.6 5.2 reshape.288
  240.2 12.5 %multiply_convert_fusion = (bf16[640,1152]{1,0:T(8,128)(2,1)}, f32[640,1152]{1,0:T(8,128)}, f32[640,1152]{1,0:T(8,128)}) fusion(f32[1152]{0:T(1024)S(1)} %add.246, bf16[1152,1152]{1,0:T(8,128)(2,1)} %reshape.288, bf16[160,1152]{1,0:T(8,128)(2,1)} %collective-permute-done.8, bf16[160,1152]{1,0:T(8,128)(2,1)} %collective-permute-done.7, ...), kind=kOutput, calls=%fused_computation.20 | convolution fusion | flops 1753251840 | bytes 11506176 | tf_op jit(solution)/shard_map/dot_general | solution.py:42
  252.8 9.1 %all-gather.12.cloned.1.call-done = bf16[1152,1152]{1,0:T(8,128)(2,1)} async-done(((bf16[144,1152]{1,0:T(8,128)(2,1)}), bf16[1152,1152]{1,0:T(8,128)(2,1)}) %all-gather.12.cloned.1.call-update) | async-done | bytes 2654224 | tf_op jit(solution)/shard_map/all_gather | solution.py:163
  261.9 6.6 %fusion.78 = (f32[1152]{0:T(1024)S(1)}, bf16[640,1152]{1,0:T(8,128)(2,1)S(1)}) fusion(f32[640,1152]{1,0:T(8,128)} %get-tuple-element.30, f32[640,1152]{1,0:T(8,128)} %get-tuple-element.86, bf16[1152,1152]{1,0:T(8,128)(2,1)} %all-gather.12.cloned.1.call-done, bf16[160,1152]{1,0:T(8,128)(2,1)} %collective-permute-done.14, ...), kind=kOutput, calls=%fused_computation.171 | convolution fusion | flops 1715649408 | bytes 11506176 | tf_op jit(solution)/shard_map/dot_general | solution.py:50
  283.9 15.8 %collective-permute-done.16 = bf16[160,1152]{1,0:T(8,128)(2,1)S(1)} collective-permute-done((bf16[160,1152]{1,0:T(8,128)(2,1)S(1)}, bf16[160,1152]{1,0:T(8,128)(2,1)S(1)}, u32[]{:S(2)}, u32[]{:S(2)}) %collective-permute-start.16) | collective-permute-done | bytes 368672 | tf_op jit(solution)/shard_map/ppermute | solution.py:72
  300.3 6.3 %collective-permute-done.10 = bf16[160,1152]{1,0:T(8,128)(2,1)S(1)} collective-permute-done((bf16[160,1152]{1,0:T(8,128)(2,1)S(1)}, bf16[160,1152]{1,0:T(8,128)(2,1)S(1)}, u32[]{:S(2)}, u32[]{:S(2)}) %collective-permute-start.10) | collective-permute-done | bytes 368672 | tf_op jit(solution)/shard_map/ppermute | solution.py:72
  313.9 19.5 %all_to_all.46 = bf16[8,160,144]{1,2,0:T(8,128)(2,1)S(1)} all-to-all(bf16[8,160,144]{1,2,0:T(8,128)(2,1)S(1)} %copy.160), channel_id=1, replica_groups=mesh['dp'=4,'seq'=8] {'seq'}, dimensions={0} | all-to-all | bytes 737280 | tf_op jit(solution)/shard_map/all_to_all | solution.py:85
  334.4 8.2 %fusion.4 = bf16[2,1280,1280]{1,2,0:T(8,128)(2,1)} fusion(bf16[2,1280,72]{1,2,0:T(8,128)(2,1)S(1)} %bitcast.144, f32[2,1280,1280]{1,2,0:T(8,128)} %copy-done, f32[2,1280]{1,0:T(2,128)S(1)} %multiply_reduce_fusion.1, f32[2,1280]{1,0:T(2,128)S(1)} %log_add_fusion, bf16[1280,2,72]{0,2,1:T(8,128)(2,1)S(1)} %reshape.290), kind=kOutput, calls=%fused_computation.8 | convolution fusion | flops 488243200 | bytes 20418560 | tf_op jit(solution)/shard_map/hqd,hkd->hqk/dot_general | solution.py:135
  368.9 5.2 reshape.295
  383.9 5.8 %convolution_convert_fusion = bf16[1152,1152]{1,0:T(8,128)(2,1)} fusion(bf16[640,1152]{1,0:T(8,128)(2,1)} %get-tuple-element.29, bf16[160,1152]{1,0:T(8,128)(2,1)} %collective-permute-done.14, bf16[160,1152]{1,0:T(8,128)(2,1)} %collective-permute-done.13, bf16[160,1152]{1,0:T(8,128)(2,1)} %collective-permute-done.12, bf16[160,1152]{1,0:T(8,128)(2,1)} %bitcast.21), kind=kOutput, calls=%fused_computation.9 | convolution fusion | flops 1705918464 | bytes 5603328 | tf_op jit(solution)/shard_map/dot_general | solution.py:46
  395.0 19.4 %all_to_all.47 = bf16[4,288,432]{2,1,0:T(8,128)(2,1)S(1)} all-to-all(bf16[4,288,432]{2,1,0:T(8,128)(2,1)} %bitcast.141), channel_id=1, replica_groups=mesh['dp'=4,'seq'=8] {'dp'}, dimensions={0} | all-to-all | bytes 1990656 | tf_op jit(solution)/shard_map/all_to_all | solution.py:214
  426.6 13.3 %reduce-scatter.12.cloned.1.call-done = bf16[144,1152]{1,0:T(8,128)(2,1)} async-done(((bf16[1152,1152]{1,0:T(8,128)(2,1)}), bf16[144,1152]{1,0:T(8,128)(2,1)}) %reduce-scatter.12.cloned.1.call-update) | async-done | bytes 331792 | tf_op jit(solution)/shard_map/reduce_scatter | solution.py:183
  441.6 38.0 %reduce-scatter.10.cloned.1.call-done = bf16[144,1152]{1,0:T(8,128)(2,1)} async-done(((bf16[1152,1152]{1,0:T(8,128)(2,1)}), bf16[144,1152]{1,0:T(8,128)(2,1)}) %reduce-scatter.10.cloned.1.call-update) | async-done | bytes 331792 | tf_op jit(solution)/shard_map/reduce_scatter | solution.py:183
  496.5 22.5 %reduce-scatter.14.cloned.1.call-done = bf16[144,1152]{1,0:T(8,128)(2,1)} async-done(((bf16[1152,1152]{1,0:T(8,128)(2,1)}), bf16[144,1152]{1,0:T(8,128)(2,1)}) %reduce-scatter.14.cloned.1.call-update) | async-done | bytes 331792 | tf_op jit(solution)/shard_map/reduce_scatter | solution.py:176
  528.1 7.5 %all-to-all-done.8 = f32[32,8,128]{2,1,0:T(8,128)S(1)} async-done(((f32[32,8,128]{2,1,0:T(8,128)}), f32[32,8,128]{2,1,0:T(8,128)S(1)}, u32[]{:S(2)}, u32[]{:S(2)}) %all-to-all-start.8) | async-done | bytes 131104 | tf_op jit(solution)/shard_map/all_to_all | solution.py:259
  543.3 5.8 %collective-permute-done.21 = bf16[160,576]{0,1:T(8,128)(2,1)S(1)} collective-permute-done((bf16[160,576]{0,1:T(8,128)(2,1)S(1)}, bf16[160,576]{0,1:T(8,128)(2,1)S(1)}, u32[]{:S(2)}, u32[]{:S(2)}) %collective-permute-start.21) | collective-permute-done | bytes 184352 | tf_op jit(solution)/shard_map/ppermute | solution.py:72
  549.1 6.4 %collective-permute-done.22 = bf16[160,576]{0,1:T(8,128)(2,1)S(1)} collective-permute-done((bf16[160,576]{0,1:T(8,128)(2,1)S(1)}, bf16[160,576]{0,1:T(8,128)(2,1)S(1)}, u32[]{:S(2)}, u32[]{:S(2)}) %collective-permute-start.22) | collective-permute-done | bytes 184352 | tf_op jit(solution)/shard_map/ppermute | solution.py:72
  (325 shorter events, 204.0 us)
Async XLA Ops:
  7.9 132.7 %all-gather.10.cloned.1.call-start = ((), (), s32[]{:S(2)}) async-start(), calls=%async_computation.15 | async-start | bytes 3317760 | tf_op jit(solution)/shard_map/all_gather | solution.py:123
  40.4 45.1 %collective-permute-start.3 = (bf16[160,1152]{1,0:T(8,128)(2,1)S(1)}, bf16[160,1152]{1,0:T(8,128)(2,1)S(1)}, u32[]{:S(2)}, u32[]{:S(2)}) collective-permute-start(bf16[160,1152]{1,0:T(8,128)(2,1)S(1)} %get-tuple-element.41), channel_id=1, source_target_pairs={{0,8},{8,0},{16,24},{24,16},{1,9},{9,1},{17,25},{25,17},{2,10},{10... | collective-permute-start | bytes 1105928 | tf_op jit(solution)/shard_map/ppermute | solution.py:72
  42.0 43.5 %collective-permute-start.4 = (bf16[160,1152]{1,0:T(8,128)(2,1)S(1)}, bf16[160,1152]{1,0:T(8,128)(2,1)S(1)}, u32[]{:S(2)}, u32[]{:S(2)}) collective-permute-start(bf16[160,1152]{1,0:T(8,128)(2,1)S(1)} %get-tuple-element.43), channel_id=1, source_target_pairs={{0,16},{8,24},{16,0},{24,8},{1,17},{9,25},{17,1},{25,9},{2,18},{10... | collective-permute-start | bytes 1105928 | tf_op jit(solution)/shard_map/ppermute | solution.py:72
  43.4 42.1 %collective-permute-start.5 = (bf16[160,1152]{1,0:T(8,128)(2,1)S(1)}, bf16[160,1152]{1,0:T(8,128)(2,1)S(1)}, u32[]{:S(2)}, u32[]{:S(2)}) collective-permute-start(bf16[160,1152]{1,0:T(8,128)(2,1)S(1)} %get-tuple-element.42), channel_id=1, source_target_pairs={{0,24},{8,16},{16,8},{24,0},{1,25},{9,17},{17,9},{25,1},{2,26},{10... | collective-permute-start | bytes 1105928 | tf_op jit(solution)/shard_map/ppermute | solution.py:72
  88.2 102.3 %all-gather.16.cloned.1.call-start = ((), (), s32[]{:S(2)}) async-start(), calls=%async_computation.22 | async-start | bytes 3041280 | tf_op jit(solution)/shard_map/all_gather | solution.py:153
  88.9 138.4 %all-gather.14.cloned.1.call-start = ((), (), s32[]{:S(2)}) async-start(), calls=%async_computation.21 | async-start | bytes 3317760 | tf_op jit(solution)/shard_map/all_gather | solution.py:159
  105.4 156.4 %all-gather.12.cloned.1.call-start = ((), (), s32[]{:S(2)}) async-start(), calls=%async_computation.16 | async-start | bytes 2985984 | tf_op jit(solution)/shard_map/all_gather | solution.py:163
  157.9 36.2 %all-to-all-start.1 = ((bf16[8,160,144]{1,2,0:T(8,128)(2,1)}), bf16[8,160,144]{1,2,0:T(8,128)(2,1)}, u32[]{:S(2)}, u32[]{:S(2)}) async-start(bf16[8,160,144]{1,2,0:T(8,128)(2,1)} %copy.155), calls=%async_computation.1 | async-start | bytes 1179648 | tf_op jit(solution)/shard_map/all_to_all | solution.py:85
  162.1 256.9 %reduce-scatter.8.cloned.1.call-start = ((), (), s32[]{:S(2)}) async-start(), calls=%async_computation.17 | async-start | bytes 3317760 | tf_op jit(solution)/shard_map/reduce_scatter | solution.py:210
  197.8 40.0 %collective-permute-start.6 = (bf16[160,1152]{1,0:T(8,128)(2,1)}, bf16[160,1152]{1,0:T(8,128)(2,1)}, u32[]{:S(2)}, u32[]{:S(2)}) collective-permute-start(bf16[160,1152]{1,0:T(8,128)(2,1)} %add_convert_fusion), channel_id=1, source_target_pairs={{0,8},{8,0},{16,24},{24,16},{1,9},{9,1},{17,25},{25,17},{2,10},{10... | collective-permute-start | bytes 1105928 | tf_op jit(solution)/shard_map/ppermute | solution.py:72
  199.1 41.1 %collective-permute-start.7 = (bf16[160,1152]{1,0:T(8,128)(2,1)}, bf16[160,1152]{1,0:T(8,128)(2,1)}, u32[]{:S(2)}, u32[]{:S(2)}) collective-permute-start(bf16[160,1152]{1,0:T(8,128)(2,1)} %add_convert_fusion), channel_id=1, source_target_pairs={{0,16},{8,24},{16,0},{24,8},{1,17},{9,25},{17,1},{25,9},{2,18},{10... | collective-permute-start | bytes 1105928 | tf_op jit(solution)/shard_map/ppermute | solution.py:72
  199.8 40.4 %collective-permute-start.8 = (bf16[160,1152]{1,0:T(8,128)(2,1)}, bf16[160,1152]{1,0:T(8,128)(2,1)}, u32[]{:S(2)}, u32[]{:S(2)}) collective-permute-start(bf16[160,1152]{1,0:T(8,128)(2,1)} %add_convert_fusion), channel_id=1, source_target_pairs={{0,24},{8,16},{16,8},{24,0},{1,25},{9,17},{17,9},{25,1},{2,26},{10... | collective-permute-start | bytes 1105928 | tf_op jit(solution)/shard_map/ppermute | solution.py:72
  201.3 51.4 %collective-permute-start.12 = (bf16[160,1152]{1,0:T(8,128)(2,1)}, bf16[160,1152]{1,0:T(8,128)(2,1)}, u32[]{:S(2)}, u32[]{:S(2)}) collective-permute-start(bf16[160,1152]{1,0:T(8,128)(2,1)} %bitcast.21), channel_id=1, source_target_pairs={{0,8},{8,0},{16,24},{24,16},{1,9},{9,1},{17,25},{25,17},{2,10},{10... | collective-permute-start | bytes 1105928 | tf_op jit(solution)/shard_map/ppermute | solution.py:72
  202.6 50.2 %collective-permute-start.13 = (bf16[160,1152]{1,0:T(8,128)(2,1)}, bf16[160,1152]{1,0:T(8,128)(2,1)}, u32[]{:S(2)}, u32[]{:S(2)}) collective-permute-start(bf16[160,1152]{1,0:T(8,128)(2,1)} %bitcast.21), channel_id=1, source_target_pairs={{0,16},{8,24},{16,0},{24,8},{1,17},{9,25},{17,1},{25,9},{2,18},{10... | collective-permute-start | bytes 1105928 | tf_op jit(solution)/shard_map/ppermute | solution.py:72
  276.8 29.8 %collective-permute-start.10 = (bf16[160,1152]{1,0:T(8,128)(2,1)S(1)}, bf16[160,1152]{1,0:T(8,128)(2,1)S(1)}, u32[]{:S(2)}, u32[]{:S(2)}) collective-permute-start(bf16[160,1152]{1,0:T(8,128)(2,1)S(1)} %get-tuple-element.40), channel_id=1, source_target_pairs={{0,16},{8,24},{16,0},{24,8},{1,17},{9,25},{17,1},{25,9},{2,18},{10... | collective-permute-start | bytes 1105928 | tf_op jit(solution)/shard_map/ppermute | solution.py:72
  358.6 81.2 %reduce-scatter.12.cloned.1.call-start = ((), (), s32[]{:S(2)}) async-start(), calls=%async_computation.19 | async-start | bytes 2985984 | tf_op jit(solution)/shard_map/reduce_scatter | solution.py:183
  374.1 105.5 %reduce-scatter.10.cloned.1.call-start = ((), (), s32[]{:S(2)}) async-start(), calls=%async_computation.18 | async-start | bytes 2985984 | tf_op jit(solution)/shard_map/reduce_scatter | solution.py:183
  383.9 135.1 %reduce-scatter.14.cloned.1.call-start = ((), (), s32[]{:S(2)}) async-start(), calls=%async_computation.20 | async-start | bytes 2985984 | tf_op jit(solution)/shard_map/reduce_scatter | solution.py:176
  415.5 65.9 %all-to-all-start.5 = ((bf16[8,36,432]{2,1,0:T(8,128)(2,1)}), bf16[8,36,432]{2,1,0:T(8,128)(2,1)S(1)}, u32[]{:S(2)}, u32[]{:S(2)}) async-start(bf16[8,36,432]{2,1,0:T(8,128)(2,1)} %reshape.292), calls=%async_computation.6 | async-start | bytes 655360 | tf_op jit(solution)/shard_map/all_to_all | solution.py:85
  422.5 62.7 %collective-permute-start.18 = (bf16[160,1152]{1,0:T(8,128)(2,1)S(1)}, bf16[160,1152]{1,0:T(8,128)(2,1)S(1)}, u32[]{:S(2)}, u32[]{:S(2)}) collective-permute-start(bf16[160,1152]{1,0:T(8,128)(2,1)S(1)} %get-tuple-element.27), channel_id=1, source_target_pairs={{0,8},{8,0},{16,24},{24,16},{1,9},{9,1},{17,25},{25,17},{2,10},{10... | collective-permute-start | bytes 1105928 | tf_op jit(solution)/shard_map/ppermute | solution.py:72
  423.4 61.8 %collective-permute-start.19 = (bf16[160,1152]{1,0:T(8,128)(2,1)S(1)}, bf16[160,1152]{1,0:T(8,128)(2,1)S(1)}, u32[]{:S(2)}, u32[]{:S(2)}) collective-permute-start(bf16[160,1152]{1,0:T(8,128)(2,1)S(1)} %get-tuple-element.27), channel_id=1, source_target_pairs={{0,16},{8,24},{16,0},{24,8},{1,17},{9,25},{17,1},{25,9},{2,18},{10... | collective-permute-start | bytes 1105928 | tf_op jit(solution)/shard_map/ppermute | solution.py:72
  424.0 61.3 %collective-permute-start.20 = (bf16[160,1152]{1,0:T(8,128)(2,1)S(1)}, bf16[160,1152]{1,0:T(8,128)(2,1)S(1)}, u32[]{:S(2)}, u32[]{:S(2)}) collective-permute-start(bf16[160,1152]{1,0:T(8,128)(2,1)S(1)} %get-tuple-element.27), channel_id=1, source_target_pairs={{0,24},{8,16},{16,8},{24,0},{1,25},{9,17},{17,9},{25,1},{2,26},{10... | collective-permute-start | bytes 1105928 | tf_op jit(solution)/shard_map/ppermute | solution.py:72
  485.2 73.2 %reduce-scatter.16.cloned.1.call-start = ((), (), s32[]{:S(2)}) async-start(), calls=%async_computation.23 | async-start | bytes 1492992
  490.9 31.3 %all-to-all-start.6 = ((bf16[4,36,1152]{2,1,0:T(8,128)(2,1)}), bf16[4,36,1152]{2,1,0:T(8,128)(2,1)S(1)}, u32[]{:S(2)}, u32[]{:S(2)}) async-start(bf16[4,36,1152]{2,1,0:T(8,128)(2,1)} %reshape.294), calls=%async_computation.8 | async-start | bytes 737280 | tf_op jit(solution)/shard_map/all_to_all | solution.py:184
  (75 other events, 1120.5 us)
Sparse Core Ops, SparseCore 0:
  9.7 26.2 all-gather.7
  88.3 39.9 all-gather.9
  131.2 59.2 all-gather.15
  192.0 35.2 all-gather.13
  228.8 33.0 all-gather.11
  358.8 36.9 reduce-scatter.7
  398.2 41.6 reduce-scatter.11
  442.3 37.3 reduce-scatter.9
  482.0 36.8 reduce-scatter.13
  521.2 33.3 reduce-scatter.15

commit v3 on v2

--- a/solution.py
+++ b/solution.py
@@ -84,6 +84,12 @@
     def seq_exchange(v):
         return lax.all_to_all(v, "seq", 0, 0, tiled=True)
 
+    def spread(v, axes, count):
+        copies = jnp.broadcast_to(v[None], (count,) + v.shape)
+        return lax.all_to_all(copies, axes, 0, 0, tiled=True)
+
+    after = lax.optimization_barrier
+
     skip_part = lax.all_gather(skip_w, "seq", axis=0, tiled=True)
 
     own_vectors = (skip_b, ln1_g, ln1_b, proj_b, ln2_g, ln2_b, fc2_b, fc1_b)
@@ -91,8 +97,7 @@
     own_size = packed.shape[0]
     padded = -(-own_size // 1024) * 1024
     packed = jnp.pad(packed, (0, padded - own_size)).reshape(padded // 128, 128)
-    vectors = lax.all_gather(packed, ("dp", "seq"), axis=0, tiled=True).reshape(n, padded)
-    vectors = vectors.astype(F32)
+    vectors = spread(packed, ("dp", "seq"), n).reshape(n, padded).astype(F32)
     small = features // n
 
     def vector(index):
@@ -102,8 +107,13 @@
     up_bias = lax.dynamic_slice_in_dim(vectors[:, 7 * small : own_size], dp_at * ns, ns, 0)
     up_bias = up_bias.reshape(hidden_part)
 
-    joined = jnp.concatenate([inputs[0], skipped[0]], axis=1)
-    joined_slices = jnp.swapaxes(joined.reshape(local, nd, joined_part), 0, 1)
+    joined_slices = jnp.stack(
+        [
+            half[:, at * joined_part : (at + 1) * joined_part]
+            for half in (inputs[0], skipped[0])
+            for at in range(nd // 2)
+        ]
+    )
     joined_blocks = []
     for k in range(nd):
         away = lax.dynamic_index_in_dim(joined_slices, dp_at ^ k, 0, keepdims=False)
@@ -117,10 +127,13 @@
         qkv_w.reshape(features // n, 3, ns, head_cols).transpose(2, 0, 1, 3)
         .reshape(ns, features // n, 3 * head_cols)
     )
-    qkv_mine = lax.all_gather(
-        qkv_mine.reshape(features // nd, 3 * head_cols), "dp", axis=0, tiled=True
-    )
+    qkv_mine = spread(qkv_mine.reshape(features // nd, 3 * head_cols), "dp", nd)
+    qkv_mine = qkv_mine.reshape(features, 3 * head_cols)
+    own_proj, skip_part = after((proj_w, skip_part))
+    w_proj = lax.all_gather(own_proj, "seq", axis=0, tiled=True)
+    normed_one, w_proj = after((normed_one, w_proj))
     normed_one_row = lax.all_gather(normed_one, "seq", axis=0, tiled=True)
+    w_proj = spread(w_proj, "dp", nd).reshape(features, features)
     triple = dot(normed_one_row, qkv_mine).astype(BF16)
     queries, keys, values = (
         jnp.swapaxes(
@@ -150,47 +163,52 @@
         return jnp.swapaxes(v.reshape(row_len, heads, HEAD_DIM), 0, 1)
 
     attended_low = heads_to_tokens(attended_heads)
-    w_proj = lax.all_gather(proj_w, ("dp", "seq"), axis=0, tiled=True)
     second = first + dot(attended_low, w_proj) + b_proj
     xhat_two, inverse_two = norm_pieces(second)
     normed_two = (xhat_two * g_two + b_two).astype(BF16)
 
     up_slices = jnp.swapaxes(fc1_w.reshape(features // n, nd, hidden_part), 0, 1)
+    up_slices = lax.all_to_all(up_slices, "dp", 0, 0, tiled=True)
+    up_slices, normed_one_row = after((up_slices, normed_one_row))
     up_part = lax.all_gather(
-        lax.all_to_all(up_slices, "dp", 0, 0, tiled=True), "seq", axis=0, tiled=False
-    )
-    up_part = jnp.swapaxes(up_part, 0, 1).reshape(features, hidden_part)
-    down_part = lax.all_gather(fc2_w, "seq", axis=0, tiled=True)
+        up_slices.reshape(features // ns, hidden_part), "seq", axis=0, tiled=True
+    )
+    own_down, up_part = after((fc2_w, up_part))
+    down_part = lax.all_gather(own_down, "seq", axis=0, tiled=True)
+    up_part = jnp.swapaxes(up_part.reshape(ns, nd, features // n, hidden_part), 0, 1)
+    up_part = up_part.reshape(features, hidden_part)
     grad_out = cotangent[0]
     grad_out_rows = gather_rows(grad_out)
     normed_two_rows = gather_rows(normed_two)
     pre = dot(normed_two_rows, up_part) + up_bias
     gelu_value, gelu_pull = jax.vjp(partial(jax.nn.gelu, approximate=False), pre)
     hidden = gelu_value.astype(BF16)
-    output = second + add_rows(dot(hidden, down_part)) + b_down
-    output = output.astype(BF16)[None]
 
     pre_grad = gelu_pull(times_transposed(grad_out_rows, down_part))[0]
     pre_low = pre_grad.astype(BF16)
     normed_two_grad = add_rows(times_transposed(pre_low, up_part))
     fc2_w_grad = lax.psum_scatter(
         inner(hidden, grad_out_rows).astype(BF16), "seq", scatter_dimension=0, tiled=True
-    ).astype(F32)
+    )
+    normed_two_grad, hidden = after((normed_two_grad, hidden))
+    output = second + add_rows(dot(hidden, down_part)) + b_down
+    output = output.astype(BF16)[None]
 
     def by_seq(grad):
         grad = grad.reshape(nd, ns, features // n, grad.shape[1]).astype(BF16)
-        grad = jnp.swapaxes(grad, 0, 1).reshape(features, grad.shape[3])
-        grad = lax.psum_scatter(grad, "seq", scatter_dimension=0, tiled=True)
-        return lax.all_to_all(
-            grad.reshape(nd, features // n, grad.shape[1]), "dp", 0, 0, tiled=True
-        )
-
-    fc1_w_grad = jnp.swapaxes(by_seq(inner(normed_two_rows, pre_low)), 0, 1)
-    fc1_w_grad = fc1_w_grad.reshape(features // n, hidden_units).astype(F32)
+        return jnp.swapaxes(grad, 0, 1).reshape(features, grad.shape[3])
+
+    def from_dp(grad):
+        grad = grad.reshape(nd, features // n, grad.shape[1])
+        return lax.all_to_all(grad, "dp", 0, 0, tiled=True)
+
+    fc1_terms, fc2_w_grad = after((by_seq(inner(normed_two_rows, pre_low)), fc2_w_grad))
+    fc1_terms = lax.psum_scatter(fc1_terms, "seq", scatter_dimension=0, tiled=True)
+    fc2_w_grad = fc2_w_grad.astype(F32)
     through_two, ln2_g_grad, ln2_b_grad = norm_back(normed_two_grad, xhat_two, inverse_two, g_two)
     second_grad = grad_out.astype(F32) + through_two
     second_low = second_grad.astype(BF16)
-    proj_w_grad = jnp.sum(by_seq(inner(attended_low, second_low)).astype(F32), axis=0)
+    proj_terms = by_seq(inner(attended_low, second_low))
     attended_grad = tokens_to_heads(times_transposed(second_low, w_proj).astype(BF16))
     delta = jnp.sum(attended_grad.astype(F32) * attended_heads, axis=2, keepdims=True)
     probs = jnp.exp(logits - lse)
@@ -207,9 +225,15 @@
         ],
         axis=1,
     )
+    triple_grad, fc1_terms = after((triple_grad, fc1_terms))
+    fc1_w_grad = jnp.swapaxes(from_dp(fc1_terms), 0, 1)
+    fc1_w_grad = fc1_w_grad.reshape(features // n, hidden_units).astype(F32)
     normed_one_grad = lax.psum_scatter(
         times_transposed(triple_grad, qkv_mine).astype(BF16), "seq", scatter_dimension=0, tiled=True
-    ).astype(F32)
+    )
+    normed_one_grad, proj_terms = after((normed_one_grad, proj_terms))
+    normed_one_grad = normed_one_grad.astype(F32)
+    proj_terms = lax.psum_scatter(proj_terms, "seq", scatter_dimension=0, tiled=True)
     qkv_terms = inner(normed_one_row, triple_grad).astype(BF16)
     qkv_terms = lax.all_to_all(
         qkv_terms.reshape(nd, features // nd, 3 * head_cols), "dp", 0, 0, tiled=True
@@ -223,8 +247,10 @@
     through_one, ln1_g_grad, ln1_b_grad = norm_back(normed_one_grad, xhat_one, inverse_one, g_one)
     first_grad = second_grad + through_one
     first_low_rows = gather_rows(first_grad.astype(BF16))
+    skip_terms, proj_terms = after((inner(joined_here, first_low_rows).astype(BF16), proj_terms))
+    proj_w_grad = jnp.sum(from_dp(proj_terms).astype(F32), axis=0)
     skip_w_grad = lax.psum_scatter(
-        inner(joined_here, first_low_rows).astype(BF16), "seq", scatter_dimension=0, tiled=True
+        skip_terms, "seq", scatter_dimension=0, tiled=True
     ).astype(F32)
     joined_grad_part = times_transposed(first_low_rows, skip_part).astype(BF16)
     away = []

time: 577 us -> 508 us (0.88)
  blocking collectives: 105 us -> 53.5 us
  waiting for transfers between devices: 206 us -> 167 us
  starting transfers between devices: 54 us -> 69.4 us
  matrix products: 85.9 us -> 94.5 us
  other arithmetic: 28.1 us -> 21.1 us
  local copies, waits for them, and re-layouts: 69.1 us -> 76 us
    all_gather x3 -> x2, waiting for transfers between devices: 59.1 us -> 0.04 us  [the longest x1 0.02 us: on_device(): down_part = lax.all_gather(own_down, 'seq', axis=0, tiled=True)]
    reduce_scatter x2, waiting for transfers between devices: 51.3 us -> 0.01 us  [the longest x1 0.01 us: on_device(): lax.psum_scatter(fc1_terms, 'seq', scatter_dimension=0, tiled=True)]
    all_to_all x2 -> x6, waiting for transfers between devices: 1.86 us -> 46.9 us  [the longest x2 18.4 us: spread(): return lax.all_to_all(copies, axes, 0, 0, tiled=True)]
    all_gather x2 -> x1, blocking collectives: 55.6 us -> 15.6 us  [on_device(): w_proj = lax.all_gather(own_proj, 'seq', axis=0, tiled=True)]
    all_to_all x3, waiting for transfers between devices: 12.7 us -> 44.1 us  [seq_exchange(): return lax.all_to_all(v, 'seq', 0, 0, tiled=True)]
    reduce_scatter x1, waiting for transfers between devices: 0.02 us -> 29 us  [on_device(): lax.psum_scatter(times_transposed(triple_grad, qkv_mine).astype(BF16), 's...]
    reduce_scatter x1, waiting for transfers between devices: 22.5 us -> 0.01 us  [on_device(): lax.psum_scatter(inner(hidden, grad_out_rows).astype(BF16), 'seq', scatte...]
    ppermute x24, waiting for transfers between devices: 46 us -> 26.9 us  [swap(): return lax.ppermute(v, 'dp', [(i, i ^ k) for i in range(nd)])]
  transfers between devices with their start and end apart: 40 -> 43, of which waited for: 17 -> 19; matrix products, arithmetic and copies ran while one was open for 23% -> 34% of each run, Pallas kernels for 0% -> 0%
where the time goes in v3:
time: 508 us; the launch traced here: 500 us
  waiting for transfers between devices  167 us (33%)
  matrix products  94.5 us (19%)
  local copies, waits for them, and re-layouts  76 us (15%)
  starting transfers between devices  69.4 us (14%)
  blocking collectives  53.5 us (11%)
  other arithmetic  21.1 us (4%)
  between operations  18.6 us (4%)
    all_to_all x3, waiting for transfers between devices, seq_exchange(): return lax.all_to_all(v, 'seq', 0, 0, tiled=True)  44.1 us
    dot_general x5, matrix products, dot(): return jnp.dot(left, right, preferred_element_type=F32)  30 us
    ppermute x24, starting transfers between devices, swap(): return lax.ppermute(v, 'dp', [(i, i ^ k) for i in range(nd)])  29.3 us
    reduce_scatter x1, waiting for transfers between devices, on_device(): lax.psum_scatter(times_transposed(triple_grad, qkv_mine).astype(BF16), 's...  29 us
    ppermute x24, waiting for transfers between devices, swap(): return lax.ppermute(v, 'dp', [(i, i ^ k) for i in range(nd)])  26.9 us
    dot_general x6, matrix products, head_dot(): return jnp.einsum(spec, left, right, preferred_element_type=F32)  24.1 us
    all_to_all x1, blocking collectives, seq_exchange(): return lax.all_to_all(v, 'seq', 0, 0, tiled=True)  23.8 us
    dot_general x5, matrix products, times_transposed(): lax.dot_general(left, right, (((1,), (1,)), ((), ())), preferred_element_...  22.1 us
  transfers between devices with their start and end apart: 43, of which 19 were waited for; matrix products, arithmetic and copies ran while one was open for 34% of the time, Pallas kernels for 0%

profile of v3, /device:TPU:0, one launch (start us, length us, event | category | flops | bytes accessed | tf_op | source)
XLA Modules:
  0.0 499.8 jit_solution(2696127043475230670)
XLA Ops:
  14.5 14.1 %all_to_all.60 = bf16[32,8,128]{2,1,0:T(8,128)(2,1)S(1)} all-to-all(bf16[32,8,128]{2,1,0:T(8,128)(2,1)S(1)} %broadcast_in_dim.31), channel_id=1, replica_groups=mesh['dp'=4,'seq'=8] {'dp','seq'}, dimensions={0} | all-to-all | bytes 131072 | tf_op jit(solution)/shard_map/all_to_all | solution.py:89
  28.6 8.5 %all-gather.6.cloned.1.call-done = bf16[576,1152]{1,0:T(8,128)(2,1)} async-done(((bf16[72,1152]{1,0:T(8,128)(2,1)}), bf16[576,1152]{1,0:T(8,128)(2,1)}) %all-gather.6.cloned.1.call-update) | async-done | bytes 1327120 | tf_op jit(solution)/shard_map/all_gather | solution.py:93
  46.9 15.6 %all-gather = bf16[8,36,1152]{2,1,0:T(8,128)(2,1)S(1)} all-gather(bf16[1,36,1152]{2,1,0:T(8,128)(2,1)S(1)} %bitcast.187), channel_id=1, replica_groups=mesh['dp'=4,'seq'=8] {'seq'}, dimensions={0}, use_global_device_ids=true | all-gather | bytes 746496 | tf_op jit(solution)/shard_map/all_gather | solution.py:133
  71.7 17.1 %all-to-all-done.1 = bf16[8,36,432]{2,1,0:T(8,128)(2,1)S(1)} async-done(((bf16[8,36,432]{2,1,0:T(8,128)(2,1)}), bf16[8,36,432]{2,1,0:T(8,128)(2,1)S(1)}, u32[]{:S(2)}, u32[]{:S(2)}) %all-to-all-start.1) | async-done | bytes 248864 | tf_op jit(solution)/shard_map/all_to_all | solution.py:85
  138.7 13.3 %all-to-all-done.4 = bf16[4,288,1152]{2,1,0:T(8,128)(2,1)} async-done(((bf16[4,288,1152]{2,1,0:T(8,128)(2,1)}), bf16[4,288,1152]{2,1,0:T(8,128)(2,1)}, u32[]{:S(2)}, u32[]{:S(2)}) %all-to-all-start.4) | async-done | bytes 2654240 | tf_op jit(solution)/shard_map/all_to_all | solution.py:89
  152.0 6.2 %all-to-all-start.3 = ((bf16[8,160,144]{1,2,0:T(8,128)(2,1)}), bf16[8,160,144]{1,2,0:T(8,128)(2,1)S(1)}, u32[]{:S(2)}, u32[]{:S(2)}) async-start(bf16[8,160,144]{1,2,0:T(8,128)(2,1)} %copy.132), calls=%async_computation.3 | async-start | bytes 1179648 | tf_op jit(solution)/shard_map/all_to_all | solution.py:85
  159.4 22.7 %all-to-all-done.3 = bf16[8,160,144]{1,2,0:T(8,128)(2,1)S(1)} async-done(((bf16[8,160,144]{1,2,0:T(8,128)(2,1)}), bf16[8,160,144]{1,2,0:T(8,128)(2,1)S(1)}, u32[]{:S(2)}, u32[]{:S(2)}) %all-to-all-start.3) | async-done | bytes 368672 | tf_op jit(solution)/shard_map/all_to_all | solution.py:85
  207.4 6.8 %collective-permute-done.7 = bf16[160,1152]{1,0:T(8,128)(2,1)S(1)} collective-permute-done((bf16[160,1152]{1,0:T(8,128)(2,1)S(1)}, bf16[160,1152]{1,0:T(8,128)(2,1)S(1)}, u32[]{:S(2)}, u32[]{:S(2)}) %collective-permute-start.7) | collective-permute-done | bytes 368672 | tf_op jit(solution)/shard_map/ppermute | solution.py:72
  214.2 12.5 %multiply_convert_fusion = (bf16[640,1152]{1,0:T(8,128)(2,1)S(1)}, f32[640,1152]{1,0:T(8,128)}, f32[640,1152]{1,0:T(8,128)}) fusion(f32[1152]{0:T(1024)S(1)} %add.246, bf16[1152,1152]{1,0:T(8,128)(2,1)} %reshape.286, bf16[160,1152]{1,0:T(8,128)(2,1)S(1)} %collective-permute-done.8, bf16[160,1152]{1,0:T(8,128)(2,1)S(1)} %collective-permute-done.7, ...), kind=kOutput, calls=%fused_computation.19 | convolution fusion | flops 1753251840 | bytes 11506176 | tf_op jit(solution)/shard_map/dot_general | solution.py:42
  233.7 7.1 %fusion.71 = (f32[1152]{0:T(1024)}, bf16[640,1152]{1,0:T(8,128)(2,1)S(1)}) fusion(f32[640,1152]{1,0:T(8,128)} %get-tuple-element.65, f32[640,1152]{1,0:T(8,128)} %get-tuple-element.125, bf16[1152,1152]{1,0:T(8,128)(2,1)} %all-gather.12.cloned.1.call-done, bf16[160,1152]{1,0:T(8,128)(2,1)} %collective-permute-done.11, ...), kind=kOutput, calls=%fused_computation.163 | convolution fusion | flops 1715649408 | bytes 11506176 | tf_op jit(solution)/shard_map/dot_general | solution.py:50
  253.1 5.2 %convert_element_type.285 = bf16[4,8,36,1152]{3,2,1,0:T(8,128)(2,1)} reshape(bf16[1152,1152]{1,0:T(8,128)(2,1)} %convolution_convert_fusion.2) | data formatting | bytes 5308416 | tf_op jit(solution)/shard_map/convert_element_type | solution.py:198
  261.9 5.2 %reshape.289 = bf16[1152,1152]{1,0:T(8,128)(2,1)} reshape(bf16[8,4,36,1152]{3,2,1,0:T(8,128)(2,1)} %copy.142) | data formatting | bytes 5308416 | tf_op jit(solution)/shard_map/reshape | solution.py:199
  268.4 6.6 %fusion.70 = (bf16[640,1152]{1,0:T(8,128)(2,1)}, f32[640,1152]{1,0:T(8,128)}) fusion(bf16[640,1152]{1,0:T(8,128)(2,1)} %copy-done.59, bf16[1152,1152]{1,0:T(8,128)(2,1)} %all-gather.12.cloned.1.call-done), kind=kOutput, calls=%fused_computation.162 | convolution fusion | flops 1699430400 | bytes 8552448 | tf_op jit(solution)/shard_map/dot_general | solution.py:42
  298.0 23.8 %all_to_all.61 = bf16[8,160,144]{1,2,0:T(8,128)(2,1)S(1)} all-to-all(bf16[8,160,144]{1,2,0:T(8,128)(2,1)S(1)} %copy.136), channel_id=1, replica_groups=mesh['dp'=4,'seq'=8] {'seq'}, dimensions={0} | all-to-all | bytes 737280 | tf_op jit(solution)/shard_map/all_to_all | solution.py:85
  322.8 8.2 %fusion.4 = bf16[2,1280,1280]{1,2,0:T(8,128)(2,1)} fusion(bf16[2,1280,72]{1,2,0:T(8,128)(2,1)S(1)} %bitcast.160, f32[2,1280,1280]{1,2,0:T(8,128)} %copy-done, f32[2,1280]{1,0:T(2,128)S(1)} %multiply_reduce_fusion.1, f32[2,1280]{1,0:T(2,128)S(1)} %log_add_fusion, bf16[1280,2,72]{0,2,1:T(8,128)(2,1)S(1)} %reshape.288), kind=kOutput, calls=%fused_computation.8 | convolution fusion | flops 488243200 | bytes 20418560 | tf_op jit(solution)/shard_map/hqd,hkd->hqk/dot_general | solution.py:148
  343.8 5.3 %convolution_convert_fusion = bf16[1280,1152]{1,0:T(8,128)(2,1)} fusion(bf16[1280,432]{0,1:T(8,128)(2,1)} %pad_maximum_fusion.4, bf16[1152,432]{1,0:T(8,128)(2,1)} %bitcast.172), kind=kOutput, calls=%fused_computation.9 | convolution fusion | flops 1275494400 | bytes 5050368 | tf_op jit(solution)/shard_map/dot_general | solution.py:50
  353.1 5.3 %reshape.290 = bf16[1152,1152]{1,0:T(8,128)(2,1)} reshape(bf16[8,4,36,1152]{3,2,1,0:T(8,128)(2,1)} %copy.144) | data formatting | bytes 5308416 | tf_op jit(solution)/shard_map/reshape | solution.py:199
  358.4 29.0 %reduce-scatter.12.cloned.1.call-done = bf16[160,1152]{1,0:T(8,128)(2,1)} async-done(((bf16[1280,1152]{1,0:T(8,128)(2,1)}), bf16[160,1152]{1,0:T(8,128)(2,1)}) %reduce-scatter.12.cloned.1.call-update) | async-done | bytes 368656 | tf_op jit(solution)/shard_map/reduce_scatter | solution.py:231
  404.3 10.5 %all-to-all-done.7 = bf16[4,288,432]{2,1,0:T(8,128)(2,1)S(1)} async-done(((bf16[4,288,432]{2,1,0:T(8,128)(2,1)}), bf16[4,288,432]{2,1,0:T(8,128)(2,1)S(1)}, u32[]{:S(2)}, u32[]{:S(2)}) %all-to-all-start.7) | async-done | bytes 995360 | tf_op jit(solution)/shard_map/all_to_all | solution.py:238
  419.5 11.5 %all-to-all-done.10 = bf16[4,36,1152]{2,1,0:T(8,128)(2,1)S(1)} async-done(((bf16[4,36,1152]{2,1,0:T(8,128)(2,1)}), bf16[4,36,1152]{2,1,0:T(8,128)(2,1)S(1)}, u32[]{:S(2)}, u32[]{:S(2)}) %all-to-all-start.10) | async-done | bytes 331808 | tf_op jit(solution)/shard_map/all_to_all | solution.py:203
  451.7 5.9 %all-to-all-done.11 = f32[32,8,128]{2,1,0:T(8,128)S(1)} async-done(((f32[32,8,128]{2,1,0:T(8,128)}), f32[32,8,128]{2,1,0:T(8,128)S(1)}, u32[]{:S(2)}, u32[]{:S(2)}) %all-to-all-start.11) | async-done | bytes 131104 | tf_op jit(solution)/shard_map/all_to_all | solution.py:285
  465.7 5.7 %collective-permute-done.21 = bf16[160,576]{0,1:T(8,128)(2,1)S(1)} collective-permute-done((bf16[160,576]{0,1:T(8,128)(2,1)S(1)}, bf16[160,576]{0,1:T(8,128)(2,1)S(1)}, u32[]{:S(2)}, u32[]{:S(2)}) %collective-permute-start.21) | collective-permute-done | bytes 184352 | tf_op jit(solution)/shard_map/ppermute | solution.py:72
  472.5 5.5 %collective-permute-done.23 = bf16[160,576]{0,1:T(8,128)(2,1)S(1)} collective-permute-done((bf16[160,576]{0,1:T(8,128)(2,1)S(1)}, bf16[160,576]{0,1:T(8,128)(2,1)S(1)}, u32[]{:S(2)}, u32[]{:S(2)}) %collective-permute-start.23) | collective-permute-done | bytes 184352 | tf_op jit(solution)/shard_map/ppermute | solution.py:72
  485.2 5.4 %all-to-all-done.9 = bf16[4,36,1152]{2,1,0:T(8,128)(2,1)S(1)} async-done(((bf16[4,36,1152]{2,1,0:T(8,128)(2,1)}), bf16[4,36,1152]{2,1,0:T(8,128)(2,1)S(1)}, u32[]{:S(2)}, u32[]{:S(2)}) %all-to-all-start.9) | async-done | bytes 331808 | tf_op jit(solution)/shard_map/all_to_all | solution.py:203
  (341 shorter events, 224.1 us)
Async XLA Ops:
  7.3 29.9 %all-gather.6.cloned.1.call-start = ((), (), s32[]{:S(2)}) async-start(), calls=%async_computation.17 | async-start | bytes 1492992 | tf_op jit(solution)/shard_map/all_gather | solution.py:93
  8.0 99.1 %all-gather.8.cloned.1.call-start = ((), (), s32[]{:S(2)}) async-start(), calls=%async_computation.18 | async-start | bytes 3317760 | tf_op jit(solution)/shard_map/all_gather | solution.py:135
  42.3 20.3 %collective-permute-start.3 = (bf16[160,1152]{1,0:T(8,128)(2,1)}, bf16[160,1152]{1,0:T(8,128)(2,1)S(1)}, u32[]{:S(2)}, u32[]{:S(2)}) collective-permute-start(bf16[160,1152]{1,0:T(8,128)(2,1)} %get-tuple-element.76), channel_id=1, source_target_pairs={{0,8},{8,0},{16,24},{24,16},{1,9},{9,1},{17,25},{25,17},{2,10},{10... | collective-permute-start | bytes 1105928 | tf_op jit(solution)/shard_map/ppermute | solution.py:72
  67.3 21.5 %all-to-all-start.1 = ((bf16[8,36,432]{2,1,0:T(8,128)(2,1)}), bf16[8,36,432]{2,1,0:T(8,128)(2,1)S(1)}, u32[]{:S(2)}, u32[]{:S(2)}) async-start(bf16[8,36,432]{2,1,0:T(8,128)(2,1)} %copy.130), calls=%async_computation.1 | async-start | bytes 655360 | tf_op jit(solution)/shard_map/all_to_all | solution.py:85
  102.9 55.4 %all-gather.10.cloned.1.call-start = ((), (), s32[]{:S(2)}) async-start(), calls=%async_computation.19 | async-start | bytes 2985984 | tf_op jit(solution)/shard_map/all_gather | solution.py:173
  117.0 35.0 %all-to-all-start.4 = ((bf16[4,288,1152]{2,1,0:T(8,128)(2,1)}), bf16[4,288,1152]{2,1,0:T(8,128)(2,1)}, u32[]{:S(2)}, u32[]{:S(2)}) async-start(bf16[4,288,1152]{2,1,0:T(8,128)(2,1)} %broadcast_in_dim.64), calls=%async_computation.4 | async-start | bytes 5308416 | tf_op jit(solution)/shard_map/all_to_all | solution.py:89
  152.0 30.1 %all-to-all-start.3 = ((bf16[8,160,144]{1,2,0:T(8,128)(2,1)}), bf16[8,160,144]{1,2,0:T(8,128)(2,1)S(1)}, u32[]{:S(2)}, u32[]{:S(2)}) async-start(bf16[8,160,144]{1,2,0:T(8,128)(2,1)} %copy.132), calls=%async_computation.3 | async-start | bytes 1179648 | tf_op jit(solution)/shard_map/all_to_all | solution.py:85
  158.2 75.4 %all-gather.12.cloned.1.call-start = ((), (), s32[]{:S(2)}) async-start(), calls=%async_computation.20 | async-start | bytes 2985984 | tf_op jit(solution)/shard_map/all_gather | solution.py:177
  158.8 116.2 %reduce-scatter.8.cloned.1.call-start = ((), (), s32[]{:S(2)}) async-start(), calls=%async_computation.21 | async-start | bytes 2985984 | tf_op jit(solution)/shard_map/reduce_scatter | solution.py:190
  185.4 21.4 %collective-permute-start.6 = (bf16[160,1152]{1,0:T(8,128)(2,1)S(1)}, bf16[160,1152]{1,0:T(8,128)(2,1)S(1)}, u32[]{:S(2)}, u32[]{:S(2)}) collective-permute-start(bf16[160,1152]{1,0:T(8,128)(2,1)S(1)} %add_convert_fusion), channel_id=1, source_target_pairs={{0,8},{8,0},{16,24},{24,16},{1,9},{9,1},{17,25},{25,17},{2,10},{10... | collective-permute-start | bytes 1105928 | tf_op jit(solution)/shard_map/ppermute | solution.py:72
  186.9 27.3 %collective-permute-start.7 = (bf16[160,1152]{1,0:T(8,128)(2,1)S(1)}, bf16[160,1152]{1,0:T(8,128)(2,1)S(1)}, u32[]{:S(2)}, u32[]{:S(2)}) collective-permute-start(bf16[160,1152]{1,0:T(8,128)(2,1)S(1)} %add_convert_fusion), channel_id=1, source_target_pairs={{0,16},{8,24},{16,0},{24,8},{1,17},{9,25},{17,1},{25,9},{2,18},{10... | collective-permute-start | bytes 1105928 | tf_op jit(solution)/shard_map/ppermute | solution.py:72
  187.0 27.2 %collective-permute-start.8 = (bf16[160,1152]{1,0:T(8,128)(2,1)S(1)}, bf16[160,1152]{1,0:T(8,128)(2,1)S(1)}, u32[]{:S(2)}, u32[]{:S(2)}) collective-permute-start(bf16[160,1152]{1,0:T(8,128)(2,1)S(1)} %add_convert_fusion), channel_id=1, source_target_pairs={{0,24},{8,16},{16,8},{24,0},{1,25},{9,17},{17,9},{25,1},{2,26},{10... | collective-permute-start | bytes 1105928 | tf_op jit(solution)/shard_map/ppermute | solution.py:72
  188.9 37.8 %collective-permute-start.10 = (bf16[160,1152]{1,0:T(8,128)(2,1)}, bf16[160,1152]{1,0:T(8,128)(2,1)S(1)}, u32[]{:S(2)}, u32[]{:S(2)}) collective-permute-start(bf16[160,1152]{1,0:T(8,128)(2,1)} %bitcast.31), channel_id=1, source_target_pairs={{0,16},{8,24},{16,0},{24,8},{1,17},{9,25},{17,1},{25,9},{2,18},{10... | collective-permute-start | bytes 1105928 | tf_op jit(solution)/shard_map/ppermute | solution.py:72
  190.4 36.4 %collective-permute-start.11 = (bf16[160,1152]{1,0:T(8,128)(2,1)}, bf16[160,1152]{1,0:T(8,128)(2,1)}, u32[]{:S(2)}, u32[]{:S(2)}) collective-permute-start(bf16[160,1152]{1,0:T(8,128)(2,1)} %bitcast.31), channel_id=1, source_target_pairs={{0,24},{8,16},{16,8},{24,0},{1,25},{9,17},{17,9},{25,1},{2,26},{10... | collective-permute-start | bytes 1105928 | tf_op jit(solution)/shard_map/ppermute | solution.py:72
  233.1 110.7 %reduce-scatter.10.cloned.1.call-start = ((), (), s32[]{:S(2)}) async-start(), calls=%async_computation.22 | async-start | bytes 2985984 | tf_op jit(solution)/shard_map/reduce_scatter | solution.py:206
  245.7 21.4 %collective-permute-start.12 = (bf16[160,1152]{1,0:T(8,128)(2,1)}, bf16[160,1152]{1,0:T(8,128)(2,1)S(1)}, u32[]{:S(2)}, u32[]{:S(2)}) collective-permute-start(bf16[160,1152]{1,0:T(8,128)(2,1)} %get-tuple-element.73), channel_id=1, source_target_pairs={{0,8},{8,0},{16,24},{24,16},{1,9},{9,1},{17,25},{25,17},{2,10},{10... | collective-permute-start | bytes 1105928 | tf_op jit(solution)/shard_map/ppermute | solution.py:72
  246.3 20.8 %collective-permute-start.13 = (bf16[160,1152]{1,0:T(8,128)(2,1)}, bf16[160,1152]{1,0:T(8,128)(2,1)S(1)}, u32[]{:S(2)}, u32[]{:S(2)}) collective-permute-start(bf16[160,1152]{1,0:T(8,128)(2,1)} %get-tuple-element.75), channel_id=1, source_target_pairs={{0,16},{8,24},{16,0},{24,8},{1,17},{9,25},{17,1},{25,9},{2,18},{10... | collective-permute-start | bytes 1105928 | tf_op jit(solution)/shard_map/ppermute | solution.py:72
  275.1 112.3 %reduce-scatter.12.cloned.1.call-start = ((), (), s32[]{:S(2)}) async-start(), calls=%async_computation.23 | async-start | bytes 3317760 | tf_op jit(solution)/shard_map/reduce_scatter | solution.py:231
  349.1 91.7 %reduce-scatter.14.cloned.1.call-start = ((), (), s32[]{:S(2)}) async-start(), calls=%async_computation.24 | async-start | bytes 2985984 | tf_op jit(solution)/shard_map/reduce_scatter | solution.py:236
  394.3 20.5 %all-to-all-start.7 = ((bf16[4,288,432]{2,1,0:T(8,128)(2,1)}), bf16[4,288,432]{2,1,0:T(8,128)(2,1)S(1)}, u32[]{:S(2)}, u32[]{:S(2)}) async-start(bf16[4,288,432]{2,1,0:T(8,128)(2,1)} %bitcast.157), calls=%async_computation.11 | async-start | bytes 2359296 | tf_op jit(solution)/shard_map/all_to_all | solution.py:238
  399.9 36.8 %collective-permute-start.18 = (bf16[160,1152]{1,0:T(8,128)(2,1)}, bf16[160,1152]{1,0:T(8,128)(2,1)S(1)}, u32[]{:S(2)}, u32[]{:S(2)}) collective-permute-start(bf16[160,1152]{1,0:T(8,128)(2,1)} %get-tuple-element.63), channel_id=1, source_target_pairs={{0,8},{8,0},{16,24},{24,16},{1,9},{9,1},{17,25},{25,17},{2,10},{10... | collective-permute-start | bytes 1105928 | tf_op jit(solution)/shard_map/ppermute | solution.py:72
  402.0 34.7 %collective-permute-start.19 = (bf16[160,1152]{1,0:T(8,128)(2,1)}, bf16[160,1152]{1,0:T(8,128)(2,1)}, u32[]{:S(2)}, u32[]{:S(2)}) collective-permute-start(bf16[160,1152]{1,0:T(8,128)(2,1)} %get-tuple-element.63), channel_id=1, source_target_pairs={{0,16},{8,24},{16,0},{24,8},{1,17},{9,25},{17,1},{25,9},{2,18},{10... | collective-permute-start | bytes 1105928 | tf_op jit(solution)/shard_map/ppermute | solution.py:72
  403.4 33.3 %collective-permute-start.20 = (bf16[160,1152]{1,0:T(8,128)(2,1)}, bf16[160,1152]{1,0:T(8,128)(2,1)}, u32[]{:S(2)}, u32[]{:S(2)}) collective-permute-start(bf16[160,1152]{1,0:T(8,128)(2,1)} %get-tuple-element.63), channel_id=1, source_target_pairs={{0,24},{8,16},{16,8},{24,0},{1,25},{9,17},{17,9},{25,1},{2,26},{10... | collective-permute-start | bytes 1105928 | tf_op jit(solution)/shard_map/ppermute | solution.py:72
  434.6 56.8 %reduce-scatter.16.cloned.1.call-start = ((), (), s32[]{:S(2)}) async-start(), calls=%async_computation.25 | async-start | bytes 1492992
  (83 other events, 1156.5 us)
Sparse Core Ops, SparseCore 0:
  9.7 27.3 all-gather.5
  65.4 41.6 all-gather.7
  109.3 32.9 all-gather.9
  160.4 37.4 all-gather.11
  233.2 36.8 reduce-scatter.7
  275.2 38.2 reduce-scatter.9
  349.2 38.1 reduce-scatter.11
  389.8 37.2 reduce-scatter.13
  440.9 34.4 reduce-scatter.15

commit v4 on v3

--- a/solution.py
+++ b/solution.py
@@ -1,8 +1,11 @@
+import math
 from functools import partial
 
 import jax
 import jax.numpy as jnp
 from jax import lax
+from jax.experimental import pallas as pl
+from jax.experimental.pallas import tpu as pltpu
 from jax.sharding import PartitionSpec as P
 
 HEADS = 16
@@ -48,6 +51,49 @@
 
 def times_transposed(left, right):
     return lax.dot_general(left, right, (((1,), (1,)), ((), ())), preferred_element_type=F32)
+
+
+def gelu_kernel(rows_at_once, x_ref, w_ref, bias_ref, value_ref, slope_ref):
+    for start in range(0, x_ref.shape[0], rows_at_once):
+        at = pl.ds(start, rows_at_once)
+        pre = dot(x_ref[at, :], w_ref[...]) + bias_ref[...]
+        bell = jnp.exp(-0.5 * pre * pre)
+        t = 1.0 / (1.0 + (0.3275911 * 0.5**0.5) * jnp.abs(pre))
+        tail = 0.5 * 1.061405429
+        for c in (-1.453152027, 1.421413741, -0.284496736, 0.254829592):
+            tail = tail * t + 0.5 * c
+        tail = tail * t * bell
+        below = jnp.where(pre < 0.0, tail, 1.0 - tail)
+        value_ref[at, :] = (pre * below).astype(BF16)
+        slope_ref[at, :] = below + pre * bell * (0.5 / math.pi) ** 0.5
+
+
+def gelu_of_matmul(x, w, bias):
+    rows, depth = x.shape
+    columns = w.shape[1]
+    step = 384 if columns % 384 == 0 else columns
+    rows_at_once = 160 if rows % 160 == 0 else rows
+    block = pl.BlockSpec((rows, step), lambda j: (0, j))
+    return pl.pallas_call(
+        partial(gelu_kernel, rows_at_once),
+        grid=(columns // step,),
+        in_specs=[
+            pl.BlockSpec((rows, depth), lambda j: (0, 0)),
+            pl.BlockSpec((depth, step), lambda j: (0, j)),
+            pl.BlockSpec((1, step), lambda j: (0, j)),
+        ],
+        out_specs=[block, block],
+        out_shape=[
+            jax.ShapeDtypeStruct((rows, columns), BF16),
+            jax.ShapeDtypeStruct((rows, columns), F32),
+        ],
+        compiler_params=pltpu.CompilerParams(vmem_limit_bytes=40 * 2**20),
+        cost_estimate=pl.CostEstimate(
+            flops=2 * rows * depth * columns,
+            bytes_accessed=2 * depth * (rows + columns) + 6 * rows * columns,
+            transcendentals=rows * columns,
+        ),
+    )(x, w, bias.reshape(1, columns))
 
 
 def on_device(
@@ -92,13 +138,21 @@
 
     skip_part = lax.all_gather(skip_w, "seq", axis=0, tiled=True)
 
+    rows = features // n
+    wide = 3 * head_cols
     own_vectors = (skip_b, ln1_g, ln1_b, proj_b, ln2_g, ln2_b, fc2_b, fc1_b)
     packed = jnp.concatenate(own_vectors)
     own_size = packed.shape[0]
-    padded = -(-own_size // 1024) * 1024
-    packed = jnp.pad(packed, (0, padded - own_size)).reshape(padded // 128, 128)
-    vectors = spread(packed, ("dp", "seq"), n).reshape(n, padded).astype(F32)
-    small = features // n
+    extra = -(-own_size // wide)
+    extra += -(rows + extra) % 8
+    packed = jnp.pad(packed, (0, extra * wide - own_size)).reshape(1, extra, wide)
+    qkv_out = qkv_w.reshape(rows, 3, ns, head_cols).transpose(2, 0, 1, 3).reshape(ns, rows, wide)
+    qkv_out = jnp.concatenate([qkv_out, jnp.broadcast_to(packed, (ns, extra, wide))], axis=1)
+    qkv_mine = spread(seq_exchange(qkv_out).reshape(ns * (rows + extra), wide), "dp", nd)
+    qkv_mine = qkv_mine.reshape(n, rows + extra, wide)
+    vectors = qkv_mine[:, rows:].reshape(n, extra * wide).astype(F32)
+    qkv_mine = qkv_mine[:, :rows].reshape(features, wide)
+    small = rows
 
     def vector(index):
         return vectors[:, index * small : (index + 1) * small].reshape(features)
@@ -123,17 +177,19 @@
     xhat_one, inverse_one = norm_pieces(first)
     normed_one = (xhat_one * g_one + b_one).astype(BF16)
 
-    qkv_mine = seq_exchange(
-        qkv_w.reshape(features // n, 3, ns, head_cols).transpose(2, 0, 1, 3)
-        .reshape(ns, features // n, 3 * head_cols)
-    )
-    qkv_mine = spread(qkv_mine.reshape(features // nd, 3 * head_cols), "dp", nd)
-    qkv_mine = qkv_mine.reshape(features, 3 * head_cols)
     own_proj, skip_part = after((proj_w, skip_part))
     w_proj = lax.all_gather(own_proj, "seq", axis=0, tiled=True)
     normed_one, w_proj = after((normed_one, w_proj))
     normed_one_row = lax.all_gather(normed_one, "seq", axis=0, tiled=True)
+    up_slices = jnp.swapaxes(fc1_w.reshape(features // n, nd, hidden_part), 0, 1)
+    up_slices = lax.all_to_all(up_slices, "dp", 0, 0, tiled=True)
     w_proj = spread(w_proj, "dp", nd).reshape(features, features)
+    normed_one_row, w_proj, up_slices, qkv_mine = after(
+        (normed_one_row, w_proj, up_slices, qkv_mine)
+    )
+    up_part = lax.all_gather(
+        up_slices.reshape(features // ns, hidden_part), "seq", axis=0, tiled=True
+    )
     triple = dot(normed_one_row, qkv_mine).astype(BF16)
     queries, keys, values = (
         jnp.swapaxes(
@@ -163,36 +219,27 @@
         return jnp.swapaxes(v.reshape(row_len, heads, HEAD_DIM), 0, 1)
 
     attended_low = heads_to_tokens(attended_heads)
-    second = first + dot(attended_low, w_proj) + b_proj
-    xhat_two, inverse_two = norm_pieces(second)
-    normed_two = (xhat_two * g_two + b_two).astype(BF16)
-
-    up_slices = jnp.swapaxes(fc1_w.reshape(features // n, nd, hidden_part), 0, 1)
-    up_slices = lax.all_to_all(up_slices, "dp", 0, 0, tiled=True)
-    up_slices, normed_one_row = after((up_slices, normed_one_row))
-    up_part = lax.all_gather(
-        up_slices.reshape(features // ns, hidden_part), "seq", axis=0, tiled=True
-    )
     own_down, up_part = after((fc2_w, up_part))
     down_part = lax.all_gather(own_down, "seq", axis=0, tiled=True)
     up_part = jnp.swapaxes(up_part.reshape(ns, nd, features // n, hidden_part), 0, 1)
     up_part = up_part.reshape(features, hidden_part)
     grad_out = cotangent[0]
     grad_out_rows = gather_rows(grad_out)
+    attended_low, up_part, grad_out_rows = after((attended_low, up_part, grad_out_rows))
+    second = first + dot(attended_low, w_proj) + b_proj
+    xhat_two, inverse_two = norm_pieces(second)
+    normed_two = (xhat_two * g_two + b_two).astype(BF16)
+
     normed_two_rows = gather_rows(normed_two)
-    pre = dot(normed_two_rows, up_part) + up_bias
-    gelu_value, gelu_pull = jax.vjp(partial(jax.nn.gelu, approximate=False), pre)
-    hidden = gelu_value.astype(BF16)
-
-    pre_grad = gelu_pull(times_transposed(grad_out_rows, down_part))[0]
+    hidden, slope = gelu_of_matmul(normed_two_rows, up_part, up_bias)
+
+    pre_grad = times_transposed(grad_out_rows, down_part) * slope
     pre_low = pre_grad.astype(BF16)
     normed_two_grad = add_rows(times_transposed(pre_low, up_part))
+    hidden_again, pre_low = after((hidden, pre_low))
     fc2_w_grad = lax.psum_scatter(
-        inner(hidden, grad_out_rows).astype(BF16), "seq", scatter_dimension=0, tiled=True
-    )
-    normed_two_grad, hidden = after((normed_two_grad, hidden))
-    output = second + add_rows(dot(hidden, down_part)) + b_down
-    output = output.astype(BF16)[None]
+        inner(hidden_again, grad_out_rows).astype(BF16), "seq", scatter_dimension=0, tiled=True
+    )
 
     def by_seq(grad):
         grad = grad.reshape(nd, ns, features // n, grad.shape[1]).astype(BF16)
@@ -202,14 +249,22 @@
         grad = grad.reshape(nd, features // n, grad.shape[1])
         return lax.all_to_all(grad, "dp", 0, 0, tiled=True)
 
-    fc1_terms, fc2_w_grad = after((by_seq(inner(normed_two_rows, pre_low)), fc2_w_grad))
+    fc1_terms = by_seq(inner(normed_two_rows, pre_low))
+    normed_two_grad, fc1_terms = after((normed_two_grad, fc1_terms))
+    fc1_terms, fc2_w_grad = after((fc1_terms, fc2_w_grad))
     fc1_terms = lax.psum_scatter(fc1_terms, "seq", scatter_dimension=0, tiled=True)
     fc2_w_grad = fc2_w_grad.astype(F32)
     through_two, ln2_g_grad, ln2_b_grad = norm_back(normed_two_grad, xhat_two, inverse_two, g_two)
     second_grad = grad_out.astype(F32) + through_two
     second_low = second_grad.astype(BF16)
-    proj_terms = by_seq(inner(attended_low, second_low))
     attended_grad = tokens_to_heads(times_transposed(second_low, w_proj).astype(BF16))
+    proj_terms = inner(attended_low, second_low).reshape(nd, features // nd, features)
+    proj_sum = lax.dynamic_index_in_dim(proj_terms, dp_at, 0, keepdims=False)
+    proj_low = proj_terms.astype(BF16)
+    for k in range(1, nd):
+        away = lax.dynamic_index_in_dim(proj_low, dp_at ^ k, 0, keepdims=False)
+        proj_sum = proj_sum + swap(away, k).astype(F32)
+    proj_sum = proj_sum.astype(BF16).reshape(ns, features // n, features)
     delta = jnp.sum(attended_grad.astype(F32) * attended_heads, axis=2, keepdims=True)
     probs = jnp.exp(logits - lse)
     prob_grad = head_dot("hqd,hkd->hqk", attended_grad, values)
@@ -225,21 +280,27 @@
         ],
         axis=1,
     )
-    triple_grad, fc1_terms = after((triple_grad, fc1_terms))
+    triple_grad, fc1_terms, proj_sum, hidden_late = after(
+        (triple_grad, fc1_terms, proj_sum, hidden)
+    )
+    normed_one_grad = lax.psum_scatter(
+        times_transposed(triple_grad, qkv_mine).astype(BF16), "seq", scatter_dimension=0, tiled=True
+    )
+    qkv_terms = inner(normed_one_row, triple_grad).astype(BF16)
+    qkv_terms = lax.all_to_all(
+        qkv_terms.reshape(nd, features // nd, wide), "dp", 0, 0, tiled=True
+    )
+    qkv_terms = jnp.sum(qkv_terms.astype(F32), axis=0).astype(BF16)
+    output = (second + add_rows(dot(hidden_late, down_part)) + b_down).astype(BF16)
     fc1_w_grad = jnp.swapaxes(from_dp(fc1_terms), 0, 1)
     fc1_w_grad = fc1_w_grad.reshape(features // n, hidden_units).astype(F32)
-    normed_one_grad = lax.psum_scatter(
-        times_transposed(triple_grad, qkv_mine).astype(BF16), "seq", scatter_dimension=0, tiled=True
-    )
-    normed_one_grad, proj_terms = after((normed_one_grad, proj_terms))
+    normed_one_grad, qkv_terms, output, fc1_w_grad, proj_sum = after(
+        (normed_one_grad, qkv_terms, output, fc1_w_grad, proj_sum)
+    )
+    output = output[None]
     normed_one_grad = normed_one_grad.astype(F32)
-    proj_terms = lax.psum_scatter(proj_terms, "seq", scatter_dimension=0, tiled=True)
-    qkv_terms = inner(normed_one_row, triple_grad).astype(BF16)
-    qkv_terms = lax.all_to_all(
-        qkv_terms.reshape(nd, features // nd, 3 * head_cols), "dp", 0, 0, tiled=True
-    )
-    qkv_terms = jnp.sum(qkv_terms.astype(F32), axis=0).astype(BF16)
-    qkv_w_grad = seq_exchange(qkv_terms.reshape(ns, features // n, 3 * head_cols))
+    proj_w_grad = jnp.sum(seq_exchange(proj_sum).astype(F32), axis=0)
+    qkv_w_grad = seq_exchange(qkv_terms.reshape(ns, features // n, wide))
     qkv_w_grad = (
         qkv_w_grad.reshape(ns, features // n, 3, head_cols)
         .transpose(1, 2, 0, 3).reshape(features // n, 3 * features).astype(F32)
@@ -247,10 +308,8 @@
     through_one, ln1_g_grad, ln1_b_grad = norm_back(normed_one_grad, xhat_one, inverse_one, g_one)
     first_grad = second_grad + through_one
     first_low_rows = gather_rows(first_grad.astype(BF16))
-    skip_terms, proj_terms = after((inner(joined_here, first_low_rows).astype(BF16), proj_terms))
-    proj_w_grad = jnp.sum(from_dp(proj_terms).astype(F32), axis=0)
     skip_w_grad = lax.psum_scatter(
-        skip_terms, "seq", scatter_dimension=0, tiled=True
+        inner(joined_here, first_low_rows).astype(BF16), "seq", scatter_dimension=0, tiled=True
     ).astype(F32)
     joined_grad_part = times_transposed(first_low_rows, skip_part).astype(BF16)
     away = []
@@ -281,6 +340,7 @@
         jnp.zeros((n, hidden_units // n), F32), up_grads, dp_at * ns, 0
     )
     vector_grads = jnp.concatenate([vector_grads, up_grads], axis=1)
+    padded = -(-own_size // 1024) * 1024
     vector_grads = jnp.pad(vector_grads, ((0, 0), (0, padded - own_size)))
     vector_grads = lax.all_to_all(
         vector_grads.reshape(n, padded // 128, 128), ("dp", "seq"), 0, 0, tiled=True

time: 508 us -> 541 us (1.065)
  waiting for transfers between devices: 167 us -> 192 us
  other arithmetic: 21.1 us -> 35.6 us
  matrix products: 94.5 us -> 82.7 us
    ppermute x24 -> x27, waiting for transfers between devices: 26.9 us -> 62 us  [swap(): return lax.ppermute(v, 'dp', [(i, i ^ k) for i in range(nd)])]
    reduce_scatter x1, waiting for transfers between devices: 29 us -> 0.02 us  [on_device(): lax.psum_scatter(times_transposed(triple_grad, qkv_mine).astype(BF16), 's...]
    all_to_all x2, waiting for transfers between devices: 18.4 us -> 41.9 us  [spread(): return lax.all_to_all(copies, axes, 0, 0, tiled=True)]
    all_to_all x2 -> x1, waiting for transfers between devices: 16.9 us -> 0.01 us  [from_dp(): return lax.all_to_all(grad, 'dp', 0, 0, tiled=True)]
    dot_general x5 -> x4, matrix products: 30 us -> 16.8 us  [dot(): return jnp.dot(left, right, preferred_element_type=F32)]
    all_gather x1, waiting for transfers between devices: 0.02 us -> 10.4 us  [on_device(): lax.all_gather(up_slices.reshape(features // ns, hidden_part), 'seq', axi...]
    all_to_all x3 -> x4, waiting for transfers between devices: 44.1 us -> 53 us  [seq_exchange(): return lax.all_to_all(v, 'seq', 0, 0, tiled=True)]
    all_gather x1, waiting for transfers between devices: 8.49 us -> 0.01 us  [on_device(): skip_part = lax.all_gather(skip_w, 'seq', axis=0, tiled=True)]
  transfers between devices with their start and end apart: 43 -> 44, of which waited for: 19 -> 25; matrix products, arithmetic and copies ran while one was open for 34% -> 29% of each run, Pallas kernels for 0% -> 1%
where the time goes in v4:
time: 541 us; the launch traced here: 534 us
  waiting for transfers between devices  192 us (35%)
  matrix products  82.7 us (15%)
  local copies, waits for them, and re-layouts  80.9 us (15%)
  starting transfers between devices  67.1 us (12%)
  blocking collectives  51.6 us (10%)
  other arithmetic  35.6 us (7%)
  between operations  18.6 us (3%)
    ppermute x27, waiting for transfers between devices, swap(): return lax.ppermute(v, 'dp', [(i, i ^ k) for i in range(nd)])  62 us
    all_to_all x4, waiting for transfers between devices, seq_exchange(): return lax.all_to_all(v, 'seq', 0, 0, tiled=True)  53 us
    all_to_all x2, waiting for transfers between devices, spread(): return lax.all_to_all(copies, axes, 0, 0, tiled=True)  41.9 us
    ppermute x27, starting transfers between devices, swap(): return lax.ppermute(v, 'dp', [(i, i ^ k) for i in range(nd)])  31.7 us
    dot_general x6, matrix products, head_dot(): return jnp.einsum(spec, left, right, preferred_element_type=F32)  30.8 us
    all_to_all x1, blocking collectives, seq_exchange(): return lax.all_to_all(v, 'seq', 0, 0, tiled=True)  25.2 us
    dot_general x5, matrix products, times_transposed(): lax.dot_general(left, right, (((1,), (1,)), ((), ())), preferred_element_...  21.5 us
    dot_general x4, matrix products, dot(): return jnp.dot(left, right, preferred_element_type=F32)  16.8 us
  transfers between devices with their start and end apart: 44, of which 25 were waited for; matrix products, arithmetic and copies ran while one was open for 29% of the time, Pallas kernels for 1%

profile of v4, /device:TPU:0, one launch (start us, length us, event | category | flops | bytes accessed | tf_op | source)
XLA Modules:
  0.0 533.7 jit_solution(13287278368641677852)
XLA Ops:
  15.8 25.2 %all_to_all.55 = bf16[8,40,432]{2,1,0:T(8,128)(2,1)S(1)} all-to-all(bf16[8,40,432]{2,1,0:T(8,128)(2,1)S(1)} %copy.121), channel_id=1, replica_groups=mesh['dp'=4,'seq'=8] {'seq'}, dimensions={0} | all-to-all | bytes 552960 | tf_op jit(solution)/shard_map/all_to_all | solution.py:131
  50.0 14.7 %all-to-all-done.1 = bf16[4,320,432]{2,1,0:T(8,128)(2,1)S(1)} async-done(((bf16[4,320,432]{2,1,0:T(8,128)(2,1)}), bf16[4,320,432]{2,1,0:T(8,128)(2,1)S(1)}, u32[]{:S(2)}, u32[]{:S(2)}) %all-to-all-start.1) | async-done | bytes 1105952 | tf_op jit(solution)/shard_map/all_to_all | solution.py:135
  80.7 15.6 %all-gather = bf16[8,36,1152]{2,1,0:T(8,128)(2,1)S(1)} all-gather(bf16[1,36,1152]{2,1,0:T(8,128)(2,1)S(1)} %bitcast.189), channel_id=1, replica_groups=mesh['dp'=4,'seq'=8] {'seq'}, dimensions={0}, use_global_device_ids=true | all-gather | bytes 746496 | tf_op jit(solution)/shard_map/all_gather | solution.py:181
  100.1 10.8 %all_to_all.56 = bf16[4,36,1152]{2,1,0:T(8,128)(2,1)} all-to-all(bf16[4,36,1152]{2,1,0:T(8,128)(2,1)S(1)} %bitcast.178), channel_id=1, replica_groups=mesh['dp'=4,'seq'=8] {'dp'}, dimensions={0} | all-to-all | bytes 663552 | tf_op jit(solution)/shard_map/all_to_all | solution.py:185
  119.5 27.3 %all-to-all-done.2 = bf16[4,288,1152]{2,1,0:T(8,128)(2,1)S(1)} async-done(((bf16[4,288,1152]{2,1,0:T(8,128)(2,1)}), bf16[4,288,1152]{2,1,0:T(8,128)(2,1)S(1)}, u32[]{:S(2)}, u32[]{:S(2)}) %all-to-all-start.2) | async-done | bytes 2654240 | tf_op jit(solution)/shard_map/all_to_all | solution.py:135
  163.9 6.4 %fusion.53 = (f32[2,1280]{1,0:T(2,128)S(1)}, f32[2,1280,1280]{1,2,0:T(8,128)}) fusion(bf16[2,1280,72]{1,2,0:T(8,128)(2,1)S(1)} %bitcast.169, bf16[2,1280,72]{1,2,0:T(8,128)(2,1)S(1)} %bitcast.167, pred[1280,1280]{0,1:T(8,128)(4,1)S(1)} %broadcast_compare_fusion), kind=kOutput, calls=%fused_computation.139 | convolution fusion | flops 481687040 | bytes 15493120 | tf_op jit(solution)/shard_map/hqd,hkd->hqk/dot_general | solution.py:204
  170.3 10.4 %all-gather.10.cloned.1.call-done = bf16[1152,1152]{1,0:T(8,128)(2,1)} async-done(((bf16[144,1152]{1,0:T(8,128)(2,1)}), bf16[1152,1152]{1,0:T(8,128)(2,1)}) %all-gather.10.cloned.1.call-update) | async-done | bytes 2654224 | tf_op jit(solution)/shard_map/all_gather | solution.py:190
  180.7 6.6 %exponential_reduce_fusion = f32[2,1280]{1,0:T(2,128)S(1)} fusion(f32[2,1280,1280]{1,2,0:T(8,128)} %get-tuple-element.148, f32[2,1280]{1,0:T(2,128)S(1)} %get-tuple-element.147), kind=kLoop, calls=%fused_computation.6 | loop fusion | flops 6551040 | bytes 13127680 | tf_op jit(solution)/shard_map/reduce_sum | solution.py:208
  203.0 23.6 %all-to-all-done.4 = bf16[8,160,144]{1,2,0:T(8,128)(2,1)} async-done(((bf16[8,160,144]{1,2,0:T(8,128)(2,1)}), bf16[8,160,144]{1,2,0:T(8,128)(2,1)}, u32[]{:S(2)}, u32[]{:S(2)}) %all-to-all-start.4) | async-done | bytes 368672 | tf_op jit(solution)/shard_map/all_to_all | solution.py:131
  247.2 8.2 %collective-permute-done.11 = bf16[160,1152]{1,0:T(8,128)(2,1)} collective-permute-done((bf16[160,1152]{1,0:T(8,128)(2,1)}, bf16[160,1152]{1,0:T(8,128)(2,1)}, u32[]{:S(2)}, u32[]{:S(2)}) %collective-permute-start.11) | collective-permute-done | bytes 368672 | tf_op jit(solution)/shard_map/ppermute | solution.py:118
  255.4 6.9 %collective-permute-done.10 = bf16[160,1152]{1,0:T(8,128)(2,1)} collective-permute-done((bf16[160,1152]{1,0:T(8,128)(2,1)}, bf16[160,1152]{1,0:T(8,128)(2,1)}, u32[]{:S(2)}, u32[]{:S(2)}) %collective-permute-start.10) | collective-permute-done | bytes 368672 | tf_op jit(solution)/shard_map/ppermute | solution.py:118
  271.9 6.6 %multiply_reduce_fusion = (f32[1152]{0:T(1024)S(1)}, bf16[640,1152]{1,0:T(8,128)(2,1)}) fusion(f32[640,1152]{1,0:T(8,128)} %copy-done, bf16[640,1152]{1,0:T(8,128)(2,1)} %pad_maximum_fusion, bf16[1152,1152]{1,0:T(8,128)(2,1)} %all-gather.12.cloned.1.call-done), kind=kOutput, calls=%fused_computation.32 | convolution fusion | flops 1700903808 | bytes 8557056 | tf_op jit(solution)/shard_map/dot_general | solution.py:53
  310.3 8.1 %reduce-scatter.7.cloned.1.call-done = bf16[144,1152]{1,0:T(8,128)(2,1)} async-done(((bf16[1152,1152]{1,0:T(8,128)(2,1)}), bf16[144,1152]{1,0:T(8,128)(2,1)}) %reduce-scatter.7.cloned.1.call-update) | async-done | bytes 331792 | tf_op jit(solution)/shard_map/reduce_scatter | solution.py:240
  338.0 18.0 %all-to-all-done.5 = bf16[8,160,144]{1,2,0:T(8,128)(2,1)} async-done(((bf16[8,160,144]{1,2,0:T(8,128)(2,1)}), bf16[8,160,144]{1,2,0:T(8,128)(2,1)}, u32[]{:S(2)}, u32[]{:S(2)}) %all-to-all-start.5) | async-done | bytes 368672 | tf_op jit(solution)/shard_map/all_to_all | solution.py:131
  360.0 8.6 %fusion.4 = bf16[2,1280,1280]{1,2,0:T(8,128)(2,1)} fusion(bf16[2,1280,72]{1,2,0:T(8,128)(2,1)} %bitcast.162, f32[2,1280,1280]{1,2,0:T(8,128)} %get-tuple-element.148, f32[2,1280]{1,0:T(2,128)S(1)} %multiply_reduce_fusion.2, f32[2,1280]{1,0:T(2,128)S(1)} %log_add_fusion, bf16[1280,2,72]{0,2,1:T(8,128)(2,1)S(1)} %reshape.291), kind=kOutput, calls=%fused_computation.8 | convolution fusion | flops 488243200 | bytes 20418560 | tf_op jit(solution)/shard_map/hqd,hkd->hqk/dot_general | solution.py:204
  368.6 5.8 %convolution_convert_fusion.8 = bf16[2,1280,72]{1,2,0:T(8,128)(2,1)S(1)} fusion(bf16[2,1280,1280]{1,2,0:T(8,128)(2,1)} %fusion.4, bf16[2,1280,72]{1,2,0:T(8,128)(2,1)S(1)} %bitcast.170), kind=kOutput, calls=%fused_computation.20 | convolution fusion | flops 472043520 | bytes 7290880 | tf_op jit(solution)/shard_map/hqk,hqd->hkd/dot_general | solution.py:204
  396.7 5.8 %fusion.56 = (bf16[640,1152]{1,0:T(8,128)(2,1)S(1)}, f32[640,1152]{1,0:T(8,128)}) fusion(bf16[640,1152]{1,0:T(8,128)(2,1)S(1)} %copy-done.3, bf16[1152,1152]{1,0:T(8,128)(2,1)} %all-gather.12.cloned.1.call-done), kind=kOutput, calls=%fused_computation.142 | convolution fusion | flops 1699430400 | bytes 8552448 | tf_op jit(solution)/shard_map/dot_general | solution.py:45
  419.3 8.0 %collective-permute-done.19 = bf16[160,1152]{1,0:T(8,128)(2,1)S(1)} collective-permute-done((bf16[160,1152]{1,0:T(8,128)(2,1)}, bf16[160,1152]{1,0:T(8,128)(2,1)S(1)}, u32[]{:S(2)}, u32[]{:S(2)}) %collective-permute-start.19) | collective-permute-done | bytes 368672 | tf_op jit(solution)/shard_map/ppermute | solution.py:118
  430.5 8.4 %all-to-all-done.6 = bf16[4,288,432]{2,1,0:T(8,128)(2,1)} async-done(((bf16[4,288,432]{2,1,0:T(8,128)(2,1)}), bf16[4,288,432]{2,1,0:T(8,128)(2,1)}, u32[]{:S(2)}, u32[]{:S(2)}) %all-to-all-start.6) | async-done | bytes 995360 | tf_op jit(solution)/shard_map/all_to_all | solution.py:290
  446.8 8.9 %collective-permute-done.23 = bf16[160,1152]{1,0:T(8,128)(2,1)S(1)} collective-permute-done((bf16[160,1152]{1,0:T(8,128)(2,1)S(1)}, bf16[160,1152]{1,0:T(8,128)(2,1)S(1)}, u32[]{:S(2)}, u32[]{:S(2)}) %collective-permute-start.23) | collective-permute-done | bytes 368672 | tf_op jit(solution)/shard_map/ppermute | solution.py:118
  455.7 6.5 %collective-permute-done.22 = bf16[160,1152]{1,0:T(8,128)(2,1)S(1)} collective-permute-done((bf16[160,1152]{1,0:T(8,128)(2,1)S(1)}, bf16[160,1152]{1,0:T(8,128)(2,1)S(1)}, u32[]{:S(2)}, u32[]{:S(2)}) %collective-permute-start.22) | collective-permute-done | bytes 368672 | tf_op jit(solution)/shard_map/ppermute | solution.py:118
  472.2 7.4 %all-to-all-done.10 = f32[32,8,128]{2,1,0:T(8,128)S(1)} async-done(((f32[32,8,128]{2,1,0:T(8,128)}), f32[32,8,128]{2,1,0:T(8,128)S(1)}, u32[]{:S(2)}, u32[]{:S(2)}) %all-to-all-start.10) | async-done | bytes 131104 | tf_op jit(solution)/shard_map/all_to_all | solution.py:345
  487.0 11.3 %all-to-all-done.8 = bf16[8,36,432]{2,1,0:T(8,128)(2,1)S(1)} async-done(((bf16[8,36,432]{2,1,0:T(8,128)(2,1)}), bf16[8,36,432]{2,1,0:T(8,128)(2,1)S(1)}, u32[]{:S(2)}, u32[]{:S(2)}) %all-to-all-start.8) | async-done | bytes 248864 | tf_op jit(solution)/shard_map/all_to_all | solution.py:131
  514.3 5.8 %collective-permute-done.25 = bf16[160,576]{0,1:T(8,128)(2,1)} collective-permute-done((bf16[160,576]{0,1:T(8,128)(2,1)}, bf16[160,576]{0,1:T(8,128)(2,1)}, u32[]{:S(2)}, u32[]{:S(2)}) %collective-permute-start.25) | collective-permute-done | bytes 184352 | tf_op jit(solution)/shard_map/ppermute | solution.py:118
  (319 shorter events, 250.1 us)
Async XLA Ops:
  7.2 64.2 %all-gather.6.cloned.1.call-start = ((), (), s32[]{:S(2)}) async-start(), calls=%async_computation.15 | async-start | bytes 1492992 | tf_op jit(solution)/shard_map/all_gather | solution.py:139
  42.2 22.5 %all-to-all-start.1 = ((bf16[4,320,432]{2,1,0:T(8,128)(2,1)}), bf16[4,320,432]{2,1,0:T(8,128)(2,1)S(1)}, u32[]{:S(2)}, u32[]{:S(2)}) async-start(bf16[4,320,432]{2,1,0:T(8,128)(2,1)} %broadcast_in_dim.34), calls=%async_computation.1 | async-start | bytes 2621440 | tf_op jit(solution)/shard_map/all_to_all | solution.py:135
  45.9 100.9 %all-gather.8.cloned.1.call-start = ((), (), s32[]{:S(2)}) async-start(), calls=%async_computation.16 | async-start | bytes 3317760 | tf_op jit(solution)/shard_map/all_gather | solution.py:183
  46.4 22.7 %collective-permute-start.2 = (bf16[160,576]{1,0:T(8,128)(2,1)S(1)}, bf16[160,576]{1,0:T(8,128)(2,1)S(1)}, u32[]{:S(2)}, u32[]{:S(2)}) collective-permute-start(bf16[160,576]{1,0:T(8,128)(2,1)S(1)} %get-tuple-element.114), channel_id=1, source_target_pairs={{0,24},{8,16},{16,8},{24,0},{1,25},{9,17},{17,9},{25,1},{2,26},{10... | collective-permute-start | bytes 552968 | tf_op jit(solution)/shard_map/ppermute | solution.py:118
  49.4 21.9 %collective-permute-start.1 = (bf16[160,576]{1,0:T(8,128)(2,1)S(1)}, bf16[160,576]{1,0:T(8,128)(2,1)S(1)}, u32[]{:S(2)}, u32[]{:S(2)}) collective-permute-start(bf16[160,576]{1,0:T(8,128)(2,1)S(1)} %get-tuple-element.115), channel_id=1, source_target_pairs={{0,16},{8,24},{16,0},{24,8},{1,17},{9,25},{17,1},{25,9},{2,18},{10... | collective-permute-start | bytes 552968 | tf_op jit(solution)/shard_map/ppermute | solution.py:118
  50.0 21.4 %collective-permute-start = (bf16[160,576]{1,0:T(8,128)(2,1)S(1)}, bf16[160,576]{1,0:T(8,128)(2,1)S(1)}, u32[]{:S(2)}, u32[]{:S(2)}) collective-permute-start(bf16[160,576]{1,0:T(8,128)(2,1)S(1)} %get-tuple-element.116), channel_id=1, source_target_pairs={{0,8},{8,0},{16,24},{24,16},{1,9},{9,1},{17,25},{25,17},{2,10},{10... | collective-permute-start | bytes 552968 | tf_op jit(solution)/shard_map/ppermute | solution.py:118
  76.8 19.6 %collective-permute-start.5 = (bf16[160,1152]{1,0:T(8,128)(2,1)}, bf16[160,1152]{1,0:T(8,128)(2,1)S(1)}, u32[]{:S(2)}, u32[]{:S(2)}) collective-permute-start(bf16[160,1152]{1,0:T(8,128)(2,1)} %get-tuple-element.104), channel_id=1, source_target_pairs={{0,24},{8,16},{16,8},{24,0},{1,25},{9,17},{17,9},{25,1},{2,26},{10... | collective-permute-start | bytes 1105928 | tf_op jit(solution)/shard_map/ppermute | solution.py:118
  112.6 34.2 %all-to-all-start.2 = ((bf16[4,288,1152]{2,1,0:T(8,128)(2,1)}), bf16[4,288,1152]{2,1,0:T(8,128)(2,1)S(1)}, u32[]{:S(2)}, u32[]{:S(2)}) async-start(bf16[4,288,1152]{2,1,0:T(8,128)(2,1)} %broadcast_in_dim.35), calls=%async_computation.2 | async-start | bytes 5308416 | tf_op jit(solution)/shard_map/all_to_all | solution.py:135
  116.2 64.4 %all-gather.10.cloned.1.call-start = ((), (), s32[]{:S(2)}) async-start(), calls=%async_computation.17 | async-start | bytes 2985984 | tf_op jit(solution)/shard_map/all_gather | solution.py:190
  148.8 123.1 %all-gather.12.cloned.1.call-start = ((), (), s32[]{:S(2)}) async-start(), calls=%async_computation.18 | async-start | bytes 2985984 | tf_op jit(solution)/shard_map/all_gather | solution.py:223
  149.4 50.6 %collective-permute-start.8 = (bf16[160,1152]{1,0:T(8,128)(2,1)}, bf16[160,1152]{1,0:T(8,128)(2,1)}, u32[]{:S(2)}, u32[]{:S(2)}) collective-permute-start(bf16[160,1152]{1,0:T(8,128)(2,1)} %bitcast.174), channel_id=1, source_target_pairs={{0,24},{8,16},{16,8},{24,0},{1,25},{9,17},{17,9},{25,1},{2,26},{10... | collective-permute-start | bytes 1105928 | tf_op jit(solution)/shard_map/ppermute | solution.py:118
  150.8 49.2 %collective-permute-start.7 = (bf16[160,1152]{1,0:T(8,128)(2,1)}, bf16[160,1152]{1,0:T(8,128)(2,1)}, u32[]{:S(2)}, u32[]{:S(2)}) collective-permute-start(bf16[160,1152]{1,0:T(8,128)(2,1)} %bitcast.175), channel_id=1, source_target_pairs={{0,16},{8,24},{16,0},{24,8},{1,17},{9,25},{17,1},{25,9},{2,18},{10... | collective-permute-start | bytes 1105928 | tf_op jit(solution)/shard_map/ppermute | solution.py:118
  152.3 47.7 %collective-permute-start.6 = (bf16[160,1152]{1,0:T(8,128)(2,1)}, bf16[160,1152]{1,0:T(8,128)(2,1)}, u32[]{:S(2)}, u32[]{:S(2)}) collective-permute-start(bf16[160,1152]{1,0:T(8,128)(2,1)} %bitcast.176), channel_id=1, source_target_pairs={{0,8},{8,0},{16,24},{24,16},{1,9},{9,1},{17,25},{25,17},{2,10},{10... | collective-permute-start | bytes 1105928 | tf_op jit(solution)/shard_map/ppermute | solution.py:118
  195.3 31.3 %all-to-all-start.4 = ((bf16[8,160,144]{1,2,0:T(8,128)(2,1)}), bf16[8,160,144]{1,2,0:T(8,128)(2,1)}, u32[]{:S(2)}, u32[]{:S(2)}) async-start(bf16[8,160,144]{1,2,0:T(8,128)(2,1)} %copy.124), calls=%async_computation.4 | async-start | bytes 1179648 | tf_op jit(solution)/shard_map/all_to_all | solution.py:131
  199.8 118.6 %reduce-scatter.7.cloned.1.call-start = ((), (), s32[]{:S(2)}) async-start(), calls=%async_computation.19 | async-start | bytes 2985984 | tf_op jit(solution)/shard_map/reduce_scatter | solution.py:240
  282.4 103.4 %reduce-scatter.9.cloned.1.call-start = ((), (), s32[]{:S(2)}) async-start(), calls=%async_computation.20 | async-start | bytes 2985984 | tf_op jit(solution)/shard_map/reduce_scatter | solution.py:255
  325.2 30.9 %all-to-all-start.5 = ((bf16[8,160,144]{1,2,0:T(8,128)(2,1)}), bf16[8,160,144]{1,2,0:T(8,128)(2,1)}, u32[]{:S(2)}, u32[]{:S(2)}) async-start(bf16[8,160,144]{1,2,0:T(8,128)(2,1)} %copy.128), calls=%async_computation.5 | async-start | bytes 1179648 | tf_op jit(solution)/shard_map/all_to_all | solution.py:131
  329.4 111.1 %reduce-scatter.11.cloned.1.call-start = ((), (), s32[]{:S(2)}) async-start(), calls=%async_computation.21 | async-start | bytes 3317760 | tf_op jit(solution)/shard_map/reduce_scatter | solution.py:286
  334.5 48.1 %collective-permute-start.17 = (bf16[288,1152]{1,0:T(8,128)(2,1)}, bf16[288,1152]{1,0:T(8,128)(2,1)}, u32[]{:S(2)}, u32[]{:S(2)}) collective-permute-start(bf16[288,1152]{1,0:T(8,128)(2,1)} %get-tuple-element.93), channel_id=1, source_target_pairs={{0,24},{8,16},{16,8},{24,0},{1,25},{9,17},{17,9},{25,1},{2,26},{10... | collective-permute-start | bytes 1990664 | tf_op jit(solution)/shard_map/ppermute | solution.py:118
  336.9 45.7 %collective-permute-start.16 = (bf16[288,1152]{1,0:T(8,128)(2,1)}, bf16[288,1152]{1,0:T(8,128)(2,1)}, u32[]{:S(2)}, u32[]{:S(2)}) collective-permute-start(bf16[288,1152]{1,0:T(8,128)(2,1)} %get-tuple-element.94), channel_id=1, source_target_pairs={{0,16},{8,24},{16,0},{24,8},{1,17},{9,25},{17,1},{25,9},{2,18},{10... | collective-permute-start | bytes 1990664 | tf_op jit(solution)/shard_map/ppermute | solution.py:118
  337.4 45.2 %collective-permute-start.15 = (bf16[288,1152]{1,0:T(8,128)(2,1)}, bf16[288,1152]{1,0:T(8,128)(2,1)}, u32[]{:S(2)}, u32[]{:S(2)}) collective-permute-start(bf16[288,1152]{1,0:T(8,128)(2,1)} %get-tuple-element.92), channel_id=1, source_target_pairs={{0,8},{8,0},{16,24},{24,16},{1,9},{9,1},{17,25},{25,17},{2,10},{10... | collective-permute-start | bytes 1990664 | tf_op jit(solution)/shard_map/ppermute | solution.py:118
  410.2 28.7 %all-to-all-start.6 = ((bf16[4,288,432]{2,1,0:T(8,128)(2,1)}), bf16[4,288,432]{2,1,0:T(8,128)(2,1)}, u32[]{:S(2)}, u32[]{:S(2)}) async-start(bf16[4,288,432]{2,1,0:T(8,128)(2,1)} %bitcast.47), calls=%async_computation.9 | async-start | bytes 2359296 | tf_op jit(solution)/shard_map/all_to_all | solution.py:290
  414.5 110.5 %reduce-scatter.13.cloned.1.call-start = ((), (), s32[]{:S(2)}) async-start(), calls=%async_computation.22 | async-start | bytes 1492992
  498.3 25.8 %all-to-all-start.9 = ((bf16[8,36,1152]{2,1,0:T(8,128)(2,1)}), bf16[8,36,1152]{2,1,0:T(8,128)(2,1)S(1)}, u32[]{:S(2)}, u32[]{:S(2)}) async-start(bf16[8,36,1152]{2,1,0:T(8,128)(2,1)} %reshape.293), calls=%async_computation.12 | async-start | bytes 1474560 | tf_op jit(solution)/shard_map/all_to_all | solution.py:131
  (69 other events, 882.3 us)
Sparse Core Ops, SparseCore 0:
  9.7 33.0 all-gather.5
  100.0 34.3 all-gather.7
  148.9 31.7 all-gather.9
  182.2 44.4 all-gather.11
  282.5 35.8 reduce-scatter.6
  320.6 44.5 reduce-scatter.8
  391.2 37.6 reduce-scatter.10
  466.1 33.0 reduce-scatter.12

commit v5 on v4

--- a/solution.py
+++ b/solution.py
@@ -135,24 +135,30 @@
         return lax.all_to_all(copies, axes, 0, 0, tiled=True)
 
     after = lax.optimization_barrier
+    core = lax.axis_index("seq") % 2
+    places = ns // 2
+
+    def other_core(v):
+        return lax.ppermute(v, "seq", [(i, i ^ 1) for i in range(ns)])
+
+    def add_over_seq(terms):
+        terms = terms.reshape((places, 2) + terms.shape[1:])
+        given = lax.dynamic_index_in_dim(terms, 1 - core, 1, keepdims=False).astype(BF16)
+        kept = lax.dynamic_index_in_dim(terms, core, 1, keepdims=False).astype(F32)
+        sums = (kept + other_core(given).astype(F32)).astype(BF16)
+        groups = [[i * 2 + c for i in range(places)] for c in range(2)]
+        return lax.all_to_all(sums, "seq", 0, 0, axis_index_groups=groups, tiled=True)
 
     skip_part = lax.all_gather(skip_w, "seq", axis=0, tiled=True)
 
-    rows = features // n
-    wide = 3 * head_cols
     own_vectors = (skip_b, ln1_g, ln1_b, proj_b, ln2_g, ln2_b, fc2_b, fc1_b)
     packed = jnp.concatenate(own_vectors)
     own_size = packed.shape[0]
-    extra = -(-own_size // wide)
-    extra += -(rows + extra) % 8
-    packed = jnp.pad(packed, (0, extra * wide - own_size)).reshape(1, extra, wide)
-    qkv_out = qkv_w.reshape(rows, 3, ns, head_cols).transpose(2, 0, 1, 3).reshape(ns, rows, wide)
-    qkv_out = jnp.concatenate([qkv_out, jnp.broadcast_to(packed, (ns, extra, wide))], axis=1)
-    qkv_mine = spread(seq_exchange(qkv_out).reshape(ns * (rows + extra), wide), "dp", nd)
-    qkv_mine = qkv_mine.reshape(n, rows + extra, wide)
-    vectors = qkv_mine[:, rows:].reshape(n, extra * wide).astype(F32)
-    qkv_mine = qkv_mine[:, :rows].reshape(features, wide)
-    small = rows
+    padded = -(-own_size // 1024) * 1024
+    packed = jnp.pad(packed, (0, padded - own_size)).reshape(padded // 128, 128)
+    vectors = spread(packed, ("dp", "seq"), n).reshape(n, padded).astype(F32)
+    small = features // n
+    wide = 3 * head_cols
 
     def vector(index):
         return vectors[:, index * small : (index + 1) * small].reshape(features)
@@ -181,11 +187,29 @@
     w_proj = lax.all_gather(own_proj, "seq", axis=0, tiled=True)
     normed_one, w_proj = after((normed_one, w_proj))
     normed_one_row = lax.all_gather(normed_one, "seq", axis=0, tiled=True)
-    up_slices = jnp.swapaxes(fc1_w.reshape(features // n, nd, hidden_part), 0, 1)
+    own_qkv, normed_one = after((qkv_w, normed_one))
+    qkv_mine = seq_exchange(
+        own_qkv.reshape(features // n, 3, ns, head_cols).transpose(2, 0, 1, 3)
+        .reshape(ns, features // n, wide)
+    )
+    qkv_mine = spread(qkv_mine.reshape(features // nd, wide), "dp", nd).reshape(features, wide)
+    own_up, qkv_mine = after((fc1_w, qkv_mine))
+    up_slices = jnp.swapaxes(own_up.reshape(features // n, nd, hidden_part), 0, 1)
     up_slices = lax.all_to_all(up_slices, "dp", 0, 0, tiled=True)
-    w_proj = spread(w_proj, "dp", nd).reshape(features, features)
-    normed_one_row, w_proj, up_slices, qkv_mine = after(
-        (normed_one_row, w_proj, up_slices, qkv_mine)
+    half = features // nd // 2
+    own_half = lax.dynamic_slice_in_dim(w_proj, core * half, half, 0)
+    all_rows = lax.dynamic_update_slice_in_dim(
+        jnp.zeros((features, features), BF16), w_proj, dp_at * 2 * half, 0
+    )
+    for k in range(1, nd):
+        place = (dp_at ^ k) * 2
+        here = swap(own_half, k)
+        there = other_core(here)
+        all_rows = lax.dynamic_update_slice_in_dim(all_rows, here, (place + core) * half, 0)
+        all_rows = lax.dynamic_update_slice_in_dim(all_rows, there, (place + 1 - core) * half, 0)
+    w_proj = all_rows
+    normed_one_row, up_slices, qkv_mine, w_proj = after(
+        (normed_one_row, up_slices, qkv_mine, w_proj)
     )
     up_part = lax.all_gather(
         up_slices.reshape(features // ns, hidden_part), "seq", axis=0, tiled=True
@@ -218,8 +242,8 @@
         v = seq_exchange(jnp.swapaxes(v.reshape(local, ns, head_cols), 0, 1))
         return jnp.swapaxes(v.reshape(row_len, heads, HEAD_DIM), 0, 1)
 
+    own_down, attended_heads = after((fc2_w, attended_heads))
     attended_low = heads_to_tokens(attended_heads)
-    own_down, up_part = after((fc2_w, up_part))
     down_part = lax.all_gather(own_down, "seq", axis=0, tiled=True)
     up_part = jnp.swapaxes(up_part.reshape(ns, nd, features // n, hidden_part), 0, 1)
     up_part = up_part.reshape(features, hidden_part)
@@ -235,25 +259,21 @@
 
     pre_grad = times_transposed(grad_out_rows, down_part) * slope
     pre_low = pre_grad.astype(BF16)
-    normed_two_grad = add_rows(times_transposed(pre_low, up_part))
-    hidden_again, pre_low = after((hidden, pre_low))
-    fc2_w_grad = lax.psum_scatter(
-        inner(hidden_again, grad_out_rows).astype(BF16), "seq", scatter_dimension=0, tiled=True
-    )
-
-    def by_seq(grad):
-        grad = grad.reshape(nd, ns, features // n, grad.shape[1]).astype(BF16)
-        return jnp.swapaxes(grad, 0, 1).reshape(features, grad.shape[3])
-
-    def from_dp(grad):
-        grad = grad.reshape(nd, features // n, grad.shape[1])
-        return lax.all_to_all(grad, "dp", 0, 0, tiled=True)
-
-    fc1_terms = by_seq(inner(normed_two_rows, pre_low))
-    normed_two_grad, fc1_terms = after((normed_two_grad, fc1_terms))
-    fc1_terms, fc2_w_grad = after((fc1_terms, fc2_w_grad))
-    fc1_terms = lax.psum_scatter(fc1_terms, "seq", scatter_dimension=0, tiled=True)
-    fc2_w_grad = fc2_w_grad.astype(F32)
+    up_back = times_transposed(pre_low, up_part)
+    up_back, pre_low = after((up_back, pre_low))
+    normed_two_grad = add_rows(up_back)
+
+    fc1_terms = inner(normed_two_rows, pre_low).astype(BF16)
+    fc1_terms = jnp.swapaxes(fc1_terms.reshape(nd, ns, features // n, hidden_part), 0, 1)
+    fc1_terms = fc1_terms.reshape(ns, nd * features // n * hidden_part // features, features)
+    fc2_terms = inner(hidden, grad_out_rows).astype(BF16)
+    fc2_terms = fc2_terms.reshape(ns, hidden_part // ns, features)
+    split_at = fc1_terms.shape[1]
+    ff_terms = jnp.concatenate([fc1_terms, fc2_terms], axis=1)
+    normed_two_grad, ff_terms = after((normed_two_grad, ff_terms))
+    ff_terms = lax.psum_scatter(
+        ff_terms.reshape(-1, features), "seq", scatter_dimension=0, tiled=True
+    )
     through_two, ln2_g_grad, ln2_b_grad = norm_back(normed_two_grad, xhat_two, inverse_two, g_two)
     second_grad = grad_out.astype(F32) + through_two
     second_low = second_grad.astype(BF16)
@@ -265,6 +285,10 @@
         away = lax.dynamic_index_in_dim(proj_low, dp_at ^ k, 0, keepdims=False)
         proj_sum = proj_sum + swap(away, k).astype(F32)
     proj_sum = proj_sum.astype(BF16).reshape(ns, features // n, features)
+    hidden_late, second_low = after((hidden, second_low))
+    down_sums = dot(hidden_late, down_part)
+    attended_grad, down_sums, proj_low = after((attended_grad, down_sums, proj_low))
+    output = (second + add_rows(down_sums) + b_down).astype(BF16)
     delta = jnp.sum(attended_grad.astype(F32) * attended_heads, axis=2, keepdims=True)
     probs = jnp.exp(logits - lse)
     prob_grad = head_dot("hqd,hkd->hqk", attended_grad, values)
@@ -280,37 +304,65 @@
         ],
         axis=1,
     )
-    triple_grad, fc1_terms, proj_sum, hidden_late = after(
-        (triple_grad, fc1_terms, proj_sum, hidden)
-    )
+    triple_grad, ff_terms, proj_sum, output = after((triple_grad, ff_terms, proj_sum, output))
+    output = output[None]
     normed_one_grad = lax.psum_scatter(
         times_transposed(triple_grad, qkv_mine).astype(BF16), "seq", scatter_dimension=0, tiled=True
     )
+    fc1_w_grad = ff_terms[:split_at].reshape(nd, features // n, hidden_part)
+    fc1_w_grad = lax.all_to_all(fc1_w_grad, "dp", 0, 0, tiled=True)
+    fc2_w_grad = ff_terms[split_at:].astype(F32)
     qkv_terms = inner(normed_one_row, triple_grad).astype(BF16)
+    proj_sum = add_over_seq(proj_sum)
+    proj_sum, qkv_terms = after((proj_sum, qkv_terms))
     qkv_terms = lax.all_to_all(
         qkv_terms.reshape(nd, features // nd, wide), "dp", 0, 0, tiled=True
     )
     qkv_terms = jnp.sum(qkv_terms.astype(F32), axis=0).astype(BF16)
-    output = (second + add_rows(dot(hidden_late, down_part)) + b_down).astype(BF16)
-    fc1_w_grad = jnp.swapaxes(from_dp(fc1_terms), 0, 1)
-    fc1_w_grad = fc1_w_grad.reshape(features // n, hidden_units).astype(F32)
-    normed_one_grad, qkv_terms, output, fc1_w_grad, proj_sum = after(
-        (normed_one_grad, qkv_terms, output, fc1_w_grad, proj_sum)
-    )
-    output = output[None]
+    normed_one_grad, qkv_terms, fc1_w_grad, fc2_w_grad, proj_sum = after(
+        (normed_one_grad, qkv_terms, fc1_w_grad, fc2_w_grad, proj_sum)
+    )
+    proj_w_grad = jnp.sum(
+        proj_sum.reshape(places, features // n, features).astype(F32), axis=0
+    )
     normed_one_grad = normed_one_grad.astype(F32)
-    proj_w_grad = jnp.sum(seq_exchange(proj_sum).astype(F32), axis=0)
+    through_one, ln1_g_grad, ln1_b_grad = norm_back(normed_one_grad, xhat_one, inverse_one, g_one)
+    first_grad = second_grad + through_one
+    first_low = first_grad.astype(BF16)
+    first_low_rows = gather_rows(first_low)
     qkv_w_grad = seq_exchange(qkv_terms.reshape(ns, features // n, wide))
+    vector_grads = jnp.stack(
+        [
+            jnp.sum(first_grad, axis=0),
+            ln1_g_grad,
+            ln1_b_grad,
+            jnp.sum(second_grad, axis=0),
+            ln2_g_grad,
+            ln2_b_grad,
+            jnp.sum(grad_out.astype(F32), axis=0),
+        ]
+    )
+    vector_grads = jnp.swapaxes(vector_grads.reshape(7, n, small), 0, 1).reshape(n, 7 * small)
+    up_grads = jnp.sum(pre_grad, axis=0).reshape(ns, hidden_units // n)
+    up_grads = lax.dynamic_update_slice_in_dim(
+        jnp.zeros((n, hidden_units // n), F32), up_grads, dp_at * ns, 0
+    )
+    vector_grads = jnp.concatenate([vector_grads, up_grads], axis=1)
+    vector_grads = jnp.pad(vector_grads, ((0, 0), (0, padded - own_size)))
+    vector_grads = lax.all_to_all(
+        vector_grads.reshape(n, padded // 128, 128), ("dp", "seq"), 0, 0, tiled=True
+    )
+    first_low_rows, qkv_w_grad, vector_grads = after((first_low_rows, qkv_w_grad, vector_grads))
+    fc1_w_grad = jnp.swapaxes(fc1_w_grad, 0, 1).reshape(features // n, hidden_units).astype(F32)
     qkv_w_grad = (
         qkv_w_grad.reshape(ns, features // n, 3, head_cols)
         .transpose(1, 2, 0, 3).reshape(features // n, 3 * features).astype(F32)
     )
-    through_one, ln1_g_grad, ln1_b_grad = norm_back(normed_one_grad, xhat_one, inverse_one, g_one)
-    first_grad = second_grad + through_one
-    first_low_rows = gather_rows(first_grad.astype(BF16))
-    skip_w_grad = lax.psum_scatter(
-        inner(joined_here, first_low_rows).astype(BF16), "seq", scatter_dimension=0, tiled=True
-    ).astype(F32)
+    skip_terms = inner(joined_here, first_low_rows).reshape(ns, 2 * features // n, features)
+    skip_w_grad = add_over_seq(skip_terms)
+    skip_w_grad = jnp.sum(
+        skip_w_grad.reshape(places, 2 * features // n, features).astype(F32), axis=0
+    )
     joined_grad_part = times_transposed(first_low_rows, skip_part).astype(BF16)
     away = []
     for k in range(nd):
@@ -323,28 +375,6 @@
     input_grad = joined_grad[None, :, :features]
     skip_grad = joined_grad[None, :, features:]
 
-    vector_grads = jnp.stack(
-        [
-            jnp.sum(first_grad, axis=0),
-            ln1_g_grad,
-            ln1_b_grad,
-            jnp.sum(second_grad, axis=0),
-            ln2_g_grad,
-            ln2_b_grad,
-            jnp.sum(grad_out.astype(F32), axis=0),
-        ]
-    )
-    vector_grads = jnp.swapaxes(vector_grads.reshape(7, n, small), 0, 1).reshape(n, 7 * small)
-    up_grads = jnp.sum(pre_grad, axis=0).reshape(ns, hidden_units // n)
-    up_grads = lax.dynamic_update_slice_in_dim(
-        jnp.zeros((n, hidden_units // n), F32), up_grads, dp_at * ns, 0
-    )
-    vector_grads = jnp.concatenate([vector_grads, up_grads], axis=1)
-    padded = -(-own_size // 1024) * 1024
-    vector_grads = jnp.pad(vector_grads, ((0, 0), (0, padded - own_size)))
-    vector_grads = lax.all_to_all(
-        vector_grads.reshape(n, padded // 128, 128), ("dp", "seq"), 0, 0, tiled=True
-    )
     vector_grads = jnp.sum(vector_grads, axis=0).reshape(padded)
     skip_b_grad, ln1_g_grad, ln1_b_grad, proj_b_grad, ln2_g_grad, ln2_b_grad, fc2_b_grad = (
         vector_grads[i * small : (i + 1) * small] for i in range(7)

time: 541 us -> 514 us (0.950)
  waiting for transfers between devices: 192 us -> 168 us
  blocking collectives: 51.6 us -> 29.6 us
  starting transfers between devices: 67.1 us -> 80.8 us
  local copies, waits for them, and re-layouts: 80.9 us -> 89.7 us
  matrix products: 82.7 us -> 75.6 us
    all_to_all x1 -> x4, waiting for transfers between devices: 0.01 us -> 31.1 us  [the longest x2 22.6 us: add_over_seq(): lax.all_to_all(sums, 'seq', 0, 0, axis_index_groups=groups, tiled=True)]
    all_to_all x2 -> x1, waiting for transfers between devices: 41.9 us -> 11.2 us  [spread(): return lax.all_to_all(copies, axes, 0, 0, tiled=True)]
    all_to_all x2 -> x1, blocking collectives: 36 us -> 14 us  [spread(): return lax.all_to_all(copies, axes, 0, 0, tiled=True)]
    all_to_all x4, waiting for transfers between devices: 53 us -> 31.9 us  [seq_exchange(): return lax.all_to_all(v, 'seq', 0, 0, tiled=True)]
    all_to_all x1 -> x4, starting transfers between devices: 3.79 us -> 15.2 us  [the longest x2 7.37 us: add_over_seq(): lax.all_to_all(sums, 'seq', 0, 0, axis_index_groups=groups, tiled=True)]
    all_gather x1, waiting for transfers between devices: 10.4 us -> 0.01 us  [on_device(): lax.all_gather(up_slices.reshape(features // ns, hidden_part), 'seq', axi...]
    all_gather x1, waiting for transfers between devices: 0.01 us -> 8.49 us  [on_device(): skip_part = lax.all_gather(skip_w, 'seq', axis=0, tiled=True)]
    reduce_scatter x2 -> x1, waiting for transfers between devices: 8.14 us -> 0.01 us  [on_device(): lax.psum_scatter(ff_terms.reshape(-1, features), 'seq', scatter_dimension...]
  transfers between devices with their start and end apart: 44 -> 52, of which waited for: 25 -> 28; matrix products, arithmetic and copies ran while one was open for 29% -> 27% of each run, Pallas kernels for 1% -> 1%
where the time goes in v5:
time: 514 us; the launch traced here: 505 us
  waiting for transfers between devices  168 us (33%)
  local copies, waits for them, and re-layouts  89.7 us (17%)
  starting transfers between devices  80.8 us (16%)
  matrix products  75.6 us (15%)
  other arithmetic  36.9 us (7%)
  blocking collectives  29.6 us (6%)
  between operations  19.1 us (4%)
  Pallas kernels  5.23 us (1%)
    ppermute x30, waiting for transfers between devices, swap(): return lax.ppermute(v, 'dp', [(i, i ^ k) for i in range(nd)])  67.5 us
    ppermute x30, starting transfers between devices, swap(): return lax.ppermute(v, 'dp', [(i, i ^ k) for i in range(nd)])  36.2 us
    all_to_all x4, waiting for transfers between devices, seq_exchange(): return lax.all_to_all(v, 'seq', 0, 0, tiled=True)  31.9 us
    dot_general x6, matrix products, head_dot(): return jnp.einsum(spec, left, right, preferred_element_type=F32)  26.9 us
    all_to_all x2, waiting for transfers between devices, add_over_seq(): lax.all_to_all(sums, 'seq', 0, 0, axis_index_groups=groups, tiled=True)  22.6 us
    dot_general x5, matrix products, times_transposed(): lax.dot_general(left, right, (((1,), (1,)), ((), ())), preferred_element_...  18.7 us
    all_to_all x4, starting transfers between devices, seq_exchange(): return lax.all_to_all(v, 'seq', 0, 0, tiled=True)  17.9 us
    unnamed x132, local copies, waits for them, and re-layouts  16.2 us
  transfers between devices with their start and end apart: 52, of which 28 were waited for; matrix products, arithmetic and copies ran while one was open for 27% of the time, Pallas kernels for 1%

profile of v5, /device:TPU:0, one launch (start us, length us, event | category | flops | bytes accessed | tf_op | source)
XLA Modules:
  0.0 505.5 jit_solution(17749282253813686847)
XLA Ops:
  14.6 14.0 %all_to_all.60 = bf16[32,8,128]{2,1,0:T(8,128)(2,1)S(1)} all-to-all(bf16[32,8,128]{2,1,0:T(8,128)(2,1)S(1)} %broadcast_in_dim.32), channel_id=1, replica_groups=mesh['dp'=4,'seq'=8] {'dp','seq'}, dimensions={0} | all-to-all | bytes 131072 | tf_op jit(solution)/shard_map/all_to_all | solution.py:135
  28.7 8.5 %all-gather.6.cloned.1.call-done = bf16[576,1152]{1,0:T(8,128)(2,1)} async-done(((bf16[72,1152]{1,0:T(8,128)(2,1)}), bf16[576,1152]{1,0:T(8,128)(2,1)}) %all-gather.6.cloned.1.call-update) | async-done | bytes 1327120 | tf_op jit(solution)/shard_map/all_gather | solution.py:152
  47.4 15.6 %all-gather = bf16[8,36,1152]{2,1,0:T(8,128)(2,1)S(1)} all-gather(bf16[1,36,1152]{2,1,0:T(8,128)(2,1)S(1)} %bitcast.221), channel_id=1, replica_groups=mesh['dp'=4,'seq'=8] {'seq'}, dimensions={0}, use_global_device_ids=true | all-gather | bytes 746496 | tf_op jit(solution)/shard_map/all_gather | solution.py:187
  78.7 7.2 %collective-permute-done.10 = bf16[144,1152]{1,0:T(8,128)(2,1)} collective-permute-done((bf16[144,1152]{1,0:T(8,128)(2,1)}, bf16[144,1152]{1,0:T(8,128)(2,1)}, u32[]{:S(2)}, u32[]{:S(2)}) %collective-permute-start.10) | collective-permute-done | bytes 331808 | tf_op jit(solution)/shard_map/ppermute | solution.py:118
  85.9 7.0 %collective-permute-done.8 = bf16[144,1152]{1,0:T(8,128)(2,1)} collective-permute-done((bf16[144,1152]{1,0:T(8,128)(2,1)}, bf16[144,1152]{1,0:T(8,128)(2,1)}, u32[]{:S(2)}, u32[]{:S(2)}) %collective-permute-start.8) | collective-permute-done | bytes 331808 | tf_op jit(solution)/shard_map/ppermute | solution.py:118
  106.8 11.2 %all-to-all-done.2 = bf16[4,288,432]{2,1,0:T(8,128)(2,1)} async-done(((bf16[4,288,432]{2,1,0:T(8,128)(2,1)}), bf16[4,288,432]{2,1,0:T(8,128)(2,1)}, u32[]{:S(2)}, u32[]{:S(2)}) %all-to-all-start.2) | async-done | bytes 995360 | tf_op jit(solution)/shard_map/all_to_all | solution.py:135
  173.3 16.1 %all-to-all-done.4 = bf16[8,160,144]{1,2,0:T(8,128)(2,1)S(1)} async-done(((bf16[8,160,144]{1,2,0:T(8,128)(2,1)}), bf16[8,160,144]{1,2,0:T(8,128)(2,1)S(1)}, u32[]{:S(2)}, u32[]{:S(2)}) %all-to-all-start.4) | async-done | bytes 368672 | tf_op jit(solution)/shard_map/all_to_all | solution.py:131
  190.4 5.1 %reshape.290 = bf16[8,4,36,1152]{3,2,1,0:T(8,128)(2,1)} reshape(bf16[1152,1152]{1,0:T(8,128)(2,1)} %all-gather.10.cloned.1.call-done) | data formatting | bytes 5308416 | tf_op jit(solution)/shard_map/reshape | solution.py:248
  210.9 9.1 %collective-permute-done.17 = bf16[160,1152]{1,0:T(8,128)(2,1)} collective-permute-done((bf16[160,1152]{1,0:T(8,128)(2,1)}, bf16[160,1152]{1,0:T(8,128)(2,1)}, u32[]{:S(2)}, u32[]{:S(2)}) %collective-permute-start.17) | collective-permute-done | bytes 368672 | tf_op jit(solution)/shard_map/ppermute | solution.py:118
  226.0 5.2 %shard_map.288 = (bf16[640,1152]{1,0:T(8,128)(2,1)S(1)}, f32[640,1152]{1,0:T(8,128)S(1)}) custom-call(bf16[640,1152]{1,0:T(8,128)(2,1)S(1)} %pad_maximum_fusion.2.x_ref, bf16[1152,1152]{1,0:T(8,128)(2,1)S(1)} %reshape.291.w_ref, f32[1,1152]{1,0:T(1,128)S(1)} %reshape_reshape.6.bias_ref), custom_call_target="tpu_custom_call" | custom-call | flops 1698693120 | bytes 8552448 | tf_op jit(solution)/shard_map/pallas_call | solution.py:77
  234.0 5.4 %multiply_reduce_fusion = (f32[1152]{0:T(1024)S(1)}, bf16[640,1152]{1,0:T(8,128)(2,1)S(1)}) fusion(f32[640,1152]{1,0:T(8,128)} %copy-done, bf16[640,1152]{1,0:T(8,128)(2,1)} %pad_maximum_fusion.1, bf16[1152,1152]{1,0:T(8,128)(2,1)} %all-gather.12.cloned.1.call-done), kind=kOutput, calls=%fused_computation.35 | convolution fusion | flops 1700903808 | bytes 8557056 | tf_op jit(solution)/shard_map/dot_general | solution.py:53
  261.4 7.7 %collective-permute-done.18 = bf16[160,1152]{1,0:T(8,128)(2,1)S(1)} collective-permute-done((bf16[160,1152]{1,0:T(8,128)(2,1)}, bf16[160,1152]{1,0:T(8,128)(2,1)S(1)}, u32[]{:S(2)}, u32[]{:S(2)}) %collective-permute-start.18) | collective-permute-done | bytes 368672 | tf_op jit(solution)/shard_map/ppermute | solution.py:118
  269.0 7.9 %collective-permute-done.20 = bf16[160,1152]{1,0:T(8,128)(2,1)S(1)} collective-permute-done((bf16[160,1152]{1,0:T(8,128)(2,1)S(1)}, bf16[160,1152]{1,0:T(8,128)(2,1)S(1)}, u32[]{:S(2)}, u32[]{:S(2)}) %collective-permute-start.20) | collective-permute-done | bytes 368672 | tf_op jit(solution)/shard_map/ppermute | solution.py:118
  295.0 5.8 %all-to-all-start.5 = ((bf16[8,160,144]{1,2,0:T(8,128)(2,1)}), bf16[8,160,144]{1,2,0:T(8,128)(2,1)}, u32[]{:S(2)}, u32[]{:S(2)}) async-start(bf16[8,160,144]{1,2,0:T(8,128)(2,1)} %copy.90), calls=%async_computation.5 | async-start | bytes 1179648 | tf_op jit(solution)/shard_map/all_to_all | solution.py:131
  314.0 13.5 %all-to-all-done.5 = bf16[8,160,144]{1,2,0:T(8,128)(2,1)} async-done(((bf16[8,160,144]{1,2,0:T(8,128)(2,1)}), bf16[8,160,144]{1,2,0:T(8,128)(2,1)}, u32[]{:S(2)}, u32[]{:S(2)}) %all-to-all-start.5) | async-done | bytes 368672 | tf_op jit(solution)/shard_map/all_to_all | solution.py:131
  334.5 8.5 %fusion.4 = bf16[2,1280,1280]{1,2,0:T(8,128)(2,1)} fusion(bf16[2,1280,72]{1,2,0:T(8,128)(2,1)S(1)} %bitcast.180, bf16[2,1280,72]{1,2,0:T(8,128)(2,1)S(1)} %bitcast.185, f32[2,1280,1280]{1,2,0:T(8,128)} %copy-done.3, f32[2,1280]{1,0:T(2,128)S(1)} %multiply_reduce_fusion.2, f32[2,1280]{1,0:T(2,128)S(1)} %log_add_fusion), kind=kOutput, calls=%fused_computation.8 | convolution fusion | flops 488243200 | bytes 20418560 | tf_op jit(solution)/shard_map/hqd,hkd->hqk/dot_general | solution.py:228
  343.0 6.2 %convolution_convert_fusion.7 = bf16[2,1280,72]{1,2,0:T(8,128)(2,1)} fusion(bf16[2,1280,1280]{1,2,0:T(8,128)(2,1)} %fusion.4, bf16[2,1280,72]{1,2,0:T(8,128)(2,1)S(1)} %bitcast.198), kind=kOutput, calls=%fused_computation.20 | convolution fusion | flops 472043520 | bytes 7290880 | tf_op jit(solution)/shard_map/hqk,hqd->hkd/dot_general | solution.py:228
  360.8 5.7 %collective-permute-done.25 = bf16[160,1152]{1,0:T(8,128)(2,1)S(1)} collective-permute-done((bf16[160,1152]{1,0:T(8,128)(2,1)}, bf16[160,1152]{1,0:T(8,128)(2,1)S(1)}, u32[]{:S(2)}, u32[]{:S(2)}) %collective-permute-start.25) | collective-permute-done | bytes 368672 | tf_op jit(solution)/shard_map/ppermute | solution.py:118
  368.7 5.2 %convolution_convert_fusion = bf16[1280,1152]{1,0:T(8,128)(2,1)} fusion(bf16[1280,432]{0,1:T(8,128)(2,1)} %pad_maximum_fusion.5, bf16[1152,432]{1,0:T(8,128)(2,1)} %bitcast.18), kind=kOutput, calls=%fused_computation.9 | convolution fusion | flops 1275494400 | bytes 5050368 | tf_op jit(solution)/shard_map/dot_general | solution.py:53
  384.5 13.6 %all-to-all-done.6 = bf16[4,36,1152]{2,1,0:T(8,128)(2,1)S(1)} async-done(((bf16[4,36,1152]{2,1,0:T(8,128)(2,1)}), bf16[4,36,1152]{2,1,0:T(8,128)(2,1)S(1)}, u32[]{:S(2)}, u32[]{:S(2)}) %all-to-all-start.6) | async-done | bytes 331808 | tf_op jit(solution)/shard_map/all_to_all | solution.py:150
  407.0 12.0 %all-to-all-done.7 = bf16[4,288,432]{2,1,0:T(8,128)(2,1)S(1)} async-done(((bf16[4,288,432]{2,1,0:T(8,128)(2,1)}), bf16[4,288,432]{2,1,0:T(8,128)(2,1)S(1)}, u32[]{:S(2)}, u32[]{:S(2)}) %all-to-all-start.7) | async-done | bytes 995360 | tf_op jit(solution)/shard_map/all_to_all | solution.py:318
  423.6 4.8 all-to-all-done.8
  449.0 7.3 %collective-permute-done.29 = bf16[160,1152]{1,0:T(8,128)(2,1)S(1)} collective-permute-done((bf16[160,1152]{1,0:T(8,128)(2,1)S(1)}, bf16[160,1152]{1,0:T(8,128)(2,1)S(1)}, u32[]{:S(2)}, u32[]{:S(2)}) %collective-permute-start.29) | collective-permute-done | bytes 368672 | tf_op jit(solution)/shard_map/ppermute | solution.py:118
  488.4 9.0 %all-to-all-done.11 = bf16[4,72,1152]{2,1,0:T(8,128)(2,1)S(1)} async-done(((bf16[4,72,1152]{2,1,0:T(8,128)(2,1)}), bf16[4,72,1152]{2,1,0:T(8,128)(2,1)S(1)}, u32[]{:S(2)}, u32[]{:S(2)}) %all-to-all-start.11) | async-done | bytes 663584 | tf_op jit(solution)/shard_map/all_to_all | solution.py:150
  (377 shorter events, 274.9 us)
Async XLA Ops:
  7.3 29.9 %all-gather.6.cloned.1.call-start = ((), (), s32[]{:S(2)}) async-start(), calls=%async_computation.14 | async-start | bytes 1492992 | tf_op jit(solution)/shard_map/all_gather | solution.py:152
  8.0 123.5 %all-gather.8.cloned.1.call-start = ((), (), s32[]{:S(2)}) async-start(), calls=%async_computation.15 | async-start | bytes 3317760 | tf_op jit(solution)/shard_map/all_gather | solution.py:189
  9.8 18.8 %collective-permute-start.2 = (bf16[160,576]{1,0:T(8,128)(2,1)S(1)}, bf16[160,576]{1,0:T(8,128)(2,1)S(1)}, u32[]{:S(2)}, u32[]{:S(2)}) collective-permute-start(bf16[160,576]{1,0:T(8,128)(2,1)S(1)} %get-tuple-element.132), channel_id=1, source_target_pairs={{0,24},{8,16},{16,8},{24,0},{1,25},{9,17},{17,9},{25,1},{2,26},{10... | collective-permute-start | bytes 552968 | tf_op jit(solution)/shard_map/ppermute | solution.py:118
  42.3 20.8 %collective-permute-start.3 = (bf16[160,1152]{1,0:T(8,128)(2,1)}, bf16[160,1152]{1,0:T(8,128)(2,1)S(1)}, u32[]{:S(2)}, u32[]{:S(2)}) collective-permute-start(bf16[160,1152]{1,0:T(8,128)(2,1)} %get-tuple-element.121), channel_id=1, source_target_pairs={{0,8},{8,0},{16,24},{24,16},{1,9},{9,1},{17,25},{25,17},{2,10},{10... | collective-permute-start | bytes 1105928 | tf_op jit(solution)/shard_map/ppermute | solution.py:118
  43.8 19.4 %collective-permute-start.5 = (bf16[160,1152]{1,0:T(8,128)(2,1)S(1)}, bf16[160,1152]{1,0:T(8,128)(2,1)S(1)}, u32[]{:S(2)}, u32[]{:S(2)}) collective-permute-start(bf16[160,1152]{1,0:T(8,128)(2,1)S(1)} %get-tuple-element.122), channel_id=1, source_target_pairs={{0,24},{8,16},{16,8},{24,0},{1,25},{9,17},{17,9},{25,1},{2,26},{10... | collective-permute-start | bytes 1105928 | tf_op jit(solution)/shard_map/ppermute | solution.py:118
  70.4 24.1 %all-to-all-start.1 = ((bf16[8,36,432]{2,1,0:T(8,128)(2,1)}), bf16[8,36,432]{2,1,0:T(8,128)(2,1)}, u32[]{:S(2)}, u32[]{:S(2)}) async-start(bf16[8,36,432]{2,1,0:T(8,128)(2,1)} %copy.82), calls=%async_computation.1 | async-start | bytes 655360 | tf_op jit(solution)/shard_map/all_to_all | solution.py:131
  77.3 26.4 %collective-permute-start.7 = (bf16[144,1152]{1,0:T(8,128)(2,1)}, bf16[144,1152]{1,0:T(8,128)(2,1)}, u32[]{:S(2)}, u32[]{:S(2)}) collective-permute-start(bf16[144,1152]{1,0:T(8,128)(2,1)} %collective-permute-done.6), channel_id=1, source_target_pairs={{0,1},{1,0},{2,3},{3,2},{4,5},{5,4},{6,7},{7,6},{8,9},{9,8},{10,11... | collective-permute-start | bytes 995336 | tf_op jit(solution)/shard_map/ppermute | solution.py:142
  85.9 40.8 %collective-permute-start.11 = (bf16[144,1152]{1,0:T(8,128)(2,1)}, bf16[144,1152]{1,0:T(8,128)(2,1)}, u32[]{:S(2)}, u32[]{:S(2)}) collective-permute-start(bf16[144,1152]{1,0:T(8,128)(2,1)} %collective-permute-done.10), channel_id=1, source_target_pairs={{0,1},{1,0},{2,3},{3,2},{4,5},{5,4},{6,7},{7,6},{8,9},{9,8},{10,11... | collective-permute-start | bytes 995336 | tf_op jit(solution)/shard_map/ppermute | solution.py:142
  98.4 19.5 %all-to-all-start.2 = ((bf16[4,288,432]{2,1,0:T(8,128)(2,1)}), bf16[4,288,432]{2,1,0:T(8,128)(2,1)}, u32[]{:S(2)}, u32[]{:S(2)}) async-start(bf16[4,288,432]{2,1,0:T(8,128)(2,1)} %broadcast_in_dim.59), calls=%async_computation.2 | async-start | bytes 2359296 | tf_op jit(solution)/shard_map/all_to_all | solution.py:135
  125.6 64.8 %all-gather.10.cloned.1.call-start = ((), (), s32[]{:S(2)}) async-start(), calls=%async_computation.16 | async-start | bytes 2985984 | tf_op jit(solution)/shard_map/all_gather | solution.py:214
  133.3 100.8 %all-gather.12.cloned.1.call-start = ((), (), s32[]{:S(2)}) async-start(), calls=%async_computation.17 | async-start | bytes 2985984 | tf_op jit(solution)/shard_map/all_gather | solution.py:247
  160.9 28.5 %all-to-all-start.4 = ((bf16[8,160,144]{1,2,0:T(8,128)(2,1)}), bf16[8,160,144]{1,2,0:T(8,128)(2,1)S(1)}, u32[]{:S(2)}, u32[]{:S(2)}) async-start(bf16[8,160,144]{1,2,0:T(8,128)(2,1)} %copy.85), calls=%async_computation.4 | async-start | bytes 1179648 | tf_op jit(solution)/shard_map/all_to_all | solution.py:131
  165.5 203.2 %reduce-scatter.3.cloned.1.call-start = ((), (), s32[]{:S(2)}) async-start(), calls=%async_computation.18 | async-start | bytes 5971968 | tf_op jit(solution)/shard_map/reduce_scatter | solution.py:274
  258.8 18.2 %collective-permute-start.20 = (bf16[160,1152]{1,0:T(8,128)(2,1)S(1)}, bf16[160,1152]{1,0:T(8,128)(2,1)S(1)}, u32[]{:S(2)}, u32[]{:S(2)}) collective-permute-start(bf16[160,1152]{1,0:T(8,128)(2,1)S(1)} %get-tuple-element.119), channel_id=1, source_target_pairs={{0,24},{8,16},{16,8},{24,0},{1,25},{9,17},{17,9},{25,1},{2,26},{10... | collective-permute-start | bytes 1105928 | tf_op jit(solution)/shard_map/ppermute | solution.py:118
  295.0 32.5 %all-to-all-start.5 = ((bf16[8,160,144]{1,2,0:T(8,128)(2,1)}), bf16[8,160,144]{1,2,0:T(8,128)(2,1)}, u32[]{:S(2)}, u32[]{:S(2)}) async-start(bf16[8,160,144]{1,2,0:T(8,128)(2,1)} %copy.90), calls=%async_computation.5 | async-start | bytes 1179648 | tf_op jit(solution)/shard_map/all_to_all | solution.py:131
  300.8 127.7 %reduce-scatter.5.cloned.1.call-start = ((), (), s32[]{:S(2)}) async-start(), calls=%async_computation.19 | async-start | bytes 3317760 | tf_op jit(solution)/shard_map/reduce_scatter | solution.py:309
  306.6 50.1 %collective-permute-start.21 = (bf16[288,1152]{1,0:T(8,128)(2,1)}, bf16[288,1152]{1,0:T(8,128)(2,1)}, u32[]{:S(2)}, u32[]{:S(2)}) collective-permute-start(bf16[288,1152]{1,0:T(8,128)(2,1)} %get-tuple-element.110), channel_id=1, source_target_pairs={{0,8},{8,0},{16,24},{24,16},{1,9},{9,1},{17,25},{25,17},{2,10},{10... | collective-permute-start | bytes 1990664 | tf_op jit(solution)/shard_map/ppermute | solution.py:118
  306.9 51.5 %collective-permute-start.23 = (bf16[288,1152]{1,0:T(8,128)(2,1)}, bf16[288,1152]{1,0:T(8,128)(2,1)}, u32[]{:S(2)}, u32[]{:S(2)}) collective-permute-start(bf16[288,1152]{1,0:T(8,128)(2,1)} %get-tuple-element.111), channel_id=1, source_target_pairs={{0,24},{8,16},{16,8},{24,0},{1,25},{9,17},{17,9},{25,1},{2,26},{10... | collective-permute-start | bytes 1990664 | tf_op jit(solution)/shard_map/ppermute | solution.py:118
  308.4 50.0 %collective-permute-start.22 = (bf16[288,1152]{1,0:T(8,128)(2,1)}, bf16[288,1152]{1,0:T(8,128)(2,1)}, u32[]{:S(2)}, u32[]{:S(2)}) collective-permute-start(bf16[288,1152]{1,0:T(8,128)(2,1)} %get-tuple-element.112), channel_id=1, source_target_pairs={{0,16},{8,24},{16,0},{24,8},{1,17},{9,25},{17,1},{25,9},{2,18},{10... | collective-permute-start | bytes 1990664 | tf_op jit(solution)/shard_map/ppermute | solution.py:118
  332.5 28.2 %collective-permute-start.24 = (bf16[160,1152]{1,0:T(8,128)(2,1)}, bf16[160,1152]{1,0:T(8,128)(2,1)}, u32[]{:S(2)}, u32[]{:S(2)}) collective-permute-start(bf16[160,1152]{1,0:T(8,128)(2,1)} %get-tuple-element.115), channel_id=1, source_target_pairs={{0,8},{8,0},{16,24},{24,16},{1,9},{9,1},{17,25},{25,17},{2,10},{10... | collective-permute-start | bytes 1105928 | tf_op jit(solution)/shard_map/ppermute | solution.py:118
  332.8 27.9 %collective-permute-start.26 = (bf16[160,1152]{1,0:T(8,128)(2,1)}, bf16[160,1152]{1,0:T(8,128)(2,1)}, u32[]{:S(2)}, u32[]{:S(2)}) collective-permute-start(bf16[160,1152]{1,0:T(8,128)(2,1)} %get-tuple-element.116), channel_id=1, source_target_pairs={{0,24},{8,16},{16,8},{24,0},{1,25},{9,17},{17,9},{25,1},{2,26},{10... | collective-permute-start | bytes 1105928 | tf_op jit(solution)/shard_map/ppermute | solution.py:118
  376.6 21.5 %all-to-all-start.6 = ((bf16[4,36,1152]{2,1,0:T(8,128)(2,1)}), bf16[4,36,1152]{2,1,0:T(8,128)(2,1)S(1)}, u32[]{:S(2)}, u32[]{:S(2)}) async-start(bf16[4,36,1152]{2,1,0:T(8,128)(2,1)} %fusion.24), calls=%async_computation.8 | async-start | bytes 737280 | tf_op jit(solution)/shard_map/all_to_all | solution.py:150
  400.6 18.4 %all-to-all-start.7 = ((bf16[4,288,432]{2,1,0:T(8,128)(2,1)}), bf16[4,288,432]{2,1,0:T(8,128)(2,1)S(1)}, u32[]{:S(2)}, u32[]{:S(2)}) async-start(bf16[4,288,432]{2,1,0:T(8,128)(2,1)} %bitcast.182), calls=%async_computation.9 | async-start | bytes 2359296 | tf_op jit(solution)/shard_map/all_to_all | solution.py:318
  476.2 21.2 %all-to-all-start.11 = ((bf16[4,72,1152]{2,1,0:T(8,128)(2,1)}), bf16[4,72,1152]{2,1,0:T(8,128)(2,1)S(1)}, u32[]{:S(2)}, u32[]{:S(2)}) async-start(bf16[4,72,1152]{2,1,0:T(8,128)(2,1)} %fusion.9), calls=%async_computation.13 | async-start | bytes 1327104 | tf_op jit(solution)/shard_map/all_to_all | solution.py:150
  (92 other events, 915.3 us)
Sparse Core Ops, SparseCore 0:
  9.7 27.3 all-gather.5
  66.2 43.1 all-gather.7
  133.4 34.1 all-gather.9
  169.1 36.0 all-gather.11
  282.3 71.1 reduce-scatter.2
  374.1 43.2 reduce-scatter.4

commit v6 on v4

v6 whole, which is shorter than its diff:
```python
import math
from functools import partial

import jax
import jax.numpy as jnp
from jax import lax
from jax.experimental import pallas as pl
from jax.experimental.pallas import tpu as pltpu
from jax.sharding import PartitionSpec as P

HEADS = 16
HEAD_DIM = 72
EPSILON = 1e-05
NEGATIVE = -1e30
F32 = jnp.float32
BF16 = jnp.bfloat16


def norm_pieces(hvals):
    centered = hvals - jnp.mean(hvals, axis=-1, keepdims=True)
    inverse = lax.rsqrt(jnp.mean(centered * centered, axis=-1, keepdims=True) + EPSILON)
    return centered * inverse, inverse


def norm_back(incoming, standardized, inverse, gain):
    scaled = incoming * gain
    passed = inverse * (
        scaled
        - jnp.mean(scaled, axis=-1, keepdims=True)
        - standardized * jnp.mean(scaled * standardized, axis=-1, keepdims=True)
    )
    return passed, jnp.sum(incoming * standardized, axis=0), jnp.sum(incoming, axis=0)


def segment_of(lengths, places):
    running = jnp.zeros((), jnp.int32)
    passed = jnp.zeros(places.shape, jnp.int32)
    for slot in range(lengths.shape[1]):
        running = running + lengths[0, slot]
        passed = passed + (running <= places).astype(jnp.int32)
    return passed


def dot(left, right):
    return jnp.dot(left, right, preferred_element_type=F32)


def inner(left, right):
    return lax.dot_general(left, right, (((0,), (0,)), ((), ())), preferred_element_type=F32)


def times_transposed(left, right):
    return lax.dot_general(left, right, (((1,), (1,)), ((), ())), preferred_element_type=F32)


def gelu_kernel(rows_at_once, x_ref, w_ref, bias_ref, value_ref, slope_ref):
    for start in range(0, x_ref.shape[0], rows_at_once):
        at = pl.ds(start, rows_at_once)
        pre = dot(x_ref[at, :], w_ref[...]) + bias_ref[...]
        bell = jnp.exp(-0.5 * pre * pre)
        t = 1.0 / (1.0 + (0.3275911 * 0.5**0.5) * jnp.abs(pre))
        tail = 0.5 * 1.061405429
        for c in (-1.453152027, 1.421413741, -0.284496736, 0.254829592):
            tail = tail * t + 0.5 * c
        tail = tail * t * bell
        below = jnp.where(pre < 0.0, tail, 1.0 - tail)
        value_ref[at, :] = (pre * below).astype(BF16)
        slope_ref[at, :] = below + pre * bell * (0.5 / math.pi) ** 0.5


def gelu_of_matmul(x, w, bias):
    rows, depth = x.shape
    columns = w.shape[1]
    step = 384 if columns % 384 == 0 else columns
    rows_at_once = 160 if rows % 160 == 0 else rows
    block = pl.BlockSpec((rows, step), lambda j: (0, j))
    return pl.pallas_call(
        partial(gelu_kernel, rows_at_once),
        grid=(columns // step,),
        in_specs=[
            pl.BlockSpec((rows, depth), lambda j: (0, 0)),
            pl.BlockSpec((depth, step), lambda j: (0, j)),
            pl.BlockSpec((1, step), lambda j: (0, j)),
        ],
        out_specs=[block, block],
        out_shape=[
            jax.ShapeDtypeStruct((rows, columns), BF16),
            jax.ShapeDtypeStruct((rows, columns), F32),
        ],
        compiler_params=pltpu.CompilerParams(vmem_limit_bytes=40 * 2**20),
        cost_estimate=pl.CostEstimate(
            flops=2 * rows * depth * columns,
            bytes_accessed=2 * depth * (rows + columns) + 6 * rows * columns,
            transcendentals=rows * columns,
        ),
    )(x, w, bias.reshape(1, columns))


def on_device(
    nd, ns,
    inputs, skipped, item_lengths,
    skip_w, qkv_w, proj_w, fc1_w, fc2_w,
    skip_b, ln1_g, ln1_b, proj_b, ln2_g, ln2_b, fc1_b, fc2_b,
    cotangent,
):
    _, local, features = inputs.shape
    hidden_units = fc1_w.shape[1]
    n = nd * ns
    row_len = local * ns
    heads = HEADS // ns
    head_cols = heads * HEAD_DIM
    wide = 3 * head_cols
    small = features // n
    scale = HEAD_DIM ** (-0.5)
    hidden_part = hidden_units // nd
    joined_part = 2 * features // nd
    part = features // nd
    places = ns // 2
    dp_at = lax.axis_index("dp")
    seq_at = lax.axis_index("seq")
    core = seq_at % 2
    after = lax.optimization_barrier

    def swap(v, k):
        return lax.ppermute(v, "dp", [(i, i ^ k) for i in range(nd)])

    def other_core(v):
        return lax.ppermute(v, "seq", [(i, i ^ 1) for i in range(ns)])

    def index(v, at, axis=0):
        return lax.dynamic_index_in_dim(v, at, axis, keepdims=False)

    def gather_rows(v):
        return jnp.concatenate([v] + [swap(v, k) for k in range(1, nd)], axis=0)

    def add_blocks(own, low):
        for k in range(1, nd):
            own = own + swap(low[k], k).astype(F32)
        return own

    def low_rows(partial_sums):
        return partial_sums.astype(BF16).reshape(nd, local, features)

    def seq_exchange(v):
        return lax.all_to_all(v, "seq", 0, 0, tiled=True)

    def core_sums(terms):
        terms = terms.reshape((places, 2) + terms.shape[1:])
        given = index(terms, 1 - core, 1).astype(BF16)
        kept = index(terms, core, 1).astype(F32)
        return (kept + other_core(given).astype(F32)).astype(BF16)

    def chip_sums(sums):
        groups = [[i * 2 + c for i in range(places)] for c in range(2)]
        terms = lax.all_to_all(sums, "seq", 0, 0, axis_index_groups=groups, tiled=True)
        return jnp.sum(terms.reshape(sums.shape).astype(F32), axis=0)

    skip_part = lax.all_gather(skip_w, "seq", axis=0, tiled=True)

    own_vectors = (skip_b, ln1_g, ln1_b, proj_b, ln2_g, ln2_b, fc2_b, fc1_b)
    packed = jnp.concatenate(own_vectors)
    own_size = packed.shape[0]
    padded = -(-own_size // 1024) * 1024
    packed = jnp.pad(packed, (0, padded - own_size)).reshape(padded // 128, 128)
    packed = jnp.broadcast_to(packed[None], (n,) + packed.shape)
    vectors = lax.all_to_all(packed, ("dp", "seq"), 0, 0, tiled=True)
    vectors = vectors.reshape(n, padded).astype(F32)

    joined_slices = jnp.stack(
        [
            half[:, at * joined_part : (at + 1) * joined_part]
            for half in (inputs[0], skipped[0])
            for at in range(nd // 2)
        ]
    )
    joined_here = jnp.concatenate(
        [index(joined_slices, dp_at)]
        + [swap(index(joined_slices, dp_at ^ k), k) for k in range(1, nd)],
        axis=0,
    )
    own_qkv, own_proj, skip_part, joined_here, vectors = after(
        (qkv_w, proj_w, skip_part, joined_here, vectors)
    )
    def vector(at):
        return vectors[:, at * small : (at + 1) * small].reshape(features)

    b_skip, g_one, b_one, b_proj, g_two, b_two, b_down = (vector(i) for i in range(7))
    up_bias = lax.dynamic_slice_in_dim(vectors[:, 7 * small : own_size], dp_at * ns, ns, 0)
    up_bias = up_bias.reshape(hidden_part)

    qkv_rows = lax.all_gather(own_qkv, "seq", axis=0, tiled=False)
    first_terms = dot(joined_here, skip_part)
    first = add_blocks(first_terms[:local], low_rows(first_terms)) + b_skip
    proj_rows = lax.all_gather(own_proj, "seq", axis=0, tiled=True)
    xhat_one, inverse_one = norm_pieces(first)
    normed_one = (xhat_one * g_one + b_one).astype(BF16)
    normed_one, proj_rows, qkv_rows = after((normed_one, proj_rows, qkv_rows))
    normed_one_row = lax.all_gather(normed_one, "seq", axis=0, tiled=True)

    qkv_mine = qkv_rows.reshape(part, 3, ns, head_cols)
    qkv_mine = index(qkv_mine, seq_at, 2).reshape(part, wide)
    qkv_blocks = jnp.zeros((features, wide), BF16)
    for k in range(nd):
        block = qkv_mine if k == 0 else swap(qkv_mine, k)
        qkv_blocks = lax.dynamic_update_slice_in_dim(qkv_blocks, block, (dp_at ^ k) * part, 0)
    qkv_mine = qkv_blocks
    up_slices = jnp.swapaxes(fc1_w.reshape(small, nd, hidden_part), 0, 1)
    up_slices = jnp.concatenate(
        [index(up_slices, dp_at)] + [swap(index(up_slices, dp_at ^ k), k) for k in range(1, nd)],
        axis=0,
    )
    half = part // 2
    own_half = lax.dynamic_slice_in_dim(proj_rows, core * half, half, 0)
    w_proj = lax.dynamic_update_slice_in_dim(
        jnp.zeros((features, features), BF16), proj_rows, dp_at * part, 0
    )
    for k in range(1, nd):
        place = (dp_at ^ k) * 2
        here = swap(own_half, k)
        there = other_core(here)
        w_proj = lax.dynamic_update_slice_in_dim(w_proj, here, (place + core) * half, 0)
        w_proj = lax.dynamic_update_slice_in_dim(w_proj, there, (place + 1 - core) * half, 0)
    normed_one_row, up_slices, qkv_mine, grad_out = after(
        (normed_one_row, up_slices, qkv_mine, cotangent[0])
    )
    up_part = lax.all_gather(up_slices, "seq", axis=0, tiled=True)
    at = lax.broadcasted_iota(jnp.int32, (features, features), 0)
    block, row = at // small, at % small
    row = ((block % nd) ^ dp_at) * part + (block // nd) * small + row
    order = (row == lax.broadcasted_iota(jnp.int32, (features, features), 1)).astype(BF16)

    triple = dot(normed_one_row, qkv_mine).astype(BF16)
    queries, keys, values = (
        jnp.swapaxes(
            triple[:, i * head_cols : (i + 1) * head_cols].reshape(row_len, heads, HEAD_DIM), 0, 1
        )
        for i in range(3)
    )
    segments = segment_of(item_lengths, jnp.arange(row_len, dtype=jnp.int32))
    allowed = (segments[:, None] == segments[None, :])[None]

    def head_dot(spec, left, right):
        return jnp.einsum(spec, left, right, preferred_element_type=F32)

    logits = jnp.where(allowed, head_dot("hqd,hkd->hqk", queries, keys) * scale, NEGATIVE)
    top = jnp.max(logits, axis=2, keepdims=True)
    total = jnp.sum(jnp.exp(logits - top), axis=2, keepdims=True)
    lse = top + jnp.log(total)
    probs_low = jnp.exp(logits - lse).astype(BF16)
    attended_heads = head_dot("hqk,hkd->hqd", probs_low, values)

    def heads_to_tokens(v):
        v = jnp.swapaxes(v.astype(BF16), 0, 1).reshape(ns, local, head_cols)
        return jnp.swapaxes(seq_exchange(v), 0, 1).reshape(local, features)

    def tokens_to_heads(v):
        v = seq_exchange(jnp.swapaxes(v.reshape(local, ns, head_cols), 0, 1))
        return jnp.swapaxes(v.reshape(row_len, heads, HEAD_DIM), 0, 1)

    grad_out_rows = gather_rows(grad_out)
    attended_low = heads_to_tokens(attended_heads)
    attended_low, w_proj, grad_out_rows = after((attended_low, w_proj, grad_out_rows))
    own_down, attended_low, up_part = after((fc2_w, attended_low, up_part))
    down_part = lax.all_gather(own_down, "seq", axis=0, tiled=True)
    second = first + dot(attended_low, w_proj) + b_proj
    xhat_two, inverse_two = norm_pieces(second)
    normed_two = (xhat_two * g_two + b_two).astype(BF16)

    normed_two_rows = gather_rows(normed_two)
    up_part = inner(order, up_part).astype(BF16)
    normed_two_rows, up_part, order = after((normed_two_rows, up_part, order))
    hidden, slope = gelu_of_matmul(normed_two_rows, up_part, up_bias)

    fc2_terms = inner(hidden, grad_out_rows).astype(BF16)
    slope, fc2_terms = after((slope, fc2_terms))
    fc2_w_grad = lax.psum_scatter(fc2_terms, "seq", scatter_dimension=0, tiled=True)
    pre_grad = times_transposed(grad_out_rows, down_part) * slope
    pre_low = pre_grad.astype(BF16)
    up_back = times_transposed(pre_low, up_part)
    up_low = low_rows(up_back)
    up_low, pre_late, normed_two_rows = after((up_low, pre_low, normed_two_rows))
    normed_two_grad = add_blocks(up_back[:local], up_low)
    fc1_terms = inner(times_transposed(normed_two_rows, order).astype(BF16), pre_late).astype(BF16)
    normed_two_grad, fc1_terms = after((normed_two_grad, fc1_terms))
    through_two, ln2_g_grad, ln2_b_grad = norm_back(normed_two_grad, xhat_two, inverse_two, g_two)
    second_grad = grad_out.astype(F32) + through_two
    second_low = second_grad.astype(BF16)
    attended_grad = times_transposed(second_low, w_proj).astype(BF16)
    attended_grad, second_late, hidden_late = after((attended_grad, second_low, hidden))
    attended_grad = tokens_to_heads(attended_grad)
    proj_terms = inner(attended_low, second_late).reshape(nd, part, features)
    down_sums = dot(hidden_late, down_part)
    proj_low = proj_terms.astype(BF16)
    proj_blocks = [swap(index(proj_low, dp_at ^ k), k) for k in range(1, nd)]
    attended_grad, down_sums, fc1_terms, fc2_w_grad, proj_blocks[0] = after(
        (attended_grad, down_sums, fc1_terms, fc2_w_grad, proj_blocks[0])
    )
    fc1_terms = lax.psum_scatter(fc1_terms, "seq", scatter_dimension=0, tiled=True)
    proj_sum = index(proj_terms, dp_at)
    for block in proj_blocks:
        proj_sum = proj_sum + block.astype(F32)
    proj_sum = proj_sum.astype(BF16).reshape(ns, small, features)
    down_low, attended_heads = after((low_rows(down_sums), attended_heads))
    output = second + add_blocks(down_sums[:local], down_low) + b_down
    output = output.astype(BF16)
    delta = jnp.sum(attended_grad.astype(F32) * attended_heads, axis=2, keepdims=True)
    probs = jnp.exp(logits - lse)
    prob_grad = head_dot("hqd,hkd->hqk", attended_grad, values)
    logit_grad = (probs * (prob_grad - delta) * scale).astype(BF16)
    triple_grad = jnp.concatenate(
        [
            jnp.swapaxes(v, 0, 1).reshape(row_len, head_cols).astype(BF16)
            for v in (
                head_dot("hqk,hkd->hqd", logit_grad, keys),
                head_dot("hqk,hqd->hkd", logit_grad, queries),
                head_dot("hqk,hqd->hkd", probs.astype(BF16), attended_grad),
            )
        ],
        axis=1,
    )
    one_back = times_transposed(triple_grad, qkv_mine).astype(BF16)
    one_back, triple_late, fc1_terms, output, proj_sum = after(
        (one_back, triple_grad, fc1_terms, output, proj_sum)
    )
    normed_one_grad = lax.psum_scatter(one_back, "seq", scatter_dimension=0, tiled=True)
    qkv_terms = inner(normed_one_row, triple_late).reshape(nd, part, wide)
    qkv_low = qkv_terms.astype(BF16)
    qkv_sum = index(qkv_terms, dp_at)
    for k in range(1, nd):
        qkv_sum = qkv_sum + swap(index(qkv_low, dp_at ^ k), k).astype(F32)
    qkv_sum = qkv_sum.astype(BF16).reshape(ns, small, wide)
    fc1_terms = fc1_terms.reshape(nd, small, hidden_part)
    fc1_blocks = jnp.stack([fc1_terms[0]] + [swap(fc1_terms[k], k) for k in range(1, nd)])
    proj_w_grad = chip_sums(core_sums(proj_sum))
    normed_one_grad, qkv_sum, fc1_blocks, proj_w_grad = after(
        (normed_one_grad, qkv_sum, fc1_blocks, proj_w_grad)
    )
    normed_one_grad = normed_one_grad.astype(F32)
    through_one, ln1_g_grad, ln1_b_grad = norm_back(normed_one_grad, xhat_one, inverse_one, g_one)
    first_grad = second_grad + through_one
    first_low = first_grad.astype(BF16)
    first_low_rows = gather_rows(first_low)
    qkv_w_grad = seq_exchange(qkv_sum)
    vector_grads = jnp.stack(
        [
            jnp.sum(first_grad, axis=0),
            ln1_g_grad,
            ln1_b_grad,
            jnp.sum(second_grad, axis=0),
            ln2_g_grad,
            ln2_b_grad,
            jnp.sum(grad_out.astype(F32), axis=0),
        ]
    )
    vector_grads = jnp.swapaxes(vector_grads.reshape(7, n, small), 0, 1).reshape(n, 7 * small)
    up_grads = jnp.sum(pre_grad, axis=0).reshape(ns, hidden_units // n)
    up_grads = lax.dynamic_update_slice_in_dim(
        jnp.zeros((n, hidden_units // n), F32), up_grads, dp_at * ns, 0
    )
    vector_grads = jnp.concatenate([vector_grads, up_grads], axis=1)
    vector_grads = jnp.pad(vector_grads, ((0, 0), (0, padded - own_size)))
    vector_grads = lax.all_to_all(
        vector_grads.reshape(n, padded // 128, 128), ("dp", "seq"), 0, 0, tiled=True
    )
    first_low_rows, qkv_w_grad, vector_grads = after((first_low_rows, qkv_w_grad, vector_grads))
    skip_terms = inner(joined_here, first_low_rows).reshape(ns, 2 * small, features)
    skip_sums = core_sums(skip_terms)
    joined_grad_part = times_transposed(first_low_rows, skip_part).astype(BF16)
    skip_sums, joined_grad_part = after((skip_sums, joined_grad_part))
    skip_w_grad = chip_sums(skip_sums)
    joined_grad_part = joined_grad_part.reshape(nd, local, joined_part)
    away = jnp.stack(
        [joined_grad_part[0]] + [swap(joined_grad_part[k], k) for k in range(1, nd)]
    )
    joined_grad = jnp.concatenate(
        [index(away, dp_at ^ k) for k in range(nd)], axis=1
    ).astype(F32)
    fc1_w_grad = jnp.concatenate([index(fc1_blocks, dp_at ^ k) for k in range(nd)], axis=1)
    qkv_w_grad = (
        qkv_w_grad.reshape(ns, small, 3, head_cols).transpose(1, 2, 0, 3)
        .reshape(small, 3 * features)
    )
    vector_grads = jnp.sum(vector_grads, axis=0).reshape(padded)
    skip_b_grad, ln1_g_grad, ln1_b_grad, proj_b_grad, ln2_g_grad, ln2_b_grad, fc2_b_grad = (
        vector_grads[i * small : (i + 1) * small] for i in range(7)
    )
    fc1_b_grad = vector_grads[7 * small : own_size]
    return (
        output[None], joined_grad[None, :, :features], joined_grad[None, :, features:],
        skip_w_grad, qkv_w_grad.astype(F32), proj_w_grad,
        fc1_w_grad.astype(F32), fc2_w_grad.astype(F32),
        skip_b_grad, ln1_g_grad, ln1_b_grad, proj_b_grad, ln2_g_grad, ln2_b_grad,
        fc1_b_grad, fc2_b_grad,
    )


def solution(mesh):
    tokens = P("dp", "seq", None)
    matrix = P(("dp", "seq"), None)
    flat = P(("dp", "seq"))
    in_specs = (tokens, tokens, P("dp", None)) + (matrix,) * 5 + (flat,) * 8 + (tokens,)
    out_specs = (tokens,) * 3 + (matrix,) * 5 + (flat,) * 8
    return jax.shard_map(
        partial(on_device, mesh.shape["dp"], mesh.shape["seq"]),
        mesh=mesh, in_specs=in_specs, out_specs=out_specs, check_vma=False,
    )
```

time: 541 us -> 481 us (0.89)
  waiting for transfers between devices: 192 us -> 126 us
  blocking collectives: 51.6 us -> 32.6 us
  other arithmetic: 35.6 us -> 45.3 us
  starting transfers between devices: 67.1 us -> 75.8 us
    all_to_all x4 -> x2, waiting for transfers between devices: 50.3 us -> 11.3 us  [chip_sums(): lax.all_to_all(sums, 'seq', 0, 0, axis_index_groups=groups, tiled=True)]
    dynamic_update_slice x0 -> x11, local copies, waits for them, and re-layouts: none -> 28.8 us  [the longest x4 19.4 us: on_device(): lax.dynamic_update_slice_in_dim(qkv_blocks, block, (dp_at ^ k) * part, 0)]
    all_to_all x4 -> x3, waiting for transfers between devices: 53 us -> 25.1 us  [seq_exchange(): return lax.all_to_all(v, 'seq', 0, 0, tiled=True)]
    all_to_all x2 -> x1, blocking collectives: 36 us -> 14.1 us  [on_device(): vectors = lax.all_to_all(packed, ('dp', 'seq'), 0, 0, tiled=True)]
    ppermute x27 -> x42, starting transfers between devices: 31.7 us -> 52.2 us  [swap(): return lax.ppermute(v, 'dp', [(i, i ^ k) for i in range(nd)])]
    reshape x13 -> x4, local copies, waits for them, and re-layouts: 21.2 us -> 8.06 us  [the longest x1 7.04 us: on_device(): qkv_mine = qkv_rows.reshape(part, 3, ns, head_cols)]
    dot_general x5 -> x6, matrix products: 13.6 us -> 24 us  [inner(): lax.dot_general(left, right, (((0,), (0,)), ((), ())), preferred_element_...]
    convert_element_type x8 -> x12, other arithmetic: 7.55 us -> 17.7 us  [the longest x1 3.99 us: on_device(): (row == lax.broadcasted_iota(jnp.int32, (features, features), 1)).astype(...]
  transfers between devices with their start and end apart: 44 -> 61, of which waited for: 25 -> 21; matrix products, arithmetic and copies ran while one was open for 29% -> 41% of each run, Pallas kernels for 1% -> 1%
where the time goes in v6:
time: 481 us; the launch traced here: 475 us
  waiting for transfers between devices  126 us (26%)
  matrix products  86.5 us (18%)
  local copies, waits for them, and re-layouts  84.5 us (18%)
  starting transfers between devices  75.8 us (16%)
  other arithmetic  45.3 us (9%)
  blocking collectives  32.6 us (7%)
  between operations  19.2 us (4%)
  Pallas kernels  5.41 us (1%)
    ppermute x42, waiting for transfers between devices, swap(): return lax.ppermute(v, 'dp', [(i, i ^ k) for i in range(nd)])  63 us
    ppermute x42, starting transfers between devices, swap(): return lax.ppermute(v, 'dp', [(i, i ^ k) for i in range(nd)])  52.2 us
    dot_general x6, matrix products, head_dot(): return jnp.einsum(spec, left, right, preferred_element_type=F32)  25.1 us
    all_to_all x3, waiting for transfers between devices, seq_exchange(): return lax.all_to_all(v, 'seq', 0, 0, tiled=True)  25.1 us
    dot_general x6, matrix products, inner(): lax.dot_general(left, right, (((0,), (0,)), ((), ())), preferred_element_...  24 us
    dot_general x5, matrix products, times_transposed(): lax.dot_general(left, right, (((1,), (1,)), ((), ())), preferred_element_...  21.2 us
    dynamic_update_slice x4, local copies, waits for them, and re-layouts, on_device(): lax.dynamic_update_slice_in_dim(qkv_blocks, block, (dp_at ^ k) * part, 0)  19.4 us
    all_gather x1, blocking collectives, on_device(): proj_rows = lax.all_gather(own_proj, 'seq', axis=0, tiled=True)  18.6 us
  transfers between devices with their start and end apart: 61, of which 21 were waited for; matrix products, arithmetic and copies ran while one was open for 41% of the time, Pallas kernels for 1%

profile of v6, /device:TPU:0, one launch (start us, length us, event | category | flops | bytes accessed | tf_op | source)
XLA Modules:
  0.0 475.0 jit_solution(2173812846752893158)
XLA Ops:
  14.5 14.1 %all_to_all.35 = bf16[32,8,128]{2,1,0:T(8,128)(2,1)S(1)} all-to-all(bf16[32,8,128]{2,1,0:T(8,128)(2,1)S(1)} %broadcast_in_dim.30), channel_id=1, replica_groups=mesh['dp'=4,'seq'=8] {'dp','seq'}, dimensions={0} | all-to-all | bytes 131072 | tf_op jit(solution)/shard_map/all_to_all | solution.py:166
  28.7 8.4 %all-gather.9.cloned.1.call-done = bf16[576,1152]{1,0:T(8,128)(2,1)} async-done(((bf16[72,1152]{1,0:T(8,128)(2,1)}), bf16[576,1152]{1,0:T(8,128)(2,1)}) %all-gather.9.cloned.1.call-update) | async-done | bytes 1327120 | tf_op jit(solution)/shard_map/all_gather | solution.py:158
  46.8 18.6 %all-gather.1 = bf16[8,36,1152]{2,1,0:T(8,128)(2,1)S(1)} all-gather(bf16[1,36,1152]{2,1,0:T(8,128)(2,1)S(1)} %bitcast.258), channel_id=1, replica_groups=mesh['dp'=4,'seq'=8] {'seq'}, dimensions={0}, use_global_device_ids=true | all-gather | bytes 746496 | tf_op jit(solution)/shard_map/all_gather | solution.py:194
  68.3 5.9 %all-gather.17.cloned.1.call-done = bf16[8,36,3456]{2,1,0:T(8,128)(2,1)} async-done(((bf16[1,36,3456]{2,1,0:T(8,128)(2,1)}), bf16[8,36,3456]{2,1,0:T(8,128)(2,1)}) %all-gather.17.cloned.1.call-update) | async-done | bytes 1990672 | tf_op jit(solution)/shard_map/all_gather | solution.py:191
  88.6 7.0 %reshape.288 = bf16[288,3,8,144]{3,2,1,0:T(8,128)(2,1)} reshape(bf16[8,36,3456]{2,1,0:T(8,128)(2,1)} %all-gather.17.cloned.1.call-done) | data formatting | bytes 3981312 | tf_op jit(solution)/shard_map/reshape | solution.py:200
  124.0 5.3 %dynamic_update_slice.37 = bf16[1152,432]{0,1:T(8,128)(2,1)S(1)} dynamic-update-slice(bf16[1152,432]{0,1:T(8,128)(2,1)S(1)} %dynamic_update_slice.36, bf16[288,432]{0,1:T(8,128)(2,1)} %copy-done.40, s32[]{:T(128)S(6)} %select_n.127, s32[]{:T(128)} %constant.156.clone.1) | dynamic-update-slice | bytes 497668 | tf_op jit(solution)/shard_map/dynamic_update_slice | solution.py:205
  131.8 5.0 %dynamic_update_slice.38 = bf16[1152,432]{0,1:T(8,128)(2,1)S(1)} dynamic-update-slice(bf16[1152,432]{0,1:T(8,128)(2,1)S(1)} %dynamic_update_slice.37, bf16[288,432]{0,1:T(8,128)(2,1)} %collective-permute-done.10, s32[]{:T(128)S(6)} %select_n.128, s32[]{:T(128)} %constant.156.clone.1) | dynamic-update-slice | bytes 497668 | tf_op jit(solution)/shard_map/dynamic_update_slice | solution.py:205
  136.9 5.2 %dynamic_update_slice.39 = bf16[1152,432]{0,1:T(8,128)(2,1)S(1)} dynamic-update-slice(bf16[1152,432]{0,1:T(8,128)(2,1)S(1)} %dynamic_update_slice.38, bf16[288,432]{0,1:T(8,128)(2,1)} %collective-permute-done.11, s32[]{:T(128)S(6)} %select_n.129, s32[]{:T(128)} %constant.156.clone.1) | dynamic-update-slice | bytes 497668 | tf_op jit(solution)/shard_map/dynamic_update_slice | solution.py:205
  177.8 13.9 %all-to-all-done.1 = bf16[8,160,144]{1,2,0:T(8,128)(2,1)S(1)} async-done(((bf16[8,160,144]{1,2,0:T(8,128)(2,1)}), bf16[8,160,144]{1,2,0:T(8,128)(2,1)S(1)}, u32[]{:S(2)}, u32[]{:S(2)}) %all-to-all-start.1) | async-done | bytes 368672 | tf_op jit(solution)/shard_map/all_to_all | solution.py:145
  212.2 8.1 %collective-permute-done.22 = bf16[160,1152]{1,0:T(8,128)(2,1)S(1)} collective-permute-done((bf16[160,1152]{1,0:T(8,128)(2,1)S(1)}, bf16[160,1152]{1,0:T(8,128)(2,1)S(1)}, u32[]{:S(2)}, u32[]{:S(2)}) %collective-permute-start.22) | collective-permute-done | bytes 368672 | tf_op jit(solution)/shard_map/ppermute | solution.py:125
  220.5 5.4 %shard_map.288 = (bf16[640,1152]{1,0:T(8,128)(2,1)S(1)}, f32[640,1152]{1,0:T(8,128)S(1)}) custom-call(bf16[640,1152]{1,0:T(8,128)(2,1)S(1)} %pad_maximum_fusion.1.x_ref, bf16[1152,1152]{1,0:T(8,128)(2,1)S(1)} %convolution_convert_fusion.3.w_ref, f32[1,1152]{1,0:T(1,128)S(1)} %reshape_reshape.6.bias_ref), custom_call_target="tpu_custom_call" | custom-call | flops 1698693120 | bytes 8552448 | tf_op jit(solution)/shard_map/pallas_call | solution.py:77
  231.5 6.1 %fusion.55 = (f32[1152]{0:T(1024)}, bf16[640,1152]{1,0:T(8,128)(2,1)S(1)}) fusion(f32[640,1152]{1,0:T(8,128)} %copy-done, bf16[640,1152]{1,0:T(8,128)(2,1)} %pad_maximum_fusion, bf16[1152,1152]{1,0:T(8,128)(2,1)} %all-gather.15.cloned.1.call-done), kind=kOutput, calls=%fused_computation.187 | convolution fusion | flops 1700903808 | bytes 8557056 | tf_op jit(solution)/shard_map/dot_general | solution.py:53
  246.0 8.8 %convolution_convert_fusion.1 = bf16[1152,1152]{1,0:T(8,128)(2,1)} fusion(bf16[640,1152]{1,0:T(8,128)(2,1)} %copy-done.71, bf16[640,1152]{1,0:T(8,128)(2,1)S(1)} %pad_maximum_fusion.1.x_ref, bf16[1152,1152]{1,0:T(8,128)(2,1)} %fusion.48), kind=kOutput, calls=%fused_computation.18 | convolution fusion | flops 3399450624 | bytes 8257536 | tf_op jit(solution)/shard_map/dot_general | solution.py:49
  254.8 6.5 %collective-permute-done.25 = bf16[160,1152]{1,0:T(8,128)(2,1)} collective-permute-done((bf16[160,1152]{1,0:T(8,128)(2,1)}, bf16[160,1152]{1,0:T(8,128)(2,1)}, u32[]{:S(2)}, u32[]{:S(2)}) %collective-permute-start.25) | collective-permute-done | bytes 368672 | tf_op jit(solution)/shard_map/ppermute | solution.py:125
  282.8 5.6 %fusion.65 = f32[640,1152]{1,0:T(8,128)} fusion(bf16[640,1152]{1,0:T(8,128)(2,1)S(1)} %get-tuple-element.99, bf16[1152,1152]{1,0:T(8,128)(2,1)} %all-gather.15.cloned.1.call-done), kind=kOutput, calls=%fused_computation.197 | convolution fusion | flops 1698693120 | bytes 7077888 | tf_op jit(solution)/shard_map/dot_general | solution.py:45
  288.3 11.1 %all-to-all-done.2 = bf16[8,160,144]{1,2,0:T(8,128)(2,1)S(1)} async-done(((bf16[8,160,144]{1,2,0:T(8,128)(2,1)}), bf16[8,160,144]{1,2,0:T(8,128)(2,1)S(1)}, u32[]{:S(2)}, u32[]{:S(2)}) %all-to-all-start.2) | async-done | bytes 368672 | tf_op jit(solution)/shard_map/all_to_all | solution.py:145
  310.3 8.4 %fusion.4 = bf16[2,1280,1280]{1,2,0:T(8,128)(2,1)} fusion(bf16[2,1280,72]{1,2,0:T(8,128)(2,1)S(1)} %bitcast.213, bf16[2,1280,72]{1,2,0:T(8,128)(2,1)S(1)} %bitcast.220, f32[2,1280,1280]{1,2,0:T(8,128)} %copy-done.3, f32[2,1280]{1,0:T(2,128)S(1)} %multiply_reduce_fusion.1, f32[2,1280]{1,0:T(2,128)S(1)} %log_add_fusion), kind=kOutput, calls=%fused_computation.12 | convolution fusion | flops 488243200 | bytes 20418560 | tf_op jit(solution)/shard_map/hqd,hkd->hqk/dot_general | solution.py:243
  318.7 5.1 %convolution_convert_fusion.9 = bf16[2,1280,72]{1,2,0:T(8,128)(2,1)S(1)} fusion(bf16[2,1280,1280]{1,2,0:T(8,128)(2,1)} %fusion.4, bf16[2,1280,72]{1,2,0:T(8,128)(2,1)S(1)} %bitcast.230), kind=kOutput, calls=%fused_computation.40 | convolution fusion | flops 472043520 | bytes 7290880 | tf_op jit(solution)/shard_map/hqk,hkd->hqd/dot_general | solution.py:243
  327.3 13.4 %collective-permute-done.31 = bf16[288,1152]{1,0:T(8,128)(2,1)S(1)} collective-permute-done((bf16[288,1152]{1,0:T(8,128)(2,1)}, bf16[288,1152]{1,0:T(8,128)(2,1)S(1)}, u32[]{:S(2)}, u32[]{:S(2)}) %collective-permute-start.31) | collective-permute-done | bytes 663584 | tf_op jit(solution)/shard_map/ppermute | solution.py:125
  384.3 6.0 %all-to-all-done.3 = bf16[4,36,1152]{2,1,0:T(8,128)(2,1)S(1)} async-done(((bf16[4,36,1152]{2,1,0:T(8,128)(2,1)}), bf16[4,36,1152]{2,1,0:T(8,128)(2,1)S(1)}, u32[]{:S(2)}, u32[]{:S(2)}) %all-to-all-start.3) | async-done | bytes 331808 | tf_op jit(solution)/shard_map/all_to_all | solution.py:155
  391.0 7.4 %reduce-scatter.8.cloned.1.call-done = bf16[160,1152]{1,0:T(8,128)(2,1)} async-done(((bf16[1280,1152]{1,0:T(8,128)(2,1)}), bf16[160,1152]{1,0:T(8,128)(2,1)}) %reduce-scatter.8.cloned.1.call-update) | async-done | bytes 368656 | tf_op jit(solution)/shard_map/reduce_scatter | solution.py:325
  420.2 8.1 %collective-permute-done.41 = bf16[160,1152]{1,0:T(8,128)(2,1)S(1)} collective-permute-done((bf16[160,1152]{1,0:T(8,128)(2,1)S(1)}, bf16[160,1152]{1,0:T(8,128)(2,1)S(1)}, u32[]{:S(2)}, u32[]{:S(2)}) %collective-permute-start.41) | collective-permute-done | bytes 368672 | tf_op jit(solution)/shard_map/ppermute | solution.py:125
  453.2 5.8 %collective-permute-done.46 = bf16[160,576]{0,1:T(8,128)(2,1)S(1)} collective-permute-done((bf16[160,576]{0,1:T(8,128)(2,1)S(1)}, bf16[160,576]{0,1:T(8,128)(2,1)S(1)}, u32[]{:S(2)}, u32[]{:S(2)}) %collective-permute-start.46) | collective-permute-done | bytes 184352 | tf_op jit(solution)/shard_map/ppermute | solution.py:125
  461.8 5.4 %all-to-all-done.6 = bf16[4,72,1152]{2,1,0:T(8,128)(2,1)S(1)} async-done(((bf16[4,72,1152]{2,1,0:T(8,128)(2,1)}), bf16[4,72,1152]{2,1,0:T(8,128)(2,1)S(1)}, u32[]{:S(2)}, u32[]{:S(2)}) %all-to-all-start.6) | async-done | bytes 663584 | tf_op jit(solution)/shard_map/all_to_all | solution.py:155
  (424 shorter events, 261.4 us)
Async XLA Ops:
  7.3 29.9 %all-gather.9.cloned.1.call-start = ((), (), s32[]{:S(2)}) async-start(), calls=%async_computation.10 | async-start | bytes 1492992 | tf_op jit(solution)/shard_map/all_gather | solution.py:158
  8.0 66.2 %all-gather.17.cloned.1.call-start = ((), (), s32[]{:S(2)}) async-start(), calls=%async_computation.17 | async-start | bytes 2488320 | tf_op jit(solution)/shard_map/all_gather | solution.py:191
  37.2 109.8 %all-gather.11.cloned.1.call-start = ((), (), s32[]{:S(2)}) async-start(), calls=%async_computation.11 | async-start | bytes 3317760 | tf_op jit(solution)/shard_map/all_gather | solution.py:198
  74.2 117.7 %all-gather.13.cloned.1.call-start = ((), (), s32[]{:S(2)}) async-start(), calls=%async_computation.12 | async-start | bytes 2985984 | tf_op jit(solution)/shard_map/all_gather | solution.py:226
  75.9 25.9 %collective-permute-start.6 = (bf16[36,1152]{1,0:T(8,128)(2,1)}, bf16[36,1152]{1,0:T(8,128)(2,1)S(1)}, u32[]{:S(2)}, u32[]{:S(2)}) collective-permute-start(bf16[36,1152]{1,0:T(8,128)(2,1)} %bitcast.206), channel_id=1, source_target_pairs={{0,8},{8,0},{16,24},{24,16},{1,9},{9,1},{17,25},{25,17},{2,10},{10... | collective-permute-start | bytes 248840 | tf_op jit(solution)/shard_map/ppermute | solution.py:125
  78.0 25.3 %collective-permute-start.7 = (bf16[36,1152]{1,0:T(8,128)(2,1)}, bf16[36,1152]{1,0:T(8,128)(2,1)S(1)}, u32[]{:S(2)}, u32[]{:S(2)}) collective-permute-start(bf16[36,1152]{1,0:T(8,128)(2,1)} %bitcast.205), channel_id=1, source_target_pairs={{0,16},{8,24},{16,0},{24,8},{1,17},{9,25},{17,1},{25,9},{2,18},{10... | collective-permute-start | bytes 248840 | tf_op jit(solution)/shard_map/ppermute | solution.py:125
  101.8 40.3 %collective-permute-start.14 = (bf16[144,1152]{1,0:T(8,128)(2,1)S(1)}, bf16[144,1152]{1,0:T(8,128)(2,1)}, u32[]{:S(2)}, u32[]{:S(2)}) collective-permute-start(bf16[144,1152]{1,0:T(8,128)(2,1)S(1)} %constant_dynamic-slice_fusion.5), channel_id=1, source_target_pairs={{0,16},{8,24},{16,0},{24,8},{1,17},{9,25},{17,1},{25,9},{2,18},{10... | collective-permute-start | bytes 995336 | tf_op jit(solution)/shard_map/ppermute | solution.py:125
  103.4 38.8 %collective-permute-start.16 = (bf16[144,1152]{1,0:T(8,128)(2,1)S(1)}, bf16[144,1152]{1,0:T(8,128)(2,1)}, u32[]{:S(2)}, u32[]{:S(2)}) collective-permute-start(bf16[144,1152]{1,0:T(8,128)(2,1)S(1)} %constant_dynamic-slice_fusion.5), channel_id=1, source_target_pairs={{0,24},{8,16},{16,8},{24,0},{1,25},{9,17},{17,9},{25,1},{2,26},{10... | collective-permute-start | bytes 995336 | tf_op jit(solution)/shard_map/ppermute | solution.py:125
  105.6 26.2 %collective-permute-start.10 = (bf16[288,432]{0,1:T(8,128)(2,1)S(1)}, bf16[288,432]{0,1:T(8,128)(2,1)}, u32[]{:S(2)}, u32[]{:S(2)}) collective-permute-start(bf16[288,432]{0,1:T(8,128)(2,1)S(1)} %bitcast.238), channel_id=1, source_target_pairs={{0,16},{8,24},{16,0},{24,8},{1,17},{9,25},{17,1},{25,9},{2,18},{10... | collective-permute-start | bytes 746504 | tf_op jit(solution)/shard_map/ppermute | solution.py:125
  110.3 26.6 %collective-permute-start.11 = (bf16[288,432]{0,1:T(8,128)(2,1)S(1)}, bf16[288,432]{0,1:T(8,128)(2,1)}, u32[]{:S(2)}, u32[]{:S(2)}) collective-permute-start(bf16[288,432]{0,1:T(8,128)(2,1)S(1)} %bitcast.239), channel_id=1, source_target_pairs={{0,24},{8,16},{16,8},{24,0},{1,25},{9,17},{17,9},{25,1},{2,26},{10... | collective-permute-start | bytes 746504 | tf_op jit(solution)/shard_map/ppermute | solution.py:125
  117.4 26.1 %collective-permute-start.13 = (bf16[144,1152]{1,0:T(8,128)(2,1)S(1)}, bf16[144,1152]{1,0:T(8,128)(2,1)}, u32[]{:S(2)}, u32[]{:S(2)}) collective-permute-start(bf16[144,1152]{1,0:T(8,128)(2,1)S(1)} %collective-permute-done.12), channel_id=1, source_target_pairs={{0,1},{1,0},{2,3},{3,2},{4,5},{5,4},{6,7},{7,6},{8,9},{9,8},{10,11... | collective-permute-start | bytes 995336 | tf_op jit(solution)/shard_map/ppermute | solution.py:128
  142.2 31.3 %collective-permute-start.17 = (bf16[144,1152]{1,0:T(8,128)(2,1)}, bf16[144,1152]{1,0:T(8,128)(2,1)}, u32[]{:S(2)}, u32[]{:S(2)}) collective-permute-start(bf16[144,1152]{1,0:T(8,128)(2,1)} %collective-permute-done.16), channel_id=1, source_target_pairs={{0,1},{1,0},{2,3},{3,2},{4,5},{5,4},{6,7},{7,6},{8,9},{9,8},{10,11... | collective-permute-start | bytes 995336 | tf_op jit(solution)/shard_map/ppermute | solution.py:128
  147.8 27.4 %collective-permute-start.18 = (bf16[160,1152]{1,0:T(8,128)(2,1)}, bf16[160,1152]{1,0:T(8,128)(2,1)}, u32[]{:S(2)}, u32[]{:S(2)}) collective-permute-start(bf16[160,1152]{1,0:T(8,128)(2,1)} %bitcast.19), channel_id=1, source_target_pairs={{0,8},{8,0},{16,24},{24,16},{1,9},{9,1},{17,25},{25,17},{2,10},{10... | collective-permute-start | bytes 1105928 | tf_op jit(solution)/shard_map/ppermute | solution.py:125
  149.2 26.0 %collective-permute-start.19 = (bf16[160,1152]{1,0:T(8,128)(2,1)}, bf16[160,1152]{1,0:T(8,128)(2,1)}, u32[]{:S(2)}, u32[]{:S(2)}) collective-permute-start(bf16[160,1152]{1,0:T(8,128)(2,1)} %bitcast.19), channel_id=1, source_target_pairs={{0,16},{8,24},{16,0},{24,8},{1,17},{9,25},{17,1},{25,9},{2,18},{10... | collective-permute-start | bytes 1105928 | tf_op jit(solution)/shard_map/ppermute | solution.py:125
  171.7 59.8 %all-gather.15.cloned.1.call-start = ((), (), s32[]{:S(2)}) async-start(), calls=%async_computation.13 | async-start | bytes 2985984 | tf_op jit(solution)/shard_map/all_gather | solution.py:264
  192.0 108.3 %reduce-scatter.4.cloned.1.call-start = ((), (), s32[]{:S(2)}) async-start(), calls=%async_computation.14 | async-start | bytes 2985984 | tf_op jit(solution)/shard_map/reduce_scatter | solution.py:276
  274.5 25.8 %collective-permute-start.27 = (bf16[288,1152]{1,0:T(8,128)(2,1)}, bf16[288,1152]{1,0:T(8,128)(2,1)}, u32[]{:S(2)}, u32[]{:S(2)}) collective-permute-start(bf16[288,1152]{1,0:T(8,128)(2,1)} %get-tuple-element.142), channel_id=1, source_target_pairs={{0,8},{8,0},{16,24},{24,16},{1,9},{9,1},{17,25},{25,17},{2,10},{10... | collective-permute-start | bytes 1990664 | tf_op jit(solution)/shard_map/ppermute | solution.py:125
  282.7 73.1 %reduce-scatter.6.cloned.1.call-start = ((), (), s32[]{:S(2)}) async-start(), calls=%async_computation.15 | async-start | bytes 2985984 | tf_op jit(solution)/shard_map/reduce_scatter | solution.py:298
  300.3 98.0 %reduce-scatter.8.cloned.1.call-start = ((), (), s32[]{:S(2)}) async-start(), calls=%async_computation.16 | async-start | bytes 3317760 | tf_op jit(solution)/shard_map/reduce_scatter | solution.py:325
  300.4 40.2 %collective-permute-start.31 = (bf16[288,1152]{1,0:T(8,128)(2,1)}, bf16[288,1152]{1,0:T(8,128)(2,1)S(1)}, u32[]{:S(2)}, u32[]{:S(2)}) collective-permute-start(bf16[288,1152]{1,0:T(8,128)(2,1)} %get-tuple-element.140), channel_id=1, source_target_pairs={{0,16},{8,24},{16,0},{24,8},{1,17},{9,25},{17,1},{25,9},{2,18},{10... | collective-permute-start | bytes 1990664 | tf_op jit(solution)/shard_map/ppermute | solution.py:125
  301.6 39.0 %collective-permute-start.32 = (bf16[288,1152]{1,0:T(8,128)(2,1)}, bf16[288,1152]{1,0:T(8,128)(2,1)S(1)}, u32[]{:S(2)}, u32[]{:S(2)}) collective-permute-start(bf16[288,1152]{1,0:T(8,128)(2,1)} %get-tuple-element.141), channel_id=1, source_target_pairs={{0,24},{8,16},{16,8},{24,0},{1,25},{9,17},{17,9},{25,1},{2,26},{10... | collective-permute-start | bytes 1990664 | tf_op jit(solution)/shard_map/ppermute | solution.py:125
  306.6 46.8 %collective-permute-start.28 = (bf16[160,1152]{1,0:T(8,128)(2,1)}, bf16[160,1152]{1,0:T(8,128)(2,1)}, u32[]{:S(2)}, u32[]{:S(2)}) collective-permute-start(bf16[160,1152]{1,0:T(8,128)(2,1)} %get-tuple-element.145), channel_id=1, source_target_pairs={{0,8},{8,0},{16,24},{24,16},{1,9},{9,1},{17,25},{25,17},{2,10},{10... | collective-permute-start | bytes 1105928 | tf_op jit(solution)/shard_map/ppermute | solution.py:125
  307.0 46.4 %collective-permute-start.29 = (bf16[160,1152]{1,0:T(8,128)(2,1)}, bf16[160,1152]{1,0:T(8,128)(2,1)}, u32[]{:S(2)}, u32[]{:S(2)}) collective-permute-start(bf16[160,1152]{1,0:T(8,128)(2,1)} %get-tuple-element.147), channel_id=1, source_target_pairs={{0,16},{8,24},{16,0},{24,8},{1,17},{9,25},{17,1},{25,9},{2,18},{10... | collective-permute-start | bytes 1105928 | tf_op jit(solution)/shard_map/ppermute | solution.py:125
  308.1 45.3 %collective-permute-start.30 = (bf16[160,1152]{1,0:T(8,128)(2,1)}, bf16[160,1152]{1,0:T(8,128)(2,1)}, u32[]{:S(2)}, u32[]{:S(2)}) collective-permute-start(bf16[160,1152]{1,0:T(8,128)(2,1)} %get-tuple-element.146), channel_id=1, source_target_pairs={{0,24},{8,16},{16,8},{24,0},{1,25},{9,17},{17,9},{25,1},{2,26},{10... | collective-permute-start | bytes 1105928 | tf_op jit(solution)/shard_map/ppermute | solution.py:125
  (113 other events, 1505.3 us)
Sparse Core Ops, SparseCore 0:
  9.7 27.3 all-gather.8
  38.8 35.3 all-gather.16
  76.4 36.1 all-gather.10
  147.1 36.4 all-gather.12
  192.1 32.9 all-gather.14
  231.6 35.5 reduce-scatter.3
  300.4 35.7 reduce-scatter.5
  356.0 42.2 reduce-scatter.7

commit v7 on v6

--- a/solution.py
+++ b/solution.py
@@ -12,6 +12,7 @@
 HEAD_DIM = 72
 EPSILON = 1e-05
 NEGATIVE = -1e30
+WIDE = 128
 F32 = jnp.float32
 BF16 = jnp.bfloat16
 
@@ -51,6 +52,144 @@
 
 def times_transposed(left, right):
     return lax.dot_general(left, right, (((1,), (1,)), ((), ())), preferred_element_type=F32)
+
+
+def attend_kernel(heads, scale, q_ref, k_ref, v_ref, seg_q_ref, seg_k_ref, out_ref, low_ref, lse_ref):
+    allowed = seg_q_ref[...] == seg_k_ref[...]
+    lane = lax.broadcasted_iota(jnp.int32, (q_ref.shape[0], WIDE), 1)
+    logs = jnp.zeros((q_ref.shape[0], WIDE), F32)
+    outs = []
+    for h in range(heads):
+        at = slice(h * WIDE, (h + 1) * WIDE)
+        logits = times_transposed(q_ref[:, at], k_ref[:, at]) * scale
+        logits = jnp.where(allowed, logits, NEGATIVE)
+        top = jnp.max(logits, axis=1, keepdims=True)
+        weights = jnp.exp(logits - top)
+        total = jnp.sum(weights, axis=1, keepdims=True)
+        outs.append(dot(weights.astype(BF16), v_ref[:, at]) / total)
+        out_ref[:, at] = outs[h]
+        logs = jnp.where(lane == h, top + jnp.log(total), logs)
+    lse_ref[...] = jnp.transpose(logs)[:8]
+    if heads == 1:
+        low_ref[...] = outs[0][:, :HEAD_DIM].astype(BF16)
+    else:
+        second = pltpu.roll(outs[1], HEAD_DIM, 1)
+        rest = heads * HEAD_DIM - WIDE
+        low_ref[:, :WIDE] = jnp.where(lane < HEAD_DIM, outs[0], second).astype(BF16)
+        low_ref[:, WIDE:] = second[:, :rest].astype(BF16)
+
+
+def attend(triple, segments, heads, scale):
+    rows = triple.shape[0]
+    wide = heads * WIDE
+    step = 256 if rows % 256 == 0 else rows
+    return pl.pallas_call(
+        partial(attend_kernel, heads, scale),
+        grid=(rows // step,),
+        in_specs=[
+            pl.BlockSpec((step, wide), lambda i: (i, 0)),
+            pl.BlockSpec((rows, wide), lambda i: (0, 1)),
+            pl.BlockSpec((rows, wide), lambda i: (0, 2)),
+            pl.BlockSpec((step, 1), lambda i: (i, 0)),
+            pl.BlockSpec((1, rows), lambda i: (0, 0)),
+        ],
+        out_specs=[
+            pl.BlockSpec((step, wide), lambda i: (i, 0)),
+            pl.BlockSpec((step, heads * HEAD_DIM), lambda i: (i, 0)),
+            pl.BlockSpec((8, step), lambda i: (0, i)),
+        ],
+        out_shape=[
+            jax.ShapeDtypeStruct((rows, wide), F32),
+            jax.ShapeDtypeStruct((rows, heads * HEAD_DIM), BF16),
+            jax.ShapeDtypeStruct((8, rows), F32),
+        ],
+        compiler_params=pltpu.CompilerParams(vmem_limit_bytes=48 * 2**20),
+        cost_estimate=pl.CostEstimate(
+            flops=8 * rows * rows * wide,
+            bytes_accessed=10 * rows * wide,
+            transcendentals=heads * rows * rows,
+        ),
+    )(triple, triple, triple, segments.reshape(rows, 1), segments.reshape(1, rows))
+
+
+def attend_back_kernel(
+    heads, scale, q_ref, k_ref, v_ref, out_grad_ref, out_ref, lse_ref, seg_q_ref, seg_k_ref,
+    dq_ref, dk_ref, dv_ref, sum_ref, grad_ref, delta_ref,
+):
+    step = pl.program_id(0)
+
+    @pl.when(step == 0)
+    def _():
+        sum_ref[...] = jnp.zeros_like(sum_ref)
+        ones = jnp.ones((8, WIDE), F32)
+        for h in range(heads):
+            grad = out_grad_ref[...]
+            if h > 0:
+                grad = pltpu.roll(grad.astype(F32), 2 * WIDE - HEAD_DIM, 1).astype(BF16)
+            grad = grad[:, :WIDE]
+            at = slice(h * WIDE, (h + 1) * WIDE)
+            grad_ref[:, at] = grad
+            delta = lax.dot_general(
+                ones, grad.astype(F32) * out_ref[:, at], (((1,), (1,)), ((), ())),
+                precision=lax.Precision.HIGHEST, preferred_element_type=F32,
+            )
+            delta_ref[h : h + 1, :] = delta[:1]
+
+    allowed = seg_k_ref[...] == seg_q_ref[...]
+    for h in range(heads):
+        at = slice(h * WIDE, (h + 1) * WIDE)
+        queries, keys, out_grad = q_ref[:, at], k_ref[:, at], grad_ref[:, at]
+        logits = times_transposed(keys, queries) * scale - lse_ref[h : h + 1, :]
+        probs = jnp.where(allowed, jnp.exp(logits), 0.0)
+        prob_grad = times_transposed(v_ref[:, at], out_grad)
+        logit_grad = (probs * (prob_grad - delta_ref[h : h + 1, :]) * scale).astype(BF16)
+        dv_ref[:, at] = dot(probs.astype(BF16), out_grad).astype(BF16)
+        dk_ref[:, at] = dot(logit_grad, queries).astype(BF16)
+        sum_ref[:, at] += inner(logit_grad, keys)
+
+    @pl.when(step == pl.num_programs(0) - 1)
+    def _():
+        dq_ref[...] = sum_ref[...].astype(BF16)
+
+
+def attend_back(triple, out_grad, out, lse, segments, heads, scale):
+    rows = triple.shape[0]
+    wide = heads * WIDE
+    step = 256 if rows % 256 == 0 else rows
+    whole = pl.BlockSpec((rows, wide), lambda i: (0, 0))
+    out_grad = jnp.pad(out_grad, ((0, 0), (0, wide - out_grad.shape[1])))
+    block = pl.BlockSpec((step, wide), lambda i: (i, 0))
+    row = pl.BlockSpec((8, rows), lambda i: (0, 0))
+    return pl.pallas_call(
+        partial(attend_back_kernel, heads, scale),
+        grid=(rows // step,),
+        in_specs=[
+            whole,
+            pl.BlockSpec((step, wide), lambda i: (i, 1)),
+            pl.BlockSpec((step, wide), lambda i: (i, 2)),
+            whole,
+            whole,
+            row,
+            pl.BlockSpec((1, rows), lambda i: (0, 0)),
+            pl.BlockSpec((step, 1), lambda i: (i, 0)),
+        ],
+        out_specs=[whole, block, block],
+        out_shape=[jax.ShapeDtypeStruct((rows, wide), BF16)] * 3,
+        scratch_shapes=[
+            pltpu.VMEM((rows, wide), F32),
+            pltpu.VMEM((rows, wide), BF16),
+            pltpu.VMEM((8, rows), F32),
+        ],
+        compiler_params=pltpu.CompilerParams(vmem_limit_bytes=48 * 2**20),
+        cost_estimate=pl.CostEstimate(
+            flops=20 * rows * rows * wide,
+            bytes_accessed=14 * rows * wide,
+            transcendentals=heads * rows * rows,
+        ),
+    )(
+        triple, triple, triple, out_grad, out, lse,
+        segments.reshape(1, rows), segments.reshape(rows, 1),
+    )
 
 
 def gelu_kernel(rows_at_once, x_ref, w_ref, bias_ref, value_ref, slope_ref):
@@ -141,6 +280,14 @@
     def low_rows(partial_sums):
         return partial_sums.astype(BF16).reshape(nd, local, features)
 
+    def widen(v):
+        v = v.reshape(v.shape[0], v.shape[1] // HEAD_DIM, HEAD_DIM)
+        return jnp.pad(v, ((0, 0), (0, 0), (0, WIDE - HEAD_DIM))).reshape(v.shape[0], -1)
+
+    def narrow(v):
+        v = v.reshape(v.shape[0], v.shape[1] // WIDE, WIDE)
+        return v[:, :, :HEAD_DIM].reshape(v.shape[0], -1)
+
     def seq_exchange(v):
         return lax.all_to_all(v, "seq", 0, 0, tiled=True)
 
@@ -178,8 +325,13 @@
         + [swap(index(joined_slices, dp_at ^ k), k) for k in range(1, nd)],
         axis=0,
     )
-    own_qkv, own_proj, skip_part, joined_here, vectors = after(
-        (qkv_w, proj_w, skip_part, joined_here, vectors)
+    at = lax.broadcasted_iota(jnp.int32, (features, features), 0)
+    block, row = at // small, at % small
+    row = ((block % nd) ^ dp_at) * part + (block // nd) * small + row
+    order = (row == lax.broadcasted_iota(jnp.int32, (features, features), 1)).astype(BF16)
+    qkv_out = qkv_w.reshape(small, 3, ns, head_cols).transpose(2, 0, 1, 3).reshape(ns, small, wide)
+    qkv_out, skip_part, joined_here, vectors, order = after(
+        (qkv_out, skip_part, joined_here, vectors, order)
     )
     def vector(at):
         return vectors[:, at * small : (at + 1) * small].reshape(features)
@@ -188,22 +340,18 @@
     up_bias = lax.dynamic_slice_in_dim(vectors[:, 7 * small : own_size], dp_at * ns, ns, 0)
     up_bias = up_bias.reshape(hidden_part)
 
-    qkv_rows = lax.all_gather(own_qkv, "seq", axis=0, tiled=False)
     first_terms = dot(joined_here, skip_part)
     first = add_blocks(first_terms[:local], low_rows(first_terms)) + b_skip
-    proj_rows = lax.all_gather(own_proj, "seq", axis=0, tiled=True)
+    qkv_mine = seq_exchange(qkv_out).reshape(part, wide)
     xhat_one, inverse_one = norm_pieces(first)
     normed_one = (xhat_one * g_one + b_one).astype(BF16)
-    normed_one, proj_rows, qkv_rows = after((normed_one, proj_rows, qkv_rows))
+    normed_one, qkv_mine, own_proj = after((normed_one, qkv_mine, proj_w))
     normed_one_row = lax.all_gather(normed_one, "seq", axis=0, tiled=True)
 
-    qkv_mine = qkv_rows.reshape(part, 3, ns, head_cols)
-    qkv_mine = index(qkv_mine, seq_at, 2).reshape(part, wide)
-    qkv_blocks = jnp.zeros((features, wide), BF16)
-    for k in range(nd):
-        block = qkv_mine if k == 0 else swap(qkv_mine, k)
-        qkv_blocks = lax.dynamic_update_slice_in_dim(qkv_blocks, block, (dp_at ^ k) * part, 0)
-    qkv_mine = qkv_blocks
+    qkv_blocks = jnp.stack([qkv_mine] + [swap(qkv_mine, k) for k in range(1, nd)])
+    qkv_mine = jnp.concatenate([index(qkv_blocks, dp_at ^ k) for k in range(nd)], axis=0)
+    qkv_mine = widen(qkv_mine)
+    proj_rows = lax.all_gather(own_proj, "seq", axis=0, tiled=True)
     up_slices = jnp.swapaxes(fc1_w.reshape(small, nd, hidden_part), 0, 1)
     up_slices = jnp.concatenate(
         [index(up_slices, dp_at)] + [swap(index(up_slices, dp_at ^ k), k) for k in range(1, nd)],
@@ -220,46 +368,26 @@
         there = other_core(here)
         w_proj = lax.dynamic_update_slice_in_dim(w_proj, here, (place + core) * half, 0)
         w_proj = lax.dynamic_update_slice_in_dim(w_proj, there, (place + 1 - core) * half, 0)
-    normed_one_row, up_slices, qkv_mine, grad_out = after(
-        (normed_one_row, up_slices, qkv_mine, cotangent[0])
+    normed_one_row, up_slices, qkv_mine, w_proj = after(
+        (normed_one_row, up_slices, qkv_mine, w_proj)
     )
     up_part = lax.all_gather(up_slices, "seq", axis=0, tiled=True)
-    at = lax.broadcasted_iota(jnp.int32, (features, features), 0)
-    block, row = at // small, at % small
-    row = ((block % nd) ^ dp_at) * part + (block // nd) * small + row
-    order = (row == lax.broadcasted_iota(jnp.int32, (features, features), 1)).astype(BF16)
-
     triple = dot(normed_one_row, qkv_mine).astype(BF16)
-    queries, keys, values = (
-        jnp.swapaxes(
-            triple[:, i * head_cols : (i + 1) * head_cols].reshape(row_len, heads, HEAD_DIM), 0, 1
-        )
-        for i in range(3)
-    )
     segments = segment_of(item_lengths, jnp.arange(row_len, dtype=jnp.int32))
-    allowed = (segments[:, None] == segments[None, :])[None]
-
-    def head_dot(spec, left, right):
-        return jnp.einsum(spec, left, right, preferred_element_type=F32)
-
-    logits = jnp.where(allowed, head_dot("hqd,hkd->hqk", queries, keys) * scale, NEGATIVE)
-    top = jnp.max(logits, axis=2, keepdims=True)
-    total = jnp.sum(jnp.exp(logits - top), axis=2, keepdims=True)
-    lse = top + jnp.log(total)
-    probs_low = jnp.exp(logits - lse).astype(BF16)
-    attended_heads = head_dot("hqk,hkd->hqd", probs_low, values)
+    attended, attended_low, lse = attend(triple, segments, heads, scale)
 
     def heads_to_tokens(v):
-        v = jnp.swapaxes(v.astype(BF16), 0, 1).reshape(ns, local, head_cols)
-        return jnp.swapaxes(seq_exchange(v), 0, 1).reshape(local, features)
+        v = seq_exchange(v.reshape(ns, local, head_cols))
+        return jnp.swapaxes(v, 0, 1).reshape(local, features)
 
     def tokens_to_heads(v):
         v = seq_exchange(jnp.swapaxes(v.reshape(local, ns, head_cols), 0, 1))
-        return jnp.swapaxes(v.reshape(row_len, heads, HEAD_DIM), 0, 1)
-
+        return v.reshape(row_len, head_cols)
+
+    attended_low, grad_out = after((attended_low, cotangent[0]))
     grad_out_rows = gather_rows(grad_out)
-    attended_low = heads_to_tokens(attended_heads)
-    attended_low, w_proj, grad_out_rows = after((attended_low, w_proj, grad_out_rows))
+    attended_low = heads_to_tokens(attended_low)
+    attended_low, grad_out_rows = after((attended_low, grad_out_rows))
     own_down, attended_low, up_part = after((fc2_w, attended_low, up_part))
     down_part = lax.all_gather(own_down, "seq", axis=0, tiled=True)
     second = first + dot(attended_low, w_proj) + b_proj
@@ -272,13 +400,21 @@
     hidden, slope = gelu_of_matmul(normed_two_rows, up_part, up_bias)
 
     fc2_terms = inner(hidden, grad_out_rows).astype(BF16)
-    slope, fc2_terms = after((slope, fc2_terms))
+    slope, fc2_terms, attended_low = after((slope, fc2_terms, attended_low))
+    attended_slices = jnp.swapaxes(attended_low.reshape(local, nd, part), 0, 1)
+    attended_rows = jnp.concatenate(
+        [index(attended_slices, dp_at)]
+        + [swap(index(attended_slices, dp_at ^ k), k) for k in range(1, nd)],
+        axis=0,
+    )
     fc2_w_grad = lax.psum_scatter(fc2_terms, "seq", scatter_dimension=0, tiled=True)
     pre_grad = times_transposed(grad_out_rows, down_part) * slope
     pre_low = pre_grad.astype(BF16)
     up_back = times_transposed(pre_low, up_part)
     up_low = low_rows(up_back)
-    up_low, pre_late, normed_two_rows = after((up_low, pre_low, normed_two_rows))
+    up_low, pre_late, normed_two_rows, attended_rows = after(
+        (up_low, pre_low, normed_two_rows, attended_rows)
+    )
     normed_two_grad = add_blocks(up_back[:local], up_low)
     fc1_terms = inner(times_transposed(normed_two_rows, order).astype(BF16), pre_late).astype(BF16)
     normed_two_grad, fc1_terms = after((normed_two_grad, fc1_terms))
@@ -286,54 +422,36 @@
     second_grad = grad_out.astype(F32) + through_two
     second_low = second_grad.astype(BF16)
     attended_grad = times_transposed(second_low, w_proj).astype(BF16)
-    attended_grad, second_late, hidden_late = after((attended_grad, second_low, hidden))
+    attended_grad, second_late, hidden_late, fc1_terms, fc2_w_grad = after(
+        (attended_grad, second_low, hidden, fc1_terms, fc2_w_grad)
+    )
+    fc1_terms = lax.psum_scatter(fc1_terms, "seq", scatter_dimension=0, tiled=True)
     attended_grad = tokens_to_heads(attended_grad)
-    proj_terms = inner(attended_low, second_late).reshape(nd, part, features)
+    second_rows = gather_rows(second_late)
     down_sums = dot(hidden_late, down_part)
-    proj_low = proj_terms.astype(BF16)
-    proj_blocks = [swap(index(proj_low, dp_at ^ k), k) for k in range(1, nd)]
-    attended_grad, down_sums, fc1_terms, fc2_w_grad, proj_blocks[0] = after(
-        (attended_grad, down_sums, fc1_terms, fc2_w_grad, proj_blocks[0])
-    )
-    fc1_terms = lax.psum_scatter(fc1_terms, "seq", scatter_dimension=0, tiled=True)
-    proj_sum = index(proj_terms, dp_at)
-    for block in proj_blocks:
-        proj_sum = proj_sum + block.astype(F32)
-    proj_sum = proj_sum.astype(BF16).reshape(ns, small, features)
-    down_low, attended_heads = after((low_rows(down_sums), attended_heads))
-    output = second + add_blocks(down_sums[:local], down_low) + b_down
-    output = output.astype(BF16)
-    delta = jnp.sum(attended_grad.astype(F32) * attended_heads, axis=2, keepdims=True)
-    probs = jnp.exp(logits - lse)
-    prob_grad = head_dot("hqd,hkd->hqk", attended_grad, values)
-    logit_grad = (probs * (prob_grad - delta) * scale).astype(BF16)
+    attended_grad, down_sums, second_rows = after((attended_grad, down_sums, second_rows))
     triple_grad = jnp.concatenate(
-        [
-            jnp.swapaxes(v, 0, 1).reshape(row_len, head_cols).astype(BF16)
-            for v in (
-                head_dot("hqk,hkd->hqd", logit_grad, keys),
-                head_dot("hqk,hqd->hkd", logit_grad, queries),
-                head_dot("hqk,hqd->hkd", probs.astype(BF16), attended_grad),
-            )
-        ],
-        axis=1,
+        attend_back(triple, attended_grad, attended, lse, segments, heads, scale), axis=1
     )
     one_back = times_transposed(triple_grad, qkv_mine).astype(BF16)
-    one_back, triple_late, fc1_terms, output, proj_sum = after(
-        (one_back, triple_grad, fc1_terms, output, proj_sum)
+    one_back, triple_late, fc1_terms, down_sums = after(
+        (one_back, triple_grad, fc1_terms, down_sums)
     )
     normed_one_grad = lax.psum_scatter(one_back, "seq", scatter_dimension=0, tiled=True)
-    qkv_terms = inner(normed_one_row, triple_late).reshape(nd, part, wide)
-    qkv_low = qkv_terms.astype(BF16)
+    qkv_terms = narrow(inner(normed_one_row, triple_late)).reshape(nd, part, wide)
+    qkv_low, down_low = qkv_terms.astype(BF16), low_rows(down_sums)
+    qkv_low, down_low, second_rows = after((qkv_low, down_low, second_rows))
+    proj_terms = inner(attended_rows, second_rows).reshape(ns, small, features)
+    proj_w_grad = chip_sums(core_sums(proj_terms))
+    output = (second + add_blocks(down_sums[:local], down_low) + b_down).astype(BF16)
     qkv_sum = index(qkv_terms, dp_at)
     for k in range(1, nd):
         qkv_sum = qkv_sum + swap(index(qkv_low, dp_at ^ k), k).astype(F32)
     qkv_sum = qkv_sum.astype(BF16).reshape(ns, small, wide)
     fc1_terms = fc1_terms.reshape(nd, small, hidden_part)
     fc1_blocks = jnp.stack([fc1_terms[0]] + [swap(fc1_terms[k], k) for k in range(1, nd)])
-    proj_w_grad = chip_sums(core_sums(proj_sum))
-    normed_one_grad, qkv_sum, fc1_blocks, proj_w_grad = after(
-        (normed_one_grad, qkv_sum, fc1_blocks, proj_w_grad)
+    normed_one_grad, qkv_sum, fc1_blocks, proj_w_grad, output = after(
+        (normed_one_grad, qkv_sum, fc1_blocks, proj_w_grad, output)
     )
     normed_one_grad = normed_one_grad.astype(F32)
     through_one, ln1_g_grad, ln1_b_grad = norm_back(normed_one_grad, xhat_one, inverse_one, g_one)
@@ -363,11 +481,10 @@
         vector_grads.reshape(n, padded // 128, 128), ("dp", "seq"), 0, 0, tiled=True
     )
     first_low_rows, qkv_w_grad, vector_grads = after((first_low_rows, qkv_w_grad, vector_grads))
-    skip_terms = inner(joined_here, first_low_rows).reshape(ns, 2 * small, features)
-    skip_sums = core_sums(skip_terms)
+    skip_terms = inner(joined_here, first_low_rows).astype(BF16)
+    skip_w_grad = lax.psum_scatter(skip_terms, "seq", scatter_dimension=0, tiled=True).astype(F32)
+    skip_terms, first_low_rows = after((skip_terms, first_low_rows))
     joined_grad_part = times_transposed(first_low_rows, skip_part).astype(BF16)
-    skip_sums, joined_grad_part = after((skip_sums, joined_grad_part))
-    skip_w_grad = chip_sums(skip_sums)
     joined_grad_part = joined_grad_part.reshape(nd, local, joined_part)
     away = jnp.stack(
         [joined_grad_part[0]] + [swap(joined_grad_part[k], k) for k in range(1, nd)]

time: 481 us -> 477 us (level)
  Pallas kernels: 5.41 us -> 27.7 us
  matrix products: 86.5 us -> 65.3 us
  blocking collectives: 32.6 us -> 18.6 us
  starting transfers between devices: 75.8 us -> 83.3 us
  other arithmetic: 45.3 us -> 38.2 us
  waiting for transfers between devices: 126 us -> 132 us
    dot_general x6 -> x0, matrix products: 25.1 us -> none  [head_dot(): return jnp.einsum(spec, left, right, preferred_element_type=F32)]
    ppermute x42 -> x45, waiting for transfers between devices: 63 us -> 86.7 us  [swap(): return lax.ppermute(v, 'dp', [(i, i ^ k) for i in range(nd)])]
    pallas_call x0 -> x2, Pallas kernels: none -> 22.4 us  [the longest x1 14 us: attend_back(): pl.pallas_call(partial(attend_back_kernel, heads, scale), grid=(rows // s...]
    dynamic_update_slice x4 -> x0, local copies, waits for them, and re-layouts: 19.4 us -> none  [on_device(): lax.dynamic_update_slice_in_dim(qkv_blocks, block, (dp_at ^ k) * part, 0)]
    all_to_all x1 -> x0, blocking collectives: 14.1 us -> none  [on_device(): vectors = lax.all_to_all(packed, ('dp', 'seq'), 0, 0, tiled=True)]
    dynamic_slice x7 -> x16, local copies, waits for them, and re-layouts: 4.55 us -> 15.1 us  [index(): return lax.dynamic_index_in_dim(v, at, axis, keepdims=False)]
    all_to_all x2 -> x1, waiting for transfers between devices: 11.3 us -> 1.08 us  [chip_sums(): lax.all_to_all(sums, 'seq', 0, 0, axis_index_groups=groups, tiled=True)]
    another operation x1 -> x4, local copies, waits for them, and re-layouts: 0.69 us -> 8.88 us
  transfers between devices with their start and end apart: 61 -> 64, of which waited for: 21 -> 35; matrix products, arithmetic and copies ran while one was open for 41% -> 36% of each run, Pallas kernels for 1% -> 6%
where the time goes in v7:
time: 477 us; the launch traced here: 469 us
  waiting for transfers between devices  132 us (28%)
  local copies, waits for them, and re-layouts  85.4 us (18%)
  starting transfers between devices  83.3 us (17%)
  matrix products  65.3 us (14%)
  other arithmetic  38.2 us (8%)
  Pallas kernels  27.7 us (6%)
  between operations  18.9 us (4%)
  blocking collectives  18.6 us (4%)
    ppermute x45, waiting for transfers between devices, swap(): return lax.ppermute(v, 'dp', [(i, i ^ k) for i in range(nd)])  86.7 us
    ppermute x45, starting transfers between devices, swap(): return lax.ppermute(v, 'dp', [(i, i ^ k) for i in range(nd)])  54.3 us
    dot_general x6, matrix products, inner(): lax.dot_general(left, right, (((0,), (0,)), ((), ())), preferred_element_...  27.5 us
    all_to_all x4, waiting for transfers between devices, seq_exchange(): return lax.all_to_all(v, 'seq', 0, 0, tiled=True)  20 us
    dot_general x5, matrix products, times_transposed(): lax.dot_general(left, right, (((1,), (1,)), ((), ())), preferred_element_...  19.6 us
    all_gather x1, blocking collectives, on_device(): proj_rows = lax.all_gather(own_proj, 'seq', axis=0, tiled=True)  18.6 us
    dot_general x4, matrix products, dot(): return jnp.dot(left, right, preferred_element_type=F32)  18.2 us
    dynamic_slice x16, local copies, waits for them, and re-layouts, index(): return lax.dynamic_index_in_dim(v, at, axis, keepdims=False)  15.1 us
  transfers between devices with their start and end apart: 64, of which 35 were waited for; matrix products, arithmetic and copies ran while one was open for 36% of the time, Pallas kernels for 6%

profile of v7, /device:TPU:0, one launch (start us, length us, event | category | flops | bytes accessed | tf_op | source)
XLA Modules:
  0.0 469.3 jit_solution(6961998594302645727)
XLA Ops:
  15.1 6.2 %all-to-all-start = ((bf16[32,8,128]{2,1,0:T(8,128)(2,1)}), bf16[32,8,128]{2,1,0:T(8,128)(2,1)S(1)}, u32[]{:S(2)}, u32[]{:S(2)}) async-start(bf16[32,8,128]{2,1,0:T(8,128)(2,1)} %broadcast_in_dim.15), calls=%async_computation | async-start | bytes 131072 | tf_op jit(solution)/shard_map/all_to_all | solution.py:313
  29.8 7.5 %all-gather.6.cloned.1.call-done = bf16[576,1152]{1,0:T(8,128)(2,1)} async-done(((bf16[72,1152]{1,0:T(8,128)(2,1)}), bf16[576,1152]{1,0:T(8,128)(2,1)}) %all-gather.6.cloned.1.call-update) | async-done | bytes 1327120 | tf_op jit(solution)/shard_map/all_gather | solution.py:305
  54.0 7.2 %collective-permute-done.4 = bf16[160,1152]{1,0:T(8,128)(2,1)S(1)} collective-permute-done((bf16[160,1152]{1,0:T(8,128)(2,1)S(1)}, bf16[160,1152]{1,0:T(8,128)(2,1)S(1)}, u32[]{:S(2)}, u32[]{:S(2)}) %collective-permute-start.4) | collective-permute-done | bytes 368672 | tf_op jit(solution)/shard_map/ppermute | solution.py:264
  76.8 18.6 %all-gather = bf16[8,36,1152]{2,1,0:T(8,128)(2,1)S(1)} all-gather(bf16[1,36,1152]{2,1,0:T(8,128)(2,1)S(1)} %bitcast.218), channel_id=1, replica_groups=mesh['dp'=4,'seq'=8] {'seq'}, dimensions={0}, use_global_device_ids=true | all-gather | bytes 746496 | tf_op jit(solution)/shard_map/all_gather | solution.py:354
  102.6 4.7 collective-permute-done.12
  129.3 5.4 %convolution_convert_fusion.4.q_ref.k_ref.v_ref = bf16[1280,768]{1,0:T(8,128)(2,1)S(1)} fusion(bf16[1280,1152]{1,0:T(8,128)(2,1)} %all-gather.8.cloned.1.call-done, bf16[1152,768]{0,1:T(8,128)(2,1)} %bitcast.186), kind=kOutput, calls=%fused_computation.24 | convolution fusion | flops 2265907200 | bytes 6684672 | tf_op jit(solution)/shard_map/dot_general | solution.py:46
  134.8 8.4 %shard_map.288 = (f32[1280,256]{1,0:T(8,128)S(1)}, bf16[1280,144]{1,0:T(8,128)(2,1)S(1)}, f32[8,1280]{1,0:T(8,128)S(1)}) custom-call(bf16[1280,768]{1,0:T(8,128)(2,1)S(1)} %convolution_convert_fusion.4.q_ref.k_ref.v_ref, bf16[1280,768]{1,0:T(8,128)(2,1)S(1)} %convolution_convert_fusion.4.q_ref.k_ref.v_ref, ...), custom_call_target="tpu_custom_call" | custom-call | flops 3355443200 | bytes 3276800 | tf_op jit(solution)/shard_map/pallas_call | solution.py:86
  151.6 4.3 collective-permute-done.20
  156.0 6.9 %collective-permute-done.19 = bf16[160,1152]{1,0:T(8,128)(2,1)} collective-permute-done((bf16[160,1152]{1,0:T(8,128)(2,1)}, bf16[160,1152]{1,0:T(8,128)(2,1)}, u32[]{:S(2)}, u32[]{:S(2)}) %collective-permute-start.19) | collective-permute-done | bytes 368672 | tf_op jit(solution)/shard_map/ppermute | solution.py:264
  182.8 5.0 %collective-permute-done.23 = bf16[160,1152]{1,0:T(8,128)(2,1)S(1)} collective-permute-done((bf16[160,1152]{1,0:T(8,128)(2,1)S(1)}, bf16[160,1152]{1,0:T(8,128)(2,1)S(1)}, u32[]{:S(2)}, u32[]{:S(2)}) %collective-permute-start.23) | collective-permute-done | bytes 368672 | tf_op jit(solution)/shard_map/ppermute | solution.py:264
  187.8 6.5 %collective-permute-done.22 = bf16[160,1152]{1,0:T(8,128)(2,1)S(1)} collective-permute-done((bf16[160,1152]{1,0:T(8,128)(2,1)S(1)}, bf16[160,1152]{1,0:T(8,128)(2,1)S(1)}, u32[]{:S(2)}, u32[]{:S(2)}) %collective-permute-start.22) | collective-permute-done | bytes 368672 | tf_op jit(solution)/shard_map/ppermute | solution.py:264
  194.8 5.3 %shard_map.289 = (bf16[640,1152]{1,0:T(8,128)(2,1)S(1)}, f32[640,1152]{1,0:T(8,128)S(1)}) custom-call(bf16[640,1152]{1,0:T(8,128)(2,1)S(1)} %pad_maximum_fusion.1.x_ref, bf16[1152,1152]{1,0:T(8,128)(2,1)S(1)} %convolution_convert_fusion.3.w_ref, f32[1,1152]{1,0:T(1,128)S(1)} %reshape_reshape.9.bias_ref), custom_call_target="tpu_custom_call" | custom-call | flops 1698693120 | bytes 8552448 | tf_op jit(solution)/shard_map/pallas_call | solution.py:216
  222.0 5.6 %fusion.46 = (f32[1152]{0:T(1024)S(1)}, bf16[640,1152]{1,0:T(8,128)(2,1)S(1)}) fusion(f32[640,1152]{1,0:T(8,128)} %copy-done, bf16[640,1152]{1,0:T(8,128)(2,1)} %pad_maximum_fusion, bf16[1152,1152]{1,0:T(8,128)(2,1)} %all-gather.12.cloned.1.call-done), kind=kOutput, calls=%fused_computation.187 | convolution fusion | flops 1700903808 | bytes 8557056 | tf_op jit(solution)/shard_map/dot_general | solution.py:54
  236.0 8.9 %convolution_convert_fusion.1 = bf16[1152,1152]{1,0:T(8,128)(2,1)} fusion(bf16[640,1152]{1,0:T(8,128)(2,1)} %copy-done.58, bf16[640,1152]{1,0:T(8,128)(2,1)S(1)} %pad_maximum_fusion.1.x_ref, bf16[1152,1152]{1,0:T(8,128)(2,1)} %fusion.10), kind=kOutput, calls=%fused_computation.9 | convolution fusion | flops 3399450624 | bytes 8257536 | tf_op jit(solution)/shard_map/dot_general | solution.py:50
  245.2 6.7 %collective-permute-done.28 = bf16[160,1152]{1,0:T(8,128)(2,1)} collective-permute-done((bf16[160,1152]{1,0:T(8,128)(2,1)}, bf16[160,1152]{1,0:T(8,128)(2,1)}, u32[]{:S(2)}, u32[]{:S(2)}) %collective-permute-start.28) | collective-permute-done | bytes 368672 | tf_op jit(solution)/shard_map/ppermute | solution.py:264
  275.0 5.7 %fusion.54 = f32[640,1152]{1,0:T(8,128)} fusion(bf16[640,1152]{1,0:T(8,128)(2,1)S(1)} %copy-done.4, bf16[1152,1152]{1,0:T(8,128)(2,1)} %all-gather.12.cloned.1.call-done), kind=kOutput, calls=%fused_computation.195 | convolution fusion | flops 1698693120 | bytes 7077888 | tf_op jit(solution)/shard_map/dot_general | solution.py:46
  284.1 17.2 %all-to-all-done.3 = bf16[8,160,144]{1,2,0:T(8,128)(2,1)} async-done(((bf16[8,160,144]{1,2,0:T(8,128)(2,1)}), bf16[8,160,144]{1,2,0:T(8,128)(2,1)}, u32[]{:S(2)}, u32[]{:S(2)}) %all-to-all-start.3) | async-done | bytes 368672 | tf_op jit(solution)/shard_map/all_to_all | solution.py:292
  302.8 14.0 %shard_map.290 = (bf16[1280,256]{1,0:T(8,128)(2,1)S(1)}, bf16[1280,256]{1,0:T(8,128)(2,1)S(1)}, bf16[1280,256]{1,0:T(8,128)(2,1)S(1)}) custom-call(bf16[1280,768]{1,0:T(8,128)(2,1)} %copy-done.5, bf16[1280,768]{1,0:T(8,128)(2,1)} %copy-done.5, bf16[1280,768]{1,0:T(8,128)(2,1)} %copy-done.5, bf16[1280,256]{1,0:T(8,128)(2,1)S(1)} %pad.18.out_grad_ref, ...), custom_call_target="tpu_custom_call" | custom-call | flops 8388608000 | bytes 4587520 | tf_op jit(solution)/shard_map/pallas_call | solution.py:163
  325.5 5.0 %fusion.55 = f32[1152,768]{0,1:T(8,128)S(1)} fusion(bf16[1280,1152]{1,0:T(8,128)(2,1)} %all-gather.8.cloned.1.call-done, bf16[1280,768]{1,0:T(8,128)(2,1)S(1)} %constant_dynamic-update-slice_fusion.8), kind=kOutput, calls=%fused_computation.196 | convolution fusion | flops 2264924160 | bytes 8454144 | tf_op jit(solution)/shard_map/dot_general | solution.py:50
  385.0 5.1 %collective-permute-done.41 = bf16[160,1152]{1,0:T(8,128)(2,1)} collective-permute-done((bf16[160,1152]{1,0:T(8,128)(2,1)}, bf16[160,1152]{1,0:T(8,128)(2,1)}, u32[]{:S(2)}, u32[]{:S(2)}) %collective-permute-start.41) | collective-permute-done | bytes 368672 | tf_op jit(solution)/shard_map/ppermute | solution.py:264
  405.1 4.7 all-to-all-done.6
  415.0 7.3 %collective-permute-done.44 = bf16[160,1152]{1,0:T(8,128)(2,1)S(1)} collective-permute-done((bf16[160,1152]{1,0:T(8,128)(2,1)S(1)}, bf16[160,1152]{1,0:T(8,128)(2,1)S(1)}, u32[]{:S(2)}, u32[]{:S(2)}) %collective-permute-start.44) | collective-permute-done | bytes 368672 | tf_op jit(solution)/shard_map/ppermute | solution.py:264
  443.5 5.5 %collective-permute-done.47 = bf16[160,576]{0,1:T(8,128)(2,1)} collective-permute-done((bf16[160,576]{0,1:T(8,128)(2,1)}, bf16[160,576]{0,1:T(8,128)(2,1)}, u32[]{:S(2)}, u32[]{:S(2)}) %collective-permute-start.47) | collective-permute-done | bytes 184352 | tf_op jit(solution)/shard_map/ppermute | solution.py:264
  452.9 7.6 %reduce-scatter.13.cloned.1.call-done = bf16[72,1152]{1,0:T(8,128)(2,1)} async-done(((bf16[576,1152]{1,0:T(8,128)(2,1)}), bf16[72,1152]{1,0:T(8,128)(2,1)}) %reduce-scatter.13.cloned.1.call-update) | async-done | bytes 165904
  (401 shorter events, 271.1 us)
Async XLA Ops:
  7.3 30.0 %all-gather.6.cloned.1.call-start = ((), (), s32[]{:S(2)}) async-start(), calls=%async_computation.11 | async-start | bytes 1492992 | tf_op jit(solution)/shard_map/all_gather | solution.py:305
  9.7 19.9 %collective-permute-start.2 = (bf16[160,576]{1,0:T(8,128)(2,1)S(1)}, bf16[160,576]{1,0:T(8,128)(2,1)S(1)}, u32[]{:S(2)}, u32[]{:S(2)}) collective-permute-start(bf16[160,576]{1,0:T(8,128)(2,1)S(1)} %get-tuple-element.181), channel_id=1, source_target_pairs={{0,24},{8,16},{16,8},{24,0},{1,25},{9,17},{17,9},{25,1},{2,26},{10... | collective-permute-start | bytes 552968 | tf_op jit(solution)/shard_map/ppermute | solution.py:264
  50.4 73.4 %all-gather.8.cloned.1.call-start = ((), (), s32[]{:S(2)}) async-start(), calls=%async_computation.12 | async-start | bytes 3317760 | tf_op jit(solution)/shard_map/all_gather | solution.py:349
  64.0 106.4 %all-gather.10.cloned.1.call-start = ((), (), s32[]{:S(2)}) async-start(), calls=%async_computation.13 | async-start | bytes 2985984 | tf_op jit(solution)/shard_map/all_gather | solution.py:374
  73.4 25.0 %collective-permute-start.11 = (bf16[288,432]{1,0:T(8,128)(2,1)S(1)}, bf16[288,432]{1,0:T(8,128)(2,1)S(1)}, u32[]{:S(2)}, u32[]{:S(2)}) collective-permute-start(bf16[288,432]{1,0:T(8,128)(2,1)S(1)} %reshape.329), channel_id=1, source_target_pairs={{0,24},{8,16},{16,8},{24,0},{1,25},{9,17},{17,9},{25,1},{2,26},{10... | collective-permute-start | bytes 746504 | tf_op jit(solution)/shard_map/ppermute | solution.py:264
  74.8 27.6 %collective-permute-start.10 = (bf16[288,432]{1,0:T(8,128)(2,1)S(1)}, bf16[288,432]{1,0:T(8,128)(2,1)S(1)}, u32[]{:S(2)}, u32[]{:S(2)}) collective-permute-start(bf16[288,432]{1,0:T(8,128)(2,1)S(1)} %reshape.329), channel_id=1, source_target_pairs={{0,16},{8,24},{16,0},{24,8},{1,17},{9,25},{17,1},{25,9},{2,18},{10... | collective-permute-start | bytes 746504 | tf_op jit(solution)/shard_map/ppermute | solution.py:264
  76.0 26.4 %collective-permute-start.9 = (bf16[288,432]{1,0:T(8,128)(2,1)S(1)}, bf16[288,432]{1,0:T(8,128)(2,1)S(1)}, u32[]{:S(2)}, u32[]{:S(2)}) collective-permute-start(bf16[288,432]{1,0:T(8,128)(2,1)S(1)} %reshape.329), channel_id=1, source_target_pairs={{0,8},{8,0},{16,24},{24,16},{1,9},{9,1},{17,25},{25,17},{2,10},{10... | collective-permute-start | bytes 746504 | tf_op jit(solution)/shard_map/ppermute | solution.py:264
  144.6 18.3 %collective-permute-start.19 = (bf16[160,1152]{1,0:T(8,128)(2,1)}, bf16[160,1152]{1,0:T(8,128)(2,1)}, u32[]{:S(2)}, u32[]{:S(2)}) collective-permute-start(bf16[160,1152]{1,0:T(8,128)(2,1)} %bitcast.27), channel_id=1, source_target_pairs={{0,16},{8,24},{16,0},{24,8},{1,17},{9,25},{17,1},{25,9},{2,18},{10... | collective-permute-start | bytes 1105928 | tf_op jit(solution)/shard_map/ppermute | solution.py:264
  145.3 17.6 %collective-permute-start.18 = (bf16[160,1152]{1,0:T(8,128)(2,1)}, bf16[160,1152]{1,0:T(8,128)(2,1)}, u32[]{:S(2)}, u32[]{:S(2)}) collective-permute-start(bf16[160,1152]{1,0:T(8,128)(2,1)} %bitcast.27), channel_id=1, source_target_pairs={{0,8},{8,0},{16,24},{24,16},{1,9},{9,1},{17,25},{25,17},{2,10},{10... | collective-permute-start | bytes 1105928 | tf_op jit(solution)/shard_map/ppermute | solution.py:264
  147.9 20.4 %all-to-all-start.2 = ((bf16[8,160,144]{1,2,0:T(8,128)(2,1)}), bf16[8,160,144]{1,2,0:T(8,128)(2,1)S(1)}, u32[]{:S(2)}, u32[]{:S(2)}) async-start(bf16[8,160,144]{1,2,0:T(8,128)(2,1)} %copy.108), calls=%async_computation.2 | async-start | bytes 1179648 | tf_op jit(solution)/shard_map/all_to_all | solution.py:292
  151.6 70.4 %all-gather.12.cloned.1.call-start = ((), (), s32[]{:S(2)}) async-start(), calls=%async_computation.14 | async-start | bytes 2985984 | tf_op jit(solution)/shard_map/all_gather | solution.py:392
  170.4 91.4 %reduce-scatter.7.cloned.1.call-start = ((), (), s32[]{:S(2)}) async-start(), calls=%async_computation.15 | async-start | bytes 2985984 | tf_op jit(solution)/shard_map/reduce_scatter | solution.py:410
  206.9 115.5 %reduce-scatter.9.cloned.1.call-start = ((), (), s32[]{:S(2)}) async-start(), calls=%async_computation.16 | async-start | bytes 2985984 | tf_op jit(solution)/shard_map/reduce_scatter | solution.py:428
  234.0 17.9 %collective-permute-start.28 = (bf16[160,1152]{1,0:T(8,128)(2,1)}, bf16[160,1152]{1,0:T(8,128)(2,1)}, u32[]{:S(2)}, u32[]{:S(2)}) collective-permute-start(bf16[160,1152]{1,0:T(8,128)(2,1)} %get-tuple-element.165), channel_id=1, source_target_pairs={{0,16},{8,24},{16,0},{24,8},{1,17},{9,25},{17,1},{25,9},{2,18},{10... | collective-permute-start | bytes 1105928 | tf_op jit(solution)/shard_map/ppermute | solution.py:264
  261.9 18.8 %collective-permute-start.32 = (bf16[160,1152]{1,0:T(8,128)(2,1)}, bf16[160,1152]{1,0:T(8,128)(2,1)}, u32[]{:S(2)}, u32[]{:S(2)}) collective-permute-start(bf16[160,1152]{1,0:T(8,128)(2,1)} %copy-done.16), channel_id=1, source_target_pairs={{0,24},{8,16},{16,8},{24,0},{1,25},{9,17},{17,9},{25,1},{2,26},{10... | collective-permute-start | bytes 1105928 | tf_op jit(solution)/shard_map/ppermute | solution.py:264
  263.4 17.8 %collective-permute-start.31 = (bf16[160,1152]{1,0:T(8,128)(2,1)}, bf16[160,1152]{1,0:T(8,128)(2,1)}, u32[]{:S(2)}, u32[]{:S(2)}) collective-permute-start(bf16[160,1152]{1,0:T(8,128)(2,1)} %copy-done.16), channel_id=1, source_target_pairs={{0,16},{8,24},{16,0},{24,8},{1,17},{9,25},{17,1},{25,9},{2,18},{10... | collective-permute-start | bytes 1105928 | tf_op jit(solution)/shard_map/ppermute | solution.py:264
  270.7 30.5 %all-to-all-start.3 = ((bf16[8,160,144]{1,2,0:T(8,128)(2,1)}), bf16[8,160,144]{1,2,0:T(8,128)(2,1)}, u32[]{:S(2)}, u32[]{:S(2)}) async-start(bf16[8,160,144]{1,2,0:T(8,128)(2,1)} %copy.114), calls=%async_computation.4 | async-start | bytes 1179648 | tf_op jit(solution)/shard_map/all_to_all | solution.py:292
  274.9 119.5 %reduce-scatter.11.cloned.1.call-start = ((), (), s32[]{:S(2)}) async-start(), calls=%async_computation.17 | async-start | bytes 3317760 | tf_op jit(solution)/shard_map/reduce_scatter | solution.py:440
  344.2 31.2 %collective-permute-start.35 = (bf16[288,432]{1,0:T(8,128)(2,1)}, bf16[288,432]{1,0:T(8,128)(2,1)}, u32[]{:S(2)}, u32[]{:S(2)}) collective-permute-start(bf16[288,432]{1,0:T(8,128)(2,1)} %bitcast.213), channel_id=1, source_target_pairs={{0,24},{8,16},{16,8},{24,0},{1,25},{9,17},{17,9},{25,1},{2,26},{10... | collective-permute-start | bytes 746504 | tf_op jit(solution)/shard_map/ppermute | solution.py:264
  348.4 27.5 %collective-permute-start.34 = (bf16[288,432]{1,0:T(8,128)(2,1)}, bf16[288,432]{1,0:T(8,128)(2,1)}, u32[]{:S(2)}, u32[]{:S(2)}) collective-permute-start(bf16[288,432]{1,0:T(8,128)(2,1)} %bitcast.212), channel_id=1, source_target_pairs={{0,16},{8,24},{16,0},{24,8},{1,17},{9,25},{17,1},{25,9},{2,18},{10... | collective-permute-start | bytes 746504 | tf_op jit(solution)/shard_map/ppermute | solution.py:264
  352.7 24.3 %collective-permute-start.33 = (bf16[288,432]{1,0:T(8,128)(2,1)}, bf16[288,432]{1,0:T(8,128)(2,1)}, u32[]{:S(2)}, u32[]{:S(2)}) collective-permute-start(bf16[288,432]{1,0:T(8,128)(2,1)} %bitcast.211), channel_id=1, source_target_pairs={{0,8},{8,0},{16,24},{24,16},{1,9},{9,1},{17,25},{25,17},{2,10},{10... | collective-permute-start | bytes 746504 | tf_op jit(solution)/shard_map/ppermute | solution.py:264
  404.2 18.1 %collective-permute-start.44 = (bf16[160,1152]{1,0:T(8,128)(2,1)S(1)}, bf16[160,1152]{1,0:T(8,128)(2,1)S(1)}, u32[]{:S(2)}, u32[]{:S(2)}) collective-permute-start(bf16[160,1152]{1,0:T(8,128)(2,1)S(1)} %get-tuple-element.153), channel_id=1, source_target_pairs={{0,16},{8,24},{16,0},{24,8},{1,17},{9,25},{17,1},{25,9},{2,18},{10... | collective-permute-start | bytes 1105928 | tf_op jit(solution)/shard_map/ppermute | solution.py:264
  404.8 18.3 %collective-permute-start.43 = (bf16[160,1152]{1,0:T(8,128)(2,1)S(1)}, bf16[160,1152]{1,0:T(8,128)(2,1)}, u32[]{:S(2)}, u32[]{:S(2)}) collective-permute-start(bf16[160,1152]{1,0:T(8,128)(2,1)S(1)} %get-tuple-element.153), channel_id=1, source_target_pairs={{0,8},{8,0},{16,24},{24,16},{1,9},{9,1},{17,25},{25,17},{2,10},{10... | collective-permute-start | bytes 1105928 | tf_op jit(solution)/shard_map/ppermute | solution.py:264
  413.2 47.4 %reduce-scatter.13.cloned.1.call-start = ((), (), s32[]{:S(2)}) async-start(), calls=%async_computation.18 | async-start | bytes 1492992
  (99 other events, 1111.5 us)
Sparse Core Ops, SparseCore 0:
  9.7 27.4 all-gather.5
  64.1 41.2 all-gather.7
  124.0 32.9 all-gather.9
  170.6 33.0 all-gather.11
  207.0 36.1 reduce-scatter.6
  262.0 44.0 reduce-scatter.8
  322.5 36.9 reduce-scatter.10
  427.0 33.5 reduce-scatter.12

commit v8 on v7

--- a/solution.py
+++ b/solution.py
@@ -52,6 +52,10 @@
 
 def times_transposed(left, right):
     return lax.dot_general(left, right, (((1,), (1,)), ((), ())), preferred_element_type=F32)
+
+
+def side_by_side(parts):
+    return jnp.concatenate([part[:, :HEAD_DIM] for part in parts], axis=1)
 
 
 def attend_kernel(heads, scale, q_ref, k_ref, v_ref, seg_q_ref, seg_k_ref, out_ref, low_ref, lse_ref):
@@ -70,13 +74,7 @@
         out_ref[:, at] = outs[h]
         logs = jnp.where(lane == h, top + jnp.log(total), logs)
     lse_ref[...] = jnp.transpose(logs)[:8]
-    if heads == 1:
-        low_ref[...] = outs[0][:, :HEAD_DIM].astype(BF16)
-    else:
-        second = pltpu.roll(outs[1], HEAD_DIM, 1)
-        rest = heads * HEAD_DIM - WIDE
-        low_ref[:, :WIDE] = jnp.where(lane < HEAD_DIM, outs[0], second).astype(BF16)
-        low_ref[:, WIDE:] = second[:, :rest].astype(BF16)
+    low_ref[...] = side_by_side(outs).astype(BF16)
 
 
 def attend(triple, segments, heads, scale):
@@ -114,7 +112,7 @@
 
 def attend_back_kernel(
     heads, scale, q_ref, k_ref, v_ref, out_grad_ref, out_ref, lse_ref, seg_q_ref, seg_k_ref,
-    dq_ref, dk_ref, dv_ref, sum_ref, grad_ref, delta_ref,
+    dq_ref, dkv_ref, sum_ref, grad_ref, delta_ref,
 ):
     step = pl.program_id(0)
 
@@ -136,6 +134,7 @@
             delta_ref[h : h + 1, :] = delta[:1]
 
     allowed = seg_k_ref[...] == seg_q_ref[...]
+    key_grads, value_grads = [], []
     for h in range(heads):
         at = slice(h * WIDE, (h + 1) * WIDE)
         queries, keys, out_grad = q_ref[:, at], k_ref[:, at], grad_ref[:, at]
@@ -143,13 +142,16 @@
         probs = jnp.where(allowed, jnp.exp(logits), 0.0)
         prob_grad = times_transposed(v_ref[:, at], out_grad)
         logit_grad = (probs * (prob_grad - delta_ref[h : h + 1, :]) * scale).astype(BF16)
-        dv_ref[:, at] = dot(probs.astype(BF16), out_grad).astype(BF16)
-        dk_ref[:, at] = dot(logit_grad, queries).astype(BF16)
+        value_grads.append(dot(probs.astype(BF16), out_grad))
+        key_grads.append(dot(logit_grad, queries))
         sum_ref[:, at] += inner(logit_grad, keys)
+    dkv_ref[...] = side_by_side(key_grads + value_grads).astype(BF16)
 
     @pl.when(step == pl.num_programs(0) - 1)
     def _():
-        dq_ref[...] = sum_ref[...].astype(BF16)
+        dq_ref[...] = side_by_side(
+            [sum_ref[:, h * WIDE : (h + 1) * WIDE] for h in range(heads)]
+        ).astype(BF16)
 
 
 def attend_back(triple, out_grad, out, lse, segments, heads, scale):
@@ -158,7 +160,6 @@
     step = 256 if rows % 256 == 0 else rows
     whole = pl.BlockSpec((rows, wide), lambda i: (0, 0))
     out_grad = jnp.pad(out_grad, ((0, 0), (0, wide - out_grad.shape[1])))
-    block = pl.BlockSpec((step, wide), lambda i: (i, 0))
     row = pl.BlockSpec((8, rows), lambda i: (0, 0))
     return pl.pallas_call(
         partial(attend_back_kernel, heads, scale),
@@ -173,8 +174,14 @@
             pl.BlockSpec((1, rows), lambda i: (0, 0)),
             pl.BlockSpec((step, 1), lambda i: (i, 0)),
         ],
-        out_specs=[whole, block, block],
-        out_shape=[jax.ShapeDtypeStruct((rows, wide), BF16)] * 3,
+        out_specs=[
+            pl.BlockSpec((rows, heads * HEAD_DIM), lambda i: (0, 0)),
+            pl.BlockSpec((step, 2 * heads * HEAD_DIM), lambda i: (i, 0)),
+        ],
+        out_shape=[
+            jax.ShapeDtypeStruct((rows, heads * HEAD_DIM), BF16),
+            jax.ShapeDtypeStruct((rows, 2 * heads * HEAD_DIM), BF16),
+        ],
         scratch_shapes=[
             pltpu.VMEM((rows, wide), F32),
             pltpu.VMEM((rows, wide), BF16),
@@ -190,6 +197,34 @@
         triple, triple, triple, out_grad, out, lse,
         segments.reshape(1, rows), segments.reshape(rows, 1),
     )
+
+
+def by_group_kernel(x_ref, w_ref, out_ref):
+    groups, rows, columns = out_ref.shape
+    product = times_transposed(x_ref[...], w_ref[...]).astype(BF16)
+    for g in range(groups):
+        out_ref[g] = product[:, g * columns : (g + 1) * columns]
+
+
+def product_by_group(x, w, groups):
+    rows, depth = x.shape
+    columns = w.shape[0] // groups
+    steps = 2
+    return pl.pallas_call(
+        by_group_kernel,
+        grid=(steps,),
+        in_specs=[
+            pl.BlockSpec((rows, depth), lambda j: (0, 0)),
+            pl.BlockSpec((w.shape[0] // steps, depth), lambda j: (j, 0)),
+        ],
+        out_specs=pl.BlockSpec((groups // steps, rows, columns), lambda j: (j, 0, 0)),
+        out_shape=jax.ShapeDtypeStruct((groups, rows, columns), BF16),
+        cost_estimate=pl.CostEstimate(
+            flops=2 * rows * depth * w.shape[0],
+            bytes_accessed=2 * depth * (rows + w.shape[0]) + 2 * rows * w.shape[0],
+            transcendentals=0,
+        ),
+    )(x, w)
 
 
 def gelu_kernel(rows_at_once, x_ref, w_ref, bias_ref, value_ref, slope_ref):
@@ -284,10 +319,6 @@
         v = v.reshape(v.shape[0], v.shape[1] // HEAD_DIM, HEAD_DIM)
         return jnp.pad(v, ((0, 0), (0, 0), (0, WIDE - HEAD_DIM))).reshape(v.shape[0], -1)
 
-    def narrow(v):
-        v = v.reshape(v.shape[0], v.shape[1] // WIDE, WIDE)
-        return v[:, :, :HEAD_DIM].reshape(v.shape[0], -1)
-
     def seq_exchange(v):
         return lax.all_to_all(v, "seq", 0, 0, tiled=True)
 
@@ -330,9 +361,8 @@
     row = ((block % nd) ^ dp_at) * part + (block // nd) * small + row
     order = (row == lax.broadcasted_iota(jnp.int32, (features, features), 1)).astype(BF16)
     qkv_out = qkv_w.reshape(small, 3, ns, head_cols).transpose(2, 0, 1, 3).reshape(ns, small, wide)
-    qkv_out, skip_part, joined_here, vectors, order = after(
-        (qkv_out, skip_part, joined_here, vectors, order)
-    )
+    segments = segment_of(item_lengths, jnp.arange(row_len, dtype=jnp.int32))
+    own_proj, skip_part, joined_here, vectors = after((proj_w, skip_part, joined_here, vectors))
     def vector(at):
         return vectors[:, at * small : (at + 1) * small].reshape(features)
 
@@ -342,16 +372,15 @@
 
     first_terms = dot(joined_here, skip_part)
     first = add_blocks(first_terms[:local], low_rows(first_terms)) + b_skip
-    qkv_mine = seq_exchange(qkv_out).reshape(part, wide)
+    proj_rows = lax.all_gather(own_proj, "seq", axis=0, tiled=True)
     xhat_one, inverse_one = norm_pieces(first)
     normed_one = (xhat_one * g_one + b_one).astype(BF16)
-    normed_one, qkv_mine, own_proj = after((normed_one, qkv_mine, proj_w))
+    normed_one, qkv_out, proj_rows = after((normed_one, qkv_out, proj_rows))
     normed_one_row = lax.all_gather(normed_one, "seq", axis=0, tiled=True)
 
+    qkv_mine = seq_exchange(qkv_out).reshape(part, wide)
     qkv_blocks = jnp.stack([qkv_mine] + [swap(qkv_mine, k) for k in range(1, nd)])
     qkv_mine = jnp.concatenate([index(qkv_blocks, dp_at ^ k) for k in range(nd)], axis=0)
-    qkv_mine = widen(qkv_mine)
-    proj_rows = lax.all_gather(own_proj, "seq", axis=0, tiled=True)
     up_slices = jnp.swapaxes(fc1_w.reshape(small, nd, hidden_part), 0, 1)
     up_slices = jnp.concatenate(
         [index(up_slices, dp_at)] + [swap(index(up_slices, dp_at ^ k), k) for k in range(1, nd)],
@@ -359,35 +388,31 @@
     )
     half = part // 2
     own_half = lax.dynamic_slice_in_dim(proj_rows, core * half, half, 0)
+    proj_halves = [swap(own_half, k) for k in range(1, nd)]
+    normed_one_row, up_slices, qkv_mine, qkv_wide, segments, proj_halves = after(
+        (normed_one_row, up_slices, qkv_mine, widen(qkv_mine), segments, proj_halves)
+    )
+    up_part = lax.all_gather(up_slices, "seq", axis=0, tiled=True)
+    triple = dot(normed_one_row, qkv_wide).astype(BF16)
+    attended, attended_low, lse = attend(triple, segments, heads, scale)
+
+    def heads_to_tokens(v):
+        v = seq_exchange(v.reshape(ns, local, head_cols))
+        return jnp.swapaxes(v, 0, 1).reshape(local, features)
+
     w_proj = lax.dynamic_update_slice_in_dim(
         jnp.zeros((features, features), BF16), proj_rows, dp_at * part, 0
     )
     for k in range(1, nd):
         place = (dp_at ^ k) * 2
-        here = swap(own_half, k)
+        here = proj_halves[k - 1]
         there = other_core(here)
         w_proj = lax.dynamic_update_slice_in_dim(w_proj, here, (place + core) * half, 0)
         w_proj = lax.dynamic_update_slice_in_dim(w_proj, there, (place + 1 - core) * half, 0)
-    normed_one_row, up_slices, qkv_mine, w_proj = after(
-        (normed_one_row, up_slices, qkv_mine, w_proj)
-    )
-    up_part = lax.all_gather(up_slices, "seq", axis=0, tiled=True)
-    triple = dot(normed_one_row, qkv_mine).astype(BF16)
-    segments = segment_of(item_lengths, jnp.arange(row_len, dtype=jnp.int32))
-    attended, attended_low, lse = attend(triple, segments, heads, scale)
-
-    def heads_to_tokens(v):
-        v = seq_exchange(v.reshape(ns, local, head_cols))
-        return jnp.swapaxes(v, 0, 1).reshape(local, features)
-
-    def tokens_to_heads(v):
-        v = seq_exchange(jnp.swapaxes(v.reshape(local, ns, head_cols), 0, 1))
-        return v.reshape(row_len, head_cols)
-
     attended_low, grad_out = after((attended_low, cotangent[0]))
     grad_out_rows = gather_rows(grad_out)
     attended_low = heads_to_tokens(attended_low)
-    attended_low, grad_out_rows = after((attended_low, grad_out_rows))
+    attended_low, grad_out_rows, w_proj = after((attended_low, grad_out_rows, w_proj))
     own_down, attended_low, up_part = after((fc2_w, attended_low, up_part))
     down_part = lax.all_gather(own_down, "seq", axis=0, tiled=True)
     second = first + dot(attended_low, w_proj) + b_proj
@@ -400,53 +425,56 @@
     hidden, slope = gelu_of_matmul(normed_two_rows, up_part, up_bias)
 
     fc2_terms = inner(hidden, grad_out_rows).astype(BF16)
-    slope, fc2_terms, attended_low = after((slope, fc2_terms, attended_low))
-    attended_slices = jnp.swapaxes(attended_low.reshape(local, nd, part), 0, 1)
-    attended_rows = jnp.concatenate(
-        [index(attended_slices, dp_at)]
-        + [swap(index(attended_slices, dp_at ^ k), k) for k in range(1, nd)],
-        axis=0,
-    )
+    slope, fc2_terms = after((slope, fc2_terms))
     fc2_w_grad = lax.psum_scatter(fc2_terms, "seq", scatter_dimension=0, tiled=True)
     pre_grad = times_transposed(grad_out_rows, down_part) * slope
     pre_low = pre_grad.astype(BF16)
     up_back = times_transposed(pre_low, up_part)
     up_low = low_rows(up_back)
-    up_low, pre_late, normed_two_rows, attended_rows = after(
-        (up_low, pre_low, normed_two_rows, attended_rows)
-    )
+    up_low, pre_late, normed_two_rows = after((up_low, pre_low, normed_two_rows))
     normed_two_grad = add_blocks(up_back[:local], up_low)
     fc1_terms = inner(times_transposed(normed_two_rows, order).astype(BF16), pre_late).astype(BF16)
-    normed_two_grad, fc1_terms = after((normed_two_grad, fc1_terms))
+    normed_two_grad, fc1_terms, fc2_w_grad = after((normed_two_grad, fc1_terms, fc2_w_grad))
+    fc1_terms = lax.psum_scatter(fc1_terms, "seq", scatter_dimension=0, tiled=True)
     through_two, ln2_g_grad, ln2_b_grad = norm_back(normed_two_grad, xhat_two, inverse_two, g_two)
     second_grad = grad_out.astype(F32) + through_two
     second_low = second_grad.astype(BF16)
-    attended_grad = times_transposed(second_low, w_proj).astype(BF16)
-    attended_grad, second_late, hidden_late, fc1_terms, fc2_w_grad = after(
-        (attended_grad, second_low, hidden, fc1_terms, fc2_w_grad)
-    )
-    fc1_terms = lax.psum_scatter(fc1_terms, "seq", scatter_dimension=0, tiled=True)
-    attended_grad = tokens_to_heads(attended_grad)
-    second_rows = gather_rows(second_late)
+    attended_grad = product_by_group(second_low, w_proj, ns)
+    attended_grad, second_late, hidden_late, attended_low = after(
+        (attended_grad, second_low, hidden, attended_low)
+    )
+    attended_grad = seq_exchange(attended_grad).reshape(row_len, head_cols)
     down_sums = dot(hidden_late, down_part)
-    attended_grad, down_sums, second_rows = after((attended_grad, down_sums, second_rows))
+    attended_slices = jnp.swapaxes(attended_low.reshape(local, nd, part), 0, 1)
+    attended_grad, down_sums, second_late, attended_slices = after(
+        (attended_grad, down_sums, second_late, attended_slices)
+    )
+    second_blocks = [second_late] + [swap(second_late, k) for k in range(1, nd)]
     triple_grad = jnp.concatenate(
         attend_back(triple, attended_grad, attended, lse, segments, heads, scale), axis=1
     )
     one_back = times_transposed(triple_grad, qkv_mine).astype(BF16)
-    one_back, triple_late, fc1_terms, down_sums = after(
-        (one_back, triple_grad, fc1_terms, down_sums)
+    one_back, triple_late, fc1_terms, down_sums, second_rows = after(
+        (one_back, triple_grad, fc1_terms, down_sums, jnp.concatenate(second_blocks, axis=0))
     )
     normed_one_grad = lax.psum_scatter(one_back, "seq", scatter_dimension=0, tiled=True)
-    qkv_terms = narrow(inner(normed_one_row, triple_late)).reshape(nd, part, wide)
+    qkv_terms = inner(normed_one_row, triple_late).reshape(nd, part, wide)
     qkv_low, down_low = qkv_terms.astype(BF16), low_rows(down_sums)
-    qkv_low, down_low, second_rows = after((qkv_low, down_low, second_rows))
+    qkv_low, down_low, second_rows, attended_slices = after(
+        (qkv_low, down_low, second_rows, attended_slices)
+    )
+    qkv_blocks = [swap(index(qkv_low, dp_at ^ k), k) for k in range(1, nd)]
+    attended_rows = jnp.concatenate(
+        [index(attended_slices, dp_at)]
+        + [swap(index(attended_slices, dp_at ^ k), k) for k in range(1, nd)],
+        axis=0,
+    )
     proj_terms = inner(attended_rows, second_rows).reshape(ns, small, features)
     proj_w_grad = chip_sums(core_sums(proj_terms))
     output = (second + add_blocks(down_sums[:local], down_low) + b_down).astype(BF16)
     qkv_sum = index(qkv_terms, dp_at)
-    for k in range(1, nd):
-        qkv_sum = qkv_sum + swap(index(qkv_low, dp_at ^ k), k).astype(F32)
+    for block in qkv_blocks:
+        qkv_sum = qkv_sum + block.astype(F32)
     qkv_sum = qkv_sum.astype(BF16).reshape(ns, small, wide)
     fc1_terms = fc1_terms.reshape(nd, small, hidden_part)
     fc1_blocks = jnp.stack([fc1_terms[0]] + [swap(fc1_terms[k], k) for k in range(1, nd)])

time: 477 us -> 443 us (0.929)
  local copies, waits for them, and re-layouts: 85.4 us -> 68 us
  waiting for transfers between devices: 132 us -> 119 us
  matrix products: 65.3 us -> 58.5 us
  starting transfers between devices: 83.3 us -> 88.5 us
    ppermute x45, waiting for transfers between devices: 86.7 us -> 54.8 us  [swap(): return lax.ppermute(v, 'dp', [(i, i ^ k) for i in range(nd)])]
    all_to_all x4, waiting for transfers between devices: 20 us -> 31.9 us  [seq_exchange(): return lax.all_to_all(v, 'seq', 0, 0, tiled=True)]
    dynamic_slice x16 -> x10, local copies, waits for them, and re-layouts: 15.1 us -> 4.49 us  [index(): return lax.dynamic_index_in_dim(v, at, axis, keepdims=False)]
    another operation x3 -> x2, local copies, waits for them, and re-layouts: 6.44 us -> 0.79 us
    dot_general x5 -> x4, matrix products: 19.6 us -> 16.2 us  [times_transposed(): lax.dot_general(left, right, (((1,), (1,)), ((), ())), preferred_element_...]
    unnamed x131 -> x120, local copies, waits for them, and re-layouts: 10.5 us -> 10.1 us
  transfers between devices with their start and end apart: 64 -> 64, of which waited for: 35 -> 26; matrix products, arithmetic and copies ran while one was open for 36% -> 32% of each run, Pallas kernels for 6% -> 7%
where the time goes in v8:
time: 443 us; the launch traced here: 437 us
  waiting for transfers between devices  119 us (27%)
  starting transfers between devices  88.5 us (20%)
  local copies, waits for them, and re-layouts  68 us (15%)
  matrix products  58.5 us (13%)
  other arithmetic  36.2 us (8%)
  Pallas kernels  31.5 us (7%)
  between operations  19.1 us (4%)
  blocking collectives  15.6 us (4%)
    ppermute x45, starting transfers between devices, swap(): return lax.ppermute(v, 'dp', [(i, i ^ k) for i in range(nd)])  56 us
    ppermute x45, waiting for transfers between devices, swap(): return lax.ppermute(v, 'dp', [(i, i ^ k) for i in range(nd)])  54.8 us
    all_to_all x4, waiting for transfers between devices, seq_exchange(): return lax.all_to_all(v, 'seq', 0, 0, tiled=True)  31.9 us
    dot_general x6, matrix products, inner(): lax.dot_general(left, right, (((0,), (0,)), ((), ())), preferred_element_...  25.2 us
    all_to_all x4, starting transfers between devices, seq_exchange(): return lax.all_to_all(v, 'seq', 0, 0, tiled=True)  17.8 us
    dot_general x4, matrix products, dot(): return jnp.dot(left, right, preferred_element_type=F32)  17 us
    dot_general x4, matrix products, times_transposed(): lax.dot_general(left, right, (((1,), (1,)), ((), ())), preferred_element_...  16.2 us
    all_gather x1, blocking collectives, on_device(): proj_rows = lax.all_gather(own_proj, 'seq', axis=0, tiled=True)  15.6 us
  transfers between devices with their start and end apart: 64, of which 26 were waited for; matrix products, arithmetic and copies ran while one was open for 32% of the time, Pallas kernels for 7%

profile of v8, /device:TPU:0, one launch (start us, length us, event | category | flops | bytes accessed | tf_op | source)
XLA Modules:
  0.0 436.7 jit_solution(8415546091163287214)
XLA Ops:
  15.1 6.3 %all-to-all-start = ((bf16[32,8,128]{2,1,0:T(8,128)(2,1)}), bf16[32,8,128]{2,1,0:T(8,128)(2,1)S(1)}, u32[]{:S(2)}, u32[]{:S(2)}) async-start(bf16[32,8,128]{2,1,0:T(8,128)(2,1)} %broadcast_in_dim.15), calls=%async_computation | async-start | bytes 131072 | tf_op jit(solution)/shard_map/all_to_all | solution.py:344
  22.6 6.9 %all-to-all-done = bf16[32,8,128]{2,1,0:T(8,128)(2,1)S(1)} async-done(((bf16[32,8,128]{2,1,0:T(8,128)(2,1)}), bf16[32,8,128]{2,1,0:T(8,128)(2,1)S(1)}, u32[]{:S(2)}, u32[]{:S(2)}) %all-to-all-start) | async-done | bytes 65568 | tf_op jit(solution)/shard_map/all_to_all | solution.py:344
  29.7 7.5 %all-gather.6.cloned.1.call-done = bf16[576,1152]{1,0:T(8,128)(2,1)} async-done(((bf16[72,1152]{1,0:T(8,128)(2,1)}), bf16[576,1152]{1,0:T(8,128)(2,1)}) %all-gather.6.cloned.1.call-update) | async-done | bytes 1327120 | tf_op jit(solution)/shard_map/all_gather | solution.py:336
  37.2 4.3 fusion.57
  47.0 15.6 %all-gather = bf16[8,36,1152]{2,1,0:T(8,128)(2,1)S(1)} all-gather(bf16[1,36,1152]{2,1,0:T(8,128)(2,1)S(1)} %bitcast.212), channel_id=1, replica_groups=mesh['dp'=4,'seq'=8] {'seq'}, dimensions={0}, use_global_device_ids=true | all-gather | bytes 746496 | tf_op jit(solution)/shard_map/all_gather | solution.py:375
  80.6 8.1 %all-to-all-done.1 = bf16[8,36,432]{2,1,0:T(8,128)(2,1)S(1)} async-done(((bf16[8,36,432]{2,1,0:T(8,128)(2,1)}), bf16[8,36,432]{2,1,0:T(8,128)(2,1)S(1)}, u32[]{:S(2)}, u32[]{:S(2)}) %all-to-all-start.1) | async-done | bytes 248864 | tf_op jit(solution)/shard_map/all_to_all | solution.py:323
  102.0 4.6 %collective-permute-done.10 = bf16[288,432]{1,0:T(8,128)(2,1)S(1)} collective-permute-done((bf16[288,432]{1,0:T(8,128)(2,1)}, bf16[288,432]{1,0:T(8,128)(2,1)S(1)}, u32[]{:S(2)}, u32[]{:S(2)}) %collective-permute-start.10) | collective-permute-done | bytes 248864 | tf_op jit(solution)/shard_map/ppermute | solution.py:299
  125.5 8.4 %shard_map.288 = (f32[1280,256]{1,0:T(8,128)S(1)}, bf16[1280,144]{1,0:T(8,128)(2,1)S(1)}, f32[8,1280]{1,0:T(8,128)S(1)}) custom-call(bf16[1280,768]{1,0:T(8,128)(2,1)S(1)} %convolution_convert_fusion.4.q_ref.k_ref.v_ref, bf16[1280,768]{1,0:T(8,128)(2,1)S(1)} %convolution_convert_fusion.4.q_ref.k_ref.v_ref, ...), custom_call_target="tpu_custom_call" | custom-call | flops 3355443200 | bytes 3276800 | tf_op jit(solution)/shard_map/pallas_call | solution.py:84
  138.6 6.1 %all-to-all-start.2 = ((bf16[8,160,144]{1,2,0:T(8,128)(2,1)}), bf16[8,160,144]{1,2,0:T(8,128)(2,1)S(1)}, u32[]{:S(2)}, u32[]{:S(2)}) async-start(bf16[8,160,144]{1,2,0:T(8,128)(2,1)} %copy.75), calls=%async_computation.2 | async-start | bytes 1179648 | tf_op jit(solution)/shard_map/all_to_all | solution.py:323
  157.3 7.8 %all-to-all-done.2 = bf16[8,160,144]{1,2,0:T(8,128)(2,1)S(1)} async-done(((bf16[8,160,144]{1,2,0:T(8,128)(2,1)}), bf16[8,160,144]{1,2,0:T(8,128)(2,1)S(1)}, u32[]{:S(2)}, u32[]{:S(2)}) %all-to-all-start.2) | async-done | bytes 368672 | tf_op jit(solution)/shard_map/all_to_all | solution.py:323
  179.5 4.6 %convolution_convert_fusion.3.w_ref = bf16[1152,1152]{1,0:T(8,128)(2,1)S(1)} fusion(bf16[1152,1152]{1,0:T(8,128)(2,1)S(1)} %copy-done.55, s32[1152]{0:T(1024)S(1)} %get-tuple-element.248, s32[1152]{0:T(1024)S(1)} %get-tuple-element.249, s32[]{:T(128)S(6)} %axis_index.23, s32[1152]{0:T(1024)S(1)} %get-tuple-element.247, s32[1152]{0:T(1024)S(1)} %get-tuple-element.250, ...), kind=kOutput, calls=%fused_computation.11 | convolution fusion | flops 3094806528 | bytes 5329156 | tf_op jit(solution)/shard_map/dot_general | solution.py:50
  187.5 8.2 %collective-permute-done.22 = bf16[160,1152]{1,0:T(8,128)(2,1)S(1)} collective-permute-done((bf16[160,1152]{1,0:T(8,128)(2,1)S(1)}, bf16[160,1152]{1,0:T(8,128)(2,1)S(1)}, u32[]{:S(2)}, u32[]{:S(2)}) %collective-permute-start.22) | collective-permute-done | bytes 368672 | tf_op jit(solution)/shard_map/ppermute | solution.py:299
  195.8 5.3 %shard_map.289 = (bf16[640,1152]{1,0:T(8,128)(2,1)S(1)}, f32[640,1152]{1,0:T(8,128)S(1)}) custom-call(bf16[640,1152]{1,0:T(8,128)(2,1)S(1)} %pad_maximum_fusion.1.x_ref, bf16[1152,1152]{1,0:T(8,128)(2,1)S(1)} %convolution_convert_fusion.3.w_ref, f32[1,1152]{1,0:T(1,128)S(1)} %reshape_reshape.6.bias_ref), custom_call_target="tpu_custom_call" | custom-call | flops 1698693120 | bytes 8552448 | tf_op jit(solution)/shard_map/pallas_call | solution.py:251
  208.1 6.1 %fusion.52 = (f32[1152]{0:T(1024)}, bf16[640,1152]{1,0:T(8,128)(2,1)S(1)}) fusion(f32[640,1152]{1,0:T(8,128)} %copy-done, bf16[640,1152]{1,0:T(8,128)(2,1)} %pad_maximum_fusion, bf16[1152,1152]{1,0:T(8,128)(2,1)} %all-gather.12.cloned.1.call-done), kind=kOutput, calls=%fused_computation.180 | convolution fusion | flops 1700903808 | bytes 8557056 | tf_op jit(solution)/shard_map/dot_general | solution.py:54
  222.6 8.9 %convolution_convert_fusion.1 = bf16[1152,1152]{1,0:T(8,128)(2,1)} fusion(bf16[640,1152]{1,0:T(8,128)(2,1)} %copy-done.56, bf16[640,1152]{1,0:T(8,128)(2,1)S(1)} %pad_maximum_fusion.1.x_ref, bf16[1152,1152]{1,0:T(8,128)(2,1)} %fusion.45), kind=kOutput, calls=%fused_computation.9 | convolution fusion | flops 3399450624 | bytes 8257536 | tf_op jit(solution)/shard_map/dot_general | solution.py:50
  231.6 6.5 %collective-permute-done.25 = bf16[160,1152]{1,0:T(8,128)(2,1)} collective-permute-done((bf16[160,1152]{1,0:T(8,128)(2,1)}, bf16[160,1152]{1,0:T(8,128)(2,1)}, u32[]{:S(2)}, u32[]{:S(2)}) %collective-permute-start.25) | collective-permute-done | bytes 368672 | tf_op jit(solution)/shard_map/ppermute | solution.py:299
  261.5 5.7 %fusion.60 = f32[640,1152]{1,0:T(8,128)} fusion(bf16[640,1152]{1,0:T(8,128)(2,1)S(1)} %copy-done.4, bf16[1152,1152]{1,0:T(8,128)(2,1)} %all-gather.12.cloned.1.call-done), kind=kOutput, calls=%fused_computation.188 | convolution fusion | flops 1698693120 | bytes 7077888 | tf_op jit(solution)/shard_map/dot_general | solution.py:46
  267.2 15.8 %all-to-all-done.3 = bf16[8,160,144]{1,2,0:T(8,128)(2,1)} async-done(((bf16[8,160,144]{1,2,0:T(8,128)(2,1)}), bf16[8,160,144]{1,2,0:T(8,128)(2,1)}, u32[]{:S(2)}, u32[]{:S(2)}) %all-to-all-start.3) | async-done | bytes 368672 | tf_op jit(solution)/shard_map/all_to_all | solution.py:323
  288.1 14.3 %shard_map.291 = (bf16[1280,144]{1,0:T(8,128)(2,1)S(1)}, bf16[1280,288]{1,0:T(8,128)(2,1)S(1)}) custom-call(bf16[1280,768]{1,0:T(8,128)(2,1)} %copy-done.5, bf16[1280,768]{1,0:T(8,128)(2,1)} %copy-done.5, bf16[1280,768]{1,0:T(8,128)(2,1)} %copy-done.5, bf16[1280,256]{1,0:T(8,128)(2,1)S(1)} %pad.18.out_grad_ref, f32[1280,256]{1,0:T(8,128)S(1)} %get-tuple-element.122.out_ref, ...), custom_call_target="tpu_custom_call" | custom-call | flops 8388608000 | bytes 4587520 | tf_op jit(solution)/shard_map/pallas_call | solution.py:164
  352.5 5.8 %collective-permute-done.41 = bf16[160,1152]{1,0:T(8,128)(2,1)} collective-permute-done((bf16[160,1152]{1,0:T(8,128)(2,1)}, bf16[160,1152]{1,0:T(8,128)(2,1)}, u32[]{:S(2)}, u32[]{:S(2)}) %collective-permute-start.41) | collective-permute-done | bytes 368672 | tf_op jit(solution)/shard_map/ppermute | solution.py:299
  372.1 4.6 %all-to-all-done.6 = f32[32,8,128]{2,1,0:T(8,128)S(1)} async-done(((f32[32,8,128]{2,1,0:T(8,128)}), f32[32,8,128]{2,1,0:T(8,128)S(1)}, u32[]{:S(2)}, u32[]{:S(2)}) %all-to-all-start.6) | async-done | bytes 131104 | tf_op jit(solution)/shard_map/all_to_all | solution.py:508
  381.2 8.5 %collective-permute-done.44 = bf16[160,1152]{1,0:T(8,128)(2,1)S(1)} collective-permute-done((bf16[160,1152]{1,0:T(8,128)(2,1)S(1)}, bf16[160,1152]{1,0:T(8,128)(2,1)S(1)}, u32[]{:S(2)}, u32[]{:S(2)}) %collective-permute-start.44) | collective-permute-done | bytes 368672 | tf_op jit(solution)/shard_map/ppermute | solution.py:299
  410.7 4.6 %collective-permute-done.48 = bf16[160,576]{0,1:T(8,128)(2,1)} collective-permute-done((bf16[160,576]{0,1:T(8,128)(2,1)S(1)}, bf16[160,576]{0,1:T(8,128)(2,1)}, u32[]{:S(2)}, u32[]{:S(2)}) %collective-permute-start.48) | collective-permute-done | bytes 184352 | tf_op jit(solution)/shard_map/ppermute | solution.py:299
  419.1 8.6 %reduce-scatter.13.cloned.1.call-done = bf16[72,1152]{1,0:T(8,128)(2,1)} async-done(((bf16[576,1152]{1,0:T(8,128)(2,1)}), bf16[72,1152]{1,0:T(8,128)(2,1)}) %reduce-scatter.13.cloned.1.call-update) | async-done | bytes 165904
  (386 shorter events, 234.4 us)
Async XLA Ops:
  7.3 30.0 %all-gather.6.cloned.1.call-start = ((), (), s32[]{:S(2)}) async-start(), calls=%async_computation.11 | async-start | bytes 1492992 | tf_op jit(solution)/shard_map/all_gather | solution.py:336
  9.7 19.9 %collective-permute-start = (bf16[160,576]{1,0:T(8,128)(2,1)S(1)}, bf16[160,576]{1,0:T(8,128)(2,1)S(1)}, u32[]{:S(2)}, u32[]{:S(2)}) collective-permute-start(bf16[160,576]{1,0:T(8,128)(2,1)S(1)} %get-tuple-element.191), channel_id=1, source_target_pairs={{0,8},{8,0},{16,24},{24,16},{1,9},{9,1},{17,25},{25,17},{2,10},{10... | collective-permute-start | bytes 552968 | tf_op jit(solution)/shard_map/ppermute | solution.py:299
  21.4 96.9 %all-gather.8.cloned.1.call-start = ((), (), s32[]{:S(2)}) async-start(), calls=%async_computation.12 | async-start | bytes 3317760 | tf_op jit(solution)/shard_map/all_gather | solution.py:379
  42.5 20.2 %collective-permute-start.3 = (bf16[160,1152]{1,0:T(8,128)(2,1)}, bf16[160,1152]{1,0:T(8,128)(2,1)S(1)}, u32[]{:S(2)}, u32[]{:S(2)}) collective-permute-start(bf16[160,1152]{1,0:T(8,128)(2,1)} %get-tuple-element.174), channel_id=1, source_target_pairs={{0,8},{8,0},{16,24},{24,16},{1,9},{9,1},{17,25},{25,17},{2,10},{10... | collective-permute-start | bytes 1105928 | tf_op jit(solution)/shard_map/ppermute | solution.py:299
  67.3 21.4 %all-to-all-start.1 = ((bf16[8,36,432]{2,1,0:T(8,128)(2,1)}), bf16[8,36,432]{2,1,0:T(8,128)(2,1)S(1)}, u32[]{:S(2)}, u32[]{:S(2)}) async-start(bf16[8,36,432]{2,1,0:T(8,128)(2,1)} %copy.69), calls=%async_computation.1 | async-start | bytes 655360 | tf_op jit(solution)/shard_map/all_to_all | solution.py:323
  70.7 96.5 %all-gather.10.cloned.1.call-start = ((), (), s32[]{:S(2)}) async-start(), calls=%async_computation.13 | async-start | bytes 2985984 | tf_op jit(solution)/shard_map/all_gather | solution.py:395
  71.7 20.7 %collective-permute-start.6 = (bf16[36,1152]{1,0:T(8,128)(2,1)S(1)}, bf16[36,1152]{1,0:T(8,128)(2,1)S(1)}, u32[]{:S(2)}, u32[]{:S(2)}) collective-permute-start(bf16[36,1152]{1,0:T(8,128)(2,1)S(1)} %bitcast.214), channel_id=1, source_target_pairs={{0,8},{8,0},{16,24},{24,16},{1,9},{9,1},{17,25},{25,17},{2,10},{10... | collective-permute-start | bytes 248840 | tf_op jit(solution)/shard_map/ppermute | solution.py:299
  73.3 19.7 %collective-permute-start.7 = (bf16[36,1152]{1,0:T(8,128)(2,1)S(1)}, bf16[36,1152]{1,0:T(8,128)(2,1)S(1)}, u32[]{:S(2)}, u32[]{:S(2)}) collective-permute-start(bf16[36,1152]{1,0:T(8,128)(2,1)S(1)} %bitcast.213), channel_id=1, source_target_pairs={{0,16},{8,24},{16,0},{24,8},{1,17},{9,25},{17,1},{25,9},{2,18},{10... | collective-permute-start | bytes 248840 | tf_op jit(solution)/shard_map/ppermute | solution.py:299
  94.5 21.6 %collective-permute-start.12 = (bf16[144,1152]{1,0:T(8,128)(2,1)}, bf16[144,1152]{1,0:T(8,128)(2,1)}, u32[]{:S(2)}, u32[]{:S(2)}) collective-permute-start(bf16[144,1152]{1,0:T(8,128)(2,1)} %constant_dynamic-slice_fusion.5), channel_id=1, source_target_pairs={{0,8},{8,0},{16,24},{24,16},{1,9},{9,1},{17,25},{25,17},{2,10},{10... | collective-permute-start | bytes 995336 | tf_op jit(solution)/shard_map/ppermute | solution.py:299
  96.0 22.2 %collective-permute-start.13 = (bf16[144,1152]{1,0:T(8,128)(2,1)}, bf16[144,1152]{1,0:T(8,128)(2,1)}, u32[]{:S(2)}, u32[]{:S(2)}) collective-permute-start(bf16[144,1152]{1,0:T(8,128)(2,1)} %constant_dynamic-slice_fusion.5), channel_id=1, source_target_pairs={{0,16},{8,24},{16,0},{24,8},{1,17},{9,25},{17,1},{25,9},{2,18},{10... | collective-permute-start | bytes 995336 | tf_op jit(solution)/shard_map/ppermute | solution.py:299
  121.2 25.3 %collective-permute-start.18 = (bf16[144,1152]{1,0:T(8,128)(2,1)}, bf16[144,1152]{1,0:T(8,128)(2,1)}, u32[]{:S(2)}, u32[]{:S(2)}) collective-permute-start(bf16[144,1152]{1,0:T(8,128)(2,1)} %collective-permute-done.12), channel_id=1, source_target_pairs={{0,1},{1,0},{2,3},{3,2},{4,5},{5,4},{6,7},{7,6},{8,9},{9,8},{10,11... | collective-permute-start | bytes 995336 | tf_op jit(solution)/shard_map/ppermute | solution.py:302
  133.9 20.8 %collective-permute-start.15 = (bf16[160,1152]{1,0:T(8,128)(2,1)}, bf16[160,1152]{1,0:T(8,128)(2,1)}, u32[]{:S(2)}, u32[]{:S(2)}) collective-permute-start(bf16[160,1152]{1,0:T(8,128)(2,1)} %bitcast.30), channel_id=1, source_target_pairs={{0,8},{8,0},{16,24},{24,16},{1,9},{9,1},{17,25},{25,17},{2,10},{10... | collective-permute-start | bytes 1105928 | tf_op jit(solution)/shard_map/ppermute | solution.py:299
  135.2 19.5 %collective-permute-start.16 = (bf16[160,1152]{1,0:T(8,128)(2,1)}, bf16[160,1152]{1,0:T(8,128)(2,1)}, u32[]{:S(2)}, u32[]{:S(2)}) collective-permute-start(bf16[160,1152]{1,0:T(8,128)(2,1)} %bitcast.30), channel_id=1, source_target_pairs={{0,16},{8,24},{16,0},{24,8},{1,17},{9,25},{17,1},{25,9},{2,18},{10... | collective-permute-start | bytes 1105928 | tf_op jit(solution)/shard_map/ppermute | solution.py:299
  138.6 26.5 %all-to-all-start.2 = ((bf16[8,160,144]{1,2,0:T(8,128)(2,1)}), bf16[8,160,144]{1,2,0:T(8,128)(2,1)S(1)}, u32[]{:S(2)}, u32[]{:S(2)}) async-start(bf16[8,160,144]{1,2,0:T(8,128)(2,1)} %copy.75), calls=%async_computation.2 | async-start | bytes 1179648 | tf_op jit(solution)/shard_map/all_to_all | solution.py:323
  144.7 63.4 %all-gather.12.cloned.1.call-start = ((), (), s32[]{:S(2)}) async-start(), calls=%async_computation.14 | async-start | bytes 2985984 | tf_op jit(solution)/shard_map/all_gather | solution.py:417
  167.3 76.4 %reduce-scatter.7.cloned.1.call-start = ((), (), s32[]{:S(2)}) async-start(), calls=%async_computation.15 | async-start | bytes 2985984 | tf_op jit(solution)/shard_map/reduce_scatter | solution.py:429
  207.8 100.9 %reduce-scatter.9.cloned.1.call-start = ((), (), s32[]{:S(2)}) async-start(), calls=%async_computation.16 | async-start | bytes 2985984 | tf_op jit(solution)/shard_map/reduce_scatter | solution.py:438
  253.2 29.9 %all-to-all-start.3 = ((bf16[8,160,144]{1,2,0:T(8,128)(2,1)}), bf16[8,160,144]{1,2,0:T(8,128)(2,1)}, u32[]{:S(2)}, u32[]{:S(2)}) async-start(bf16[8,160,144]{1,2,0:T(8,128)(2,1)} %copy.77), calls=%async_computation.4 | async-start | bytes 1179648 | tf_op jit(solution)/shard_map/all_to_all | solution.py:323
  257.4 104.1 %reduce-scatter.11.cloned.1.call-start = ((), (), s32[]{:S(2)}) async-start(), calls=%async_computation.17 | async-start | bytes 3317760 | tf_op jit(solution)/shard_map/reduce_scatter | solution.py:460
  284.5 22.9 %collective-permute-start.27 = (bf16[160,1152]{1,0:T(8,128)(2,1)}, bf16[160,1152]{1,0:T(8,128)(2,1)}, u32[]{:S(2)}, u32[]{:S(2)}) collective-permute-start(bf16[160,1152]{1,0:T(8,128)(2,1)} %convert_element_type.196.x_ref), channel_id=1, source_target_pairs={{0,8},{8,0},{16,24},{24,16},{1,9},{9,1},{17,25},{25,17},{2,10},{10... | collective-permute-start | bytes 1105928 | tf_op jit(solution)/shard_map/ppermute | solution.py:299
  286.1 21.2 %collective-permute-start.28 = (bf16[160,1152]{1,0:T(8,128)(2,1)}, bf16[160,1152]{1,0:T(8,128)(2,1)}, u32[]{:S(2)}, u32[]{:S(2)}) collective-permute-start(bf16[160,1152]{1,0:T(8,128)(2,1)} %convert_element_type.196.x_ref), channel_id=1, source_target_pairs={{0,16},{8,24},{16,0},{24,8},{1,17},{9,25},{17,1},{25,9},{2,18},{10... | collective-permute-start | bytes 1105928 | tf_op jit(solution)/shard_map/ppermute | solution.py:299
  287.6 19.7 %collective-permute-start.29 = (bf16[160,1152]{1,0:T(8,128)(2,1)}, bf16[160,1152]{1,0:T(8,128)(2,1)}, u32[]{:S(2)}, u32[]{:S(2)}) collective-permute-start(bf16[160,1152]{1,0:T(8,128)(2,1)} %convert_element_type.196.x_ref), channel_id=1, source_target_pairs={{0,24},{8,16},{16,8},{24,0},{1,25},{9,17},{17,9},{25,1},{2,26},{10... | collective-permute-start | bytes 1105928 | tf_op jit(solution)/shard_map/ppermute | solution.py:299
  337.2 21.1 %collective-permute-start.41 = (bf16[160,1152]{1,0:T(8,128)(2,1)}, bf16[160,1152]{1,0:T(8,128)(2,1)}, u32[]{:S(2)}, u32[]{:S(2)}) collective-permute-start(bf16[160,1152]{1,0:T(8,128)(2,1)} %get-tuple-element.170), channel_id=1, source_target_pairs={{0,16},{8,24},{16,0},{24,8},{1,17},{9,25},{17,1},{25,9},{2,18},{10... | collective-permute-start | bytes 1105928 | tf_op jit(solution)/shard_map/ppermute | solution.py:299
  380.9 46.9 %reduce-scatter.13.cloned.1.call-start = ((), (), s32[]{:S(2)}) async-start(), calls=%async_computation.18 | async-start | bytes 1492992
  (97 other events, 1210.8 us)
Sparse Core Ops, SparseCore 0:
  9.7 27.4 all-gather.5
  65.5 41.5 all-gather.7
  118.4 38.8 all-gather.9
  167.4 32.9 all-gather.11
  208.0 35.6 reduce-scatter.6
  245.8 45.1 reduce-scatter.8
  308.9 38.8 reduce-scatter.10
  394.5 33.1 reduce-scatter.12

commit v9 on v8

--- a/solution.py
+++ b/solution.py
@@ -227,10 +227,14 @@
     )(x, w)
 
 
-def gelu_kernel(rows_at_once, x_ref, w_ref, bias_ref, value_ref, slope_ref):
+def feed_forward_kernel(
+    local, rows_at_once, x_ref, grad_ref, up_ref, down_ref, bias_ref,
+    hidden_ref, low_ref, sums_ref, back_ref, own_ref,
+):
+    sums = jnp.zeros(sums_ref.shape, F32)
     for start in range(0, x_ref.shape[0], rows_at_once):
         at = pl.ds(start, rows_at_once)
-        pre = dot(x_ref[at, :], w_ref[...]) + bias_ref[...]
+        pre = dot(x_ref[at, :], up_ref[...]) + bias_ref[...]
         bell = jnp.exp(-0.5 * pre * pre)
         t = 1.0 / (1.0 + (0.3275911 * 0.5**0.5) * jnp.abs(pre))
         tail = 0.5 * 1.061405429
@@ -238,36 +242,39 @@
             tail = tail * t + 0.5 * c
         tail = tail * t * bell
         below = jnp.where(pre < 0.0, tail, 1.0 - tail)
-        value_ref[at, :] = (pre * below).astype(BF16)
-        slope_ref[at, :] = below + pre * bell * (0.5 / math.pi) ** 0.5
-
-
-def gelu_of_matmul(x, w, bias):
+        hidden_ref[at, :] = (pre * below).astype(BF16)
+        slope = below + pre * bell * (0.5 / math.pi) ** 0.5
+        pre_grad = times_transposed(grad_ref[at, :], down_ref[...]) * slope
+        sums = sums + jnp.sum(pre_grad, axis=0, keepdims=True)
+        low = pre_grad.astype(BF16)
+        low_ref[at, :] = low
+        back = times_transposed(low, up_ref[...])
+        if start == 0:
+            own_ref[...] = back[:local]
+        back_ref[at, :] = back.astype(BF16)
+    sums_ref[...] = sums
+
+
+def feed_forward(x, grad, up, down, bias, local):
     rows, depth = x.shape
-    columns = w.shape[1]
-    step = 384 if columns % 384 == 0 else columns
-    rows_at_once = 160 if rows % 160 == 0 else rows
-    block = pl.BlockSpec((rows, step), lambda j: (0, j))
+    columns = up.shape[1]
+    rows_at_once = 640 if rows % 640 == 0 else rows
     return pl.pallas_call(
-        partial(gelu_kernel, rows_at_once),
-        grid=(columns // step,),
-        in_specs=[
-            pl.BlockSpec((rows, depth), lambda j: (0, 0)),
-            pl.BlockSpec((depth, step), lambda j: (0, j)),
-            pl.BlockSpec((1, step), lambda j: (0, j)),
-        ],
-        out_specs=[block, block],
+        partial(feed_forward_kernel, local, rows_at_once),
         out_shape=[
             jax.ShapeDtypeStruct((rows, columns), BF16),
-            jax.ShapeDtypeStruct((rows, columns), F32),
-        ],
-        compiler_params=pltpu.CompilerParams(vmem_limit_bytes=40 * 2**20),
+            jax.ShapeDtypeStruct((rows, columns), BF16),
+            jax.ShapeDtypeStruct((1, columns), F32),
+            jax.ShapeDtypeStruct((rows, depth), BF16),
+            jax.ShapeDtypeStruct((local, depth), F32),
+        ],
+        compiler_params=pltpu.CompilerParams(vmem_limit_bytes=52 * 2**20),
         cost_estimate=pl.CostEstimate(
-            flops=2 * rows * depth * columns,
-            bytes_accessed=2 * depth * (rows + columns) + 6 * rows * columns,
+            flops=6 * rows * depth * columns,
+            bytes_accessed=4 * depth * (rows + columns) + 4 * rows * columns + 2 * rows * depth,
             transcendentals=rows * columns,
         ),
-    )(x, w, bias.reshape(1, columns))
+    )(x, grad, up, down, bias.reshape(1, columns))
 
 
 def on_device(
@@ -379,8 +386,6 @@
     normed_one_row = lax.all_gather(normed_one, "seq", axis=0, tiled=True)
 
     qkv_mine = seq_exchange(qkv_out).reshape(part, wide)
-    qkv_blocks = jnp.stack([qkv_mine] + [swap(qkv_mine, k) for k in range(1, nd)])
-    qkv_mine = jnp.concatenate([index(qkv_blocks, dp_at ^ k) for k in range(nd)], axis=0)
     up_slices = jnp.swapaxes(fc1_w.reshape(small, nd, hidden_part), 0, 1)
     up_slices = jnp.concatenate(
         [index(up_slices, dp_at)] + [swap(index(up_slices, dp_at ^ k), k) for k in range(1, nd)],
@@ -389,8 +394,10 @@
     half = part // 2
     own_half = lax.dynamic_slice_in_dim(proj_rows, core * half, half, 0)
     proj_halves = [swap(own_half, k) for k in range(1, nd)]
-    normed_one_row, up_slices, qkv_mine, qkv_wide, segments, proj_halves = after(
-        (normed_one_row, up_slices, qkv_mine, widen(qkv_mine), segments, proj_halves)
+    qkv_mine, up_slices, proj_halves = after((qkv_mine, up_slices, proj_halves))
+    qkv_mine = lax.all_gather(qkv_mine, "dp", axis=0, tiled=True)
+    normed_one_row, up_slices, qkv_mine, qkv_wide, segments, order = after(
+        (normed_one_row, up_slices, qkv_mine, widen(qkv_mine), segments, order)
     )
     up_part = lax.all_gather(up_slices, "seq", axis=0, tiled=True)
     triple = dot(normed_one_row, qkv_wide).astype(BF16)
@@ -422,47 +429,40 @@
     normed_two_rows = gather_rows(normed_two)
     up_part = inner(order, up_part).astype(BF16)
     normed_two_rows, up_part, order = after((normed_two_rows, up_part, order))
-    hidden, slope = gelu_of_matmul(normed_two_rows, up_part, up_bias)
-
+    hidden, pre_low, up_sums, up_low, own_back = feed_forward(
+        normed_two_rows, grad_out_rows, up_part, down_part, up_bias, local
+    )
+
+    normed_two_grad = add_blocks(own_back, up_low.reshape(nd, local, features))
     fc2_terms = inner(hidden, grad_out_rows).astype(BF16)
-    slope, fc2_terms = after((slope, fc2_terms))
     fc2_w_grad = lax.psum_scatter(fc2_terms, "seq", scatter_dimension=0, tiled=True)
-    pre_grad = times_transposed(grad_out_rows, down_part) * slope
-    pre_low = pre_grad.astype(BF16)
-    up_back = times_transposed(pre_low, up_part)
-    up_low = low_rows(up_back)
-    up_low, pre_late, normed_two_rows = after((up_low, pre_low, normed_two_rows))
-    normed_two_grad = add_blocks(up_back[:local], up_low)
-    fc1_terms = inner(times_transposed(normed_two_rows, order).astype(BF16), pre_late).astype(BF16)
-    normed_two_grad, fc1_terms, fc2_w_grad = after((normed_two_grad, fc1_terms, fc2_w_grad))
-    fc1_terms = lax.psum_scatter(fc1_terms, "seq", scatter_dimension=0, tiled=True)
+    fc1_terms = inner(times_transposed(normed_two_rows, order).astype(BF16), pre_low).astype(BF16)
+    normed_two_grad, fc2_terms, fc1_terms = after((normed_two_grad, fc2_terms, fc1_terms))
     through_two, ln2_g_grad, ln2_b_grad = norm_back(normed_two_grad, xhat_two, inverse_two, g_two)
     second_grad = grad_out.astype(F32) + through_two
     second_low = second_grad.astype(BF16)
     attended_grad = product_by_group(second_low, w_proj, ns)
-    attended_grad, second_late, hidden_late, attended_low = after(
-        (attended_grad, second_low, hidden, attended_low)
-    )
+    attended_grad, second_late, hidden_late, attended_low, fc1_terms = after(
+        (attended_grad, second_low, hidden, attended_low, fc1_terms)
+    )
+    fc1_terms = lax.psum_scatter(fc1_terms, "seq", scatter_dimension=0, tiled=True)
     attended_grad = seq_exchange(attended_grad).reshape(row_len, head_cols)
     down_sums = dot(hidden_late, down_part)
     attended_slices = jnp.swapaxes(attended_low.reshape(local, nd, part), 0, 1)
     attended_grad, down_sums, second_late, attended_slices = after(
         (attended_grad, down_sums, second_late, attended_slices)
     )
-    second_blocks = [second_late] + [swap(second_late, k) for k in range(1, nd)]
     triple_grad = jnp.concatenate(
         attend_back(triple, attended_grad, attended, lse, segments, heads, scale), axis=1
     )
     one_back = times_transposed(triple_grad, qkv_mine).astype(BF16)
-    one_back, triple_late, fc1_terms, down_sums, second_rows = after(
-        (one_back, triple_grad, fc1_terms, down_sums, jnp.concatenate(second_blocks, axis=0))
+    one_back, triple_late, down_sums, second_late, fc1_terms, fc2_w_grad = after(
+        (one_back, triple_grad, down_sums, second_late, fc1_terms, fc2_w_grad)
     )
     normed_one_grad = lax.psum_scatter(one_back, "seq", scatter_dimension=0, tiled=True)
+    second_rows = gather_rows(second_late)
     qkv_terms = inner(normed_one_row, triple_late).reshape(nd, part, wide)
-    qkv_low, down_low = qkv_terms.astype(BF16), low_rows(down_sums)
-    qkv_low, down_low, second_rows, attended_slices = after(
-        (qkv_low, down_low, second_rows, attended_slices)
-    )
+    qkv_low, second_rows = after((qkv_terms.astype(BF16), second_rows))
     qkv_blocks = [swap(index(qkv_low, dp_at ^ k), k) for k in range(1, nd)]
     attended_rows = jnp.concatenate(
         [index(attended_slices, dp_at)]
@@ -471,22 +471,29 @@
     )
     proj_terms = inner(attended_rows, second_rows).reshape(ns, small, features)
     proj_w_grad = chip_sums(core_sums(proj_terms))
-    output = (second + add_blocks(down_sums[:local], down_low) + b_down).astype(BF16)
     qkv_sum = index(qkv_terms, dp_at)
     for block in qkv_blocks:
         qkv_sum = qkv_sum + block.astype(F32)
     qkv_sum = qkv_sum.astype(BF16).reshape(ns, small, wide)
-    fc1_terms = fc1_terms.reshape(nd, small, hidden_part)
-    fc1_blocks = jnp.stack([fc1_terms[0]] + [swap(fc1_terms[k], k) for k in range(1, nd)])
-    normed_one_grad, qkv_sum, fc1_blocks, proj_w_grad, output = after(
-        (normed_one_grad, qkv_sum, fc1_blocks, proj_w_grad, output)
-    )
+    normed_one_grad, qkv_sum, proj_w_grad = after((normed_one_grad, qkv_sum, proj_w_grad))
     normed_one_grad = normed_one_grad.astype(F32)
     through_one, ln1_g_grad, ln1_b_grad = norm_back(normed_one_grad, xhat_one, inverse_one, g_one)
     first_grad = second_grad + through_one
     first_low = first_grad.astype(BF16)
     first_low_rows = gather_rows(first_low)
+    first_low_rows, qkv_sum, first_grad, fc1_terms, down_sums = after(
+        (first_low_rows, qkv_sum, first_grad, fc1_terms, down_sums)
+    )
+    skip_terms = inner(joined_here, first_low_rows).astype(BF16)
+    skip_w_grad = lax.psum_scatter(skip_terms, "seq", scatter_dimension=0, tiled=True).astype(F32)
+    skip_terms, first_low_rows, first_grad, qkv_sum, fc1_terms, down_sums = after(
+        (skip_terms, first_low_rows, first_grad, qkv_sum, fc1_terms, down_sums)
+    )
     qkv_w_grad = seq_exchange(qkv_sum)
+    fc1_terms = fc1_terms.reshape(nd, small, hidden_part)
+    fc1_blocks = jnp.stack([fc1_terms[0]] + [swap(fc1_terms[k], k) for k in range(1, nd)])
+    output = second + add_blocks(down_sums[:local], low_rows(down_sums)) + b_down
+    output = output.astype(BF16)
     vector_grads = jnp.stack(
         [
             jnp.sum(first_grad, axis=0),
@@ -499,7 +506,7 @@
         ]
     )
     vector_grads = jnp.swapaxes(vector_grads.reshape(7, n, small), 0, 1).reshape(n, 7 * small)
-    up_grads = jnp.sum(pre_grad, axis=0).reshape(ns, hidden_units // n)
+    up_grads = up_sums.reshape(ns, hidden_units // n)
     up_grads = lax.dynamic_update_slice_in_dim(
         jnp.zeros((n, hidden_units // n), F32), up_grads, dp_at * ns, 0
     )
@@ -508,10 +515,6 @@
     vector_grads = lax.all_to_all(
         vector_grads.reshape(n, padded // 128, 128), ("dp", "seq"), 0, 0, tiled=True
     )
-    first_low_rows, qkv_w_grad, vector_grads = after((first_low_rows, qkv_w_grad, vector_grads))
-    skip_terms = inner(joined_here, first_low_rows).astype(BF16)
-    skip_w_grad = lax.psum_scatter(skip_terms, "seq", scatter_dimension=0, tiled=True).astype(F32)
-    skip_terms, first_low_rows = after((skip_terms, first_low_rows))
     joined_grad_part = times_transposed(first_low_rows, skip_part).astype(BF16)
     joined_grad_part = joined_grad_part.reshape(nd, local, joined_part)
     away = jnp.stack(

time: 443 us -> 439 us (level)
  local copies, waits for them, and re-layouts: 68 us -> 50.6 us
  blocking collectives: 15.6 us -> 30 us
  matrix products: 58.5 us -> 48.8 us
  waiting for transfers between devices: 119 us -> 128 us
  Pallas kernels: 31.5 us -> 37.8 us
    all_gather x0 -> x1, blocking collectives: none -> 13.8 us  [on_device(): qkv_mine = lax.all_gather(qkv_mine, 'dp', axis=0, tiled=True)]
    ppermute x45 -> x42, waiting for transfers between devices: 54.8 us -> 65.3 us  [swap(): return lax.ppermute(v, 'dp', [(i, i ^ k) for i in range(nd)])]
    dot_general x4 -> x2, matrix products: 16.2 us -> 6.34 us  [times_transposed(): lax.dot_general(left, right, (((1,), (1,)), ((), ())), preferred_element_...]
    unnamed x9, waiting for transfers between devices: 9.37 us -> 0.79 us
    all_gather x1, waiting for transfers between devices: 0.02 us -> 7.93 us  [on_device(): down_part = lax.all_gather(own_down, 'seq', axis=0, tiled=True)]
    pallas_call x1, Pallas kernels: 5.31 us -> 11.6 us  [feed_forward(): pl.pallas_call(partial(feed_forward_kernel, local, rows_at_once), out_sha...]
    all_to_all x4, waiting for transfers between devices: 31.9 us -> 37.2 us  [seq_exchange(): return lax.all_to_all(v, 'seq', 0, 0, tiled=True)]
    all_to_all x1, waiting for transfers between devices: 4.62 us -> 0.01 us  [on_device(): lax.all_to_all(vector_grads.reshape(n, padded // 128, 128), ('dp', 'seq')...]
  transfers between devices with their start and end apart: 64 -> 61, of which waited for: 26 -> 22; matrix products, arithmetic and copies ran while one was open for 32% -> 24% of each run, Pallas kernels for 7% -> 6%
where the time goes in v9:
time: 439 us; the launch traced here: 431 us
  waiting for transfers between devices  128 us (29%)
  starting transfers between devices  84.5 us (19%)
  local copies, waits for them, and re-layouts  50.6 us (12%)
  matrix products  48.8 us (11%)
  Pallas kernels  37.8 us (9%)
  other arithmetic  32.3 us (7%)
  blocking collectives  30 us (7%)
  between operations  18.8 us (4%)
    ppermute x42, waiting for transfers between devices, swap(): return lax.ppermute(v, 'dp', [(i, i ^ k) for i in range(nd)])  65.3 us
    ppermute x42, starting transfers between devices, swap(): return lax.ppermute(v, 'dp', [(i, i ^ k) for i in range(nd)])  53 us
    all_to_all x4, waiting for transfers between devices, seq_exchange(): return lax.all_to_all(v, 'seq', 0, 0, tiled=True)  37.2 us
    dot_general x6, matrix products, inner(): lax.dot_general(left, right, (((0,), (0,)), ((), ())), preferred_element_...  27.9 us
    all_gather x1, blocking collectives, on_device(): proj_rows = lax.all_gather(own_proj, 'seq', axis=0, tiled=True)  16.3 us
    all_to_all x4, starting transfers between devices, seq_exchange(): return lax.all_to_all(v, 'seq', 0, 0, tiled=True)  15.8 us
    dot_general x4, matrix products, dot(): return jnp.dot(left, right, preferred_element_type=F32)  14.6 us
    pallas_call x1, Pallas kernels, attend_back(): pl.pallas_call(partial(attend_back_kernel, heads, scale), grid=(rows // s...  14.2 us
  transfers between devices with their start and end apart: 61, of which 22 were waited for; matrix products, arithmetic and copies ran while one was open for 24% of the time, Pallas kernels for 6%

profile of v9, /device:TPU:0, one launch (start us, length us, event | category | flops | bytes accessed | tf_op | source)
XLA Modules:
  0.0 430.9 jit_solution(9229200677818831669)
XLA Ops:
  15.1 6.3 %all-to-all-start = ((bf16[32,8,128]{2,1,0:T(8,128)(2,1)}), bf16[32,8,128]{2,1,0:T(8,128)(2,1)S(1)}, u32[]{:S(2)}, u32[]{:S(2)}) async-start(bf16[32,8,128]{2,1,0:T(8,128)(2,1)} %broadcast_in_dim.15), calls=%async_computation | async-start | bytes 131072 | tf_op jit(solution)/shard_map/all_to_all | solution.py:351
  22.6 6.9 %all-to-all-done = bf16[32,8,128]{2,1,0:T(8,128)(2,1)S(1)} async-done(((bf16[32,8,128]{2,1,0:T(8,128)(2,1)}), bf16[32,8,128]{2,1,0:T(8,128)(2,1)S(1)}, u32[]{:S(2)}, u32[]{:S(2)}) %all-to-all-start) | async-done | bytes 65568 | tf_op jit(solution)/shard_map/all_to_all | solution.py:351
  30.6 6.6 %all-gather.6.cloned.1.call-done = bf16[576,1152]{1,0:T(8,128)(2,1)} async-done(((bf16[72,1152]{1,0:T(8,128)(2,1)}), bf16[576,1152]{1,0:T(8,128)(2,1)}) %all-gather.6.cloned.1.call-update) | async-done | bytes 1327120 | tf_op jit(solution)/shard_map/all_gather | solution.py:343
  48.5 16.3 %all-gather = bf16[8,36,1152]{2,1,0:T(8,128)(2,1)} all-gather(bf16[1,36,1152]{2,1,0:T(8,128)(2,1)S(1)} %bitcast.180), channel_id=1, replica_groups=mesh['dp'=4,'seq'=8] {'seq'}, dimensions={0}, use_global_device_ids=true | all-gather | bytes 746496 | tf_op jit(solution)/shard_map/all_gather | solution.py:382
  92.5 15.5 %all-to-all-done.1 = bf16[8,36,432]{2,1,0:T(8,128)(2,1)S(1)} async-done(((bf16[8,36,432]{2,1,0:T(8,128)(2,1)}), bf16[8,36,432]{2,1,0:T(8,128)(2,1)S(1)}, u32[]{:S(2)}, u32[]{:S(2)}) %all-to-all-start.1) | async-done | bytes 248864 | tf_op jit(solution)/shard_map/all_to_all | solution.py:330
  108.1 13.8 %all_gather.21 = bf16[1152,432]{1,0:T(8,128)(2,1)S(1)} all-gather(bf16[288,432]{1,0:T(8,128)(2,1)S(1)} %reshape.208), channel_id=1, replica_groups=mesh['dp'=4,'seq'=8] {'dp'}, dimensions={0}, use_global_device_ids=true | all-gather | bytes 1244160 | tf_op jit(solution)/shard_map/all_gather | solution.py:398
  131.2 8.4 %shard_map.288 = (f32[1280,256]{1,0:T(8,128)S(1)}, bf16[1280,144]{1,0:T(8,128)(2,1)S(1)}, f32[8,1280]{1,0:T(8,128)S(1)}) custom-call(bf16[1280,768]{1,0:T(8,128)(2,1)S(1)} %convolution_convert_fusion.4.q_ref.k_ref.v_ref, bf16[1280,768]{1,0:T(8,128)(2,1)S(1)} %convolution_convert_fusion.4.q_ref.k_ref.v_ref, ...), custom_call_target="tpu_custom_call" | custom-call | flops 3355443200 | bytes 3276800 | tf_op jit(solution)/shard_map/pallas_call | solution.py:84
  152.5 7.9 %collective-permute-done.13 = bf16[160,1152]{1,0:T(8,128)(2,1)} collective-permute-done((bf16[160,1152]{1,0:T(8,128)(2,1)S(1)}, bf16[160,1152]{1,0:T(8,128)(2,1)}, u32[]{:S(2)}, u32[]{:S(2)}) %collective-permute-start.13) | collective-permute-done | bytes 368672 | tf_op jit(solution)/shard_map/ppermute | solution.py:306
  162.8 5.5 %all-to-all-done.2 = bf16[8,160,144]{1,2,0:T(8,128)(2,1)S(1)} async-done(((bf16[8,160,144]{1,2,0:T(8,128)(2,1)}), bf16[8,160,144]{1,2,0:T(8,128)(2,1)S(1)}, u32[]{:S(2)}, u32[]{:S(2)}) %all-to-all-start.2) | async-done | bytes 368672 | tf_op jit(solution)/shard_map/all_to_all | solution.py:330
  176.4 5.3 %convolution_convert_fusion.3.up_ref = bf16[1152,1152]{1,0:T(8,128)(2,1)} fusion(bf16[1152,1152]{1,0:T(8,128)(2,1)S(1)} %copy-done.17, bf16[1152,1152]{1,0:T(8,128)(2,1)S(1)} %copy-done.38), kind=kOutput, calls=%fused_computation.11 | convolution fusion | flops 3058974720 | bytes 7962624 | tf_op jit(solution)/shard_map/dot_general | solution.py:50
  184.4 8.2 %collective-permute-done.19 = bf16[160,1152]{1,0:T(8,128)(2,1)S(1)} collective-permute-done((bf16[160,1152]{1,0:T(8,128)(2,1)S(1)}, bf16[160,1152]{1,0:T(8,128)(2,1)S(1)}, u32[]{:S(2)}, u32[]{:S(2)}) %collective-permute-start.19) | collective-permute-done | bytes 368672 | tf_op jit(solution)/shard_map/ppermute | solution.py:306
  193.8 7.9 %all-gather.12.cloned.1.call-done.down_ref = bf16[1152,1152]{1,0:T(8,128)(2,1)} async-done(((bf16[144,1152]{1,0:T(8,128)(2,1)}), bf16[1152,1152]{1,0:T(8,128)(2,1)}) %all-gather.12.cloned.1.call-update) | async-done | bytes 2654224 | tf_op jit(solution)/shard_map/all_gather | solution.py:424
  201.7 11.6 %shard_map.289 = (bf16[640,1152]{1,0:T(8,128)(2,1)}, bf16[640,1152]{1,0:T(8,128)(2,1)}, f32[1,1152]{1,0:T(1,128)S(1)}, bf16[640,1152]{1,0:T(8,128)(2,1)}, f32[160,1152]{1,0:T(8,128)S(1)}) custom-call(bf16[640,1152]{1,0:T(8,128)(2,1)} %pad_maximum_fusion.1.x_ref, bf16[640,1152]{1,0:T(8,128)(2,1)} %pad_maximum_fusion.grad_ref, ...), custom_call_target="tpu_custom_call" | custom-call | flops 5096079360 | bytes 12681216 | tf_op jit(solution)/shard_map/pallas_call | solution.py:262
  213.4 5.3 %convolution_convert_fusion.2 = bf16[1152,1152]{1,0:T(8,128)(2,1)} fusion(bf16[640,1152]{1,0:T(8,128)(2,1)} %get-tuple-element.123, bf16[640,1152]{1,0:T(8,128)(2,1)S(1)} %copy-done.22), kind=kOutput, calls=%fused_computation.10 | convolution fusion | flops 1700020224 | bytes 5603328 | tf_op jit(solution)/shard_map/dot_general | solution.py:50
  224.6 9.2 %convolution_convert_fusion.1 = bf16[1152,1152]{1,0:T(8,128)(2,1)} fusion(bf16[640,1152]{1,0:T(8,128)(2,1)} %get-tuple-element.119, bf16[640,1152]{1,0:T(8,128)(2,1)} %pad_maximum_fusion.1.x_ref, bf16[1152,1152]{1,0:T(8,128)(2,1)} %fusion.10), kind=kOutput, calls=%fused_computation.9 | convolution fusion | flops 3399450624 | bytes 8257536 | tf_op jit(solution)/shard_map/dot_general | solution.py:50
  233.9 7.4 %collective-permute-done.22 = bf16[160,1152]{1,0:T(8,128)(2,1)} collective-permute-done((bf16[160,1152]{1,0:T(8,128)(2,1)}, bf16[160,1152]{1,0:T(8,128)(2,1)}, u32[]{:S(2)}, u32[]{:S(2)}) %collective-permute-start.22) | collective-permute-done | bytes 368672 | tf_op jit(solution)/shard_map/ppermute | solution.py:306
  255.6 6.2 %fusion.58 = f32[640,1152]{1,0:T(8,128)} fusion(bf16[640,1152]{1,0:T(8,128)(2,1)} %get-tuple-element.123, bf16[1152,1152]{1,0:T(8,128)(2,1)} %all-gather.12.cloned.1.call-done.down_ref), kind=kOutput, calls=%fused_computation.175 | convolution fusion | flops 1698693120 | bytes 7077888 | tf_op jit(solution)/shard_map/dot_general | solution.py:46
  261.7 13.9 %all-to-all-done.3 = bf16[8,160,144]{1,2,0:T(8,128)(2,1)} async-done(((bf16[8,160,144]{1,2,0:T(8,128)(2,1)}), bf16[8,160,144]{1,2,0:T(8,128)(2,1)}, u32[]{:S(2)}, u32[]{:S(2)}) %all-to-all-start.3) | async-done | bytes 368672 | tf_op jit(solution)/shard_map/all_to_all | solution.py:330
  277.2 14.2 %shard_map.291 = (bf16[1280,144]{1,0:T(8,128)(2,1)S(1)}, bf16[1280,288]{1,0:T(8,128)(2,1)S(1)}) custom-call(bf16[1280,768]{1,0:T(8,128)(2,1)} %copy-done, bf16[1280,768]{1,0:T(8,128)(2,1)} %copy-done, bf16[1280,768]{1,0:T(8,128)(2,1)} %copy-done, bf16[1280,256]{1,0:T(8,128)(2,1)S(1)} %pad.18.out_grad_ref, f32[1280,256]{1,0:T(8,128)S(1)} %copy-done.2, ...), custom_call_target="tpu_custom_call" | custom-call | flops 8388608000 | bytes 4587520 | tf_op jit(solution)/shard_map/pallas_call | solution.py:164
  313.0 7.6 %collective-permute-done.25 = bf16[160,1152]{1,0:T(8,128)(2,1)S(1)} collective-permute-done((bf16[160,1152]{1,0:T(8,128)(2,1)S(1)}, bf16[160,1152]{1,0:T(8,128)(2,1)S(1)}, u32[]{:S(2)}, u32[]{:S(2)}) %collective-permute-start.25) | collective-permute-done | bytes 368672 | tf_op jit(solution)/shard_map/ppermute | solution.py:306
  356.9 5.2 %collective-permute-done.34 = bf16[160,1152]{1,0:T(8,128)(2,1)S(1)} collective-permute-done((bf16[160,1152]{1,0:T(8,128)(2,1)S(1)}, bf16[160,1152]{1,0:T(8,128)(2,1)S(1)}, u32[]{:S(2)}, u32[]{:S(2)}) %collective-permute-start.34) | collective-permute-done | bytes 368672 | tf_op jit(solution)/shard_map/ppermute | solution.py:306
  362.1 6.1 %collective-permute-done.35 = bf16[160,1152]{1,0:T(8,128)(2,1)S(1)} collective-permute-done((bf16[160,1152]{1,0:T(8,128)(2,1)S(1)}, bf16[160,1152]{1,0:T(8,128)(2,1)S(1)}, u32[]{:S(2)}, u32[]{:S(2)}) %collective-permute-start.35) | collective-permute-done | bytes 368672 | tf_op jit(solution)/shard_map/ppermute | solution.py:306
  396.0 5.4 %collective-permute-done.41 = bf16[160,576]{0,1:T(8,128)(2,1)S(1)} collective-permute-done((bf16[160,576]{0,1:T(8,128)(2,1)S(1)}, bf16[160,576]{0,1:T(8,128)(2,1)S(1)}, u32[]{:S(2)}, u32[]{:S(2)}) %collective-permute-start.41) | collective-permute-done | bytes 184352 | tf_op jit(solution)/shard_map/ppermute | solution.py:306
  410.2 5.1 %collective-permute-done.38 = bf16[160,1152]{1,0:T(8,128)(2,1)} collective-permute-done((bf16[160,1152]{1,0:T(8,128)(2,1)S(1)}, bf16[160,1152]{1,0:T(8,128)(2,1)}, u32[]{:S(2)}, u32[]{:S(2)}) %collective-permute-start.38) | collective-permute-done | bytes 368672 | tf_op jit(solution)/shard_map/ppermute | solution.py:306
  (337 shorter events, 206.2 us)
Async XLA Ops:
  7.3 30.0 %all-gather.6.cloned.1.call-start = ((), (), s32[]{:S(2)}) async-start(), calls=%async_computation.11 | async-start | bytes 1492992 | tf_op jit(solution)/shard_map/all_gather | solution.py:343
  9.7 19.9 %collective-permute-start = (bf16[160,576]{1,0:T(8,128)(2,1)S(1)}, bf16[160,576]{1,0:T(8,128)(2,1)S(1)}, u32[]{:S(2)}, u32[]{:S(2)}) collective-permute-start(bf16[160,576]{1,0:T(8,128)(2,1)S(1)} %get-tuple-element.193), channel_id=1, source_target_pairs={{0,8},{8,0},{16,24},{24,16},{1,9},{9,1},{17,25},{25,17},{2,10},{10... | collective-permute-start | bytes 552968 | tf_op jit(solution)/shard_map/ppermute | solution.py:306
  21.4 102.8 %all-gather.8.cloned.1.call-start = ((), (), s32[]{:S(2)}) async-start(), calls=%async_computation.12 | async-start | bytes 3317760 | tf_op jit(solution)/shard_map/all_gather | solution.py:386
  41.2 25.5 %collective-permute-start.3 = (bf16[160,1152]{1,0:T(8,128)(2,1)}, bf16[160,1152]{1,0:T(8,128)(2,1)}, u32[]{:S(2)}, u32[]{:S(2)}) collective-permute-start(bf16[160,1152]{1,0:T(8,128)(2,1)} %get-tuple-element.180), channel_id=1, source_target_pairs={{0,8},{8,0},{16,24},{24,16},{1,9},{9,1},{17,25},{25,17},{2,10},{10... | collective-permute-start | bytes 1105928 | tf_op jit(solution)/shard_map/ppermute | solution.py:306
  42.6 24.1 %collective-permute-start.4 = (bf16[160,1152]{1,0:T(8,128)(2,1)}, bf16[160,1152]{1,0:T(8,128)(2,1)}, u32[]{:S(2)}, u32[]{:S(2)}) collective-permute-start(bf16[160,1152]{1,0:T(8,128)(2,1)} %get-tuple-element.182), channel_id=1, source_target_pairs={{0,16},{8,24},{16,0},{24,8},{1,17},{9,25},{17,1},{25,9},{2,18},{10... | collective-permute-start | bytes 1105928 | tf_op jit(solution)/shard_map/ppermute | solution.py:306
  44.1 22.7 %collective-permute-start.5 = (bf16[160,1152]{1,0:T(8,128)(2,1)}, bf16[160,1152]{1,0:T(8,128)(2,1)}, u32[]{:S(2)}, u32[]{:S(2)}) collective-permute-start(bf16[160,1152]{1,0:T(8,128)(2,1)} %get-tuple-element.181), channel_id=1, source_target_pairs={{0,24},{8,16},{16,8},{24,0},{1,25},{9,17},{17,9},{25,1},{2,26},{10... | collective-permute-start | bytes 1105928 | tf_op jit(solution)/shard_map/ppermute | solution.py:306
  83.9 24.1 %all-to-all-start.1 = ((bf16[8,36,432]{2,1,0:T(8,128)(2,1)}), bf16[8,36,432]{2,1,0:T(8,128)(2,1)S(1)}, u32[]{:S(2)}, u32[]{:S(2)}) async-start(bf16[8,36,432]{2,1,0:T(8,128)(2,1)} %copy.95), calls=%async_computation.1 | async-start | bytes 655360 | tf_op jit(solution)/shard_map/all_to_all | solution.py:330
  87.4 81.2 %all-gather.10.cloned.1.call-start = ((), (), s32[]{:S(2)}) async-start(), calls=%async_computation.13 | async-start | bytes 2985984 | tf_op jit(solution)/shard_map/all_gather | solution.py:402
  87.5 20.6 %collective-permute-start.10 = (bf16[144,1152]{1,0:T(8,128)(2,1)S(1)}, bf16[144,1152]{1,0:T(8,128)(2,1)S(1)}, u32[]{:S(2)}, u32[]{:S(2)}) collective-permute-start(bf16[144,1152]{1,0:T(8,128)(2,1)S(1)} %constant_dynamic-slice_fusion.5), channel_id=1, source_target_pairs={{0,16},{8,24},{16,0},{24,8},{1,17},{9,25},{17,1},{25,9},{2,18},{10... | collective-permute-start | bytes 995336 | tf_op jit(solution)/shard_map/ppermute | solution.py:306
  125.3 25.5 %collective-permute-start.17 = (bf16[144,1152]{1,0:T(8,128)(2,1)}, bf16[144,1152]{1,0:T(8,128)(2,1)}, u32[]{:S(2)}, u32[]{:S(2)}) collective-permute-start(bf16[144,1152]{1,0:T(8,128)(2,1)} %collective-permute-done.11), channel_id=1, source_target_pairs={{0,1},{1,0},{2,3},{3,2},{4,5},{5,4},{6,7},{7,6},{8,9},{9,8},{10,11... | collective-permute-start | bytes 995336 | tf_op jit(solution)/shard_map/ppermute | solution.py:309
  145.4 22.9 %all-to-all-start.2 = ((bf16[8,160,144]{1,2,0:T(8,128)(2,1)}), bf16[8,160,144]{1,2,0:T(8,128)(2,1)S(1)}, u32[]{:S(2)}, u32[]{:S(2)}) async-start(bf16[8,160,144]{1,2,0:T(8,128)(2,1)} %copy.98), calls=%async_computation.2 | async-start | bytes 1179648 | tf_op jit(solution)/shard_map/all_to_all | solution.py:330
  148.9 52.8 %all-gather.12.cloned.1.call-start = ((), (), s32[]{:S(2)}) async-start(), calls=%async_computation.14 | async-start | bytes 2985984 | tf_op jit(solution)/shard_map/all_gather | solution.py:424
  168.6 127.7 %reduce-scatter.9.cloned.1.call-start = ((), (), s32[]{:S(2)}) async-start(), calls=%async_computation.16 | async-start | bytes 2985984 | tf_op jit(solution)/shard_map/reduce_scatter | solution.py:438
  218.7 78.2 %reduce-scatter.7.cloned.1.call-start = ((), (), s32[]{:S(2)}) async-start(), calls=%async_computation.15 | async-start | bytes 2985984 | tf_op jit(solution)/shard_map/reduce_scatter | solution.py:448
  250.0 25.6 %all-to-all-start.3 = ((bf16[8,160,144]{1,2,0:T(8,128)(2,1)}), bf16[8,160,144]{1,2,0:T(8,128)(2,1)}, u32[]{:S(2)}, u32[]{:S(2)}) async-start(bf16[8,160,144]{1,2,0:T(8,128)(2,1)} %copy.100), calls=%async_computation.3 | async-start | bytes 1179648 | tf_op jit(solution)/shard_map/all_to_all | solution.py:330
  254.2 93.5 %reduce-scatter.11.cloned.1.call-start = ((), (), s32[]{:S(2)}) async-start(), calls=%async_computation.17 | async-start | bytes 3317760 | tf_op jit(solution)/shard_map/reduce_scatter | solution.py:462
  297.3 23.4 %collective-permute-start.30 = (bf16[160,288]{1,0:T(8,128)(2,1)S(1)}, bf16[160,288]{1,0:T(8,128)(2,1)S(1)}, u32[]{:S(2)}, u32[]{:S(2)}) collective-permute-start(bf16[160,288]{1,0:T(8,128)(2,1)S(1)} %get-tuple-element.201), channel_id=1, source_target_pairs={{0,8},{8,0},{16,24},{24,16},{1,9},{9,1},{17,25},{25,17},{2,10},{10... | collective-permute-start | bytes 276488 | tf_op jit(solution)/shard_map/ppermute | solution.py:306
  298.5 22.2 %collective-permute-start.31 = (bf16[160,288]{1,0:T(8,128)(2,1)S(1)}, bf16[160,288]{1,0:T(8,128)(2,1)S(1)}, u32[]{:S(2)}, u32[]{:S(2)}) collective-permute-start(bf16[160,288]{1,0:T(8,128)(2,1)S(1)} %get-tuple-element.200), channel_id=1, source_target_pairs={{0,16},{8,24},{16,0},{24,8},{1,17},{9,25},{17,1},{25,9},{2,18},{10... | collective-permute-start | bytes 276488 | tf_op jit(solution)/shard_map/ppermute | solution.py:306
  300.9 19.7 %collective-permute-start.25 = (bf16[160,1152]{1,0:T(8,128)(2,1)S(1)}, bf16[160,1152]{1,0:T(8,128)(2,1)S(1)}, u32[]{:S(2)}, u32[]{:S(2)}) collective-permute-start(bf16[160,1152]{1,0:T(8,128)(2,1)S(1)} %copy-done.16), channel_id=1, source_target_pairs={{0,16},{8,24},{16,0},{24,8},{1,17},{9,25},{17,1},{25,9},{2,18},{10... | collective-permute-start | bytes 1105928 | tf_op jit(solution)/shard_map/ppermute | solution.py:306
  336.6 85.6 %reduce-scatter.13.cloned.1.call-start = ((), (), s32[]{:S(2)}) async-start(), calls=%async_computation.18 | async-start | bytes 1492992
  373.1 31.2 %all-to-all-start.6 = ((f32[32,8,128]{2,1,0:T(8,128)}), f32[32,8,128]{2,1,0:T(8,128)S(1)}, u32[]{:S(2)}, u32[]{:S(2)}) async-start(f32[32,8,128]{2,1,0:T(8,128)} %bitcast.71), calls=%async_computation.9 | async-start | bytes 262144 | tf_op jit(solution)/shard_map/all_to_all | solution.py:515
  387.2 23.0 %collective-permute-start.37 = (bf16[160,1152]{1,0:T(8,128)(2,1)S(1)}, bf16[160,1152]{1,0:T(8,128)(2,1)}, u32[]{:S(2)}, u32[]{:S(2)}) collective-permute-start(bf16[160,1152]{1,0:T(8,128)(2,1)S(1)} %get-tuple-element.174), channel_id=1, source_target_pairs={{0,8},{8,0},{16,24},{24,16},{1,9},{9,1},{17,25},{25,17},{2,10},{10... | collective-permute-start | bytes 1105928 | tf_op jit(solution)/shard_map/ppermute | solution.py:306
  389.0 26.4 %collective-permute-start.38 = (bf16[160,1152]{1,0:T(8,128)(2,1)S(1)}, bf16[160,1152]{1,0:T(8,128)(2,1)}, u32[]{:S(2)}, u32[]{:S(2)}) collective-permute-start(bf16[160,1152]{1,0:T(8,128)(2,1)S(1)} %get-tuple-element.176), channel_id=1, source_target_pairs={{0,16},{8,24},{16,0},{24,8},{1,17},{9,25},{17,1},{25,9},{2,18},{10... | collective-permute-start | bytes 1105928 | tf_op jit(solution)/shard_map/ppermute | solution.py:306
  393.4 22.0 %collective-permute-start.39 = (bf16[160,1152]{1,0:T(8,128)(2,1)S(1)}, bf16[160,1152]{1,0:T(8,128)(2,1)}, u32[]{:S(2)}, u32[]{:S(2)}) collective-permute-start(bf16[160,1152]{1,0:T(8,128)(2,1)S(1)} %get-tuple-element.175), channel_id=1, source_target_pairs={{0,24},{8,16},{16,8},{24,0},{1,25},{9,17},{17,9},{25,1},{2,26},{10... | collective-permute-start | bytes 1105928 | tf_op jit(solution)/shard_map/ppermute | solution.py:306
  (76 other events, 866.8 us)
Sparse Core Ops, SparseCore 0:
  9.7 27.4 all-gather.5
  70.2 43.0 all-gather.7
  124.4 34.8 all-gather.9
  168.7 32.9 all-gather.11
  218.8 36.7 reduce-scatter.8
  257.8 39.0 reduce-scatter.6
  299.2 37.9 reduce-scatter.10
  372.0 33.2 reduce-scatter.12

commit v10 on v9

--- a/solution.py
+++ b/solution.py
@@ -229,7 +229,7 @@
 
 def feed_forward_kernel(
     local, rows_at_once, x_ref, grad_ref, up_ref, down_ref, bias_ref,
-    hidden_ref, low_ref, sums_ref, back_ref, own_ref,
+    hidden_ref, low_ref, sums_ref, own_ref, *back_refs,
 ):
     sums = jnp.zeros(sums_ref.shape, F32)
     for start in range(0, x_ref.shape[0], rows_at_once):
@@ -249,9 +249,12 @@
         low = pre_grad.astype(BF16)
         low_ref[at, :] = low
         back = times_transposed(low, up_ref[...])
-        if start == 0:
-            own_ref[...] = back[:local]
-        back_ref[at, :] = back.astype(BF16)
+        for k in range(start // local, (start + rows_at_once) // local):
+            block = back[k * local - start : (k + 1) * local - start]
+            if k == 0:
+                own_ref[...] = block
+            else:
+                back_refs[k - 1][...] = block.astype(BF16)
     sums_ref[...] = sums
 
 
@@ -265,9 +268,9 @@
             jax.ShapeDtypeStruct((rows, columns), BF16),
             jax.ShapeDtypeStruct((rows, columns), BF16),
             jax.ShapeDtypeStruct((1, columns), F32),
-            jax.ShapeDtypeStruct((rows, depth), BF16),
             jax.ShapeDtypeStruct((local, depth), F32),
-        ],
+        ]
+        + [jax.ShapeDtypeStruct((local, depth), BF16)] * (rows // local - 1),
         compiler_params=pltpu.CompilerParams(vmem_limit_bytes=52 * 2**20),
         cost_estimate=pl.CostEstimate(
             flops=6 * rows * depth * columns,
@@ -340,7 +343,10 @@
         terms = lax.all_to_all(sums, "seq", 0, 0, axis_index_groups=groups, tiled=True)
         return jnp.sum(terms.reshape(sums.shape).astype(F32), axis=0)
 
-    skip_part = lax.all_gather(skip_w, "seq", axis=0, tiled=True)
+    skip_rows = skip_w.shape[0]
+    skip_proj = jnp.concatenate([skip_w, jnp.pad(proj_w, ((0, -(skip_rows + small) % 8), (0, 0)))])
+    skip_proj = lax.all_gather(skip_proj, "seq", axis=0, tiled=False)
+    skip_part = skip_proj[:, :skip_rows].reshape(joined_part, features)
 
     own_vectors = (skip_b, ln1_g, ln1_b, proj_b, ln2_g, ln2_b, fc2_b, fc1_b)
     packed = jnp.concatenate(own_vectors)
@@ -369,7 +375,10 @@
     order = (row == lax.broadcasted_iota(jnp.int32, (features, features), 1)).astype(BF16)
     qkv_out = qkv_w.reshape(small, 3, ns, head_cols).transpose(2, 0, 1, 3).reshape(ns, small, wide)
     segments = segment_of(item_lengths, jnp.arange(row_len, dtype=jnp.int32))
-    own_proj, skip_part, joined_here, vectors = after((proj_w, skip_part, joined_here, vectors))
+    qkv_out = qkv_w.reshape(small, 3, ns, head_cols).transpose(2, 0, 1, 3).reshape(ns, small, wide)
+    qkv_out, skip_proj, skip_part, joined_here, vectors = after(
+        (qkv_out, skip_proj, skip_part, joined_here, vectors)
+    )
     def vector(at):
         return vectors[:, at * small : (at + 1) * small].reshape(features)
 
@@ -379,13 +388,14 @@
 
     first_terms = dot(joined_here, skip_part)
     first = add_blocks(first_terms[:local], low_rows(first_terms)) + b_skip
-    proj_rows = lax.all_gather(own_proj, "seq", axis=0, tiled=True)
+    qkv_mine = seq_exchange(qkv_out).reshape(part, wide)
+    proj_rows = skip_proj[:, skip_rows : skip_rows + small].reshape(part, features)
     xhat_one, inverse_one = norm_pieces(first)
     normed_one = (xhat_one * g_one + b_one).astype(BF16)
-    normed_one, qkv_out, proj_rows = after((normed_one, qkv_out, proj_rows))
+    normed_one, qkv_mine, proj_rows = after((normed_one, qkv_mine, proj_rows))
     normed_one_row = lax.all_gather(normed_one, "seq", axis=0, tiled=True)
 
-    qkv_mine = seq_exchange(qkv_out).reshape(part, wide)
+    qkv_mine = lax.all_gather(qkv_mine, "dp", axis=0, tiled=True)
     up_slices = jnp.swapaxes(fc1_w.reshape(small, nd, hidden_part), 0, 1)
     up_slices = jnp.concatenate(
         [index(up_slices, dp_at)] + [swap(index(up_slices, dp_at ^ k), k) for k in range(1, nd)],
@@ -394,12 +404,13 @@
     half = part // 2
     own_half = lax.dynamic_slice_in_dim(proj_rows, core * half, half, 0)
     proj_halves = [swap(own_half, k) for k in range(1, nd)]
-    qkv_mine, up_slices, proj_halves = after((qkv_mine, up_slices, proj_halves))
-    qkv_mine = lax.all_gather(qkv_mine, "dp", axis=0, tiled=True)
-    normed_one_row, up_slices, qkv_mine, qkv_wide, segments, order = after(
-        (normed_one_row, up_slices, qkv_mine, widen(qkv_mine), segments, order)
-    )
-    up_part = lax.all_gather(up_slices, "seq", axis=0, tiled=True)
+    normed_one_row, up_slices, qkv_mine, qkv_wide, segments, order, proj_halves = after(
+        (normed_one_row, up_slices, qkv_mine, widen(qkv_mine), segments, order, proj_halves)
+    )
+    up_rows = up_slices.size // features
+    up_down = jnp.concatenate([up_slices.reshape(up_rows, features), fc2_w], axis=0)
+    up_down = lax.all_gather(up_down, "seq", axis=0, tiled=False)
+
     triple = dot(normed_one_row, qkv_wide).astype(BF16)
     attended, attended_low, lse = attend(triple, segments, heads, scale)
 
@@ -420,44 +431,53 @@
     grad_out_rows = gather_rows(grad_out)
     attended_low = heads_to_tokens(attended_low)
     attended_low, grad_out_rows, w_proj = after((attended_low, grad_out_rows, w_proj))
-    own_down, attended_low, up_part = after((fc2_w, attended_low, up_part))
-    down_part = lax.all_gather(own_down, "seq", axis=0, tiled=True)
     second = first + dot(attended_low, w_proj) + b_proj
     xhat_two, inverse_two = norm_pieces(second)
     normed_two = (xhat_two * g_two + b_two).astype(BF16)
 
     normed_two_rows = gather_rows(normed_two)
-    up_part = inner(order, up_part).astype(BF16)
-    normed_two_rows, up_part, order = after((normed_two_rows, up_part, order))
-    hidden, pre_low, up_sums, up_low, own_back = feed_forward(
+    up_part = inner(order, up_down[:, :up_rows].reshape(features, hidden_part)).astype(BF16)
+    down_part = up_down[:, up_rows:].reshape(hidden_part, features)
+    normed_two_rows, up_part, down_part, order = after(
+        (normed_two_rows, up_part, down_part, order)
+    )
+    hidden, pre_low, up_sums, normed_two_grad, *up_blocks = feed_forward(
         normed_two_rows, grad_out_rows, up_part, down_part, up_bias, local
     )
 
-    normed_two_grad = add_blocks(own_back, up_low.reshape(nd, local, features))
+    up_blocks = [swap(block, k + 1) for k, block in enumerate(up_blocks)]
+    fc1_terms = inner(times_transposed(normed_two_rows, order).astype(BF16), pre_low).astype(BF16)
+    up_blocks[0], hidden = after((up_blocks[0], hidden))
     fc2_terms = inner(hidden, grad_out_rows).astype(BF16)
     fc2_w_grad = lax.psum_scatter(fc2_terms, "seq", scatter_dimension=0, tiled=True)
-    fc1_terms = inner(times_transposed(normed_two_rows, order).astype(BF16), pre_low).astype(BF16)
+    for block in up_blocks:
+        normed_two_grad = normed_two_grad + block.astype(F32)
     normed_two_grad, fc2_terms, fc1_terms = after((normed_two_grad, fc2_terms, fc1_terms))
     through_two, ln2_g_grad, ln2_b_grad = norm_back(normed_two_grad, xhat_two, inverse_two, g_two)
     second_grad = grad_out.astype(F32) + through_two
     second_low = second_grad.astype(BF16)
     attended_grad = product_by_group(second_low, w_proj, ns)
-    attended_grad, second_late, hidden_late, attended_low, fc1_terms = after(
-        (attended_grad, second_low, hidden, attended_low, fc1_terms)
-    )
-    fc1_terms = lax.psum_scatter(fc1_terms, "seq", scatter_dimension=0, tiled=True)
+    attended_grad, second_late, hidden_late, attended_low = after(
+        (attended_grad, second_low, hidden, attended_low)
+    )
     attended_grad = seq_exchange(attended_grad).reshape(row_len, head_cols)
     down_sums = dot(hidden_late, down_part)
     attended_slices = jnp.swapaxes(attended_low.reshape(local, nd, part), 0, 1)
-    attended_grad, down_sums, second_late, attended_slices = after(
-        (attended_grad, down_sums, second_late, attended_slices)
+    down_blocks = low_rows(down_sums)
+    down_blocks = [swap(down_blocks[k], k) for k in range(1, nd)]
+    attended_grad, down_blocks[0], second_late, attended_slices = after(
+        (attended_grad, down_blocks[0], second_late, attended_slices)
     )
     triple_grad = jnp.concatenate(
         attend_back(triple, attended_grad, attended, lse, segments, heads, scale), axis=1
     )
     one_back = times_transposed(triple_grad, qkv_mine).astype(BF16)
-    one_back, triple_late, down_sums, second_late, fc1_terms, fc2_w_grad = after(
-        (one_back, triple_grad, down_sums, second_late, fc1_terms, fc2_w_grad)
+    output = second + down_sums[:local] + b_down
+    for block in down_blocks:
+        output = output + block.astype(F32)
+    output = output.astype(BF16)
+    one_back, triple_late, output, second_late, fc2_w_grad = after(
+        (one_back, triple_grad, output, second_late, fc2_w_grad)
     )
     normed_one_grad = lax.psum_scatter(one_back, "seq", scatter_dimension=0, tiled=True)
     second_rows = gather_rows(second_late)
@@ -470,30 +490,31 @@
         axis=0,
     )
     proj_terms = inner(attended_rows, second_rows).reshape(ns, small, features)
-    proj_w_grad = chip_sums(core_sums(proj_terms))
+    proj_sums = core_sums(proj_terms)
     qkv_sum = index(qkv_terms, dp_at)
     for block in qkv_blocks:
         qkv_sum = qkv_sum + block.astype(F32)
     qkv_sum = qkv_sum.astype(BF16).reshape(ns, small, wide)
-    normed_one_grad, qkv_sum, proj_w_grad = after((normed_one_grad, qkv_sum, proj_w_grad))
+    normed_one_grad, qkv_sum, proj_sums, fc1_terms = after(
+        (normed_one_grad, qkv_sum, proj_sums, fc1_terms)
+    )
+    fc1_terms = lax.psum_scatter(fc1_terms, "seq", scatter_dimension=0, tiled=True)
     normed_one_grad = normed_one_grad.astype(F32)
     through_one, ln1_g_grad, ln1_b_grad = norm_back(normed_one_grad, xhat_one, inverse_one, g_one)
     first_grad = second_grad + through_one
     first_low = first_grad.astype(BF16)
     first_low_rows = gather_rows(first_low)
-    first_low_rows, qkv_sum, first_grad, fc1_terms, down_sums = after(
-        (first_low_rows, qkv_sum, first_grad, fc1_terms, down_sums)
-    )
+    qkv_w_grad = seq_exchange(qkv_sum)
+    first_low_rows, first_grad, qkv_w_grad = after((first_low_rows, first_grad, qkv_w_grad))
     skip_terms = inner(joined_here, first_low_rows).astype(BF16)
+    skip_terms, fc1_terms = after((skip_terms, fc1_terms))
     skip_w_grad = lax.psum_scatter(skip_terms, "seq", scatter_dimension=0, tiled=True).astype(F32)
-    skip_terms, first_low_rows, first_grad, qkv_sum, fc1_terms, down_sums = after(
-        (skip_terms, first_low_rows, first_grad, qkv_sum, fc1_terms, down_sums)
-    )
-    qkv_w_grad = seq_exchange(qkv_sum)
+    skip_terms, first_low_rows, first_grad, fc1_terms, proj_sums = after(
+        (skip_terms, first_low_rows, first_grad, fc1_terms, proj_sums)
+    )
+    proj_w_grad = chip_sums(proj_sums)
     fc1_terms = fc1_terms.reshape(nd, small, hidden_part)
     fc1_blocks = jnp.stack([fc1_terms[0]] + [swap(fc1_terms[k], k) for k in range(1, nd)])
-    output = second + add_blocks(down_sums[:local], low_rows(down_sums)) + b_down
-    output = output.astype(BF16)
     vector_grads = jnp.stack(
         [
             jnp.sum(first_grad, axis=0),

time: 439 us -> 462 us (1.052)
  local copies, waits for them, and re-layouts: 50.6 us -> 67.7 us
  waiting for transfers between devices: 128 us -> 141 us
  blocking collectives: 30 us -> 23.5 us
    all_gather x1 -> x0, blocking collectives: 16.3 us -> none  [on_device(): proj_rows = lax.all_gather(own_proj, 'seq', axis=0, tiled=True)]
    all_gather x1, blocking collectives: 13.8 us -> 23.5 us  [on_device(): qkv_mine = lax.all_gather(qkv_mine, 'dp', axis=0, tiled=True)]
    reduce_scatter x1, waiting for transfers between devices: 0.68 us -> 9.62 us  [on_device(): lax.psum_scatter(fc1_terms, 'seq', scatter_dimension=0, tiled=True)]
    slice x0 -> x4, local copies, waits for them, and re-layouts: none -> 8.28 us  [the longest x1 4.66 us: on_device(): down_part = up_down[:, up_rows:].reshape(hidden_part, features)]
    ppermute x42, waiting for transfers between devices: 65.3 us -> 71.3 us  [swap(): return lax.ppermute(v, 'dp', [(i, i ^ k) for i in range(nd)])]
    all_gather x3 -> x2, waiting for transfers between devices: 14.6 us -> 12.5 us  [the longest x1 12.5 us: on_device(): skip_proj = lax.all_gather(skip_proj, 'seq', axis=0, tiled=False)]
    unnamed x84 -> x102, local copies, waits for them, and re-layouts: 9.34 us -> 7.34 us
  transfers between devices with their start and end apart: 61 -> 60, of which waited for: 22 -> 22; matrix products, arithmetic and copies ran while one was open for 24% -> 28% of each run, Pallas kernels for 6% -> 6%
where the time goes in v10:
time: 462 us; the launch traced here: 454 us
  waiting for transfers between devices  141 us (31%)
  starting transfers between devices  82 us (18%)
  local copies, waits for them, and re-layouts  67.7 us (15%)
  matrix products  49.8 us (11%)
  Pallas kernels  36.2 us (8%)
  other arithmetic  35.2 us (8%)
  blocking collectives  23.5 us (5%)
  between operations  19 us (4%)
    ppermute x42, waiting for transfers between devices, swap(): return lax.ppermute(v, 'dp', [(i, i ^ k) for i in range(nd)])  71.3 us
    ppermute x42, starting transfers between devices, swap(): return lax.ppermute(v, 'dp', [(i, i ^ k) for i in range(nd)])  52 us
    all_to_all x4, waiting for transfers between devices, seq_exchange(): return lax.all_to_all(v, 'seq', 0, 0, tiled=True)  33.4 us
    dot_general x6, matrix products, inner(): lax.dot_general(left, right, (((0,), (0,)), ((), ())), preferred_element_...  28.7 us
    all_gather x1, blocking collectives, on_device(): qkv_mine = lax.all_gather(qkv_mine, 'dp', axis=0, tiled=True)  23.5 us
    dot_general x4, matrix products, dot(): return jnp.dot(left, right, preferred_element_type=F32)  16.2 us
    all_to_all x4, starting transfers between devices, seq_exchange(): return lax.all_to_all(v, 'seq', 0, 0, tiled=True)  14.6 us
    pallas_call x1, Pallas kernels, attend_back(): pl.pallas_call(partial(attend_back_kernel, heads, scale), grid=(rows // s...  14.1 us
  transfers between devices with their start and end apart: 60, of which 22 were waited for; matrix products, arithmetic and copies ran while one was open for 28% of the time, Pallas kernels for 6%

profile of v10, /device:TPU:0, one launch (start us, length us, event | category | flops | bytes accessed | tf_op | source)
XLA Modules:
  0.0 454.3 jit_solution(11651553903876879074)
XLA Ops:
  16.1 6.3 %all-to-all-start = ((bf16[32,8,128]{2,1,0:T(8,128)(2,1)}), bf16[32,8,128]{2,1,0:T(8,128)(2,1)S(1)}, u32[]{:S(2)}, u32[]{:S(2)}) async-start(bf16[32,8,128]{2,1,0:T(8,128)(2,1)} %broadcast_in_dim.15), calls=%async_computation | async-start | bytes 131072 | tf_op jit(solution)/shard_map/all_to_all | solution.py:357
  23.7 7.5 %all-to-all-done = bf16[32,8,128]{2,1,0:T(8,128)(2,1)S(1)} async-done(((bf16[32,8,128]{2,1,0:T(8,128)(2,1)}), bf16[32,8,128]{2,1,0:T(8,128)(2,1)S(1)}, u32[]{:S(2)}, u32[]{:S(2)}) %all-to-all-start) | async-done | bytes 65568 | tf_op jit(solution)/shard_map/all_to_all | solution.py:357
  31.3 12.5 %all-gather.8.cloned.1.call-done = bf16[896,1152]{1,0:T(8,128)(2,1)} async-done(((bf16[112,1152]{1,0:T(8,128)(2,1)}), bf16[896,1152]{1,0:T(8,128)(2,1)}) %all-gather.8.cloned.1.call-update) | async-done | bytes 2064400 | tf_op jit(solution)/shard_map/all_gather | solution.py:348
  60.9 8.4 %collective-permute-done.4 = bf16[160,1152]{1,0:T(8,128)(2,1)S(1)} collective-permute-done((bf16[160,1152]{1,0:T(8,128)(2,1)}, bf16[160,1152]{1,0:T(8,128)(2,1)S(1)}, u32[]{:S(2)}, u32[]{:S(2)}) %collective-permute-start.4) | collective-permute-done | bytes 368672 | tf_op jit(solution)/shard_map/ppermute | solution.py:309
  90.1 23.5 %all_gather.21 = bf16[1152,432]{1,0:T(8,128)(2,1)S(1)} all-gather(bf16[288,432]{1,0:T(8,128)(2,1)S(1)} %reshape.214), channel_id=1, replica_groups=mesh['dp'=4,'seq'=8] {'dp'}, dimensions={0}, use_global_device_ids=true | all-gather | bytes 1244160 | tf_op jit(solution)/shard_map/all_gather | solution.py:398
  126.5 8.4 %shard_map.288 = (f32[1280,256]{1,0:T(8,128)S(1)}, bf16[1280,144]{1,0:T(8,128)(2,1)S(1)}, f32[8,1280]{1,0:T(8,128)S(1)}) custom-call(bf16[1280,768]{1,0:T(8,128)(2,1)S(1)} %convolution_convert_fusion.4.q_ref.k_ref.v_ref, bf16[1280,768]{1,0:T(8,128)(2,1)S(1)} %convolution_convert_fusion.4.q_ref.k_ref.v_ref, ...), custom_call_target="tpu_custom_call" | custom-call | flops 3355443200 | bytes 3276800 | tf_op jit(solution)/shard_map/pallas_call | solution.py:84
  156.7 20.2 %all-to-all-done.2 = bf16[8,160,144]{1,2,0:T(8,128)(2,1)S(1)} async-done(((bf16[8,160,144]{1,2,0:T(8,128)(2,1)}), bf16[8,160,144]{1,2,0:T(8,128)(2,1)S(1)}, u32[]{:S(2)}, u32[]{:S(2)}) %all-to-all-start.2) | async-done | bytes 368672 | tf_op jit(solution)/shard_map/all_to_all | solution.py:333
  187.4 7.0 %collective-permute-done.18 = bf16[160,1152]{1,0:T(8,128)(2,1)S(1)} collective-permute-done((bf16[160,1152]{1,0:T(8,128)(2,1)S(1)}, bf16[160,1152]{1,0:T(8,128)(2,1)S(1)}, u32[]{:S(2)}, u32[]{:S(2)}) %collective-permute-start.18) | collective-permute-done | bytes 368672 | tf_op jit(solution)/shard_map/ppermute | solution.py:309
  194.4 6.9 %collective-permute-done.19 = bf16[160,1152]{1,0:T(8,128)(2,1)S(1)} collective-permute-done((bf16[160,1152]{1,0:T(8,128)(2,1)S(1)}, bf16[160,1152]{1,0:T(8,128)(2,1)S(1)}, u32[]{:S(2)}, u32[]{:S(2)}) %collective-permute-start.19) | collective-permute-done | bytes 368672 | tf_op jit(solution)/shard_map/ppermute | solution.py:309
  207.2 5.4 %convolution_convert_fusion.3.up_ref = bf16[1152,1152]{1,0:T(8,128)(2,1)} fusion(bf16[1152,1152]{1,0:T(8,128)(2,1)S(1)} %copy-done.17, bf16[1152,1152]{1,0:T(8,128)(2,1)S(1)} %bitcast.164), kind=kOutput, calls=%fused_computation.11 | convolution fusion | flops 3058974720 | bytes 7962624 | tf_op jit(solution)/shard_map/dot_general | solution.py:50
  212.7 10.2 %shard_map.289 = (bf16[640,1152]{1,0:T(8,128)(2,1)}, bf16[640,1152]{1,0:T(8,128)(2,1)}, f32[1,1152]{1,0:T(1,128)S(1)}, f32[160,1152]{1,0:T(8,128)S(1)}, bf16[160...) custom-call(bf16[640,1152]{1,0:T(8,128)(2,1)} %pad_maximum_fusion.1.x_ref, ...), custom_call_target="tpu_custom_call" | custom-call | flops 5096079360 | bytes 12681216 | tf_op jit(solution)/shard_map/pallas_call | solution.py:265
  226.4 8.0 %collective-permute-done.21 = bf16[160,1152]{1,0:T(8,128)(2,1)S(1)} collective-permute-done((bf16[160,1152]{1,0:T(8,128)(2,1)S(1)}, bf16[160,1152]{1,0:T(8,128)(2,1)S(1)}, u32[]{:S(2)}, u32[]{:S(2)}) %collective-permute-start.21) | collective-permute-done | bytes 368672 | tf_op jit(solution)/shard_map/ppermute | solution.py:309
  235.2 5.3 %convolution_convert_fusion.2 = bf16[1152,1152]{1,0:T(8,128)(2,1)} fusion(bf16[640,1152]{1,0:T(8,128)(2,1)} %get-tuple-element.122, bf16[640,1152]{1,0:T(8,128)(2,1)S(1)} %copy-done.20), kind=kOutput, calls=%fused_computation.10 | convolution fusion | flops 1700020224 | bytes 5603328 | tf_op jit(solution)/shard_map/dot_general | solution.py:50
  240.5 9.4 %convolution_convert_fusion.1 = bf16[1152,1152]{1,0:T(8,128)(2,1)} fusion(bf16[640,1152]{1,0:T(8,128)(2,1)} %get-tuple-element.119, bf16[640,1152]{1,0:T(8,128)(2,1)} %pad_maximum_fusion.1.x_ref, bf16[1152,1152]{1,0:T(8,128)(2,1)} %fusion.10), kind=kOutput, calls=%fused_computation.9 | convolution fusion | flops 3399450624 | bytes 8257536 | tf_op jit(solution)/shard_map/dot_general | solution.py:50
  264.7 6.1 %fusion.64 = (bf16[640,1152]{1,0:T(8,128)(2,1)S(1)}, f32[640,1152]{1,0:T(8,128)}) fusion(bf16[640,1152]{1,0:T(8,128)(2,1)} %get-tuple-element.122, bf16[1152,1152]{1,0:T(8,128)(2,1)} %bitcast.163), kind=kOutput, calls=%fused_computation.182 | convolution fusion | flops 1699430400 | bytes 8552448 | tf_op jit(solution)/shard_map/dot_general | solution.py:46
  278.5 8.0 %all-to-all-done.3 = bf16[8,160,144]{1,2,0:T(8,128)(2,1)} async-done(((bf16[8,160,144]{1,2,0:T(8,128)(2,1)}), bf16[8,160,144]{1,2,0:T(8,128)(2,1)}, u32[]{:S(2)}, u32[]{:S(2)}) %all-to-all-start.3) | async-done | bytes 368672 | tf_op jit(solution)/shard_map/all_to_all | solution.py:333
  288.1 14.1 %shard_map.291 = (bf16[1280,144]{1,0:T(8,128)(2,1)S(1)}, bf16[1280,288]{1,0:T(8,128)(2,1)S(1)}) custom-call(bf16[1280,768]{1,0:T(8,128)(2,1)} %copy-done, bf16[1280,768]{1,0:T(8,128)(2,1)} %copy-done, bf16[1280,768]{1,0:T(8,128)(2,1)} %copy-done, bf16[1280,256]{1,0:T(8,128)(2,1)S(1)} %pad.23.out_grad_ref, f32[1280,256]{1,0:T(8,128)S(1)} %get-tuple-element.126.out_ref, ...), custom_call_target="tpu_custom_call" | custom-call | flops 8388608000 | bytes 4587520 | tf_op jit(solution)/shard_map/pallas_call | solution.py:164
  326.8 8.5 %collective-permute-done.28 = bf16[160,1152]{1,0:T(8,128)(2,1)S(1)} collective-permute-done((bf16[160,1152]{1,0:T(8,128)(2,1)S(1)}, bf16[160,1152]{1,0:T(8,128)(2,1)S(1)}, u32[]{:S(2)}, u32[]{:S(2)}) %collective-permute-start.28) | collective-permute-done | bytes 368672 | tf_op jit(solution)/shard_map/ppermute | solution.py:309
  342.3 5.2 %collective-permute-done.30 = bf16[288,432]{1,0:T(8,128)(2,1)S(1)} collective-permute-done((bf16[288,432]{1,0:T(8,128)(2,1)S(1)}, bf16[288,432]{1,0:T(8,128)(2,1)S(1)}, u32[]{:S(2)}, u32[]{:S(2)}) %collective-permute-start.30) | collective-permute-done | bytes 248864 | tf_op jit(solution)/shard_map/ppermute | solution.py:309
  347.5 5.4 %collective-permute-done.31 = bf16[288,432]{1,0:T(8,128)(2,1)S(1)} collective-permute-done((bf16[288,432]{1,0:T(8,128)(2,1)S(1)}, bf16[288,432]{1,0:T(8,128)(2,1)S(1)}, u32[]{:S(2)}, u32[]{:S(2)}) %collective-permute-start.31) | collective-permute-done | bytes 248864 | tf_op jit(solution)/shard_map/ppermute | solution.py:309
  377.5 5.2 %all-to-all-done.4 = bf16[8,36,432]{2,1,0:T(8,128)(2,1)S(1)} async-done(((bf16[8,36,432]{2,1,0:T(8,128)(2,1)}), bf16[8,36,432]{2,1,0:T(8,128)(2,1)S(1)}, u32[]{:S(2)}, u32[]{:S(2)}) %all-to-all-start.4) | async-done | bytes 248864 | tf_op jit(solution)/shard_map/all_to_all | solution.py:333
  388.6 9.6 %reduce-scatter.11.cloned.1.call-done = bf16[144,1152]{1,0:T(8,128)(2,1)} async-done(((bf16[1152,1152]{1,0:T(8,128)(2,1)}), bf16[144,1152]{1,0:T(8,128)(2,1)}) %reduce-scatter.11.cloned.1.call-update) | async-done | bytes 331792 | tf_op jit(solution)/shard_map/reduce_scatter | solution.py:501
  422.2 5.2 %collective-permute-done.41 = bf16[160,576]{0,1:T(8,128)(2,1)S(1)} collective-permute-done((bf16[160,576]{0,1:T(8,128)(2,1)S(1)}, bf16[160,576]{0,1:T(8,128)(2,1)S(1)}, u32[]{:S(2)}, u32[]{:S(2)}) %collective-permute-start.41) | collective-permute-done | bytes 184352 | tf_op jit(solution)/shard_map/ppermute | solution.py:309
  438.1 6.6 %all-to-all-done.5 = bf16[4,36,1152]{2,1,0:T(8,128)(2,1)S(1)} async-done(((bf16[4,36,1152]{2,1,0:T(8,128)(2,1)}), bf16[4,36,1152]{2,1,0:T(8,128)(2,1)S(1)}, u32[]{:S(2)}, u32[]{:S(2)}) %all-to-all-start.5) | async-done | bytes 331808 | tf_op jit(solution)/shard_map/all_to_all | solution.py:343
  (354 shorter events, 222.5 us)
Async XLA Ops:
  7.2 36.6 %all-gather.8.cloned.1.call-start = ((), (), s32[]{:S(2)}) async-start(), calls=%async_computation.15 | async-start | bytes 2322432 | tf_op jit(solution)/shard_map/all_gather | solution.py:348
  10.8 20.4 %collective-permute-start = (bf16[160,576]{1,0:T(8,128)(2,1)S(1)}, bf16[160,576]{1,0:T(8,128)(2,1)S(1)}, u32[]{:S(2)}, u32[]{:S(2)}) collective-permute-start(bf16[160,576]{1,0:T(8,128)(2,1)S(1)} %get-tuple-element.190), channel_id=1, source_target_pairs={{0,8},{8,0},{16,24},{24,16},{1,9},{9,1},{17,25},{25,17},{2,10},{10... | collective-permute-start | bytes 552968 | tf_op jit(solution)/shard_map/ppermute | solution.py:309
  59.3 58.5 %all-gather.6.cloned.1.call-start = ((), (), s32[]{:S(2)}) async-start(), calls=%async_computation.11 | async-start | bytes 3317760 | tf_op jit(solution)/shard_map/all_gather | solution.py:396
  73.0 129.6 %all-gather.10.cloned.1.call-start = ((), (), s32[]{:S(2)}) async-start(), calls=%async_computation.16 | async-start | bytes 5971968 | tf_op jit(solution)/shard_map/all_gather | solution.py:412
  86.5 31.3 %collective-permute-start.10 = (bf16[144,1152]{1,0:T(8,128)(2,1)}, bf16[144,1152]{1,0:T(8,128)(2,1)}, u32[]{:S(2)}, u32[]{:S(2)}) collective-permute-start(bf16[144,1152]{1,0:T(8,128)(2,1)} %constant_dynamic-slice_fusion.5), channel_id=1, source_target_pairs={{0,16},{8,24},{16,0},{24,8},{1,17},{9,25},{17,1},{25,9},{2,18},{10... | collective-permute-start | bytes 995336 | tf_op jit(solution)/shard_map/ppermute | solution.py:309
  88.0 29.8 %collective-permute-start.11 = (bf16[144,1152]{1,0:T(8,128)(2,1)}, bf16[144,1152]{1,0:T(8,128)(2,1)}, u32[]{:S(2)}, u32[]{:S(2)}) collective-permute-start(bf16[144,1152]{1,0:T(8,128)(2,1)} %constant_dynamic-slice_fusion.5), channel_id=1, source_target_pairs={{0,24},{8,16},{16,8},{24,0},{1,25},{9,17},{17,9},{25,1},{2,26},{10... | collective-permute-start | bytes 995336 | tf_op jit(solution)/shard_map/ppermute | solution.py:309
  89.2 28.7 %collective-permute-start.9 = (bf16[144,1152]{1,0:T(8,128)(2,1)}, bf16[144,1152]{1,0:T(8,128)(2,1)}, u32[]{:S(2)}, u32[]{:S(2)}) collective-permute-start(bf16[144,1152]{1,0:T(8,128)(2,1)} %constant_dynamic-slice_fusion.5), channel_id=1, source_target_pairs={{0,8},{8,0},{16,24},{24,16},{1,9},{9,1},{17,25},{25,17},{2,10},{10... | collective-permute-start | bytes 995336 | tf_op jit(solution)/shard_map/ppermute | solution.py:309
  122.0 23.0 %collective-permute-start.15 = (bf16[144,1152]{1,0:T(8,128)(2,1)}, bf16[144,1152]{1,0:T(8,128)(2,1)}, u32[]{:S(2)}, u32[]{:S(2)}) collective-permute-start(bf16[144,1152]{1,0:T(8,128)(2,1)} %collective-permute-done.9), channel_id=1, source_target_pairs={{0,1},{1,0},{2,3},{3,2},{4,5},{5,4},{6,7},{7,6},{8,9},{9,8},{10,11... | collective-permute-start | bytes 995336 | tf_op jit(solution)/shard_map/ppermute | solution.py:312
  139.6 37.3 %all-to-all-start.2 = ((bf16[8,160,144]{1,2,0:T(8,128)(2,1)}), bf16[8,160,144]{1,2,0:T(8,128)(2,1)S(1)}, u32[]{:S(2)}, u32[]{:S(2)}) async-start(bf16[8,160,144]{1,2,0:T(8,128)(2,1)} %copy.80), calls=%async_computation.2 | async-start | bytes 1179648 | tf_op jit(solution)/shard_map/all_to_all | solution.py:333
  143.2 166.7 %reduce-scatter.7.cloned.1.call-start = ((), (), s32[]{:S(2)}) async-start(), calls=%async_computation.12 | async-start | bytes 2985984 | tf_op jit(solution)/shard_map/reduce_scatter | solution.py:452
  224.6 25.4 %collective-permute-start.22 = (bf16[160,1152]{1,0:T(8,128)(2,1)S(1)}, bf16[160,1152]{1,0:T(8,128)(2,1)}, u32[]{:S(2)}, u32[]{:S(2)}) collective-permute-start(bf16[160,1152]{1,0:T(8,128)(2,1)S(1)} %get-tuple-element.115), channel_id=1, source_target_pairs={{0,16},{8,24},{16,0},{24,8},{1,17},{9,25},{17,1},{25,9},{2,18},{10... | collective-permute-start | bytes 1105928 | tf_op jit(solution)/shard_map/ppermute | solution.py:309
  224.9 25.1 %collective-permute-start.23 = (bf16[160,1152]{1,0:T(8,128)(2,1)S(1)}, bf16[160,1152]{1,0:T(8,128)(2,1)}, u32[]{:S(2)}, u32[]{:S(2)}) collective-permute-start(bf16[160,1152]{1,0:T(8,128)(2,1)S(1)} %get-tuple-element.116), channel_id=1, source_target_pairs={{0,24},{8,16},{16,8},{24,0},{1,25},{9,17},{17,9},{25,1},{2,26},{10... | collective-permute-start | bytes 1105928 | tf_op jit(solution)/shard_map/ppermute | solution.py:309
  260.4 26.1 %all-to-all-start.3 = ((bf16[8,160,144]{1,2,0:T(8,128)(2,1)}), bf16[8,160,144]{1,2,0:T(8,128)(2,1)}, u32[]{:S(2)}, u32[]{:S(2)}) async-start(bf16[8,160,144]{1,2,0:T(8,128)(2,1)} %copy.82), calls=%async_computation.3 | async-start | bytes 1179648 | tf_op jit(solution)/shard_map/all_to_all | solution.py:333
  264.6 92.4 %reduce-scatter.9.cloned.1.call-start = ((), (), s32[]{:S(2)}) async-start(), calls=%async_computation.13 | async-start | bytes 3317760 | tf_op jit(solution)/shard_map/reduce_scatter | solution.py:482
  276.6 30.8 %collective-permute-start.25 = (bf16[160,1152]{1,0:T(8,128)(2,1)}, bf16[160,1152]{1,0:T(8,128)(2,1)}, u32[]{:S(2)}, u32[]{:S(2)}) collective-permute-start(bf16[160,1152]{1,0:T(8,128)(2,1)} %get-tuple-element.174), channel_id=1, source_target_pairs={{0,16},{8,24},{16,0},{24,8},{1,17},{9,25},{17,1},{25,9},{2,18},{10... | collective-permute-start | bytes 1105928 | tf_op jit(solution)/shard_map/ppermute | solution.py:309
  276.9 30.5 %collective-permute-start.26 = (bf16[160,1152]{1,0:T(8,128)(2,1)}, bf16[160,1152]{1,0:T(8,128)(2,1)}, u32[]{:S(2)}, u32[]{:S(2)}) collective-permute-start(bf16[160,1152]{1,0:T(8,128)(2,1)} %get-tuple-element.175), channel_id=1, source_target_pairs={{0,24},{8,16},{16,8},{24,0},{1,25},{9,17},{17,9},{25,1},{2,26},{10... | collective-permute-start | bytes 1105928 | tf_op jit(solution)/shard_map/ppermute | solution.py:309
  309.9 88.3 %reduce-scatter.11.cloned.1.call-start = ((), (), s32[]{:S(2)}) async-start(), calls=%async_computation.14 | async-start | bytes 2985984 | tf_op jit(solution)/shard_map/reduce_scatter | solution.py:501
  310.3 25.1 %collective-permute-start.33 = (bf16[160,288]{1,0:T(8,128)(2,1)S(1)}, bf16[160,288]{1,0:T(8,128)(2,1)S(1)}, u32[]{:S(2)}, u32[]{:S(2)}) collective-permute-start(bf16[160,288]{1,0:T(8,128)(2,1)S(1)} %get-tuple-element.198), channel_id=1, source_target_pairs={{0,8},{8,0},{16,24},{24,16},{1,9},{9,1},{17,25},{25,17},{2,10},{10... | collective-permute-start | bytes 276488 | tf_op jit(solution)/shard_map/ppermute | solution.py:309
  311.9 23.5 %collective-permute-start.34 = (bf16[160,288]{1,0:T(8,128)(2,1)S(1)}, bf16[160,288]{1,0:T(8,128)(2,1)S(1)}, u32[]{:S(2)}, u32[]{:S(2)}) collective-permute-start(bf16[160,288]{1,0:T(8,128)(2,1)S(1)} %get-tuple-element.197), channel_id=1, source_target_pairs={{0,16},{8,24},{16,0},{24,8},{1,17},{9,25},{17,1},{25,9},{2,18},{10... | collective-permute-start | bytes 276488 | tf_op jit(solution)/shard_map/ppermute | solution.py:309
  313.9 21.4 %collective-permute-start.28 = (bf16[160,1152]{1,0:T(8,128)(2,1)S(1)}, bf16[160,1152]{1,0:T(8,128)(2,1)S(1)}, u32[]{:S(2)}, u32[]{:S(2)}) collective-permute-start(bf16[160,1152]{1,0:T(8,128)(2,1)S(1)} %copy-done.13), channel_id=1, source_target_pairs={{0,16},{8,24},{16,0},{24,8},{1,17},{9,25},{17,1},{25,9},{2,18},{10... | collective-permute-start | bytes 1105928 | tf_op jit(solution)/shard_map/ppermute | solution.py:309
  314.4 20.8 %collective-permute-start.29 = (bf16[160,1152]{1,0:T(8,128)(2,1)S(1)}, bf16[160,1152]{1,0:T(8,128)(2,1)S(1)}, u32[]{:S(2)}, u32[]{:S(2)}) collective-permute-start(bf16[160,1152]{1,0:T(8,128)(2,1)S(1)} %copy-done.13), channel_id=1, source_target_pairs={{0,24},{8,16},{16,8},{24,0},{1,25},{9,17},{17,9},{25,1},{2,26},{10... | collective-permute-start | bytes 1105928 | tf_op jit(solution)/shard_map/ppermute | solution.py:309
  363.1 19.6 %all-to-all-start.4 = ((bf16[8,36,432]{2,1,0:T(8,128)(2,1)}), bf16[8,36,432]{2,1,0:T(8,128)(2,1)S(1)}, u32[]{:S(2)}, u32[]{:S(2)}) async-start(bf16[8,36,432]{2,1,0:T(8,128)(2,1)} %reshape.228), calls=%async_computation.6 | async-start | bytes 655360 | tf_op jit(solution)/shard_map/all_to_all | solution.py:333
  366.5 78.9 %reduce-scatter.13.cloned.1.call-start = ((), (), s32[]{:S(2)}) async-start(), calls=%async_computation.17 | async-start | bytes 1492992
  402.3 28.0 %all-to-all-start.6 = ((f32[32,8,128]{2,1,0:T(8,128)}), f32[32,8,128]{2,1,0:T(8,128)}, u32[]{:S(2)}, u32[]{:S(2)}) async-start(f32[32,8,128]{2,1,0:T(8,128)} %bitcast.75), calls=%async_computation.9 | async-start | bytes 262144 | tf_op jit(solution)/shard_map/all_to_all | solution.py:536
  (84 other events, 919.3 us)
Sparse Core Ops, SparseCore 0:
  10.2 33.4 all-gather.7
  73.1 34.6 all-gather.5
  118.9 66.9 all-gather.9
  240.6 40.9 reduce-scatter.6
  310.0 38.4 reduce-scatter.8
  357.1 41.0 reduce-scatter.10
  400.6 32.9 reduce-scatter.12

commit v11 on v8

--- a/solution.py
+++ b/solution.py
@@ -227,10 +227,10 @@
     )(x, w)
 
 
-def gelu_kernel(rows_at_once, x_ref, w_ref, bias_ref, value_ref, slope_ref):
+def gelu_kernel(rows_at_once, x_ref, up_ref, bias_ref, value_ref, slope_ref):
     for start in range(0, x_ref.shape[0], rows_at_once):
         at = pl.ds(start, rows_at_once)
-        pre = dot(x_ref[at, :], w_ref[...]) + bias_ref[...]
+        pre = dot(x_ref[at, :], up_ref[...]) + bias_ref[...]
         bell = jnp.exp(-0.5 * pre * pre)
         t = 1.0 / (1.0 + (0.3275911 * 0.5**0.5) * jnp.abs(pre))
         tail = 0.5 * 1.061405429
@@ -242,14 +242,13 @@
         slope_ref[at, :] = below + pre * bell * (0.5 / math.pi) ** 0.5
 
 
-def gelu_of_matmul(x, w, bias):
+def gelu_of_matmul(x, up, bias):
     rows, depth = x.shape
-    columns = w.shape[1]
+    columns = up.shape[1]
     step = 384 if columns % 384 == 0 else columns
-    rows_at_once = 160 if rows % 160 == 0 else rows
     block = pl.BlockSpec((rows, step), lambda j: (0, j))
     return pl.pallas_call(
-        partial(gelu_kernel, rows_at_once),
+        partial(gelu_kernel, 640 if rows % 640 == 0 else rows),
         grid=(columns // step,),
         in_specs=[
             pl.BlockSpec((rows, depth), lambda j: (0, 0)),
@@ -267,7 +266,40 @@
             bytes_accessed=2 * depth * (rows + columns) + 6 * rows * columns,
             transcendentals=rows * columns,
         ),
-    )(x, w, bias.reshape(1, columns))
+    )(x, up, bias.reshape(1, columns))
+
+
+def feed_back_kernel(
+    local, grad_ref, up_ref, down_ref, slope_ref, low_ref, sums_ref, own_ref, *back_refs
+):
+    pre_grad = times_transposed(grad_ref[...], down_ref[...]) * slope_ref[...]
+    sums_ref[...] = jnp.sum(pre_grad, axis=0, keepdims=True)
+    low = pre_grad.astype(BF16)
+    low_ref[...] = low
+    back = times_transposed(low, up_ref[...])
+    own_ref[...] = back[:local]
+    for k, back_ref in enumerate(back_refs):
+        back_ref[...] = back[(k + 1) * local : (k + 2) * local].astype(BF16)
+
+
+def feed_back(grad, up, down, slope, local):
+    rows, depth = grad.shape
+    columns = up.shape[1]
+    return pl.pallas_call(
+        partial(feed_back_kernel, local),
+        out_shape=[
+            jax.ShapeDtypeStruct((rows, columns), BF16),
+            jax.ShapeDtypeStruct((1, columns), F32),
+            jax.ShapeDtypeStruct((local, depth), F32),
+        ]
+        + [jax.ShapeDtypeStruct((local, depth), BF16)] * (rows // local - 1),
+        compiler_params=pltpu.CompilerParams(vmem_limit_bytes=52 * 2**20),
+        cost_estimate=pl.CostEstimate(
+            flops=4 * rows * depth * columns,
+            bytes_accessed=4 * depth * columns + 6 * rows * columns + 4 * rows * depth,
+            transcendentals=0,
+        ),
+    )(grad, up, down, slope)
 
 
 def on_device(
@@ -379,18 +411,18 @@
     normed_one_row = lax.all_gather(normed_one, "seq", axis=0, tiled=True)
 
     qkv_mine = seq_exchange(qkv_out).reshape(part, wide)
-    qkv_blocks = jnp.stack([qkv_mine] + [swap(qkv_mine, k) for k in range(1, nd)])
-    qkv_mine = jnp.concatenate([index(qkv_blocks, dp_at ^ k) for k in range(nd)], axis=0)
-    up_slices = jnp.swapaxes(fc1_w.reshape(small, nd, hidden_part), 0, 1)
+    half = part // 2
+    own_half = lax.dynamic_slice_in_dim(proj_rows, core * half, half, 0)
+    proj_halves = [swap(own_half, k) for k in range(1, nd)]
+    qkv_mine, own_up, proj_halves = after((qkv_mine, fc1_w, proj_halves))
+    qkv_mine = lax.all_gather(qkv_mine, "dp", axis=0, tiled=True)
+    up_slices = jnp.swapaxes(own_up.reshape(small, nd, hidden_part), 0, 1)
     up_slices = jnp.concatenate(
         [index(up_slices, dp_at)] + [swap(index(up_slices, dp_at ^ k), k) for k in range(1, nd)],
         axis=0,
     )
-    half = part // 2
-    own_half = lax.dynamic_slice_in_dim(proj_rows, core * half, half, 0)
-    proj_halves = [swap(own_half, k) for k in range(1, nd)]
-    normed_one_row, up_slices, qkv_mine, qkv_wide, segments, proj_halves = after(
-        (normed_one_row, up_slices, qkv_mine, widen(qkv_mine), segments, proj_halves)
+    normed_one_row, up_slices, qkv_mine, qkv_wide, segments = after(
+        (normed_one_row, up_slices, qkv_mine, widen(qkv_mine), segments)
     )
     up_part = lax.all_gather(up_slices, "seq", axis=0, tiled=True)
     triple = dot(normed_one_row, qkv_wide).astype(BF16)
@@ -400,6 +432,9 @@
         v = seq_exchange(v.reshape(ns, local, head_cols))
         return jnp.swapaxes(v, 0, 1).reshape(local, features)
 
+    attended_low, grad_out, proj_halves, proj_rows = after(
+        (attended_low, cotangent[0], proj_halves, proj_rows)
+    )
     w_proj = lax.dynamic_update_slice_in_dim(
         jnp.zeros((features, features), BF16), proj_rows, dp_at * part, 0
     )
@@ -409,10 +444,11 @@
         there = other_core(here)
         w_proj = lax.dynamic_update_slice_in_dim(w_proj, here, (place + core) * half, 0)
         w_proj = lax.dynamic_update_slice_in_dim(w_proj, there, (place + 1 - core) * half, 0)
-    attended_low, grad_out = after((attended_low, cotangent[0]))
     grad_out_rows = gather_rows(grad_out)
     attended_low = heads_to_tokens(attended_low)
-    attended_low, grad_out_rows, w_proj = after((attended_low, grad_out_rows, w_proj))
+    attended_low, grad_out_rows, w_proj, order = after(
+        (attended_low, grad_out_rows, w_proj, order)
+    )
     own_down, attended_low, up_part = after((fc2_w, attended_low, up_part))
     down_part = lax.all_gather(own_down, "seq", axis=0, tiled=True)
     second = first + dot(attended_low, w_proj) + b_proj
@@ -425,44 +461,47 @@
     hidden, slope = gelu_of_matmul(normed_two_rows, up_part, up_bias)
 
     fc2_terms = inner(hidden, grad_out_rows).astype(BF16)
+    fc2_w_grad = lax.psum_scatter(fc2_terms, "seq", scatter_dimension=0, tiled=True)
     slope, fc2_terms = after((slope, fc2_terms))
-    fc2_w_grad = lax.psum_scatter(fc2_terms, "seq", scatter_dimension=0, tiled=True)
-    pre_grad = times_transposed(grad_out_rows, down_part) * slope
-    pre_low = pre_grad.astype(BF16)
-    up_back = times_transposed(pre_low, up_part)
-    up_low = low_rows(up_back)
-    up_low, pre_late, normed_two_rows = after((up_low, pre_low, normed_two_rows))
-    normed_two_grad = add_blocks(up_back[:local], up_low)
-    fc1_terms = inner(times_transposed(normed_two_rows, order).astype(BF16), pre_late).astype(BF16)
-    normed_two_grad, fc1_terms, fc2_w_grad = after((normed_two_grad, fc1_terms, fc2_w_grad))
-    fc1_terms = lax.psum_scatter(fc1_terms, "seq", scatter_dimension=0, tiled=True)
+    pre_low, up_sums, normed_two_grad, *up_blocks = feed_back(
+        grad_out_rows, up_part, down_part, slope, local
+    )
+    up_blocks = [swap(block, k + 1) for k, block in enumerate(up_blocks)]
+    fc1_terms = inner(times_transposed(normed_two_rows, order).astype(BF16), pre_low).astype(BF16)
+    for block in up_blocks:
+        normed_two_grad = normed_two_grad + block.astype(F32)
+    normed_two_grad, fc1_terms = after((normed_two_grad, fc1_terms))
     through_two, ln2_g_grad, ln2_b_grad = norm_back(normed_two_grad, xhat_two, inverse_two, g_two)
     second_grad = grad_out.astype(F32) + through_two
     second_low = second_grad.astype(BF16)
     attended_grad = product_by_group(second_low, w_proj, ns)
-    attended_grad, second_late, hidden_late, attended_low = after(
-        (attended_grad, second_low, hidden, attended_low)
-    )
+    attended_grad, second_late, hidden_late, attended_low, fc1_terms = after(
+        (attended_grad, second_low, hidden, attended_low, fc1_terms)
+    )
+    fc1_terms = lax.psum_scatter(fc1_terms, "seq", scatter_dimension=0, tiled=True)
     attended_grad = seq_exchange(attended_grad).reshape(row_len, head_cols)
     down_sums = dot(hidden_late, down_part)
     attended_slices = jnp.swapaxes(attended_low.reshape(local, nd, part), 0, 1)
-    attended_grad, down_sums, second_late, attended_slices = after(
-        (attended_grad, down_sums, second_late, attended_slices)
-    )
-    second_blocks = [second_late] + [swap(second_late, k) for k in range(1, nd)]
+    down_blocks = low_rows(down_sums)
+    down_blocks = [swap(down_blocks[k], k) for k in range(1, nd)]
+    attended_grad, down_blocks[0], second_late, attended_slices = after(
+        (attended_grad, down_blocks[0], second_late, attended_slices)
+    )
     triple_grad = jnp.concatenate(
         attend_back(triple, attended_grad, attended, lse, segments, heads, scale), axis=1
     )
     one_back = times_transposed(triple_grad, qkv_mine).astype(BF16)
-    one_back, triple_late, fc1_terms, down_sums, second_rows = after(
-        (one_back, triple_grad, fc1_terms, down_sums, jnp.concatenate(second_blocks, axis=0))
+    output = second + down_sums[:local] + b_down
+    for block in down_blocks:
+        output = output + block.astype(F32)
+    output = output.astype(BF16)
+    one_back, triple_late, output, second_late, fc1_terms, fc2_w_grad = after(
+        (one_back, triple_grad, output, second_late, fc1_terms, fc2_w_grad)
     )
     normed_one_grad = lax.psum_scatter(one_back, "seq", scatter_dimension=0, tiled=True)
+    second_rows = gather_rows(second_late)
     qkv_terms = inner(normed_one_row, triple_late).reshape(nd, part, wide)
-    qkv_low, down_low = qkv_terms.astype(BF16), low_rows(down_sums)
-    qkv_low, down_low, second_rows, attended_slices = after(
-        (qkv_low, down_low, second_rows, attended_slices)
-    )
+    qkv_low, second_rows = after((qkv_terms.astype(BF16), second_rows))
     qkv_blocks = [swap(index(qkv_low, dp_at ^ k), k) for k in range(1, nd)]
     attended_rows = jnp.concatenate(
         [index(attended_slices, dp_at)]
@@ -470,23 +509,27 @@
         axis=0,
     )
     proj_terms = inner(attended_rows, second_rows).reshape(ns, small, features)
-    proj_w_grad = chip_sums(core_sums(proj_terms))
-    output = (second + add_blocks(down_sums[:local], down_low) + b_down).astype(BF16)
+    proj_sums = core_sums(proj_terms)
     qkv_sum = index(qkv_terms, dp_at)
     for block in qkv_blocks:
         qkv_sum = qkv_sum + block.astype(F32)
     qkv_sum = qkv_sum.astype(BF16).reshape(ns, small, wide)
-    fc1_terms = fc1_terms.reshape(nd, small, hidden_part)
-    fc1_blocks = jnp.stack([fc1_terms[0]] + [swap(fc1_terms[k], k) for k in range(1, nd)])
-    normed_one_grad, qkv_sum, fc1_blocks, proj_w_grad, output = after(
-        (normed_one_grad, qkv_sum, fc1_blocks, proj_w_grad, output)
-    )
+    normed_one_grad, qkv_sum, proj_sums = after((normed_one_grad, qkv_sum, proj_sums))
     normed_one_grad = normed_one_grad.astype(F32)
     through_one, ln1_g_grad, ln1_b_grad = norm_back(normed_one_grad, xhat_one, inverse_one, g_one)
     first_grad = second_grad + through_one
     first_low = first_grad.astype(BF16)
     first_low_rows = gather_rows(first_low)
     qkv_w_grad = seq_exchange(qkv_sum)
+    first_low_rows, first_grad, qkv_w_grad = after((first_low_rows, first_grad, qkv_w_grad))
+    skip_terms = inner(joined_here, first_low_rows).astype(BF16)
+    skip_w_grad = lax.psum_scatter(skip_terms, "seq", scatter_dimension=0, tiled=True).astype(F32)
+    skip_terms, first_low_rows, first_grad, fc1_terms, proj_sums, qkv_w_grad = after(
+        (skip_terms, first_low_rows, first_grad, fc1_terms, proj_sums, qkv_w_grad)
+    )
+    proj_w_grad = chip_sums(proj_sums)
+    fc1_terms = fc1_terms.reshape(nd, small, hidden_part)
+    fc1_blocks = jnp.stack([fc1_terms[0]] + [swap(fc1_terms[k], k) for k in range(1, nd)])
     vector_grads = jnp.stack(
         [
             jnp.sum(first_grad, axis=0),
@@ -499,7 +542,7 @@
         ]
     )
     vector_grads = jnp.swapaxes(vector_grads.reshape(7, n, small), 0, 1).reshape(n, 7 * small)
-    up_grads = jnp.sum(pre_grad, axis=0).reshape(ns, hidden_units // n)
+    up_grads = up_sums.reshape(ns, hidden_units // n)
     up_grads = lax.dynamic_update_slice_in_dim(
         jnp.zeros((n, hidden_units // n), F32), up_grads, dp_at * ns, 0
     )
@@ -508,15 +551,11 @@
     vector_grads = lax.all_to_all(
         vector_grads.reshape(n, padded // 128, 128), ("dp", "seq"), 0, 0, tiled=True
     )
-    first_low_rows, qkv_w_grad, vector_grads = after((first_low_rows, qkv_w_grad, vector_grads))
-    skip_terms = inner(joined_here, first_low_rows).astype(BF16)
-    skip_w_grad = lax.psum_scatter(skip_terms, "seq", scatter_dimension=0, tiled=True).astype(F32)
-    skip_terms, first_low_rows = after((skip_terms, first_low_rows))
     joined_grad_part = times_transposed(first_low_rows, skip_part).astype(BF16)
     joined_grad_part = joined_grad_part.reshape(nd, local, joined_part)
-    away = jnp.stack(
-        [joined_grad_part[0]] + [swap(joined_grad_part[k], k) for k in range(1, nd)]
-    )
+    away = [joined_grad_part[0]] + [swap(joined_grad_part[k], k) for k in range(1, nd)]
+    away, proj_w_grad = after((away, proj_w_grad))
+    away = jnp.stack(away)
     joined_grad = jnp.concatenate(
         [index(away, dp_at ^ k) for k in range(nd)], axis=1
     ).astype(F32)

time: 443 us -> 430 us (0.971)
  blocking collectives: 15.6 us -> 31.5 us
  waiting for transfers between devices: 119 us -> 104 us
  Pallas kernels: 31.5 us -> 41 us
  local copies, waits for them, and re-layouts: 68 us -> 59.3 us
  matrix products: 58.5 us -> 50.3 us
  starting transfers between devices: 88.5 us -> 80.3 us
    all_gather x0 -> x1, blocking collectives: none -> 15 us  [on_device(): qkv_mine = lax.all_gather(qkv_mine, 'dp', axis=0, tiled=True)]
    all_to_all x1, waiting for transfers between devices: 0.01 us -> 10.7 us  [chip_sums(): lax.all_to_all(sums, 'seq', 0, 0, axis_index_groups=groups, tiled=True)]
    dot_general x4 -> x2, matrix products: 16.2 us -> 6.15 us  [times_transposed(): lax.dot_general(left, right, (((1,), (1,)), ((), ())), preferred_element_...]
    pallas_call x1 -> x2, Pallas kernels: 5.31 us -> 14.7 us  [the longest x1 9.04 us: feed_back(): pl.pallas_call(partial(feed_back_kernel, local), out_shape=[jax.ShapeDtyp...]
    unnamed x9, waiting for transfers between devices: 9.37 us -> 0.79 us
    ppermute x45 -> x42, waiting for transfers between devices: 54.8 us -> 47 us  [swap(): return lax.ppermute(v, 'dp', [(i, i ^ k) for i in range(nd)])]
    ppermute x45 -> x42, starting transfers between devices: 56 us -> 48.5 us  [swap(): return lax.ppermute(v, 'dp', [(i, i ^ k) for i in range(nd)])]
    all_to_all x1, waiting for transfers between devices: 4.62 us -> 0.01 us  [on_device(): lax.all_to_all(vector_grads.reshape(n, padded // 128, 128), ('dp', 'seq')...]
  transfers between devices with their start and end apart: 64 -> 61, of which waited for: 26 -> 15; matrix products, arithmetic and copies ran while one was open for 32% -> 30% of each run, Pallas kernels for 7% -> 10%
where the time goes in v11:
time: 430 us; the launch traced here: 422 us
  waiting for transfers between devices  104 us (24%)
  starting transfers between devices  80.3 us (19%)
  local copies, waits for them, and re-layouts  59.3 us (14%)
  matrix products  50.3 us (12%)
  Pallas kernels  41 us (10%)
  other arithmetic  37.2 us (9%)
  blocking collectives  31.5 us (7%)
  between operations  19 us (4%)
    ppermute x42, starting transfers between devices, swap(): return lax.ppermute(v, 'dp', [(i, i ^ k) for i in range(nd)])  48.5 us
    ppermute x42, waiting for transfers between devices, swap(): return lax.ppermute(v, 'dp', [(i, i ^ k) for i in range(nd)])  47 us
    all_to_all x4, waiting for transfers between devices, seq_exchange(): return lax.all_to_all(v, 'seq', 0, 0, tiled=True)  32.5 us
    dot_general x6, matrix products, inner(): lax.dot_general(left, right, (((0,), (0,)), ((), ())), preferred_element_...  27.9 us
    all_gather x1, blocking collectives, on_device(): proj_rows = lax.all_gather(own_proj, 'seq', axis=0, tiled=True)  16.5 us
    dot_general x4, matrix products, dot(): return jnp.dot(left, right, preferred_element_type=F32)  16.3 us
    all_gather x1, blocking collectives, on_device(): qkv_mine = lax.all_gather(qkv_mine, 'dp', axis=0, tiled=True)  15 us
    all_to_all x4, starting transfers between devices, seq_exchange(): return lax.all_to_all(v, 'seq', 0, 0, tiled=True)  14.6 us
  transfers between devices with their start and end apart: 61, of which 15 were waited for; matrix products, arithmetic and copies ran while one was open for 30% of the time, Pallas kernels for 10%

profile of v11, /device:TPU:0, one launch (start us, length us, event | category | flops | bytes accessed | tf_op | source)
XLA Modules:
  0.0 422.4 jit_solution(17678461873027731436)
XLA Ops:
  15.1 6.3 %all-to-all-start = ((bf16[32,8,128]{2,1,0:T(8,128)(2,1)}), bf16[32,8,128]{2,1,0:T(8,128)(2,1)S(1)}, u32[]{:S(2)}, u32[]{:S(2)}) async-start(bf16[32,8,128]{2,1,0:T(8,128)(2,1)} %broadcast_in_dim.15), calls=%async_computation | async-start | bytes 131072 | tf_op jit(solution)/shard_map/all_to_all | solution.py:376
  23.4 6.2 %all-to-all-done = bf16[32,8,128]{2,1,0:T(8,128)(2,1)S(1)} async-done(((bf16[32,8,128]{2,1,0:T(8,128)(2,1)}), bf16[32,8,128]{2,1,0:T(8,128)(2,1)S(1)}, u32[]{:S(2)}, u32[]{:S(2)}) %all-to-all-start) | async-done | bytes 65568 | tf_op jit(solution)/shard_map/all_to_all | solution.py:376
  30.6 6.6 %all-gather.6.cloned.1.call-done = bf16[576,1152]{1,0:T(8,128)(2,1)} async-done(((bf16[72,1152]{1,0:T(8,128)(2,1)}), bf16[576,1152]{1,0:T(8,128)(2,1)}) %all-gather.6.cloned.1.call-update) | async-done | bytes 1327120 | tf_op jit(solution)/shard_map/all_gather | solution.py:368
  46.9 16.5 %all-gather = bf16[8,36,1152]{2,1,0:T(8,128)(2,1)} all-gather(bf16[1,36,1152]{2,1,0:T(8,128)(2,1)} %bitcast.172), channel_id=1, replica_groups=mesh['dp'=4,'seq'=8] {'seq'}, dimensions={0}, use_global_device_ids=true | all-gather | bytes 746496 | tf_op jit(solution)/shard_map/all_gather | solution.py:407
  82.9 16.3 %all-to-all-done.1 = bf16[8,36,432]{2,1,0:T(8,128)(2,1)S(1)} async-done(((bf16[8,36,432]{2,1,0:T(8,128)(2,1)}), bf16[8,36,432]{2,1,0:T(8,128)(2,1)S(1)}, u32[]{:S(2)}, u32[]{:S(2)}) %all-to-all-start.1) | async-done | bytes 248864 | tf_op jit(solution)/shard_map/all_to_all | solution.py:355
  105.6 15.0 %all_gather.21 = bf16[1152,432]{1,0:T(8,128)(2,1)S(1)} all-gather(bf16[288,432]{1,0:T(8,128)(2,1)S(1)} %reshape.202), channel_id=1, replica_groups=mesh['dp'=4,'seq'=8] {'dp'}, dimensions={0}, use_global_device_ids=true | all-gather | bytes 1244160 | tf_op jit(solution)/shard_map/all_gather | solution.py:418
  128.5 4.7 %convolution_convert_fusion.4.q_ref.k_ref.v_ref = bf16[1280,768]{1,0:T(8,128)(2,1)S(1)} fusion(bf16[1280,1152]{1,0:T(8,128)(2,1)} %all-gather.8.cloned.1.call-done, bf16[1152,768]{0,1:T(8,128)(2,1)S(1)} %bitcast.156), kind=kOutput, calls=%fused_computation.23 | convolution fusion | flops 2265907200 | bytes 6684672 | tf_op jit(solution)/shard_map/dot_general | solution.py:46
  133.2 8.4 %shard_map.288 = (f32[1280,256]{1,0:T(8,128)S(1)}, bf16[1280,144]{1,0:T(8,128)(2,1)S(1)}, f32[8,1280]{1,0:T(8,128)S(1)}) custom-call(bf16[1280,768]{1,0:T(8,128)(2,1)S(1)} %convolution_convert_fusion.4.q_ref.k_ref.v_ref, bf16[1280,768]{1,0:T(8,128)(2,1)S(1)} %convolution_convert_fusion.4.q_ref.k_ref.v_ref, ...), custom_call_target="tpu_custom_call" | custom-call | flops 3355443200 | bytes 3276800 | tf_op jit(solution)/shard_map/pallas_call | solution.py:84
  186.2 8.2 %collective-permute-done.19 = bf16[160,1152]{1,0:T(8,128)(2,1)S(1)} collective-permute-done((bf16[160,1152]{1,0:T(8,128)(2,1)S(1)}, bf16[160,1152]{1,0:T(8,128)(2,1)S(1)}, u32[]{:S(2)}, u32[]{:S(2)}) %collective-permute-start.19) | collective-permute-done | bytes 368672 | tf_op jit(solution)/shard_map/ppermute | solution.py:331
  194.5 5.7 %shard_map.289 = (bf16[640,1152]{1,0:T(8,128)(2,1)S(1)}, f32[640,1152]{1,0:T(8,128)S(1)}) custom-call(bf16[640,1152]{1,0:T(8,128)(2,1)S(1)} %pad_maximum_fusion.1.x_ref, bf16[1152,1152]{1,0:T(8,128)(2,1)S(1)} %convolution_convert_fusion.3.up_ref, f32[1,1152]{1,0:T(1,128)S(1)} %reshape_reshape.6.bias_ref), custom_call_target="tpu_custom_call" | custom-call | flops 1698693120 | bytes 8552448 | tf_op jit(solution)/shard_map/pallas_call | solution.py:250
  207.1 9.0 %shard_map.290 = (bf16[640,1152]{1,0:T(8,128)(2,1)}, f32[1,1152]{1,0:T(1,128)S(1)}, f32[160,1152]{1,0:T(8,128)S(1)}, bf16[160,1152]{1,0:T(8,128)(2,1)}, bf16[160...) custom-call(bf16[640,1152]{1,0:T(8,128)(2,1)} %pad_maximum_fusion.grad_ref, bf16[1152,1152]{1,0:T(8,128)(2,1)} %copy-done.1, ...), custom_call_target="tpu_custom_call" | custom-call | flops 3397386240 | bytes 12681216 | tf_op jit(solution)/shard_map/pallas_call | solution.py:288
  219.7 8.9 %convolution_convert_fusion.1 = bf16[1152,1152]{1,0:T(8,128)(2,1)} fusion(bf16[640,1152]{1,0:T(8,128)(2,1)} %get-tuple-element.138, bf16[640,1152]{1,0:T(8,128)(2,1)S(1)} %pad_maximum_fusion.1.x_ref, bf16[1152,1152]{1,0:T(8,128)(2,1)} %fusion.10), kind=kOutput, calls=%fused_computation.9 | convolution fusion | flops 3399450624 | bytes 8257536 | tf_op jit(solution)/shard_map/dot_general | solution.py:50
  228.6 6.5 %collective-permute-done.22 = bf16[160,1152]{1,0:T(8,128)(2,1)} collective-permute-done((bf16[160,1152]{1,0:T(8,128)(2,1)}, bf16[160,1152]{1,0:T(8,128)(2,1)}, u32[]{:S(2)}, u32[]{:S(2)}) %collective-permute-start.22) | collective-permute-done | bytes 368672 | tf_op jit(solution)/shard_map/ppermute | solution.py:331
  245.0 4.2 all-to-all-start.3
  249.2 5.9 %fusion.62 = (bf16[640,1152]{1,0:T(8,128)(2,1)S(1)}, f32[640,1152]{1,0:T(8,128)}) fusion(bf16[640,1152]{1,0:T(8,128)(2,1)S(1)} %copy-done.3, bf16[1152,1152]{1,0:T(8,128)(2,1)} %all-gather.12.cloned.1.call-done.down_ref), kind=kOutput, calls=%fused_computation.177 | convolution fusion | flops 1699430400 | bytes 8552448 | tf_op jit(solution)/shard_map/dot_general | solution.py:46
  262.9 12.5 %all-to-all-done.3 = bf16[8,160,144]{1,2,0:T(8,128)(2,1)} async-done(((bf16[8,160,144]{1,2,0:T(8,128)(2,1)}), bf16[8,160,144]{1,2,0:T(8,128)(2,1)}, u32[]{:S(2)}, u32[]{:S(2)}) %all-to-all-start.3) | async-done | bytes 368672 | tf_op jit(solution)/shard_map/all_to_all | solution.py:355
  276.9 14.4 %shard_map.292 = (bf16[1280,144]{1,0:T(8,128)(2,1)S(1)}, bf16[1280,288]{1,0:T(8,128)(2,1)S(1)}) custom-call(bf16[1280,768]{1,0:T(8,128)(2,1)} %copy-done.4, bf16[1280,768]{1,0:T(8,128)(2,1)} %copy-done.4, bf16[1280,768]{1,0:T(8,128)(2,1)} %copy-done.4, bf16[1280,256]{1,0:T(8,128)(2,1)S(1)} %pad.18.out_grad_ref, f32[1280,256]{1,0:T(8,128)S(1)} %copy-done.6, ...), custom_call_target="tpu_custom_call" | custom-call | flops 8388608000 | bytes 4587520 | tf_op jit(solution)/shard_map/pallas_call | solution.py:164
  303.5 5.4 %fusion.63 = f32[1152,432]{1,0:T(8,128)} fusion(bf16[1280,1152]{1,0:T(8,128)(2,1)} %all-gather.8.cloned.1.call-done, bf16[1280,432]{1,0:T(8,128)(2,1)} %copy-done.26), kind=kOutput, calls=%fused_computation.178 | convolution fusion | flops 1274019840 | bytes 6045696 | tf_op jit(solution)/shard_map/dot_general | solution.py:50
  314.2 8.2 %collective-permute-done.28 = bf16[160,1152]{1,0:T(8,128)(2,1)S(1)} collective-permute-done((bf16[160,1152]{1,0:T(8,128)(2,1)S(1)}, bf16[160,1152]{1,0:T(8,128)(2,1)S(1)}, u32[]{:S(2)}, u32[]{:S(2)}) %collective-permute-start.28) | collective-permute-done | bytes 368672 | tf_op jit(solution)/shard_map/ppermute | solution.py:331
  331.8 5.2 %collective-permute-done.30 = bf16[288,432]{1,0:T(8,128)(2,1)S(1)} collective-permute-done((bf16[288,432]{1,0:T(8,128)(2,1)S(1)}, bf16[288,432]{1,0:T(8,128)(2,1)S(1)}, u32[]{:S(2)}, u32[]{:S(2)}) %collective-permute-start.30) | collective-permute-done | bytes 248864 | tf_op jit(solution)/shard_map/ppermute | solution.py:331
  337.0 4.8 %collective-permute-done.31 = bf16[288,432]{1,0:T(8,128)(2,1)} collective-permute-done((bf16[288,432]{1,0:T(8,128)(2,1)S(1)}, bf16[288,432]{1,0:T(8,128)(2,1)}, u32[]{:S(2)}, u32[]{:S(2)}) %collective-permute-start.31) | collective-permute-done | bytes 248864 | tf_op jit(solution)/shard_map/ppermute | solution.py:331
  360.4 4.9 %collective-permute-done.38 = bf16[160,1152]{1,0:T(8,128)(2,1)} collective-permute-done((bf16[160,1152]{1,0:T(8,128)(2,1)S(1)}, bf16[160,1152]{1,0:T(8,128)(2,1)}, u32[]{:S(2)}, u32[]{:S(2)}) %collective-permute-start.38) | collective-permute-done | bytes 368672 | tf_op jit(solution)/shard_map/ppermute | solution.py:331
  391.1 4.9 %all-to-all-start.5 = ((bf16[4,36,1152]{2,1,0:T(8,128)(2,1)}), bf16[4,36,1152]{2,1,0:T(8,128)(2,1)S(1)}, u32[]{:S(2)}, u32[]{:S(2)}) async-start(bf16[4,36,1152]{2,1,0:T(8,128)(2,1)} %fusion.28), calls=%async_computation.8 | async-start | bytes 737280 | tf_op jit(solution)/shard_map/all_to_all | solution.py:365
  398.2 10.7 %all-to-all-done.5 = bf16[4,36,1152]{2,1,0:T(8,128)(2,1)S(1)} async-done(((bf16[4,36,1152]{2,1,0:T(8,128)(2,1)}), bf16[4,36,1152]{2,1,0:T(8,128)(2,1)S(1)}, u32[]{:S(2)}, u32[]{:S(2)}) %all-to-all-start.5) | async-done | bytes 331808 | tf_op jit(solution)/shard_map/all_to_all | solution.py:365
  (350 shorter events, 204.0 us)
Async XLA Ops:
  7.3 30.0 %all-gather.6.cloned.1.call-start = ((), (), s32[]{:S(2)}) async-start(), calls=%async_computation.11 | async-start | bytes 1492992 | tf_op jit(solution)/shard_map/all_gather | solution.py:368
  21.4 103.3 %all-gather.8.cloned.1.call-start = ((), (), s32[]{:S(2)}) async-start(), calls=%async_computation.12 | async-start | bytes 3317760 | tf_op jit(solution)/shard_map/all_gather | solution.py:411
  41.2 24.2 %collective-permute-start.3 = (bf16[160,1152]{1,0:T(8,128)(2,1)}, bf16[160,1152]{1,0:T(8,128)(2,1)S(1)}, u32[]{:S(2)}, u32[]{:S(2)}) collective-permute-start(bf16[160,1152]{1,0:T(8,128)(2,1)} %get-tuple-element.199), channel_id=1, source_target_pairs={{0,8},{8,0},{16,24},{24,16},{1,9},{9,1},{17,25},{25,17},{2,10},{10... | collective-permute-start | bytes 1105928 | tf_op jit(solution)/shard_map/ppermute | solution.py:331
  42.6 22.8 %collective-permute-start.4 = (bf16[160,1152]{1,0:T(8,128)(2,1)}, bf16[160,1152]{1,0:T(8,128)(2,1)}, u32[]{:S(2)}, u32[]{:S(2)}) collective-permute-start(bf16[160,1152]{1,0:T(8,128)(2,1)} %get-tuple-element.201), channel_id=1, source_target_pairs={{0,16},{8,24},{16,0},{24,8},{1,17},{9,25},{17,1},{25,9},{2,18},{10... | collective-permute-start | bytes 1105928 | tf_op jit(solution)/shard_map/ppermute | solution.py:331
  44.0 21.4 %collective-permute-start.5 = (bf16[160,1152]{1,0:T(8,128)(2,1)}, bf16[160,1152]{1,0:T(8,128)(2,1)}, u32[]{:S(2)}, u32[]{:S(2)}) collective-permute-start(bf16[160,1152]{1,0:T(8,128)(2,1)} %get-tuple-element.200), channel_id=1, source_target_pairs={{0,24},{8,16},{16,8},{24,0},{1,25},{9,17},{17,9},{25,1},{2,26},{10... | collective-permute-start | bytes 1105928 | tf_op jit(solution)/shard_map/ppermute | solution.py:331
  75.8 23.4 %all-to-all-start.1 = ((bf16[8,36,432]{2,1,0:T(8,128)(2,1)}), bf16[8,36,432]{2,1,0:T(8,128)(2,1)S(1)}, u32[]{:S(2)}, u32[]{:S(2)}) async-start(bf16[8,36,432]{2,1,0:T(8,128)(2,1)} %copy.61), calls=%async_computation.1 | async-start | bytes 655360 | tf_op jit(solution)/shard_map/all_to_all | solution.py:355
  79.2 91.1 %all-gather.10.cloned.1.call-start = ((), (), s32[]{:S(2)}) async-start(), calls=%async_computation.13 | async-start | bytes 2985984 | tf_op jit(solution)/shard_map/all_gather | solution.py:427
  100.8 22.1 %collective-permute-start.10 = (bf16[36,1152]{1,0:T(8,128)(2,1)}, bf16[36,1152]{1,0:T(8,128)(2,1)S(1)}, u32[]{:S(2)}, u32[]{:S(2)}) collective-permute-start(bf16[36,1152]{1,0:T(8,128)(2,1)} %bitcast.146), channel_id=1, source_target_pairs={{0,16},{8,24},{16,0},{24,8},{1,17},{9,25},{17,1},{25,9},{2,18},{10... | collective-permute-start | bytes 248840 | tf_op jit(solution)/shard_map/ppermute | solution.py:331
  141.6 20.2 %collective-permute-start.12 = (bf16[160,1152]{1,0:T(8,128)(2,1)}, bf16[160,1152]{1,0:T(8,128)(2,1)}, u32[]{:S(2)}, u32[]{:S(2)}) collective-permute-start(bf16[160,1152]{1,0:T(8,128)(2,1)} %bitcast.20), channel_id=1, source_target_pairs={{0,8},{8,0},{16,24},{24,16},{1,9},{9,1},{17,25},{25,17},{2,10},{10... | collective-permute-start | bytes 1105928 | tf_op jit(solution)/shard_map/ppermute | solution.py:331
  146.8 21.3 %all-to-all-start.2 = ((bf16[8,160,144]{1,2,0:T(8,128)(2,1)}), bf16[8,160,144]{1,2,0:T(8,128)(2,1)S(1)}, u32[]{:S(2)}, u32[]{:S(2)}) async-start(bf16[8,160,144]{1,2,0:T(8,128)(2,1)} %copy.64), calls=%async_computation.2 | async-start | bytes 1179648 | tf_op jit(solution)/shard_map/all_to_all | solution.py:355
  150.4 56.8 %all-gather.12.cloned.1.call-start = ((), (), s32[]{:S(2)}) async-start(), calls=%async_computation.14 | async-start | bytes 2985984 | tf_op jit(solution)/shard_map/all_gather | solution.py:453
  170.3 128.7 %reduce-scatter.9.cloned.1.call-start = ((), (), s32[]{:S(2)}) async-start(), calls=%async_computation.16 | async-start | bytes 2985984 | tf_op jit(solution)/shard_map/reduce_scatter | solution.py:464
  206.9 92.1 %reduce-scatter.7.cloned.1.call-start = ((), (), s32[]{:S(2)}) async-start(), calls=%async_computation.15 | async-start | bytes 2985984 | tf_op jit(solution)/shard_map/reduce_scatter | solution.py:481
  245.0 30.4 %all-to-all-start.3 = ((bf16[8,160,144]{1,2,0:T(8,128)(2,1)}), bf16[8,160,144]{1,2,0:T(8,128)(2,1)}, u32[]{:S(2)}, u32[]{:S(2)}) async-start(bf16[8,160,144]{1,2,0:T(8,128)(2,1)} %copy.66), calls=%async_computation.3 | async-start | bytes 1179648 | tf_op jit(solution)/shard_map/all_to_all | solution.py:355
  249.2 96.8 %reduce-scatter.11.cloned.1.call-start = ((), (), s32[]{:S(2)}) async-start(), calls=%async_computation.17 | async-start | bytes 3317760 | tf_op jit(solution)/shard_map/reduce_scatter | solution.py:501
  256.2 20.6 %collective-permute-start.24 = (bf16[160,1152]{1,0:T(8,128)(2,1)}, bf16[160,1152]{1,0:T(8,128)(2,1)}, u32[]{:S(2)}, u32[]{:S(2)}) collective-permute-start(bf16[160,1152]{1,0:T(8,128)(2,1)} %get-tuple-element.198), channel_id=1, source_target_pairs={{0,8},{8,0},{16,24},{24,16},{1,9},{9,1},{17,25},{25,17},{2,10},{10... | collective-permute-start | bytes 1105928 | tf_op jit(solution)/shard_map/ppermute | solution.py:331
  259.8 36.7 %collective-permute-start.25 = (bf16[160,1152]{1,0:T(8,128)(2,1)}, bf16[160,1152]{1,0:T(8,128)(2,1)}, u32[]{:S(2)}, u32[]{:S(2)}) collective-permute-start(bf16[160,1152]{1,0:T(8,128)(2,1)} %get-tuple-element.196), channel_id=1, source_target_pairs={{0,16},{8,24},{16,0},{24,8},{1,17},{9,25},{17,1},{25,9},{2,18},{10... | collective-permute-start | bytes 1105928 | tf_op jit(solution)/shard_map/ppermute | solution.py:331
  260.9 35.6 %collective-permute-start.26 = (bf16[160,1152]{1,0:T(8,128)(2,1)}, bf16[160,1152]{1,0:T(8,128)(2,1)}, u32[]{:S(2)}, u32[]{:S(2)}) collective-permute-start(bf16[160,1152]{1,0:T(8,128)(2,1)} %get-tuple-element.197), channel_id=1, source_target_pairs={{0,24},{8,16},{16,8},{24,0},{1,25},{9,17},{17,9},{25,1},{2,26},{10... | collective-permute-start | bytes 1105928 | tf_op jit(solution)/shard_map/ppermute | solution.py:331
  299.1 23.5 %collective-permute-start.33 = (bf16[160,288]{1,0:T(8,128)(2,1)S(1)}, bf16[160,288]{1,0:T(8,128)(2,1)S(1)}, u32[]{:S(2)}, u32[]{:S(2)}) collective-permute-start(bf16[160,288]{1,0:T(8,128)(2,1)S(1)} %get-tuple-element.220), channel_id=1, source_target_pairs={{0,8},{8,0},{16,24},{24,16},{1,9},{9,1},{17,25},{25,17},{2,10},{10... | collective-permute-start | bytes 276488 | tf_op jit(solution)/shard_map/ppermute | solution.py:331
  299.2 23.4 %collective-permute-start.34 = (bf16[160,288]{1,0:T(8,128)(2,1)S(1)}, bf16[160,288]{1,0:T(8,128)(2,1)S(1)}, u32[]{:S(2)}, u32[]{:S(2)}) collective-permute-start(bf16[160,288]{1,0:T(8,128)(2,1)S(1)} %get-tuple-element.219), channel_id=1, source_target_pairs={{0,16},{8,24},{16,0},{24,8},{1,17},{9,25},{17,1},{25,9},{2,18},{10... | collective-permute-start | bytes 276488 | tf_op jit(solution)/shard_map/ppermute | solution.py:331
  301.2 21.2 %collective-permute-start.28 = (bf16[160,1152]{1,0:T(8,128)(2,1)S(1)}, bf16[160,1152]{1,0:T(8,128)(2,1)S(1)}, u32[]{:S(2)}, u32[]{:S(2)}) collective-permute-start(bf16[160,1152]{1,0:T(8,128)(2,1)S(1)} %copy-done.17), channel_id=1, source_target_pairs={{0,16},{8,24},{16,0},{24,8},{1,17},{9,25},{17,1},{25,9},{2,18},{10... | collective-permute-start | bytes 1105928 | tf_op jit(solution)/shard_map/ppermute | solution.py:331
  355.8 57.7 %reduce-scatter.13.cloned.1.call-start = ((), (), s32[]{:S(2)}) async-start(), calls=%async_computation.18 | async-start | bytes 1492992
  384.4 25.2 %collective-permute-start.40 = (bf16[160,576]{0,1:T(8,128)(2,1)}, bf16[160,576]{0,1:T(8,128)(2,1)S(1)}, u32[]{:S(2)}, u32[]{:S(2)}) collective-permute-start(bf16[160,576]{0,1:T(8,128)(2,1)} %get-tuple-element.215), channel_id=1, source_target_pairs={{0,8},{8,0},{16,24},{24,16},{1,9},{9,1},{17,25},{25,17},{2,10},{10... | collective-permute-start | bytes 552968 | tf_op jit(solution)/shard_map/ppermute | solution.py:331
  386.2 23.5 %collective-permute-start.41 = (bf16[160,576]{0,1:T(8,128)(2,1)S(1)}, bf16[160,576]{0,1:T(8,128)(2,1)}, u32[]{:S(2)}, u32[]{:S(2)}) collective-permute-start(bf16[160,576]{0,1:T(8,128)(2,1)S(1)} %get-tuple-element.214), channel_id=1, source_target_pairs={{0,16},{8,24},{16,0},{24,8},{1,17},{9,25},{17,1},{25,9},{2,18},{10... | collective-permute-start | bytes 552968 | tf_op jit(solution)/shard_map/ppermute | solution.py:331
  (83 other events, 961.9 us)
Sparse Core Ops, SparseCore 0:
  9.7 27.4 all-gather.5
  68.7 43.0 all-gather.7
  124.8 32.9 all-gather.9
  170.5 32.9 all-gather.11
  207.0 35.6 reduce-scatter.8
  244.9 45.4 reduce-scatter.6
  299.2 35.5 reduce-scatter.10
  371.6 35.4 reduce-scatter.12

commit v12 on v11

--- a/solution.py
+++ b/solution.py
@@ -394,7 +394,7 @@
     order = (row == lax.broadcasted_iota(jnp.int32, (features, features), 1)).astype(BF16)
     qkv_out = qkv_w.reshape(small, 3, ns, head_cols).transpose(2, 0, 1, 3).reshape(ns, small, wide)
     segments = segment_of(item_lengths, jnp.arange(row_len, dtype=jnp.int32))
-    own_proj, skip_part, joined_here, vectors = after((proj_w, skip_part, joined_here, vectors))
+    qkv_out, skip_part, joined_here, vectors = after((qkv_out, skip_part, joined_here, vectors))
     def vector(at):
         return vectors[:, at * small : (at + 1) * small].reshape(features)
 
@@ -404,25 +404,25 @@
 
     first_terms = dot(joined_here, skip_part)
     first = add_blocks(first_terms[:local], low_rows(first_terms)) + b_skip
-    proj_rows = lax.all_gather(own_proj, "seq", axis=0, tiled=True)
+    qkv_mine = seq_exchange(qkv_out).reshape(part, wide)
     xhat_one, inverse_one = norm_pieces(first)
     normed_one = (xhat_one * g_one + b_one).astype(BF16)
-    normed_one, qkv_out, proj_rows = after((normed_one, qkv_out, proj_rows))
+    normed_one, qkv_mine, own_proj, own_up = after((normed_one, qkv_mine, proj_w, fc1_w))
     normed_one_row = lax.all_gather(normed_one, "seq", axis=0, tiled=True)
 
-    qkv_mine = seq_exchange(qkv_out).reshape(part, wide)
+    qkv_mine = lax.all_gather(qkv_mine, "dp", axis=0, tiled=True)
+    qkv_mine, own_proj = after((qkv_mine, own_proj))
+    proj_rows = lax.all_gather(own_proj, "seq", axis=0, tiled=True)
     half = part // 2
     own_half = lax.dynamic_slice_in_dim(proj_rows, core * half, half, 0)
     proj_halves = [swap(own_half, k) for k in range(1, nd)]
-    qkv_mine, own_up, proj_halves = after((qkv_mine, fc1_w, proj_halves))
-    qkv_mine = lax.all_gather(qkv_mine, "dp", axis=0, tiled=True)
     up_slices = jnp.swapaxes(own_up.reshape(small, nd, hidden_part), 0, 1)
     up_slices = jnp.concatenate(
         [index(up_slices, dp_at)] + [swap(index(up_slices, dp_at ^ k), k) for k in range(1, nd)],
         axis=0,
     )
-    normed_one_row, up_slices, qkv_mine, qkv_wide, segments = after(
-        (normed_one_row, up_slices, qkv_mine, widen(qkv_mine), segments)
+    normed_one_row, up_slices, qkv_mine, qkv_wide, segments, proj_halves[0], order = after(
+        (normed_one_row, up_slices, qkv_mine, widen(qkv_mine), segments, proj_halves[0], order)
     )
     up_part = lax.all_gather(up_slices, "seq", axis=0, tiled=True)
     triple = dot(normed_one_row, qkv_wide).astype(BF16)
@@ -478,11 +478,11 @@
     attended_grad, second_late, hidden_late, attended_low, fc1_terms = after(
         (attended_grad, second_low, hidden, attended_low, fc1_terms)
     )
-    fc1_terms = lax.psum_scatter(fc1_terms, "seq", scatter_dimension=0, tiled=True)
     attended_grad = seq_exchange(attended_grad).reshape(row_len, head_cols)
     down_sums = dot(hidden_late, down_part)
     attended_slices = jnp.swapaxes(attended_low.reshape(local, nd, part), 0, 1)
-    down_blocks = low_rows(down_sums)
+    down_blocks, fc1_terms = after((low_rows(down_sums), fc1_terms))
+    fc1_terms = lax.psum_scatter(fc1_terms, "seq", scatter_dimension=0, tiled=True)
     down_blocks = [swap(down_blocks[k], k) for k in range(1, nd)]
     attended_grad, down_blocks[0], second_late, attended_slices = after(
         (attended_grad, down_blocks[0], second_late, attended_slices)
@@ -514,20 +514,21 @@
     for block in qkv_blocks:
         qkv_sum = qkv_sum + block.astype(F32)
     qkv_sum = qkv_sum.astype(BF16).reshape(ns, small, wide)
-    normed_one_grad, qkv_sum, proj_sums = after((normed_one_grad, qkv_sum, proj_sums))
     normed_one_grad = normed_one_grad.astype(F32)
     through_one, ln1_g_grad, ln1_b_grad = norm_back(normed_one_grad, xhat_one, inverse_one, g_one)
     first_grad = second_grad + through_one
     first_low = first_grad.astype(BF16)
     first_low_rows = gather_rows(first_low)
+    proj_w_grad = chip_sums(proj_sums)
     qkv_w_grad = seq_exchange(qkv_sum)
-    first_low_rows, first_grad, qkv_w_grad = after((first_low_rows, first_grad, qkv_w_grad))
+    first_low_rows, first_grad, qkv_w_grad, proj_w_grad = after(
+        (first_low_rows, first_grad, qkv_w_grad, proj_w_grad)
+    )
     skip_terms = inner(joined_here, first_low_rows).astype(BF16)
     skip_w_grad = lax.psum_scatter(skip_terms, "seq", scatter_dimension=0, tiled=True).astype(F32)
-    skip_terms, first_low_rows, first_grad, fc1_terms, proj_sums, qkv_w_grad = after(
-        (skip_terms, first_low_rows, first_grad, fc1_terms, proj_sums, qkv_w_grad)
-    )
-    proj_w_grad = chip_sums(proj_sums)
+    skip_terms, first_low_rows, first_grad, fc1_terms, qkv_w_grad = after(
+        (skip_terms, first_low_rows, first_grad, fc1_terms, qkv_w_grad)
+    )
     fc1_terms = fc1_terms.reshape(nd, small, hidden_part)
     fc1_blocks = jnp.stack([fc1_terms[0]] + [swap(fc1_terms[k], k) for k in range(1, nd)])
     vector_grads = jnp.stack(
@@ -554,7 +555,6 @@
     joined_grad_part = times_transposed(first_low_rows, skip_part).astype(BF16)
     joined_grad_part = joined_grad_part.reshape(nd, local, joined_part)
     away = [joined_grad_part[0]] + [swap(joined_grad_part[k], k) for k in range(1, nd)]
-    away, proj_w_grad = after((away, proj_w_grad))
     away = jnp.stack(away)
     joined_grad = jnp.concatenate(
         [index(away, dp_at ^ k) for k in range(nd)], axis=1

time: 430 us -> 421 us (0.979)
  waiting for transfers between devices: 104 us -> 98.4 us
    ppermute x42, waiting for transfers between devices: 47 us -> 62.3 us  [swap(): return lax.ppermute(v, 'dp', [(i, i ^ k) for i in range(nd)])]
    all_to_all x4, waiting for transfers between devices: 32.5 us -> 21.2 us  [seq_exchange(): return lax.all_to_all(v, 'seq', 0, 0, tiled=True)]
    all_to_all x1, waiting for transfers between devices: 10.7 us -> 0.5 us  [chip_sums(): lax.all_to_all(sums, 'seq', 0, 0, axis_index_groups=groups, tiled=True)]
    unnamed x98 -> x86, local copies, waits for them, and re-layouts: 8.04 us -> 9.74 us
  transfers between devices with their start and end apart: 61 -> 61, of which waited for: 15 -> 20; matrix products, arithmetic and copies ran while one was open for 30% -> 31% of each run, Pallas kernels for 10% -> 10%
where the time goes in v12:
time: 421 us; the launch traced here: 415 us
  waiting for transfers between devices  98.4 us (23%)
  starting transfers between devices  80.6 us (19%)
  local copies, waits for them, and re-layouts  57.5 us (14%)
  matrix products  49.4 us (12%)
  Pallas kernels  40.8 us (10%)
  other arithmetic  37.3 us (9%)
  blocking collectives  32.4 us (8%)
  between operations  19 us (5%)
    ppermute x42, waiting for transfers between devices, swap(): return lax.ppermute(v, 'dp', [(i, i ^ k) for i in range(nd)])  62.3 us
    ppermute x42, starting transfers between devices, swap(): return lax.ppermute(v, 'dp', [(i, i ^ k) for i in range(nd)])  49.2 us
    dot_general x6, matrix products, inner(): lax.dot_general(left, right, (((0,), (0,)), ((), ())), preferred_element_...  26.4 us
    all_to_all x4, waiting for transfers between devices, seq_exchange(): return lax.all_to_all(v, 'seq', 0, 0, tiled=True)  21.2 us
    all_gather x1, blocking collectives, on_device(): proj_rows = lax.all_gather(own_proj, 'seq', axis=0, tiled=True)  18.8 us
    dot_general x4, matrix products, dot(): return jnp.dot(left, right, preferred_element_type=F32)  16.8 us
    all_to_all x4, starting transfers between devices, seq_exchange(): return lax.all_to_all(v, 'seq', 0, 0, tiled=True)  15.3 us
    pallas_call x1, Pallas kernels, attend_back(): pl.pallas_call(partial(attend_back_kernel, heads, scale), grid=(rows // s...  14.2 us
  transfers between devices with their start and end apart: 61, of which 20 were waited for; matrix products, arithmetic and copies ran while one was open for 31% of the time, Pallas kernels for 10%

profile of v12, /device:TPU:0, one launch (start us, length us, event | category | flops | bytes accessed | tf_op | source)
XLA Modules:
  0.0 415.3 jit_solution(8734357716558602292)
XLA Ops:
  15.1 6.3 %all-to-all-start = ((bf16[32,8,128]{2,1,0:T(8,128)(2,1)}), bf16[32,8,128]{2,1,0:T(8,128)(2,1)S(1)}, u32[]{:S(2)}, u32[]{:S(2)}) async-start(bf16[32,8,128]{2,1,0:T(8,128)(2,1)} %broadcast_in_dim.15), calls=%async_computation | async-start | bytes 131072 | tf_op jit(solution)/shard_map/all_to_all | solution.py:376
  22.6 7.0 %all-to-all-done = bf16[32,8,128]{2,1,0:T(8,128)(2,1)S(1)} async-done(((bf16[32,8,128]{2,1,0:T(8,128)(2,1)}), bf16[32,8,128]{2,1,0:T(8,128)(2,1)S(1)}, u32[]{:S(2)}, u32[]{:S(2)}) %all-to-all-start) | async-done | bytes 65568 | tf_op jit(solution)/shard_map/all_to_all | solution.py:376
  30.6 6.6 %all-gather.6.cloned.1.call-done = bf16[576,1152]{1,0:T(8,128)(2,1)} async-done(((bf16[72,1152]{1,0:T(8,128)(2,1)}), bf16[576,1152]{1,0:T(8,128)(2,1)}) %all-gather.6.cloned.1.call-update) | async-done | bytes 1327120 | tf_op jit(solution)/shard_map/all_gather | solution.py:368
  53.0 8.3 %collective-permute-done.4 = bf16[160,1152]{1,0:T(8,128)(2,1)} collective-permute-done((bf16[160,1152]{1,0:T(8,128)(2,1)}, bf16[160,1152]{1,0:T(8,128)(2,1)}, u32[]{:S(2)}, u32[]{:S(2)}) %collective-permute-start.4) | collective-permute-done | bytes 368672 | tf_op jit(solution)/shard_map/ppermute | solution.py:331
  71.5 13.6 %all_gather.20 = bf16[1152,432]{1,0:T(8,128)(2,1)S(1)} all-gather(bf16[288,432]{1,0:T(8,128)(2,1)S(1)} %reshape.197), channel_id=1, replica_groups=mesh['dp'=4,'seq'=8] {'dp'}, dimensions={0}, use_global_device_ids=true | all-gather | bytes 1244160 | tf_op jit(solution)/shard_map/all_gather | solution.py:413
  85.1 18.8 %all-gather = bf16[8,36,1152]{2,1,0:T(8,128)(2,1)S(1)} all-gather(bf16[1,36,1152]{2,1,0:T(8,128)(2,1)S(1)} %bitcast.181), channel_id=1, replica_groups=mesh['dp'=4,'seq'=8] {'seq'}, dimensions={0}, use_global_device_ids=true | all-gather | bytes 746496 | tf_op jit(solution)/shard_map/all_gather | solution.py:415
  123.9 5.1 %convolution_convert_fusion.4.q_ref.k_ref.v_ref = bf16[1280,768]{1,0:T(8,128)(2,1)S(1)} fusion(bf16[1280,1152]{1,0:T(8,128)(2,1)} %all-gather.8.cloned.1.call-done, bf16[1152,768]{0,1:T(8,128)(2,1)} %bitcast.165), kind=kOutput, calls=%fused_computation.23 | convolution fusion | flops 2265907200 | bytes 6684672 | tf_op jit(solution)/shard_map/dot_general | solution.py:46
  129.3 8.4 %shard_map.288 = (f32[1280,256]{1,0:T(8,128)S(1)}, bf16[1280,144]{1,0:T(8,128)(2,1)S(1)}, f32[8,1280]{1,0:T(8,128)S(1)}) custom-call(bf16[1280,768]{1,0:T(8,128)(2,1)S(1)} %convolution_convert_fusion.4.q_ref.k_ref.v_ref, bf16[1280,768]{1,0:T(8,128)(2,1)S(1)} %convolution_convert_fusion.4.q_ref.k_ref.v_ref, ...), custom_call_target="tpu_custom_call" | custom-call | flops 3355443200 | bytes 3276800 | tf_op jit(solution)/shard_map/pallas_call | solution.py:84
  143.1 4.2 %all-to-all-start.2 = ((bf16[8,160,144]{1,2,0:T(8,128)(2,1)}), bf16[8,160,144]{1,2,0:T(8,128)(2,1)}, u32[]{:S(2)}, u32[]{:S(2)}) async-start(bf16[8,160,144]{1,2,0:T(8,128)(2,1)} %copy.64), calls=%async_computation.2 | async-start | bytes 1179648 | tf_op jit(solution)/shard_map/all_to_all | solution.py:355
  174.8 4.0 convolution_convert_fusion.3.up_ref
  182.7 8.1 %collective-permute-done.19 = bf16[160,1152]{1,0:T(8,128)(2,1)S(1)} collective-permute-done((bf16[160,1152]{1,0:T(8,128)(2,1)S(1)}, bf16[160,1152]{1,0:T(8,128)(2,1)S(1)}, u32[]{:S(2)}, u32[]{:S(2)}) %collective-permute-start.19) | collective-permute-done | bytes 368672 | tf_op jit(solution)/shard_map/ppermute | solution.py:331
  191.0 5.7 %shard_map.289 = (bf16[640,1152]{1,0:T(8,128)(2,1)S(1)}, f32[640,1152]{1,0:T(8,128)S(1)}) custom-call(bf16[640,1152]{1,0:T(8,128)(2,1)S(1)} %pad_maximum_fusion.1.x_ref, bf16[1152,1152]{1,0:T(8,128)(2,1)S(1)} %convolution_convert_fusion.3.up_ref, f32[1,1152]{1,0:T(1,128)S(1)} %reshape_reshape.6.bias_ref), custom_call_target="tpu_custom_call" | custom-call | flops 1698693120 | bytes 8552448 | tf_op jit(solution)/shard_map/pallas_call | solution.py:250
  203.6 9.0 %shard_map.290 = (bf16[640,1152]{1,0:T(8,128)(2,1)}, f32[1,1152]{1,0:T(1,128)S(1)}, f32[160,1152]{1,0:T(8,128)S(1)}, bf16[160,1152]{1,0:T(8,128)(2,1)}, bf16[160...) custom-call(bf16[640,1152]{1,0:T(8,128)(2,1)} %pad_maximum_fusion.grad_ref, bf16[1152,1152]{1,0:T(8,128)(2,1)} %copy-done.1, ...), custom_call_target="tpu_custom_call" | custom-call | flops 3397386240 | bytes 12681216 | tf_op jit(solution)/shard_map/pallas_call | solution.py:288
  216.1 8.9 %convolution_convert_fusion.1 = bf16[1152,1152]{1,0:T(8,128)(2,1)} fusion(bf16[640,1152]{1,0:T(8,128)(2,1)} %get-tuple-element.132, bf16[640,1152]{1,0:T(8,128)(2,1)S(1)} %pad_maximum_fusion.1.x_ref, bf16[1152,1152]{1,0:T(8,128)(2,1)} %fusion.10), kind=kOutput, calls=%fused_computation.9 | convolution fusion | flops 3399450624 | bytes 8257536 | tf_op jit(solution)/shard_map/dot_general | solution.py:50
  225.0 6.7 %collective-permute-done.22 = bf16[160,1152]{1,0:T(8,128)(2,1)} collective-permute-done((bf16[160,1152]{1,0:T(8,128)(2,1)}, bf16[160,1152]{1,0:T(8,128)(2,1)}, u32[]{:S(2)}, u32[]{:S(2)}) %collective-permute-start.22) | collective-permute-done | bytes 368672 | tf_op jit(solution)/shard_map/ppermute | solution.py:331
  239.3 6.1 %fusion.60 = (bf16[640,1152]{1,0:T(8,128)(2,1)}, f32[640,1152]{1,0:T(8,128)}) fusion(bf16[640,1152]{1,0:T(8,128)(2,1)S(1)} %copy-done.3, bf16[1152,1152]{1,0:T(8,128)(2,1)} %all-gather.12.cloned.1.call-done.down_ref), kind=kOutput, calls=%fused_computation.179 | convolution fusion | flops 1699430400 | bytes 8552448 | tf_op jit(solution)/shard_map/dot_general | solution.py:46
  247.7 4.2 %all-to-all-start.3 = ((bf16[8,160,144]{1,2,0:T(8,128)(2,1)}), bf16[8,160,144]{1,2,0:T(8,128)(2,1)}, u32[]{:S(2)}, u32[]{:S(2)}) async-start(bf16[8,160,144]{1,2,0:T(8,128)(2,1)} %copy.66), calls=%async_computation.3 | async-start | bytes 1179648 | tf_op jit(solution)/shard_map/all_to_all | solution.py:355
  261.1 17.8 %all-to-all-done.3 = bf16[8,160,144]{1,2,0:T(8,128)(2,1)} async-done(((bf16[8,160,144]{1,2,0:T(8,128)(2,1)}), bf16[8,160,144]{1,2,0:T(8,128)(2,1)}, u32[]{:S(2)}, u32[]{:S(2)}) %all-to-all-start.3) | async-done | bytes 368672 | tf_op jit(solution)/shard_map/all_to_all | solution.py:355
  280.4 14.2 %shard_map.292 = (bf16[1280,144]{1,0:T(8,128)(2,1)S(1)}, bf16[1280,288]{1,0:T(8,128)(2,1)S(1)}) custom-call(bf16[1280,768]{1,0:T(8,128)(2,1)} %copy-done.4, bf16[1280,768]{1,0:T(8,128)(2,1)} %copy-done.4, bf16[1280,768]{1,0:T(8,128)(2,1)} %copy-done.4, bf16[1280,256]{1,0:T(8,128)(2,1)S(1)} %pad.18.out_grad_ref, f32[1280,256]{1,0:T(8,128)S(1)} %copy-done.6, ...), custom_call_target="tpu_custom_call" | custom-call | flops 8388608000 | bytes 4587520 | tf_op jit(solution)/shard_map/pallas_call | solution.py:164
  307.7 3.9 fusion.61
  317.5 8.5 %collective-permute-done.31 = bf16[160,1152]{1,0:T(8,128)(2,1)S(1)} collective-permute-done((bf16[160,1152]{1,0:T(8,128)(2,1)S(1)}, bf16[160,1152]{1,0:T(8,128)(2,1)S(1)}, u32[]{:S(2)}, u32[]{:S(2)}) %collective-permute-start.31) | collective-permute-done | bytes 368672 | tf_op jit(solution)/shard_map/ppermute | solution.py:331
  360.1 5.8 %collective-permute-done.28 = bf16[160,1152]{1,0:T(8,128)(2,1)S(1)} collective-permute-done((bf16[160,1152]{1,0:T(8,128)(2,1)}, bf16[160,1152]{1,0:T(8,128)(2,1)S(1)}, u32[]{:S(2)}, u32[]{:S(2)}) %collective-permute-start.28) | collective-permute-done | bytes 368672 | tf_op jit(solution)/shard_map/ppermute | solution.py:331
  373.2 4.0 all-to-all-start.6
  395.3 4.9 %collective-permute-done.41 = bf16[160,576]{0,1:T(8,128)(2,1)} collective-permute-done((bf16[160,576]{0,1:T(8,128)(2,1)S(1)}, bf16[160,576]{0,1:T(8,128)(2,1)}, u32[]{:S(2)}, u32[]{:S(2)}) %collective-permute-start.41) | collective-permute-done | bytes 184352 | tf_op jit(solution)/shard_map/ppermute | solution.py:331
  (338 shorter events, 206.3 us)
Async XLA Ops:
  7.3 30.0 %all-gather.6.cloned.1.call-start = ((), (), s32[]{:S(2)}) async-start(), calls=%async_computation.11 | async-start | bytes 1492992 | tf_op jit(solution)/shard_map/all_gather | solution.py:368
  9.7 19.9 %collective-permute-start = (bf16[160,576]{1,0:T(8,128)(2,1)S(1)}, bf16[160,576]{1,0:T(8,128)(2,1)S(1)}, u32[]{:S(2)}, u32[]{:S(2)}) collective-permute-start(bf16[160,576]{1,0:T(8,128)(2,1)S(1)} %get-tuple-element.200), channel_id=1, source_target_pairs={{0,8},{8,0},{16,24},{24,16},{1,9},{9,1},{17,25},{25,17},{2,10},{10... | collective-permute-start | bytes 552968 | tf_op jit(solution)/shard_map/ppermute | solution.py:331
  42.6 18.7 %collective-permute-start.4 = (bf16[160,1152]{1,0:T(8,128)(2,1)}, bf16[160,1152]{1,0:T(8,128)(2,1)}, u32[]{:S(2)}, u32[]{:S(2)}) collective-permute-start(bf16[160,1152]{1,0:T(8,128)(2,1)} %get-tuple-element.189), channel_id=1, source_target_pairs={{0,16},{8,24},{16,0},{24,8},{1,17},{9,25},{17,1},{25,9},{2,18},{10... | collective-permute-start | bytes 1105928 | tf_op jit(solution)/shard_map/ppermute | solution.py:331
  50.0 71.1 %all-gather.8.cloned.1.call-start = ((), (), s32[]{:S(2)}) async-start(), calls=%async_computation.12 | async-start | bytes 3317760 | tf_op jit(solution)/shard_map/all_gather | solution.py:411
  64.7 102.2 %all-gather.10.cloned.1.call-start = ((), (), s32[]{:S(2)}) async-start(), calls=%async_computation.13 | async-start | bytes 2985984 | tf_op jit(solution)/shard_map/all_gather | solution.py:427
  137.9 21.7 %collective-permute-start.12 = (bf16[160,1152]{1,0:T(8,128)(2,1)}, bf16[160,1152]{1,0:T(8,128)(2,1)}, u32[]{:S(2)}, u32[]{:S(2)}) collective-permute-start(bf16[160,1152]{1,0:T(8,128)(2,1)} %bitcast.20), channel_id=1, source_target_pairs={{0,8},{8,0},{16,24},{24,16},{1,9},{9,1},{17,25},{25,17},{2,10},{10... | collective-permute-start | bytes 1105928 | tf_op jit(solution)/shard_map/ppermute | solution.py:331
  139.1 20.5 %collective-permute-start.13 = (bf16[160,1152]{1,0:T(8,128)(2,1)}, bf16[160,1152]{1,0:T(8,128)(2,1)}, u32[]{:S(2)}, u32[]{:S(2)}) collective-permute-start(bf16[160,1152]{1,0:T(8,128)(2,1)} %bitcast.20), channel_id=1, source_target_pairs={{0,16},{8,24},{16,0},{24,8},{1,17},{9,25},{17,1},{25,9},{2,18},{10... | collective-permute-start | bytes 1105928 | tf_op jit(solution)/shard_map/ppermute | solution.py:331
  139.9 19.7 %collective-permute-start.14 = (bf16[160,1152]{1,0:T(8,128)(2,1)}, bf16[160,1152]{1,0:T(8,128)(2,1)}, u32[]{:S(2)}, u32[]{:S(2)}) collective-permute-start(bf16[160,1152]{1,0:T(8,128)(2,1)} %bitcast.20), channel_id=1, source_target_pairs={{0,24},{8,16},{16,8},{24,0},{1,25},{9,17},{17,9},{25,1},{2,26},{10... | collective-permute-start | bytes 1105928 | tf_op jit(solution)/shard_map/ppermute | solution.py:331
  143.1 22.5 %all-to-all-start.2 = ((bf16[8,160,144]{1,2,0:T(8,128)(2,1)}), bf16[8,160,144]{1,2,0:T(8,128)(2,1)}, u32[]{:S(2)}, u32[]{:S(2)}) async-start(bf16[8,160,144]{1,2,0:T(8,128)(2,1)} %copy.64), calls=%async_computation.2 | async-start | bytes 1179648 | tf_op jit(solution)/shard_map/all_to_all | solution.py:355
  147.3 56.3 %all-gather.12.cloned.1.call-start = ((), (), s32[]{:S(2)}) async-start(), calls=%async_computation.14 | async-start | bytes 2985984 | tf_op jit(solution)/shard_map/all_gather | solution.py:453
  166.9 135.4 %reduce-scatter.9.cloned.1.call-start = ((), (), s32[]{:S(2)}) async-start(), calls=%async_computation.16 | async-start | bytes 2985984 | tf_op jit(solution)/shard_map/reduce_scatter | solution.py:464
  203.4 98.9 %reduce-scatter.7.cloned.1.call-start = ((), (), s32[]{:S(2)}) async-start(), calls=%async_computation.15 | async-start | bytes 2985984 | tf_op jit(solution)/shard_map/reduce_scatter | solution.py:485
  247.7 31.2 %all-to-all-start.3 = ((bf16[8,160,144]{1,2,0:T(8,128)(2,1)}), bf16[8,160,144]{1,2,0:T(8,128)(2,1)}, u32[]{:S(2)}, u32[]{:S(2)}) async-start(bf16[8,160,144]{1,2,0:T(8,128)(2,1)} %copy.66), calls=%async_computation.3 | async-start | bytes 1179648 | tf_op jit(solution)/shard_map/all_to_all | solution.py:355
  251.9 90.2 %reduce-scatter.11.cloned.1.call-start = ((), (), s32[]{:S(2)}) async-start(), calls=%async_computation.17 | async-start | bytes 3317760 | tf_op jit(solution)/shard_map/reduce_scatter | solution.py:501
  254.4 25.9 %collective-permute-start.24 = (bf16[160,1152]{1,0:T(8,128)(2,1)}, bf16[160,1152]{1,0:T(8,128)(2,1)}, u32[]{:S(2)}, u32[]{:S(2)}) collective-permute-start(bf16[160,1152]{1,0:T(8,128)(2,1)} %get-tuple-element.186), channel_id=1, source_target_pairs={{0,8},{8,0},{16,24},{24,16},{1,9},{9,1},{17,25},{25,17},{2,10},{10... | collective-permute-start | bytes 1105928 | tf_op jit(solution)/shard_map/ppermute | solution.py:331
  257.8 42.0 %collective-permute-start.25 = (bf16[160,1152]{1,0:T(8,128)(2,1)}, bf16[160,1152]{1,0:T(8,128)(2,1)}, u32[]{:S(2)}, u32[]{:S(2)}) collective-permute-start(bf16[160,1152]{1,0:T(8,128)(2,1)} %get-tuple-element.184), channel_id=1, source_target_pairs={{0,16},{8,24},{16,0},{24,8},{1,17},{9,25},{17,1},{25,9},{2,18},{10... | collective-permute-start | bytes 1105928 | tf_op jit(solution)/shard_map/ppermute | solution.py:331
  259.6 40.2 %collective-permute-start.26 = (bf16[160,1152]{1,0:T(8,128)(2,1)}, bf16[160,1152]{1,0:T(8,128)(2,1)}, u32[]{:S(2)}, u32[]{:S(2)}) collective-permute-start(bf16[160,1152]{1,0:T(8,128)(2,1)} %get-tuple-element.185), channel_id=1, source_target_pairs={{0,24},{8,16},{16,8},{24,0},{1,25},{9,17},{17,9},{25,1},{2,26},{10... | collective-permute-start | bytes 1105928 | tf_op jit(solution)/shard_map/ppermute | solution.py:331
  302.4 23.7 %collective-permute-start.36 = (bf16[160,288]{1,0:T(8,128)(2,1)S(1)}, bf16[160,288]{1,0:T(8,128)(2,1)S(1)}, u32[]{:S(2)}, u32[]{:S(2)}) collective-permute-start(bf16[160,288]{1,0:T(8,128)(2,1)S(1)} %get-tuple-element.208), channel_id=1, source_target_pairs={{0,8},{8,0},{16,24},{24,16},{1,9},{9,1},{17,25},{25,17},{2,10},{10... | collective-permute-start | bytes 276488 | tf_op jit(solution)/shard_map/ppermute | solution.py:331
  302.5 23.6 %collective-permute-start.37 = (bf16[160,288]{1,0:T(8,128)(2,1)S(1)}, bf16[160,288]{1,0:T(8,128)(2,1)S(1)}, u32[]{:S(2)}, u32[]{:S(2)}) collective-permute-start(bf16[160,288]{1,0:T(8,128)(2,1)S(1)} %get-tuple-element.207), channel_id=1, source_target_pairs={{0,16},{8,24},{16,0},{24,8},{1,17},{9,25},{17,1},{25,9},{2,18},{10... | collective-permute-start | bytes 276488 | tf_op jit(solution)/shard_map/ppermute | solution.py:331
  304.5 21.4 %collective-permute-start.31 = (bf16[160,1152]{1,0:T(8,128)(2,1)S(1)}, bf16[160,1152]{1,0:T(8,128)(2,1)S(1)}, u32[]{:S(2)}, u32[]{:S(2)}) collective-permute-start(bf16[160,1152]{1,0:T(8,128)(2,1)S(1)} %copy-done.17), channel_id=1, source_target_pairs={{0,16},{8,24},{16,0},{24,8},{1,17},{9,25},{17,1},{25,9},{2,18},{10... | collective-permute-start | bytes 1105928 | tf_op jit(solution)/shard_map/ppermute | solution.py:331
  306.5 19.4 %collective-permute-start.32 = (bf16[160,1152]{1,0:T(8,128)(2,1)S(1)}, bf16[160,1152]{1,0:T(8,128)(2,1)S(1)}, u32[]{:S(2)}, u32[]{:S(2)}) collective-permute-start(bf16[160,1152]{1,0:T(8,128)(2,1)S(1)} %copy-done.17), channel_id=1, source_target_pairs={{0,24},{8,16},{16,8},{24,0},{1,25},{9,17},{17,9},{25,1},{2,26},{10... | collective-permute-start | bytes 1105928 | tf_op jit(solution)/shard_map/ppermute | solution.py:331
  347.3 18.6 %collective-permute-start.28 = (bf16[160,1152]{1,0:T(8,128)(2,1)}, bf16[160,1152]{1,0:T(8,128)(2,1)S(1)}, u32[]{:S(2)}, u32[]{:S(2)}) collective-permute-start(bf16[160,1152]{1,0:T(8,128)(2,1)} %get-tuple-element.178), channel_id=1, source_target_pairs={{0,16},{8,24},{16,0},{24,8},{1,17},{9,25},{17,1},{25,9},{2,18},{10... | collective-permute-start | bytes 1105928 | tf_op jit(solution)/shard_map/ppermute | solution.py:331
  356.7 49.7 %reduce-scatter.13.cloned.1.call-start = ((), (), s32[]{:S(2)}) async-start(), calls=%async_computation.18 | async-start | bytes 1492992
  373.2 31.8 %all-to-all-start.6 = ((f32[32,8,128]{2,1,0:T(8,128)}), f32[32,8,128]{2,1,0:T(8,128)S(1)}, u32[]{:S(2)}, u32[]{:S(2)}) async-start(f32[32,8,128]{2,1,0:T(8,128)} %bitcast.75), calls=%async_computation.9 | async-start | bytes 262144 | tf_op jit(solution)/shard_map/all_to_all | solution.py:552
  (77 other events, 845.7 us)
Sparse Core Ops, SparseCore 0:
  9.7 27.4 all-gather.5
  64.8 41.0 all-gather.7
  121.2 34.4 all-gather.9
  167.1 32.9 all-gather.11
  203.5 35.8 reduce-scatter.8
  245.6 43.0 reduce-scatter.6
  302.4 35.7 reduce-scatter.10
  372.2 34.0 reduce-scatter.12

commit v13 on v12

--- a/solution.py
+++ b/solution.py
@@ -410,19 +410,20 @@
     normed_one, qkv_mine, own_proj, own_up = after((normed_one, qkv_mine, proj_w, fc1_w))
     normed_one_row = lax.all_gather(normed_one, "seq", axis=0, tiled=True)
 
+    up_slices = jnp.swapaxes(own_up.reshape(small, nd, hidden_part), 0, 1)
+    up_slices = jnp.concatenate(
+        [index(up_slices, dp_at)] + [swap(index(up_slices, dp_at ^ k), k) for k in range(1, nd)],
+        axis=0,
+    )
+    qkv_mine, up_slices, order = after((qkv_mine, up_slices, order))
     qkv_mine = lax.all_gather(qkv_mine, "dp", axis=0, tiled=True)
     qkv_mine, own_proj = after((qkv_mine, own_proj))
     proj_rows = lax.all_gather(own_proj, "seq", axis=0, tiled=True)
     half = part // 2
     own_half = lax.dynamic_slice_in_dim(proj_rows, core * half, half, 0)
     proj_halves = [swap(own_half, k) for k in range(1, nd)]
-    up_slices = jnp.swapaxes(own_up.reshape(small, nd, hidden_part), 0, 1)
-    up_slices = jnp.concatenate(
-        [index(up_slices, dp_at)] + [swap(index(up_slices, dp_at ^ k), k) for k in range(1, nd)],
-        axis=0,
-    )
-    normed_one_row, up_slices, qkv_mine, qkv_wide, segments, proj_halves[0], order = after(
-        (normed_one_row, up_slices, qkv_mine, widen(qkv_mine), segments, proj_halves[0], order)
+    normed_one_row, qkv_mine, qkv_wide, segments, proj_rows = after(
+        (normed_one_row, qkv_mine, widen(qkv_mine), segments, proj_rows)
     )
     up_part = lax.all_gather(up_slices, "seq", axis=0, tiled=True)
     triple = dot(normed_one_row, qkv_wide).astype(BF16)
@@ -478,11 +479,11 @@
     attended_grad, second_late, hidden_late, attended_low, fc1_terms = after(
         (attended_grad, second_low, hidden, attended_low, fc1_terms)
     )
+    fc1_terms = lax.psum_scatter(fc1_terms, "seq", scatter_dimension=0, tiled=True)
     attended_grad = seq_exchange(attended_grad).reshape(row_len, head_cols)
     down_sums = dot(hidden_late, down_part)
     attended_slices = jnp.swapaxes(attended_low.reshape(local, nd, part), 0, 1)
-    down_blocks, fc1_terms = after((low_rows(down_sums), fc1_terms))
-    fc1_terms = lax.psum_scatter(fc1_terms, "seq", scatter_dimension=0, tiled=True)
+    down_blocks = low_rows(down_sums)
     down_blocks = [swap(down_blocks[k], k) for k in range(1, nd)]
     attended_grad, down_blocks[0], second_late, attended_slices = after(
         (attended_grad, down_blocks[0], second_late, attended_slices)

time: 421 us -> 404 us (0.960)
  waiting for transfers between devices: 98.4 us -> 84.1 us
    all_to_all x4, waiting for transfers between devices: 21.2 us -> 13.5 us  [seq_exchange(): return lax.all_to_all(v, 'seq', 0, 0, tiled=True)]
    ppermute x42, waiting for transfers between devices: 62.3 us -> 55.2 us  [swap(): return lax.ppermute(v, 'dp', [(i, i ^ k) for i in range(nd)])]
where the time goes in v13:
time: 404 us; the launch traced here: 396 us
  waiting for transfers between devices  84.1 us (21%)
  starting transfers between devices  80.1 us (20%)
  local copies, waits for them, and re-layouts  55.8 us (14%)
  matrix products  49 us (12%)
  Pallas kernels  41 us (10%)
  other arithmetic  36.4 us (9%)
  blocking collectives  31.1 us (8%)
  between operations  19 us (5%)
    ppermute x42, waiting for transfers between devices, swap(): return lax.ppermute(v, 'dp', [(i, i ^ k) for i in range(nd)])  55.2 us
    ppermute x42, starting transfers between devices, swap(): return lax.ppermute(v, 'dp', [(i, i ^ k) for i in range(nd)])  48 us
    dot_general x6, matrix products, inner(): lax.dot_general(left, right, (((0,), (0,)), ((), ())), preferred_element_...  26.4 us
    all_gather x1, blocking collectives, on_device(): proj_rows = lax.all_gather(own_proj, 'seq', axis=0, tiled=True)  17.5 us
    dot_general x4, matrix products, dot(): return jnp.dot(left, right, preferred_element_type=F32)  16.5 us
    all_to_all x4, starting transfers between devices, seq_exchange(): return lax.all_to_all(v, 'seq', 0, 0, tiled=True)  15.2 us
    pallas_call x1, Pallas kernels, attend_back(): pl.pallas_call(partial(attend_back_kernel, heads, scale), grid=(rows // s...  14.4 us
    all_gather x1, blocking collectives, on_device(): qkv_mine = lax.all_gather(qkv_mine, 'dp', axis=0, tiled=True)  13.6 us
  transfers between devices with their start and end apart: 61, of which 20 were waited for; matrix products, arithmetic and copies ran while one was open for 31% of the time, Pallas kernels for 10%

profile of v13, /device:TPU:0, one launch (start us, length us, event | category | flops | bytes accessed | tf_op | source)
XLA Modules:
  0.0 396.5 jit_solution(9473416614967228161)
XLA Ops:
  15.1 6.3 %all-to-all-start = ((bf16[32,8,128]{2,1,0:T(8,128)(2,1)}), bf16[32,8,128]{2,1,0:T(8,128)(2,1)S(1)}, u32[]{:S(2)}, u32[]{:S(2)}) async-start(bf16[32,8,128]{2,1,0:T(8,128)(2,1)} %broadcast_in_dim.15), calls=%async_computation | async-start | bytes 131072 | tf_op jit(solution)/shard_map/all_to_all | solution.py:376
  22.6 7.0 %all-to-all-done = bf16[32,8,128]{2,1,0:T(8,128)(2,1)S(1)} async-done(((bf16[32,8,128]{2,1,0:T(8,128)(2,1)}), bf16[32,8,128]{2,1,0:T(8,128)(2,1)S(1)}, u32[]{:S(2)}, u32[]{:S(2)}) %all-to-all-start) | async-done | bytes 65568 | tf_op jit(solution)/shard_map/all_to_all | solution.py:376
  30.6 6.6 %all-gather.6.cloned.1.call-done = bf16[576,1152]{1,0:T(8,128)(2,1)} async-done(((bf16[72,1152]{1,0:T(8,128)(2,1)}), bf16[576,1152]{1,0:T(8,128)(2,1)}) %all-gather.6.cloned.1.call-update) | async-done | bytes 1327120 | tf_op jit(solution)/shard_map/all_gather | solution.py:368
  52.9 8.3 %collective-permute-done.4 = bf16[160,1152]{1,0:T(8,128)(2,1)} collective-permute-done((bf16[160,1152]{1,0:T(8,128)(2,1)}, bf16[160,1152]{1,0:T(8,128)(2,1)}, u32[]{:S(2)}, u32[]{:S(2)}) %collective-permute-start.4) | collective-permute-done | bytes 368672 | tf_op jit(solution)/shard_map/ppermute | solution.py:331
  78.7 13.6 %all_gather.20 = bf16[1152,432]{1,0:T(8,128)(2,1)S(1)} all-gather(bf16[288,432]{1,0:T(8,128)(2,1)S(1)} %reshape.201), channel_id=1, replica_groups=mesh['dp'=4,'seq'=8] {'dp'}, dimensions={0}, use_global_device_ids=true | all-gather | bytes 1244160 | tf_op jit(solution)/shard_map/all_gather | solution.py:419
  92.3 17.5 %all-gather = bf16[8,36,1152]{2,1,0:T(8,128)(2,1)S(1)} all-gather(bf16[1,36,1152]{2,1,0:T(8,128)(2,1)S(1)} %bitcast.174), channel_id=1, replica_groups=mesh['dp'=4,'seq'=8] {'seq'}, dimensions={0}, use_global_device_ids=true | all-gather | bytes 746496 | tf_op jit(solution)/shard_map/all_gather | solution.py:421
  116.4 5.1 %convolution_convert_fusion.4.q_ref.k_ref.v_ref = bf16[1280,768]{1,0:T(8,128)(2,1)S(1)} fusion(bf16[1280,1152]{1,0:T(8,128)(2,1)} %all-gather.8.cloned.1.call-done, bf16[1152,768]{0,1:T(8,128)(2,1)} %bitcast.159), kind=kOutput, calls=%fused_computation.23 | convolution fusion | flops 2265907200 | bytes 6684672 | tf_op jit(solution)/shard_map/dot_general | solution.py:46
  121.8 8.4 %shard_map.288 = (f32[1280,256]{1,0:T(8,128)S(1)}, bf16[1280,144]{1,0:T(8,128)(2,1)S(1)}, f32[8,1280]{1,0:T(8,128)S(1)}) custom-call(bf16[1280,768]{1,0:T(8,128)(2,1)S(1)} %convolution_convert_fusion.4.q_ref.k_ref.v_ref, bf16[1280,768]{1,0:T(8,128)(2,1)S(1)} %convolution_convert_fusion.4.q_ref.k_ref.v_ref, ...), custom_call_target="tpu_custom_call" | custom-call | flops 3355443200 | bytes 3276800 | tf_op jit(solution)/shard_map/pallas_call | solution.py:84
  165.8 4.0 %convolution_convert_fusion.3.up_ref = bf16[1152,1152]{1,0:T(8,128)(2,1)S(1)} fusion(bf16[1152,1152]{1,0:T(8,128)(2,1)S(1)} %copy-done.20, bf16[1152,1152]{1,0:T(8,128)(2,1)S(1)} %copy-done.39), kind=kOutput, calls=%fused_computation.11 | convolution fusion | flops 3058974720 | bytes 7962624 | tf_op jit(solution)/shard_map/dot_general | solution.py:50
  173.8 7.2 %collective-permute-done.19 = bf16[160,1152]{1,0:T(8,128)(2,1)S(1)} collective-permute-done((bf16[160,1152]{1,0:T(8,128)(2,1)S(1)}, bf16[160,1152]{1,0:T(8,128)(2,1)S(1)}, u32[]{:S(2)}, u32[]{:S(2)}) %collective-permute-start.19) | collective-permute-done | bytes 368672 | tf_op jit(solution)/shard_map/ppermute | solution.py:331
  181.1 5.7 %shard_map.289 = (bf16[640,1152]{1,0:T(8,128)(2,1)S(1)}, f32[640,1152]{1,0:T(8,128)S(1)}) custom-call(bf16[640,1152]{1,0:T(8,128)(2,1)S(1)} %pad_maximum_fusion.1.x_ref, bf16[1152,1152]{1,0:T(8,128)(2,1)S(1)} %convolution_convert_fusion.3.up_ref, f32[1,1152]{1,0:T(1,128)S(1)} %reshape_reshape.6.bias_ref), custom_call_target="tpu_custom_call" | custom-call | flops 1698693120 | bytes 8552448 | tf_op jit(solution)/shard_map/pallas_call | solution.py:250
  193.7 9.0 %shard_map.290 = (bf16[640,1152]{1,0:T(8,128)(2,1)}, f32[1,1152]{1,0:T(1,128)S(1)}, f32[160,1152]{1,0:T(8,128)S(1)}, bf16[160,1152]{1,0:T(8,128)(2,1)}, bf16[160...) custom-call(bf16[640,1152]{1,0:T(8,128)(2,1)} %pad_maximum_fusion.grad_ref, bf16[1152,1152]{1,0:T(8,128)(2,1)} %copy-done.1, ...), custom_call_target="tpu_custom_call" | custom-call | flops 3397386240 | bytes 12681216 | tf_op jit(solution)/shard_map/pallas_call | solution.py:288
  206.2 8.9 %convolution_convert_fusion.1 = bf16[1152,1152]{1,0:T(8,128)(2,1)} fusion(bf16[640,1152]{1,0:T(8,128)(2,1)} %get-tuple-element.132, bf16[640,1152]{1,0:T(8,128)(2,1)S(1)} %pad_maximum_fusion.1.x_ref, bf16[1152,1152]{1,0:T(8,128)(2,1)} %fusion.10), kind=kOutput, calls=%fused_computation.9 | convolution fusion | flops 3399450624 | bytes 8257536 | tf_op jit(solution)/shard_map/dot_general | solution.py:50
  215.1 6.0 %collective-permute-done.22 = bf16[160,1152]{1,0:T(8,128)(2,1)} collective-permute-done((bf16[160,1152]{1,0:T(8,128)(2,1)}, bf16[160,1152]{1,0:T(8,128)(2,1)}, u32[]{:S(2)}, u32[]{:S(2)}) %collective-permute-start.22) | collective-permute-done | bytes 368672 | tf_op jit(solution)/shard_map/ppermute | solution.py:331
  231.0 4.7 %all-to-all-start.3 = ((bf16[8,160,144]{1,2,0:T(8,128)(2,1)}), bf16[8,160,144]{1,2,0:T(8,128)(2,1)}, u32[]{:S(2)}, u32[]{:S(2)}) async-start(bf16[8,160,144]{1,2,0:T(8,128)(2,1)} %copy.66), calls=%async_computation.3 | async-start | bytes 1179648 | tf_op jit(solution)/shard_map/all_to_all | solution.py:355
  235.8 5.7 %fusion.61 = (bf16[640,1152]{1,0:T(8,128)(2,1)S(1)}, f32[640,1152]{1,0:T(8,128)}) fusion(bf16[640,1152]{1,0:T(8,128)(2,1)S(1)} %copy-done.3, bf16[1152,1152]{1,0:T(8,128)(2,1)} %all-gather.12.cloned.1.call-done.down_ref), kind=kOutput, calls=%fused_computation.177 | convolution fusion | flops 1699430400 | bytes 8552448 | tf_op jit(solution)/shard_map/dot_general | solution.py:46
  249.3 11.8 %all-to-all-done.3 = bf16[8,160,144]{1,2,0:T(8,128)(2,1)} async-done(((bf16[8,160,144]{1,2,0:T(8,128)(2,1)}), bf16[8,160,144]{1,2,0:T(8,128)(2,1)}, u32[]{:S(2)}, u32[]{:S(2)}) %all-to-all-start.3) | async-done | bytes 368672 | tf_op jit(solution)/shard_map/all_to_all | solution.py:355
  262.7 14.4 %shard_map.292 = (bf16[1280,144]{1,0:T(8,128)(2,1)S(1)}, bf16[1280,288]{1,0:T(8,128)(2,1)S(1)}) custom-call(bf16[1280,768]{1,0:T(8,128)(2,1)} %copy-done.4, bf16[1280,768]{1,0:T(8,128)(2,1)} %copy-done.4, bf16[1280,768]{1,0:T(8,128)(2,1)} %copy-done.4, bf16[1280,256]{1,0:T(8,128)(2,1)S(1)} %pad.18.out_grad_ref, f32[1280,256]{1,0:T(8,128)S(1)} %copy-done.6, ...), custom_call_target="tpu_custom_call" | custom-call | flops 8388608000 | bytes 4587520 | tf_op jit(solution)/shard_map/pallas_call | solution.py:164
  294.7 4.4 %collective-permute-done.30 = bf16[160,1152]{1,0:T(8,128)(2,1)S(1)} collective-permute-done((bf16[160,1152]{1,0:T(8,128)(2,1)S(1)}, bf16[160,1152]{1,0:T(8,128)(2,1)S(1)}, u32[]{:S(2)}, u32[]{:S(2)}) %collective-permute-start.30) | collective-permute-done | bytes 368672 | tf_op jit(solution)/shard_map/ppermute | solution.py:331
  299.9 7.0 %collective-permute-done.31 = bf16[160,1152]{1,0:T(8,128)(2,1)S(1)} collective-permute-done((bf16[160,1152]{1,0:T(8,128)(2,1)S(1)}, bf16[160,1152]{1,0:T(8,128)(2,1)S(1)}, u32[]{:S(2)}, u32[]{:S(2)}) %collective-permute-start.31) | collective-permute-done | bytes 368672 | tf_op jit(solution)/shard_map/ppermute | solution.py:331
  319.4 4.2 %all-to-all-start.5 = ((bf16[4,36,1152]{2,1,0:T(8,128)(2,1)}), bf16[4,36,1152]{2,1,0:T(8,128)(2,1)S(1)}, u32[]{:S(2)}, u32[]{:S(2)}) async-start(bf16[4,36,1152]{2,1,0:T(8,128)(2,1)} %fusion.28), calls=%async_computation.8 | async-start | bytes 737280 | tf_op jit(solution)/shard_map/all_to_all | solution.py:365
  341.7 5.1 %collective-permute-done.28 = bf16[160,1152]{1,0:T(8,128)(2,1)S(1)} collective-permute-done((bf16[160,1152]{1,0:T(8,128)(2,1)}, bf16[160,1152]{1,0:T(8,128)(2,1)S(1)}, u32[]{:S(2)}, u32[]{:S(2)}) %collective-permute-start.28) | collective-permute-done | bytes 368672 | tf_op jit(solution)/shard_map/ppermute | solution.py:331
  354.3 4.2 %all-to-all-start.6 = ((f32[32,8,128]{2,1,0:T(8,128)}), f32[32,8,128]{2,1,0:T(8,128)S(1)}, u32[]{:S(2)}, u32[]{:S(2)}) async-start(f32[32,8,128]{2,1,0:T(8,128)} %bitcast.71), calls=%async_computation.9 | async-start | bytes 262144 | tf_op jit(solution)/shard_map/all_to_all | solution.py:553
  376.5 4.9 %collective-permute-done.41 = bf16[160,576]{0,1:T(8,128)(2,1)} collective-permute-done((bf16[160,576]{0,1:T(8,128)(2,1)S(1)}, bf16[160,576]{0,1:T(8,128)(2,1)}, u32[]{:S(2)}, u32[]{:S(2)}) %collective-permute-start.41) | collective-permute-done | bytes 184352 | tf_op jit(solution)/shard_map/ppermute | solution.py:331
  (338 shorter events, 197.5 us)
Async XLA Ops:
  7.3 30.0 %all-gather.6.cloned.1.call-start = ((), (), s32[]{:S(2)}) async-start(), calls=%async_computation.11 | async-start | bytes 1492992 | tf_op jit(solution)/shard_map/all_gather | solution.py:368
  9.7 19.9 %collective-permute-start = (bf16[160,576]{1,0:T(8,128)(2,1)S(1)}, bf16[160,576]{1,0:T(8,128)(2,1)S(1)}, u32[]{:S(2)}, u32[]{:S(2)}) collective-permute-start(bf16[160,576]{1,0:T(8,128)(2,1)S(1)} %get-tuple-element.198), channel_id=1, source_target_pairs={{0,8},{8,0},{16,24},{24,16},{1,9},{9,1},{17,25},{25,17},{2,10},{10... | collective-permute-start | bytes 552968 | tf_op jit(solution)/shard_map/ppermute | solution.py:331
  42.6 18.7 %collective-permute-start.4 = (bf16[160,1152]{1,0:T(8,128)(2,1)}, bf16[160,1152]{1,0:T(8,128)(2,1)}, u32[]{:S(2)}, u32[]{:S(2)}) collective-permute-start(bf16[160,1152]{1,0:T(8,128)(2,1)} %get-tuple-element.187), channel_id=1, source_target_pairs={{0,16},{8,24},{16,0},{24,8},{1,17},{9,25},{17,1},{25,9},{2,18},{10... | collective-permute-start | bytes 1105928 | tf_op jit(solution)/shard_map/ppermute | solution.py:331
  45.9 18.6 %all-to-all-start.1 = ((bf16[8,36,432]{2,1,0:T(8,128)(2,1)}), bf16[8,36,432]{2,1,0:T(8,128)(2,1)S(1)}, u32[]{:S(2)}, u32[]{:S(2)}) async-start(bf16[8,36,432]{2,1,0:T(8,128)(2,1)} %copy.61), calls=%async_computation.1 | async-start | bytes 655360 | tf_op jit(solution)/shard_map/all_to_all | solution.py:355
  49.3 67.1 %all-gather.8.cloned.1.call-start = ((), (), s32[]{:S(2)}) async-start(), calls=%async_computation.12 | async-start | bytes 3317760 | tf_op jit(solution)/shard_map/all_gather | solution.py:411
  64.6 93.2 %all-gather.10.cloned.1.call-start = ((), (), s32[]{:S(2)}) async-start(), calls=%async_computation.13 | async-start | bytes 2985984 | tf_op jit(solution)/shard_map/all_gather | solution.py:428
  110.7 19.5 %collective-permute-start.10 = (bf16[144,1152]{1,0:T(8,128)(2,1)}, bf16[144,1152]{1,0:T(8,128)(2,1)}, u32[]{:S(2)}, u32[]{:S(2)}) collective-permute-start(bf16[144,1152]{1,0:T(8,128)(2,1)} %constant_dynamic-slice_fusion.5), channel_id=1, source_target_pairs={{0,16},{8,24},{16,0},{24,8},{1,17},{9,25},{17,1},{25,9},{2,18},{10... | collective-permute-start | bytes 995336 | tf_op jit(solution)/shard_map/ppermute | solution.py:331
  130.2 21.2 %collective-permute-start.12 = (bf16[160,1152]{1,0:T(8,128)(2,1)}, bf16[160,1152]{1,0:T(8,128)(2,1)}, u32[]{:S(2)}, u32[]{:S(2)}) collective-permute-start(bf16[160,1152]{1,0:T(8,128)(2,1)} %bitcast.20), channel_id=1, source_target_pairs={{0,8},{8,0},{16,24},{24,16},{1,9},{9,1},{17,25},{25,17},{2,10},{10... | collective-permute-start | bytes 1105928 | tf_op jit(solution)/shard_map/ppermute | solution.py:331
  131.3 20.1 %collective-permute-start.13 = (bf16[160,1152]{1,0:T(8,128)(2,1)}, bf16[160,1152]{1,0:T(8,128)(2,1)}, u32[]{:S(2)}, u32[]{:S(2)}) collective-permute-start(bf16[160,1152]{1,0:T(8,128)(2,1)} %bitcast.20), channel_id=1, source_target_pairs={{0,16},{8,24},{16,0},{24,8},{1,17},{9,25},{17,1},{25,9},{2,18},{10... | collective-permute-start | bytes 1105928 | tf_op jit(solution)/shard_map/ppermute | solution.py:331
  132.7 18.8 %collective-permute-start.14 = (bf16[160,1152]{1,0:T(8,128)(2,1)}, bf16[160,1152]{1,0:T(8,128)(2,1)}, u32[]{:S(2)}, u32[]{:S(2)}) collective-permute-start(bf16[160,1152]{1,0:T(8,128)(2,1)} %bitcast.20), channel_id=1, source_target_pairs={{0,24},{8,16},{16,8},{24,0},{1,25},{9,17},{17,9},{25,1},{2,26},{10... | collective-permute-start | bytes 1105928 | tf_op jit(solution)/shard_map/ppermute | solution.py:331
  135.5 20.2 %all-to-all-start.2 = ((bf16[8,160,144]{1,2,0:T(8,128)(2,1)}), bf16[8,160,144]{1,2,0:T(8,128)(2,1)S(1)}, u32[]{:S(2)}, u32[]{:S(2)}) async-start(bf16[8,160,144]{1,2,0:T(8,128)(2,1)} %copy.64), calls=%async_computation.2 | async-start | bytes 1179648 | tf_op jit(solution)/shard_map/all_to_all | solution.py:355
  139.0 54.7 %all-gather.12.cloned.1.call-start = ((), (), s32[]{:S(2)}) async-start(), calls=%async_computation.14 | async-start | bytes 2985984 | tf_op jit(solution)/shard_map/all_gather | solution.py:454
  157.9 126.9 %reduce-scatter.9.cloned.1.call-start = ((), (), s32[]{:S(2)}) async-start(), calls=%async_computation.16 | async-start | bytes 2985984 | tf_op jit(solution)/shard_map/reduce_scatter | solution.py:465
  193.5 91.3 %reduce-scatter.7.cloned.1.call-start = ((), (), s32[]{:S(2)}) async-start(), calls=%async_computation.15 | async-start | bytes 2985984 | tf_op jit(solution)/shard_map/reduce_scatter | solution.py:482
  231.0 30.1 %all-to-all-start.3 = ((bf16[8,160,144]{1,2,0:T(8,128)(2,1)}), bf16[8,160,144]{1,2,0:T(8,128)(2,1)}, u32[]{:S(2)}, u32[]{:S(2)}) async-start(bf16[8,160,144]{1,2,0:T(8,128)(2,1)} %copy.66), calls=%async_computation.3 | async-start | bytes 1179648 | tf_op jit(solution)/shard_map/all_to_all | solution.py:355
  235.8 87.8 %reduce-scatter.11.cloned.1.call-start = ((), (), s32[]{:S(2)}) async-start(), calls=%async_computation.17 | async-start | bytes 3317760 | tf_op jit(solution)/shard_map/reduce_scatter | solution.py:502
  242.6 19.9 %collective-permute-start.24 = (bf16[160,1152]{1,0:T(8,128)(2,1)}, bf16[160,1152]{1,0:T(8,128)(2,1)}, u32[]{:S(2)}, u32[]{:S(2)}) collective-permute-start(bf16[160,1152]{1,0:T(8,128)(2,1)} %get-tuple-element.184), channel_id=1, source_target_pairs={{0,8},{8,0},{16,24},{24,16},{1,9},{9,1},{17,25},{25,17},{2,10},{10... | collective-permute-start | bytes 1105928 | tf_op jit(solution)/shard_map/ppermute | solution.py:331
  246.5 35.8 %collective-permute-start.25 = (bf16[160,1152]{1,0:T(8,128)(2,1)}, bf16[160,1152]{1,0:T(8,128)(2,1)}, u32[]{:S(2)}, u32[]{:S(2)}) collective-permute-start(bf16[160,1152]{1,0:T(8,128)(2,1)} %get-tuple-element.182), channel_id=1, source_target_pairs={{0,16},{8,24},{16,0},{24,8},{1,17},{9,25},{17,1},{25,9},{2,18},{10... | collective-permute-start | bytes 1105928 | tf_op jit(solution)/shard_map/ppermute | solution.py:331
  247.5 34.7 %collective-permute-start.26 = (bf16[160,1152]{1,0:T(8,128)(2,1)}, bf16[160,1152]{1,0:T(8,128)(2,1)}, u32[]{:S(2)}, u32[]{:S(2)}) collective-permute-start(bf16[160,1152]{1,0:T(8,128)(2,1)} %get-tuple-element.183), channel_id=1, source_target_pairs={{0,24},{8,16},{16,8},{24,0},{1,25},{9,17},{17,9},{25,1},{2,26},{10... | collective-permute-start | bytes 1105928 | tf_op jit(solution)/shard_map/ppermute | solution.py:331
  284.9 22.2 %collective-permute-start.36 = (bf16[160,288]{1,0:T(8,128)(2,1)S(1)}, bf16[160,288]{1,0:T(8,128)(2,1)S(1)}, u32[]{:S(2)}, u32[]{:S(2)}) collective-permute-start(bf16[160,288]{1,0:T(8,128)(2,1)S(1)} %get-tuple-element.206), channel_id=1, source_target_pairs={{0,8},{8,0},{16,24},{24,16},{1,9},{9,1},{17,25},{25,17},{2,10},{10... | collective-permute-start | bytes 276488 | tf_op jit(solution)/shard_map/ppermute | solution.py:331
  284.9 22.1 %collective-permute-start.37 = (bf16[160,288]{1,0:T(8,128)(2,1)S(1)}, bf16[160,288]{1,0:T(8,128)(2,1)S(1)}, u32[]{:S(2)}, u32[]{:S(2)}) collective-permute-start(bf16[160,288]{1,0:T(8,128)(2,1)S(1)} %get-tuple-element.205), channel_id=1, source_target_pairs={{0,16},{8,24},{16,0},{24,8},{1,17},{9,25},{17,1},{25,9},{2,18},{10... | collective-permute-start | bytes 276488 | tf_op jit(solution)/shard_map/ppermute | solution.py:331
  287.1 19.8 %collective-permute-start.31 = (bf16[160,1152]{1,0:T(8,128)(2,1)S(1)}, bf16[160,1152]{1,0:T(8,128)(2,1)S(1)}, u32[]{:S(2)}, u32[]{:S(2)}) collective-permute-start(bf16[160,1152]{1,0:T(8,128)(2,1)S(1)} %copy-done.17), channel_id=1, source_target_pairs={{0,16},{8,24},{16,0},{24,8},{1,17},{9,25},{17,1},{25,9},{2,18},{10... | collective-permute-start | bytes 1105928 | tf_op jit(solution)/shard_map/ppermute | solution.py:331
  338.1 49.4 %reduce-scatter.13.cloned.1.call-start = ((), (), s32[]{:S(2)}) async-start(), calls=%async_computation.18 | async-start | bytes 1492992
  354.3 32.0 %all-to-all-start.6 = ((f32[32,8,128]{2,1,0:T(8,128)}), f32[32,8,128]{2,1,0:T(8,128)S(1)}, u32[]{:S(2)}, u32[]{:S(2)}) async-start(f32[32,8,128]{2,1,0:T(8,128)} %bitcast.71), calls=%async_computation.9 | async-start | bytes 262144 | tf_op jit(solution)/shard_map/all_to_all | solution.py:553
  (77 other events, 798.3 us)
Sparse Core Ops, SparseCore 0:
  9.7 27.4 all-gather.5
  64.8 37.1 all-gather.7
  104.2 33.8 all-gather.9
  158.0 33.0 all-gather.11
  193.6 36.9 reduce-scatter.8
  232.8 44.4 reduce-scatter.6
  284.9 35.9 reduce-scatter.10
  353.2 34.2 reduce-scatter.12

commit v14 on v13

--- a/solution.py
+++ b/solution.py
@@ -394,7 +394,16 @@
     order = (row == lax.broadcasted_iota(jnp.int32, (features, features), 1)).astype(BF16)
     qkv_out = qkv_w.reshape(small, 3, ns, head_cols).transpose(2, 0, 1, 3).reshape(ns, small, wide)
     segments = segment_of(item_lengths, jnp.arange(row_len, dtype=jnp.int32))
-    qkv_out, skip_part, joined_here, vectors = after((qkv_out, skip_part, joined_here, vectors))
+    up_slices = jnp.swapaxes(fc1_w.reshape(small, nd, hidden_part), 0, 1)
+    up_slices = jnp.concatenate(
+        [index(up_slices, dp_at)] + [swap(index(up_slices, dp_at ^ k), k) for k in range(1, nd)],
+        axis=0,
+    )
+    joined_here, grad_out = after((joined_here, cotangent[0]))
+    grad_out_rows = gather_rows(grad_out)
+    qkv_out, skip_part, joined_here, vectors, up_slices, grad_out_rows = after(
+        (qkv_out, skip_part, joined_here, vectors, up_slices, grad_out_rows)
+    )
     def vector(at):
         return vectors[:, at * small : (at + 1) * small].reshape(features)
 
@@ -407,15 +416,10 @@
     qkv_mine = seq_exchange(qkv_out).reshape(part, wide)
     xhat_one, inverse_one = norm_pieces(first)
     normed_one = (xhat_one * g_one + b_one).astype(BF16)
-    normed_one, qkv_mine, own_proj, own_up = after((normed_one, qkv_mine, proj_w, fc1_w))
+    normed_one, qkv_mine, own_proj = after((normed_one, qkv_mine, proj_w))
     normed_one_row = lax.all_gather(normed_one, "seq", axis=0, tiled=True)
 
-    up_slices = jnp.swapaxes(own_up.reshape(small, nd, hidden_part), 0, 1)
-    up_slices = jnp.concatenate(
-        [index(up_slices, dp_at)] + [swap(index(up_slices, dp_at ^ k), k) for k in range(1, nd)],
-        axis=0,
-    )
-    qkv_mine, up_slices, order = after((qkv_mine, up_slices, order))
+    qkv_mine, order = after((qkv_mine, order))
     qkv_mine = lax.all_gather(qkv_mine, "dp", axis=0, tiled=True)
     qkv_mine, own_proj = after((qkv_mine, own_proj))
     proj_rows = lax.all_gather(own_proj, "seq", axis=0, tiled=True)
@@ -433,9 +437,7 @@
         v = seq_exchange(v.reshape(ns, local, head_cols))
         return jnp.swapaxes(v, 0, 1).reshape(local, features)
 
-    attended_low, grad_out, proj_halves, proj_rows = after(
-        (attended_low, cotangent[0], proj_halves, proj_rows)
-    )
+    attended_low, proj_halves, proj_rows = after((attended_low, proj_halves, proj_rows))
     w_proj = lax.dynamic_update_slice_in_dim(
         jnp.zeros((features, features), BF16), proj_rows, dp_at * part, 0
     )
@@ -445,7 +447,6 @@
         there = other_core(here)
         w_proj = lax.dynamic_update_slice_in_dim(w_proj, here, (place + core) * half, 0)
         w_proj = lax.dynamic_update_slice_in_dim(w_proj, there, (place + 1 - core) * half, 0)
-    grad_out_rows = gather_rows(grad_out)
     attended_low = heads_to_tokens(attended_low)
     attended_low, grad_out_rows, w_proj, order = after(
         (attended_low, grad_out_rows, w_proj, order)

time: 404 us -> 413 us (1.022)
  waiting for transfers between devices: 84.1 us -> 90.9 us
    ppermute x42, waiting for transfers between devices: 55.2 us -> 69.1 us  [swap(): return lax.ppermute(v, 'dp', [(i, i ^ k) for i in range(nd)])]
    all_to_all x1, waiting for transfers between devices: 6.98 us -> 0.01 us  [on_device(): vectors = lax.all_to_all(packed, ('dp', 'seq'), 0, 0, tiled=True)]
    all_gather x1, waiting for transfers between devices: 6.62 us -> 0.01 us  [on_device(): skip_part = lax.all_gather(skip_w, 'seq', axis=0, tiled=True)]
    all_to_all x4, waiting for transfers between devices: 13.5 us -> 19.5 us  [seq_exchange(): return lax.all_to_all(v, 'seq', 0, 0, tiled=True)]
    unnamed x86 -> x90, local copies, waits for them, and re-layouts: 7.99 us -> 8.47 us
  transfers between devices with their start and end apart: 61 -> 61, of which waited for: 20 -> 21; matrix products, arithmetic and copies ran while one was open for 31% -> 31% of each run, Pallas kernels for 10% -> 10%
where the time goes in v14:
time: 413 us; the launch traced here: 405 us
  waiting for transfers between devices  90.9 us (22%)
  starting transfers between devices  80.1 us (19%)
  local copies, waits for them, and re-layouts  57.3 us (14%)
  matrix products  49.2 us (12%)
  Pallas kernels  40.9 us (10%)
  other arithmetic  35 us (8%)
  blocking collectives  33.1 us (8%)
  between operations  19 us (5%)
    ppermute x42, waiting for transfers between devices, swap(): return lax.ppermute(v, 'dp', [(i, i ^ k) for i in range(nd)])  69.1 us
    ppermute x42, starting transfers between devices, swap(): return lax.ppermute(v, 'dp', [(i, i ^ k) for i in range(nd)])  49.4 us
    dot_general x6, matrix products, inner(): lax.dot_general(left, right, (((0,), (0,)), ((), ())), preferred_element_...  26.3 us
    all_gather x1, blocking collectives, on_device(): proj_rows = lax.all_gather(own_proj, 'seq', axis=0, tiled=True)  20.3 us
    all_to_all x4, waiting for transfers between devices, seq_exchange(): return lax.all_to_all(v, 'seq', 0, 0, tiled=True)  19.5 us
    dot_general x4, matrix products, dot(): return jnp.dot(left, right, preferred_element_type=F32)  16.7 us
    all_to_all x4, starting transfers between devices, seq_exchange(): return lax.all_to_all(v, 'seq', 0, 0, tiled=True)  16.3 us
    pallas_call x1, Pallas kernels, attend_back(): pl.pallas_call(partial(attend_back_kernel, heads, scale), grid=(rows // s...  14.4 us
  transfers between devices with their start and end apart: 61, of which 21 were waited for; matrix products, arithmetic and copies ran while one was open for 31% of the time, Pallas kernels for 10%

profile of v14, /device:TPU:0, one launch (start us, length us, event | category | flops | bytes accessed | tf_op | source)
XLA Modules:
  0.0 405.4 jit_solution(1940449726290690873)
XLA Ops:
  18.7 4.1 %collective-permute-done.1 = bf16[160,576]{1,0:T(8,128)(2,1)S(1)} collective-permute-done((bf16[160,576]{1,0:T(8,128)(2,1)S(1)}, bf16[160,576]{1,0:T(8,128)(2,1)S(1)}, u32[]{:S(2)}, u32[]{:S(2)}) %collective-permute-start.1) | collective-permute-done | bytes 184352 | tf_op jit(solution)/shard_map/ppermute | solution.py:331
  33.5 4.2 %all-to-all-start = ((bf16[32,8,128]{2,1,0:T(8,128)(2,1)}), bf16[32,8,128]{2,1,0:T(8,128)(2,1)S(1)}, u32[]{:S(2)}, u32[]{:S(2)}) async-start(bf16[32,8,128]{2,1,0:T(8,128)(2,1)} %broadcast_in_dim.15), calls=%async_computation | async-start | bytes 131072 | tf_op jit(solution)/shard_map/all_to_all | solution.py:376
  38.9 8.7 %collective-permute-done.4 = bf16[36,1152]{1,0:T(8,128)(2,1)S(1)} collective-permute-done((bf16[36,1152]{1,0:T(8,128)(2,1)S(1)}, bf16[36,1152]{1,0:T(8,128)(2,1)S(1)}, u32[]{:S(2)}, u32[]{:S(2)}) %collective-permute-start.4) | collective-permute-done | bytes 82976 | tf_op jit(solution)/shard_map/ppermute | solution.py:331
  59.3 5.0 %all-to-all-start.1 = ((bf16[8,36,432]{2,1,0:T(8,128)(2,1)}), bf16[8,36,432]{2,1,0:T(8,128)(2,1)S(1)}, u32[]{:S(2)}, u32[]{:S(2)}) async-start(bf16[8,36,432]{2,1,0:T(8,128)(2,1)} %copy.61), calls=%async_computation.1 | async-start | bytes 655360 | tf_op jit(solution)/shard_map/all_to_all | solution.py:355
  64.3 7.4 %collective-permute-done.10 = bf16[160,1152]{1,0:T(8,128)(2,1)} collective-permute-done((bf16[160,1152]{1,0:T(8,128)(2,1)}, bf16[160,1152]{1,0:T(8,128)(2,1)}, u32[]{:S(2)}, u32[]{:S(2)}) %collective-permute-start.10) | collective-permute-done | bytes 368672 | tf_op jit(solution)/shard_map/ppermute | solution.py:331
  85.2 12.8 %all_gather.20 = bf16[1152,432]{1,0:T(8,128)(2,1)S(1)} all-gather(bf16[288,432]{1,0:T(8,128)(2,1)S(1)} %reshape.202), channel_id=1, replica_groups=mesh['dp'=4,'seq'=8] {'dp'}, dimensions={0}, use_global_device_ids=true | all-gather | bytes 1244160 | tf_op jit(solution)/shard_map/all_gather | solution.py:423
  98.0 20.3 %all-gather = bf16[8,36,1152]{2,1,0:T(8,128)(2,1)S(1)} all-gather(bf16[1,36,1152]{2,1,0:T(8,128)(2,1)S(1)} %bitcast.179), channel_id=1, replica_groups=mesh['dp'=4,'seq'=8] {'seq'}, dimensions={0}, use_global_device_ids=true | all-gather | bytes 746496 | tf_op jit(solution)/shard_map/all_gather | solution.py:425
  124.9 5.3 %convolution_convert_fusion.4.q_ref.k_ref.v_ref = bf16[1280,768]{1,0:T(8,128)(2,1)S(1)} fusion(bf16[1280,1152]{1,0:T(8,128)(2,1)} %all-gather.8.cloned.1.call-done, bf16[1152,768]{0,1:T(8,128)(2,1)} %bitcast.159), kind=kOutput, calls=%fused_computation.23 | convolution fusion | flops 2265907200 | bytes 6684672 | tf_op jit(solution)/shard_map/dot_general | solution.py:46
  130.5 8.4 %shard_map.288 = (f32[1280,256]{1,0:T(8,128)S(1)}, bf16[1280,144]{1,0:T(8,128)(2,1)S(1)}, f32[8,1280]{1,0:T(8,128)S(1)}) custom-call(bf16[1280,768]{1,0:T(8,128)(2,1)S(1)} %convolution_convert_fusion.4.q_ref.k_ref.v_ref, bf16[1280,768]{1,0:T(8,128)(2,1)S(1)} %convolution_convert_fusion.4.q_ref.k_ref.v_ref, ...), custom_call_target="tpu_custom_call" | custom-call | flops 3355443200 | bytes 3276800 | tf_op jit(solution)/shard_map/pallas_call | solution.py:84
  157.4 7.7 %all-to-all-done.2 = bf16[8,160,144]{1,2,0:T(8,128)(2,1)S(1)} async-done(((bf16[8,160,144]{1,2,0:T(8,128)(2,1)}), bf16[8,160,144]{1,2,0:T(8,128)(2,1)S(1)}, u32[]{:S(2)}, u32[]{:S(2)}) %all-to-all-start.2) | async-done | bytes 368672 | tf_op jit(solution)/shard_map/all_to_all | solution.py:355
  183.0 8.1 %collective-permute-done.19 = bf16[160,1152]{1,0:T(8,128)(2,1)S(1)} collective-permute-done((bf16[160,1152]{1,0:T(8,128)(2,1)S(1)}, bf16[160,1152]{1,0:T(8,128)(2,1)S(1)}, u32[]{:S(2)}, u32[]{:S(2)}) %collective-permute-start.19) | collective-permute-done | bytes 368672 | tf_op jit(solution)/shard_map/ppermute | solution.py:331
  191.3 5.7 %shard_map.289 = (bf16[640,1152]{1,0:T(8,128)(2,1)S(1)}, f32[640,1152]{1,0:T(8,128)S(1)}) custom-call(bf16[640,1152]{1,0:T(8,128)(2,1)S(1)} %pad_maximum_fusion.1.x_ref, bf16[1152,1152]{1,0:T(8,128)(2,1)S(1)} %convolution_convert_fusion.3.up_ref, f32[1,1152]{1,0:T(1,128)S(1)} %reshape_reshape.6.bias_ref), custom_call_target="tpu_custom_call" | custom-call | flops 1698693120 | bytes 8552448 | tf_op jit(solution)/shard_map/pallas_call | solution.py:250
  203.9 9.0 %shard_map.290 = (bf16[640,1152]{1,0:T(8,128)(2,1)}, f32[1,1152]{1,0:T(1,128)S(1)}, f32[160,1152]{1,0:T(8,128)S(1)}, bf16[160,1152]{1,0:T(8,128)(2,1)}, bf16[160...) custom-call(bf16[640,1152]{1,0:T(8,128)(2,1)} %pad_maximum_fusion.grad_ref, bf16[1152,1152]{1,0:T(8,128)(2,1)} %copy-done.1, ...), custom_call_target="tpu_custom_call" | custom-call | flops 3397386240 | bytes 12681216 | tf_op jit(solution)/shard_map/pallas_call | solution.py:288
  216.4 8.9 %convolution_convert_fusion.1 = bf16[1152,1152]{1,0:T(8,128)(2,1)} fusion(bf16[640,1152]{1,0:T(8,128)(2,1)} %get-tuple-element.134, bf16[640,1152]{1,0:T(8,128)(2,1)S(1)} %pad_maximum_fusion.1.x_ref, bf16[1152,1152]{1,0:T(8,128)(2,1)} %fusion.10), kind=kOutput, calls=%fused_computation.9 | convolution fusion | flops 3399450624 | bytes 8257536 | tf_op jit(solution)/shard_map/dot_general | solution.py:50
  225.3 6.4 %collective-permute-done.22 = bf16[160,1152]{1,0:T(8,128)(2,1)} collective-permute-done((bf16[160,1152]{1,0:T(8,128)(2,1)}, bf16[160,1152]{1,0:T(8,128)(2,1)}, u32[]{:S(2)}, u32[]{:S(2)}) %collective-permute-start.22) | collective-permute-done | bytes 368672 | tf_op jit(solution)/shard_map/ppermute | solution.py:331
  240.6 4.2 %all-to-all-start.3 = ((bf16[8,160,144]{1,2,0:T(8,128)(2,1)}), bf16[8,160,144]{1,2,0:T(8,128)(2,1)}, u32[]{:S(2)}, u32[]{:S(2)}) async-start(bf16[8,160,144]{1,2,0:T(8,128)(2,1)} %copy.66), calls=%async_computation.3 | async-start | bytes 1179648 | tf_op jit(solution)/shard_map/all_to_all | solution.py:355
  244.9 5.7 %fusion.61 = (bf16[640,1152]{1,0:T(8,128)(2,1)S(1)}, f32[640,1152]{1,0:T(8,128)}) fusion(bf16[640,1152]{1,0:T(8,128)(2,1)S(1)} %copy-done.3, bf16[1152,1152]{1,0:T(8,128)(2,1)} %all-gather.12.cloned.1.call-done.down_ref), kind=kOutput, calls=%fused_computation.177 | convolution fusion | flops 1699430400 | bytes 8552448 | tf_op jit(solution)/shard_map/dot_general | solution.py:46
  258.4 11.8 %all-to-all-done.3 = bf16[8,160,144]{1,2,0:T(8,128)(2,1)} async-done(((bf16[8,160,144]{1,2,0:T(8,128)(2,1)}), bf16[8,160,144]{1,2,0:T(8,128)(2,1)}, u32[]{:S(2)}, u32[]{:S(2)}) %all-to-all-start.3) | async-done | bytes 368672 | tf_op jit(solution)/shard_map/all_to_all | solution.py:355
  271.7 14.4 %shard_map.292 = (bf16[1280,144]{1,0:T(8,128)(2,1)S(1)}, bf16[1280,288]{1,0:T(8,128)(2,1)S(1)}) custom-call(bf16[1280,768]{1,0:T(8,128)(2,1)} %copy-done.4, bf16[1280,768]{1,0:T(8,128)(2,1)} %copy-done.4, bf16[1280,768]{1,0:T(8,128)(2,1)} %copy-done.4, bf16[1280,256]{1,0:T(8,128)(2,1)S(1)} %pad.18.out_grad_ref, f32[1280,256]{1,0:T(8,128)S(1)} %copy-done.6, ...), custom_call_target="tpu_custom_call" | custom-call | flops 8388608000 | bytes 4587520 | tf_op jit(solution)/shard_map/pallas_call | solution.py:164
  303.8 4.4 %collective-permute-done.30 = bf16[160,1152]{1,0:T(8,128)(2,1)S(1)} collective-permute-done((bf16[160,1152]{1,0:T(8,128)(2,1)S(1)}, bf16[160,1152]{1,0:T(8,128)(2,1)S(1)}, u32[]{:S(2)}, u32[]{:S(2)}) %collective-permute-start.30) | collective-permute-done | bytes 368672 | tf_op jit(solution)/shard_map/ppermute | solution.py:331
  309.0 7.0 %collective-permute-done.31 = bf16[160,1152]{1,0:T(8,128)(2,1)S(1)} collective-permute-done((bf16[160,1152]{1,0:T(8,128)(2,1)S(1)}, bf16[160,1152]{1,0:T(8,128)(2,1)S(1)}, u32[]{:S(2)}, u32[]{:S(2)}) %collective-permute-start.31) | collective-permute-done | bytes 368672 | tf_op jit(solution)/shard_map/ppermute | solution.py:331
  328.4 4.2 %all-to-all-start.5 = ((bf16[4,36,1152]{2,1,0:T(8,128)(2,1)}), bf16[4,36,1152]{2,1,0:T(8,128)(2,1)S(1)}, u32[]{:S(2)}, u32[]{:S(2)}) async-start(bf16[4,36,1152]{2,1,0:T(8,128)(2,1)} %fusion.28), calls=%async_computation.8 | async-start | bytes 737280 | tf_op jit(solution)/shard_map/all_to_all | solution.py:365
  363.3 4.1 %all-to-all-start.6 = ((f32[32,8,128]{2,1,0:T(8,128)}), f32[32,8,128]{2,1,0:T(8,128)S(1)}, u32[]{:S(2)}, u32[]{:S(2)}) async-start(f32[32,8,128]{2,1,0:T(8,128)} %bitcast.71), calls=%async_computation.9 | async-start | bytes 262144 | tf_op jit(solution)/shard_map/all_to_all | solution.py:554
  385.5 4.9 %collective-permute-done.41 = bf16[160,576]{0,1:T(8,128)(2,1)} collective-permute-done((bf16[160,576]{0,1:T(8,128)(2,1)S(1)}, bf16[160,576]{0,1:T(8,128)(2,1)}, u32[]{:S(2)}, u32[]{:S(2)}) %collective-permute-start.41) | collective-permute-done | bytes 184352 | tf_op jit(solution)/shard_map/ppermute | solution.py:331
  (342 shorter events, 204.0 us)
Async XLA Ops:
  7.2 43.4 %all-gather.6.cloned.1.call-start = ((), (), s32[]{:S(2)}) async-start(), calls=%async_computation.11 | async-start | bytes 1492992 | tf_op jit(solution)/shard_map/all_gather | solution.py:368
  25.5 23.8 %collective-permute-start.6 = (bf16[160,1152]{1,0:T(8,128)(2,1)S(1)}, bf16[160,1152]{1,0:T(8,128)(2,1)S(1)}, u32[]{:S(2)}, u32[]{:S(2)}) collective-permute-start(bf16[160,1152]{1,0:T(8,128)(2,1)S(1)} %bitcast.160), channel_id=1, source_target_pairs={{0,8},{8,0},{16,24},{24,16},{1,9},{9,1},{17,25},{25,17},{2,10},{10... | collective-permute-start | bytes 1105928 | tf_op jit(solution)/shard_map/ppermute | solution.py:331
  26.9 22.4 %collective-permute-start.7 = (bf16[160,1152]{1,0:T(8,128)(2,1)S(1)}, bf16[160,1152]{1,0:T(8,128)(2,1)S(1)}, u32[]{:S(2)}, u32[]{:S(2)}) collective-permute-start(bf16[160,1152]{1,0:T(8,128)(2,1)S(1)} %bitcast.161), channel_id=1, source_target_pairs={{0,16},{8,24},{16,0},{24,8},{1,17},{9,25},{17,1},{25,9},{2,18},{10... | collective-permute-start | bytes 1105928 | tf_op jit(solution)/shard_map/ppermute | solution.py:331
  27.5 21.9 %collective-permute-start.8 = (bf16[160,1152]{1,0:T(8,128)(2,1)S(1)}, bf16[160,1152]{1,0:T(8,128)(2,1)S(1)}, u32[]{:S(2)}, u32[]{:S(2)}) collective-permute-start(bf16[160,1152]{1,0:T(8,128)(2,1)S(1)} %bitcast.162), channel_id=1, source_target_pairs={{0,24},{8,16},{16,8},{24,0},{1,25},{9,17},{17,9},{25,1},{2,26},{10... | collective-permute-start | bytes 1105928 | tf_op jit(solution)/shard_map/ppermute | solution.py:331
  29.0 18.6 %collective-permute-start.4 = (bf16[36,1152]{1,0:T(8,128)(2,1)S(1)}, bf16[36,1152]{1,0:T(8,128)(2,1)S(1)}, u32[]{:S(2)}, u32[]{:S(2)}) collective-permute-start(bf16[36,1152]{1,0:T(8,128)(2,1)S(1)} %bitcast.181), channel_id=1, source_target_pairs={{0,16},{8,24},{16,0},{24,8},{1,17},{9,25},{17,1},{25,9},{2,18},{10... | collective-permute-start | bytes 248840 | tf_op jit(solution)/shard_map/ppermute | solution.py:331
  64.3 60.7 %all-gather.8.cloned.1.call-start = ((), (), s32[]{:S(2)}) async-start(), calls=%async_computation.12 | async-start | bytes 3317760 | tf_op jit(solution)/shard_map/all_gather | solution.py:420
  76.4 90.9 %all-gather.10.cloned.1.call-start = ((), (), s32[]{:S(2)}) async-start(), calls=%async_computation.13 | async-start | bytes 2985984 | tf_op jit(solution)/shard_map/all_gather | solution.py:432
  119.1 19.7 %collective-permute-start.12 = (bf16[144,1152]{1,0:T(8,128)(2,1)}, bf16[144,1152]{1,0:T(8,128)(2,1)}, u32[]{:S(2)}, u32[]{:S(2)}) collective-permute-start(bf16[144,1152]{1,0:T(8,128)(2,1)} %constant_dynamic-slice_fusion.5), channel_id=1, source_target_pairs={{0,8},{8,0},{16,24},{24,16},{1,9},{9,1},{17,25},{25,17},{2,10},{10... | collective-permute-start | bytes 995336 | tf_op jit(solution)/shard_map/ppermute | solution.py:331
  140.7 24.3 %all-to-all-start.2 = ((bf16[8,160,144]{1,2,0:T(8,128)(2,1)}), bf16[8,160,144]{1,2,0:T(8,128)(2,1)S(1)}, u32[]{:S(2)}, u32[]{:S(2)}) async-start(bf16[8,160,144]{1,2,0:T(8,128)(2,1)} %copy.64), calls=%async_computation.2 | async-start | bytes 1179648 | tf_op jit(solution)/shard_map/all_to_all | solution.py:355
  144.3 59.6 %all-gather.12.cloned.1.call-start = ((), (), s32[]{:S(2)}) async-start(), calls=%async_computation.14 | async-start | bytes 2985984 | tf_op jit(solution)/shard_map/all_gather | solution.py:455
  167.2 126.6 %reduce-scatter.9.cloned.1.call-start = ((), (), s32[]{:S(2)}) async-start(), calls=%async_computation.16 | async-start | bytes 2985984 | tf_op jit(solution)/shard_map/reduce_scatter | solution.py:466
  173.1 18.1 %collective-permute-start.19 = (bf16[160,1152]{1,0:T(8,128)(2,1)S(1)}, bf16[160,1152]{1,0:T(8,128)(2,1)S(1)}, u32[]{:S(2)}, u32[]{:S(2)}) collective-permute-start(bf16[160,1152]{1,0:T(8,128)(2,1)S(1)} %add_convert_fusion), channel_id=1, source_target_pairs={{0,16},{8,24},{16,0},{24,8},{1,17},{9,25},{17,1},{25,9},{2,18},{10... | collective-permute-start | bytes 1105928 | tf_op jit(solution)/shard_map/ppermute | solution.py:331
  203.6 90.2 %reduce-scatter.7.cloned.1.call-start = ((), (), s32[]{:S(2)}) async-start(), calls=%async_computation.15 | async-start | bytes 2985984 | tf_op jit(solution)/shard_map/reduce_scatter | solution.py:483
  240.6 29.5 %all-to-all-start.3 = ((bf16[8,160,144]{1,2,0:T(8,128)(2,1)}), bf16[8,160,144]{1,2,0:T(8,128)(2,1)}, u32[]{:S(2)}, u32[]{:S(2)}) async-start(bf16[8,160,144]{1,2,0:T(8,128)(2,1)} %copy.66), calls=%async_computation.3 | async-start | bytes 1179648 | tf_op jit(solution)/shard_map/all_to_all | solution.py:355
  244.8 87.7 %reduce-scatter.11.cloned.1.call-start = ((), (), s32[]{:S(2)}) async-start(), calls=%async_computation.17 | async-start | bytes 3317760 | tf_op jit(solution)/shard_map/reduce_scatter | solution.py:503
  251.7 19.9 %collective-permute-start.24 = (bf16[160,1152]{1,0:T(8,128)(2,1)}, bf16[160,1152]{1,0:T(8,128)(2,1)}, u32[]{:S(2)}, u32[]{:S(2)}) collective-permute-start(bf16[160,1152]{1,0:T(8,128)(2,1)} %get-tuple-element.186), channel_id=1, source_target_pairs={{0,8},{8,0},{16,24},{24,16},{1,9},{9,1},{17,25},{25,17},{2,10},{10... | collective-permute-start | bytes 1105928 | tf_op jit(solution)/shard_map/ppermute | solution.py:331
  255.6 35.8 %collective-permute-start.25 = (bf16[160,1152]{1,0:T(8,128)(2,1)}, bf16[160,1152]{1,0:T(8,128)(2,1)}, u32[]{:S(2)}, u32[]{:S(2)}) collective-permute-start(bf16[160,1152]{1,0:T(8,128)(2,1)} %get-tuple-element.184), channel_id=1, source_target_pairs={{0,16},{8,24},{16,0},{24,8},{1,17},{9,25},{17,1},{25,9},{2,18},{10... | collective-permute-start | bytes 1105928 | tf_op jit(solution)/shard_map/ppermute | solution.py:331
  256.7 34.7 %collective-permute-start.26 = (bf16[160,1152]{1,0:T(8,128)(2,1)}, bf16[160,1152]{1,0:T(8,128)(2,1)}, u32[]{:S(2)}, u32[]{:S(2)}) collective-permute-start(bf16[160,1152]{1,0:T(8,128)(2,1)} %get-tuple-element.185), channel_id=1, source_target_pairs={{0,24},{8,16},{16,8},{24,0},{1,25},{9,17},{17,9},{25,1},{2,26},{10... | collective-permute-start | bytes 1105928 | tf_op jit(solution)/shard_map/ppermute | solution.py:331
  293.9 22.2 %collective-permute-start.36 = (bf16[160,288]{1,0:T(8,128)(2,1)S(1)}, bf16[160,288]{1,0:T(8,128)(2,1)S(1)}, u32[]{:S(2)}, u32[]{:S(2)}) collective-permute-start(bf16[160,288]{1,0:T(8,128)(2,1)S(1)} %get-tuple-element.208), channel_id=1, source_target_pairs={{0,8},{8,0},{16,24},{24,16},{1,9},{9,1},{17,25},{25,17},{2,10},{10... | collective-permute-start | bytes 276488 | tf_op jit(solution)/shard_map/ppermute | solution.py:331
  294.0 22.1 %collective-permute-start.37 = (bf16[160,288]{1,0:T(8,128)(2,1)S(1)}, bf16[160,288]{1,0:T(8,128)(2,1)S(1)}, u32[]{:S(2)}, u32[]{:S(2)}) collective-permute-start(bf16[160,288]{1,0:T(8,128)(2,1)S(1)} %get-tuple-element.207), channel_id=1, source_target_pairs={{0,16},{8,24},{16,0},{24,8},{1,17},{9,25},{17,1},{25,9},{2,18},{10... | collective-permute-start | bytes 276488 | tf_op jit(solution)/shard_map/ppermute | solution.py:331
  296.1 19.9 %collective-permute-start.31 = (bf16[160,1152]{1,0:T(8,128)(2,1)S(1)}, bf16[160,1152]{1,0:T(8,128)(2,1)S(1)}, u32[]{:S(2)}, u32[]{:S(2)}) collective-permute-start(bf16[160,1152]{1,0:T(8,128)(2,1)S(1)} %copy-done.17), channel_id=1, source_target_pairs={{0,16},{8,24},{16,0},{24,8},{1,17},{9,25},{17,1},{25,9},{2,18},{10... | collective-permute-start | bytes 1105928 | tf_op jit(solution)/shard_map/ppermute | solution.py:331
  338.0 18.0 %collective-permute-start.29 = (bf16[160,1152]{1,0:T(8,128)(2,1)}, bf16[160,1152]{1,0:T(8,128)(2,1)}, u32[]{:S(2)}, u32[]{:S(2)}) collective-permute-start(bf16[160,1152]{1,0:T(8,128)(2,1)} %get-tuple-element.178), channel_id=1, source_target_pairs={{0,24},{8,16},{16,8},{24,0},{1,25},{9,17},{17,9},{25,1},{2,26},{10... | collective-permute-start | bytes 1105928 | tf_op jit(solution)/shard_map/ppermute | solution.py:331
  347.1 49.4 %reduce-scatter.13.cloned.1.call-start = ((), (), s32[]{:S(2)}) async-start(), calls=%async_computation.18 | async-start | bytes 1492992
  363.3 31.9 %all-to-all-start.6 = ((f32[32,8,128]{2,1,0:T(8,128)}), f32[32,8,128]{2,1,0:T(8,128)S(1)}, u32[]{:S(2)}, u32[]{:S(2)}) async-start(f32[32,8,128]{2,1,0:T(8,128)} %bitcast.71), calls=%async_computation.9 | async-start | bytes 262144 | tf_op jit(solution)/shard_map/all_to_all | solution.py:554
  (79 other events, 981.3 us)
Sparse Core Ops, SparseCore 0:
  9.7 26.2 all-gather.5
  76.5 41.9 all-gather.7
  120.7 37.0 all-gather.9
  167.4 32.9 all-gather.11
  203.7 35.7 reduce-scatter.8
  241.7 44.7 reduce-scatter.6
  294.0 35.8 reduce-scatter.10
  362.2 34.1 reduce-scatter.12

commit v15 on v14

--- a/solution.py
+++ b/solution.py
@@ -399,10 +399,8 @@
         [index(up_slices, dp_at)] + [swap(index(up_slices, dp_at ^ k), k) for k in range(1, nd)],
         axis=0,
     )
-    joined_here, grad_out = after((joined_here, cotangent[0]))
-    grad_out_rows = gather_rows(grad_out)
-    qkv_out, skip_part, joined_here, vectors, up_slices, grad_out_rows = after(
-        (qkv_out, skip_part, joined_here, vectors, up_slices, grad_out_rows)
+    qkv_out, skip_part, joined_here, vectors, up_slices = after(
+        (qkv_out, skip_part, joined_here, vectors, up_slices)
     )
     def vector(at):
         return vectors[:, at * small : (at + 1) * small].reshape(features)
@@ -437,7 +435,9 @@
         v = seq_exchange(v.reshape(ns, local, head_cols))
         return jnp.swapaxes(v, 0, 1).reshape(local, features)
 
-    attended_low, proj_halves, proj_rows = after((attended_low, proj_halves, proj_rows))
+    attended_low, grad_out, proj_halves, proj_rows = after(
+        (attended_low, cotangent[0], proj_halves, proj_rows)
+    )
     w_proj = lax.dynamic_update_slice_in_dim(
         jnp.zeros((features, features), BF16), proj_rows, dp_at * part, 0
     )
@@ -447,6 +447,7 @@
         there = other_core(here)
         w_proj = lax.dynamic_update_slice_in_dim(w_proj, here, (place + core) * half, 0)
         w_proj = lax.dynamic_update_slice_in_dim(w_proj, there, (place + 1 - core) * half, 0)
+    grad_out_rows = gather_rows(grad_out)
     attended_low = heads_to_tokens(attended_low)
     attended_low, grad_out_rows, w_proj, order = after(
         (attended_low, grad_out_rows, w_proj, order)

time: 413 us -> 402 us (0.973)
  waiting for transfers between devices: 90.9 us -> 82.8 us
    ppermute x42, waiting for transfers between devices: 69.1 us -> 60.5 us  [swap(): return lax.ppermute(v, 'dp', [(i, i ^ k) for i in range(nd)])]
    all_to_all x4, waiting for transfers between devices: 19.5 us -> 14.6 us  [seq_exchange(): return lax.all_to_all(v, 'seq', 0, 0, tiled=True)]
    unnamed x90 -> x86, local copies, waits for them, and re-layouts: 8.47 us -> 8.16 us
  transfers between devices with their start and end apart: 61 -> 61, of which waited for: 21 -> 17; matrix products, arithmetic and copies ran while one was open for 31% -> 32% of each run, Pallas kernels for 10% -> 10%
where the time goes in v15:
time: 402 us; the launch traced here: 396 us
  waiting for transfers between devices  82.8 us (21%)
  starting transfers between devices  79.1 us (20%)
  local copies, waits for them, and re-layouts  55.9 us (14%)
  matrix products  49.4 us (12%)
  Pallas kernels  40.9 us (10%)
  other arithmetic  36.4 us (9%)
  blocking collectives  32 us (8%)
  between operations  19 us (5%)
    ppermute x42, waiting for transfers between devices, swap(): return lax.ppermute(v, 'dp', [(i, i ^ k) for i in range(nd)])  60.5 us
    ppermute x42, starting transfers between devices, swap(): return lax.ppermute(v, 'dp', [(i, i ^ k) for i in range(nd)])  51.1 us
    dot_general x6, matrix products, inner(): lax.dot_general(left, right, (((0,), (0,)), ((), ())), preferred_element_...  26.4 us
    all_gather x1, blocking collectives, on_device(): proj_rows = lax.all_gather(own_proj, 'seq', axis=0, tiled=True)  18.5 us
    dot_general x4, matrix products, dot(): return jnp.dot(left, right, preferred_element_type=F32)  16.9 us
    all_to_all x4, starting transfers between devices, seq_exchange(): return lax.all_to_all(v, 'seq', 0, 0, tiled=True)  14.7 us
    all_to_all x4, waiting for transfers between devices, seq_exchange(): return lax.all_to_all(v, 'seq', 0, 0, tiled=True)  14.6 us
    pallas_call x1, Pallas kernels, attend_back(): pl.pallas_call(partial(attend_back_kernel, heads, scale), grid=(rows // s...  14.4 us
  transfers between devices with their start and end apart: 61, of which 17 were waited for; matrix products, arithmetic and copies ran while one was open for 32% of the time, Pallas kernels for 10%

profile of v15, /device:TPU:0, one launch (start us, length us, event | category | flops | bytes accessed | tf_op | source)
XLA Modules:
  0.0 395.7 jit_solution(3828507361878744262)
XLA Ops:
  20.2 4.0 %all-to-all-start = ((bf16[32,8,128]{2,1,0:T(8,128)(2,1)}), bf16[32,8,128]{2,1,0:T(8,128)(2,1)S(1)}, u32[]{:S(2)}, u32[]{:S(2)}) async-start(bf16[32,8,128]{2,1,0:T(8,128)(2,1)} %broadcast_in_dim.15), calls=%async_computation | async-start | bytes 131072 | tf_op jit(solution)/shard_map/all_to_all | solution.py:376
  53.3 8.4 %collective-permute-done.7 = bf16[160,1152]{1,0:T(8,128)(2,1)} collective-permute-done((bf16[160,1152]{1,0:T(8,128)(2,1)}, bf16[160,1152]{1,0:T(8,128)(2,1)}, u32[]{:S(2)}, u32[]{:S(2)}) %collective-permute-start.7) | collective-permute-done | bytes 368672 | tf_op jit(solution)/shard_map/ppermute | solution.py:331
  73.9 13.5 %all_gather.20 = bf16[1152,432]{1,0:T(8,128)(2,1)S(1)} all-gather(bf16[288,432]{1,0:T(8,128)(2,1)S(1)} %reshape.202), channel_id=1, replica_groups=mesh['dp'=4,'seq'=8] {'dp'}, dimensions={0}, use_global_device_ids=true | all-gather | bytes 1244160 | tf_op jit(solution)/shard_map/all_gather | solution.py:421
  87.4 18.5 %all-gather = bf16[8,36,1152]{2,1,0:T(8,128)(2,1)S(1)} all-gather(bf16[1,36,1152]{2,1,0:T(8,128)(2,1)S(1)} %bitcast.174), channel_id=1, replica_groups=mesh['dp'=4,'seq'=8] {'seq'}, dimensions={0}, use_global_device_ids=true | all-gather | bytes 746496 | tf_op jit(solution)/shard_map/all_gather | solution.py:423
  112.6 5.3 %convolution_convert_fusion.4.q_ref.k_ref.v_ref = bf16[1280,768]{1,0:T(8,128)(2,1)S(1)} fusion(bf16[1280,1152]{1,0:T(8,128)(2,1)} %all-gather.8.cloned.1.call-done, bf16[1152,768]{0,1:T(8,128)(2,1)} %bitcast.159), kind=kOutput, calls=%fused_computation.23 | convolution fusion | flops 2265907200 | bytes 6684672 | tf_op jit(solution)/shard_map/dot_general | solution.py:46
  118.2 8.4 %shard_map.288 = (f32[1280,256]{1,0:T(8,128)S(1)}, bf16[1280,144]{1,0:T(8,128)(2,1)S(1)}, f32[8,1280]{1,0:T(8,128)S(1)}) custom-call(bf16[1280,768]{1,0:T(8,128)(2,1)S(1)} %convolution_convert_fusion.4.q_ref.k_ref.v_ref, bf16[1280,768]{1,0:T(8,128)(2,1)S(1)} %convolution_convert_fusion.4.q_ref.k_ref.v_ref, ...), custom_call_target="tpu_custom_call" | custom-call | flops 3355443200 | bytes 3276800 | tf_op jit(solution)/shard_map/pallas_call | solution.py:84
  162.5 4.0 %convolution_convert_fusion.3.up_ref = bf16[1152,1152]{1,0:T(8,128)(2,1)S(1)} fusion(bf16[1152,1152]{1,0:T(8,128)(2,1)S(1)} %copy-done.20, bf16[1152,1152]{1,0:T(8,128)(2,1)S(1)} %copy-done.39), kind=kOutput, calls=%fused_computation.11 | convolution fusion | flops 3058974720 | bytes 7962624 | tf_op jit(solution)/shard_map/dot_general | solution.py:50
  166.6 3.9 collective-permute-done.18
  170.5 8.2 %collective-permute-done.19 = bf16[160,1152]{1,0:T(8,128)(2,1)S(1)} collective-permute-done((bf16[160,1152]{1,0:T(8,128)(2,1)S(1)}, bf16[160,1152]{1,0:T(8,128)(2,1)S(1)}, u32[]{:S(2)}, u32[]{:S(2)}) %collective-permute-start.19) | collective-permute-done | bytes 368672 | tf_op jit(solution)/shard_map/ppermute | solution.py:331
  178.8 5.7 %shard_map.289 = (bf16[640,1152]{1,0:T(8,128)(2,1)S(1)}, f32[640,1152]{1,0:T(8,128)S(1)}) custom-call(bf16[640,1152]{1,0:T(8,128)(2,1)S(1)} %pad_maximum_fusion.1.x_ref, bf16[1152,1152]{1,0:T(8,128)(2,1)S(1)} %convolution_convert_fusion.3.up_ref, f32[1,1152]{1,0:T(1,128)S(1)} %reshape_reshape.6.bias_ref), custom_call_target="tpu_custom_call" | custom-call | flops 1698693120 | bytes 8552448 | tf_op jit(solution)/shard_map/pallas_call | solution.py:250
  187.2 3.9 convolution_convert_fusion.2
  191.4 9.0 %shard_map.290 = (bf16[640,1152]{1,0:T(8,128)(2,1)}, f32[1,1152]{1,0:T(1,128)S(1)}, f32[160,1152]{1,0:T(8,128)S(1)}, bf16[160,1152]{1,0:T(8,128)(2,1)}, bf16[160...) custom-call(bf16[640,1152]{1,0:T(8,128)(2,1)} %pad_maximum_fusion.grad_ref, bf16[1152,1152]{1,0:T(8,128)(2,1)} %copy-done.1, ...), custom_call_target="tpu_custom_call" | custom-call | flops 3397386240 | bytes 12681216 | tf_op jit(solution)/shard_map/pallas_call | solution.py:288
  203.9 8.9 %convolution_convert_fusion.1 = bf16[1152,1152]{1,0:T(8,128)(2,1)} fusion(bf16[640,1152]{1,0:T(8,128)(2,1)} %get-tuple-element.130, bf16[640,1152]{1,0:T(8,128)(2,1)S(1)} %pad_maximum_fusion.1.x_ref, bf16[1152,1152]{1,0:T(8,128)(2,1)} %fusion.10), kind=kOutput, calls=%fused_computation.9 | convolution fusion | flops 3399450624 | bytes 8257536 | tf_op jit(solution)/shard_map/dot_general | solution.py:50
  212.8 6.5 %collective-permute-done.22 = bf16[160,1152]{1,0:T(8,128)(2,1)} collective-permute-done((bf16[160,1152]{1,0:T(8,128)(2,1)}, bf16[160,1152]{1,0:T(8,128)(2,1)}, u32[]{:S(2)}, u32[]{:S(2)}) %collective-permute-start.22) | collective-permute-done | bytes 368672 | tf_op jit(solution)/shard_map/ppermute | solution.py:331
  229.2 4.2 %all-to-all-start.3 = ((bf16[8,160,144]{1,2,0:T(8,128)(2,1)}), bf16[8,160,144]{1,2,0:T(8,128)(2,1)}, u32[]{:S(2)}, u32[]{:S(2)}) async-start(bf16[8,160,144]{1,2,0:T(8,128)(2,1)} %copy.66), calls=%async_computation.3 | async-start | bytes 1179648 | tf_op jit(solution)/shard_map/all_to_all | solution.py:355
  233.5 5.9 %fusion.61 = (bf16[640,1152]{1,0:T(8,128)(2,1)S(1)}, f32[640,1152]{1,0:T(8,128)}) fusion(bf16[640,1152]{1,0:T(8,128)(2,1)S(1)} %copy-done.3, bf16[1152,1152]{1,0:T(8,128)(2,1)} %all-gather.12.cloned.1.call-done.down_ref), kind=kOutput, calls=%fused_computation.177 | convolution fusion | flops 1699430400 | bytes 8552448 | tf_op jit(solution)/shard_map/dot_general | solution.py:46
  247.1 12.6 %all-to-all-done.3 = bf16[8,160,144]{1,2,0:T(8,128)(2,1)} async-done(((bf16[8,160,144]{1,2,0:T(8,128)(2,1)}), bf16[8,160,144]{1,2,0:T(8,128)(2,1)}, u32[]{:S(2)}, u32[]{:S(2)}) %all-to-all-start.3) | async-done | bytes 368672 | tf_op jit(solution)/shard_map/all_to_all | solution.py:355
  261.2 14.4 %shard_map.292 = (bf16[1280,144]{1,0:T(8,128)(2,1)S(1)}, bf16[1280,288]{1,0:T(8,128)(2,1)S(1)}) custom-call(bf16[1280,768]{1,0:T(8,128)(2,1)} %copy-done.4, bf16[1280,768]{1,0:T(8,128)(2,1)} %copy-done.4, bf16[1280,768]{1,0:T(8,128)(2,1)} %copy-done.4, bf16[1280,256]{1,0:T(8,128)(2,1)S(1)} %pad.18.out_grad_ref, f32[1280,256]{1,0:T(8,128)S(1)} %copy-done.6, ...), custom_call_target="tpu_custom_call" | custom-call | flops 8388608000 | bytes 4587520 | tf_op jit(solution)/shard_map/pallas_call | solution.py:164
  287.8 3.9 fusion.62
  293.2 4.4 %collective-permute-done.30 = bf16[160,1152]{1,0:T(8,128)(2,1)S(1)} collective-permute-done((bf16[160,1152]{1,0:T(8,128)(2,1)S(1)}, bf16[160,1152]{1,0:T(8,128)(2,1)S(1)}, u32[]{:S(2)}, u32[]{:S(2)}) %collective-permute-start.30) | collective-permute-done | bytes 368672 | tf_op jit(solution)/shard_map/ppermute | solution.py:331
  298.5 8.2 %collective-permute-done.31 = bf16[160,1152]{1,0:T(8,128)(2,1)S(1)} collective-permute-done((bf16[160,1152]{1,0:T(8,128)(2,1)S(1)}, bf16[160,1152]{1,0:T(8,128)(2,1)S(1)}, u32[]{:S(2)}, u32[]{:S(2)}) %collective-permute-start.31) | collective-permute-done | bytes 368672 | tf_op jit(solution)/shard_map/ppermute | solution.py:331
  341.1 5.6 %collective-permute-done.28 = bf16[160,1152]{1,0:T(8,128)(2,1)S(1)} collective-permute-done((bf16[160,1152]{1,0:T(8,128)(2,1)}, bf16[160,1152]{1,0:T(8,128)(2,1)S(1)}, u32[]{:S(2)}, u32[]{:S(2)}) %collective-permute-start.28) | collective-permute-done | bytes 368672 | tf_op jit(solution)/shard_map/ppermute | solution.py:331
  349.0 3.8 convolution_convert_fusion.6
  375.7 4.9 %collective-permute-done.41 = bf16[160,576]{0,1:T(8,128)(2,1)} collective-permute-done((bf16[160,576]{0,1:T(8,128)(2,1)S(1)}, bf16[160,576]{0,1:T(8,128)(2,1)}, u32[]{:S(2)}, u32[]{:S(2)}) %collective-permute-start.41) | collective-permute-done | bytes 184352 | tf_op jit(solution)/shard_map/ppermute | solution.py:331
  (338 shorter events, 200.7 us)
Async XLA Ops:
  7.2 30.4 %all-gather.6.cloned.1.call-start = ((), (), s32[]{:S(2)}) async-start(), calls=%async_computation.11 | async-start | bytes 1492992 | tf_op jit(solution)/shard_map/all_gather | solution.py:368
  9.7 23.0 %collective-permute-start = (bf16[160,576]{1,0:T(8,128)(2,1)S(1)}, bf16[160,576]{1,0:T(8,128)(2,1)S(1)}, u32[]{:S(2)}, u32[]{:S(2)}) collective-permute-start(bf16[160,576]{1,0:T(8,128)(2,1)S(1)} %get-tuple-element.196), channel_id=1, source_target_pairs={{0,8},{8,0},{16,24},{24,16},{1,9},{9,1},{17,25},{25,17},{2,10},{10... | collective-permute-start | bytes 552968 | tf_op jit(solution)/shard_map/ppermute | solution.py:331
  12.8 20.0 %collective-permute-start.1 = (bf16[160,576]{1,0:T(8,128)(2,1)S(1)}, bf16[160,576]{1,0:T(8,128)(2,1)S(1)}, u32[]{:S(2)}, u32[]{:S(2)}) collective-permute-start(bf16[160,576]{1,0:T(8,128)(2,1)S(1)} %get-tuple-element.195), channel_id=1, source_target_pairs={{0,16},{8,24},{16,0},{24,8},{1,17},{9,25},{17,1},{25,9},{2,18},{10... | collective-permute-start | bytes 552968 | tf_op jit(solution)/shard_map/ppermute | solution.py:331
  49.7 62.9 %all-gather.8.cloned.1.call-start = ((), (), s32[]{:S(2)}) async-start(), calls=%async_computation.12 | async-start | bytes 3317760 | tf_op jit(solution)/shard_map/all_gather | solution.py:418
  65.1 89.5 %all-gather.10.cloned.1.call-start = ((), (), s32[]{:S(2)}) async-start(), calls=%async_computation.13 | async-start | bytes 2985984 | tf_op jit(solution)/shard_map/all_gather | solution.py:430
  106.9 19.7 %collective-permute-start.10 = (bf16[144,1152]{1,0:T(8,128)(2,1)}, bf16[144,1152]{1,0:T(8,128)(2,1)}, u32[]{:S(2)}, u32[]{:S(2)}) collective-permute-start(bf16[144,1152]{1,0:T(8,128)(2,1)} %constant_dynamic-slice_fusion.5), channel_id=1, source_target_pairs={{0,16},{8,24},{16,0},{24,8},{1,17},{9,25},{17,1},{25,9},{2,18},{10... | collective-permute-start | bytes 995336 | tf_op jit(solution)/shard_map/ppermute | solution.py:331
  126.6 21.2 %collective-permute-start.12 = (bf16[160,1152]{1,0:T(8,128)(2,1)}, bf16[160,1152]{1,0:T(8,128)(2,1)}, u32[]{:S(2)}, u32[]{:S(2)}) collective-permute-start(bf16[160,1152]{1,0:T(8,128)(2,1)} %bitcast.20), channel_id=1, source_target_pairs={{0,8},{8,0},{16,24},{24,16},{1,9},{9,1},{17,25},{25,17},{2,10},{10... | collective-permute-start | bytes 1105928 | tf_op jit(solution)/shard_map/ppermute | solution.py:331
  127.5 20.2 %collective-permute-start.13 = (bf16[160,1152]{1,0:T(8,128)(2,1)}, bf16[160,1152]{1,0:T(8,128)(2,1)}, u32[]{:S(2)}, u32[]{:S(2)}) collective-permute-start(bf16[160,1152]{1,0:T(8,128)(2,1)} %bitcast.20), channel_id=1, source_target_pairs={{0,16},{8,24},{16,0},{24,8},{1,17},{9,25},{17,1},{25,9},{2,18},{10... | collective-permute-start | bytes 1105928 | tf_op jit(solution)/shard_map/ppermute | solution.py:331
  128.8 19.0 %collective-permute-start.14 = (bf16[160,1152]{1,0:T(8,128)(2,1)}, bf16[160,1152]{1,0:T(8,128)(2,1)}, u32[]{:S(2)}, u32[]{:S(2)}) collective-permute-start(bf16[160,1152]{1,0:T(8,128)(2,1)} %bitcast.20), channel_id=1, source_target_pairs={{0,24},{8,16},{16,8},{24,0},{1,25},{9,17},{17,9},{25,1},{2,26},{10... | collective-permute-start | bytes 1105928 | tf_op jit(solution)/shard_map/ppermute | solution.py:331
  131.8 20.7 %all-to-all-start.2 = ((bf16[8,160,144]{1,2,0:T(8,128)(2,1)}), bf16[8,160,144]{1,2,0:T(8,128)(2,1)S(1)}, u32[]{:S(2)}, u32[]{:S(2)}) async-start(bf16[8,160,144]{1,2,0:T(8,128)(2,1)} %copy.64), calls=%async_computation.2 | async-start | bytes 1179648 | tf_op jit(solution)/shard_map/all_to_all | solution.py:355
  135.4 56.0 %all-gather.12.cloned.1.call-start = ((), (), s32[]{:S(2)}) async-start(), calls=%async_computation.14 | async-start | bytes 2985984 | tf_op jit(solution)/shard_map/all_gather | solution.py:456
  154.7 128.6 %reduce-scatter.9.cloned.1.call-start = ((), (), s32[]{:S(2)}) async-start(), calls=%async_computation.16 | async-start | bytes 2985984 | tf_op jit(solution)/shard_map/reduce_scatter | solution.py:467
  191.2 92.1 %reduce-scatter.7.cloned.1.call-start = ((), (), s32[]{:S(2)}) async-start(), calls=%async_computation.15 | async-start | bytes 2985984 | tf_op jit(solution)/shard_map/reduce_scatter | solution.py:484
  229.2 30.5 %all-to-all-start.3 = ((bf16[8,160,144]{1,2,0:T(8,128)(2,1)}), bf16[8,160,144]{1,2,0:T(8,128)(2,1)}, u32[]{:S(2)}, u32[]{:S(2)}) async-start(bf16[8,160,144]{1,2,0:T(8,128)(2,1)} %copy.66), calls=%async_computation.3 | async-start | bytes 1179648 | tf_op jit(solution)/shard_map/all_to_all | solution.py:355
  233.4 89.3 %reduce-scatter.11.cloned.1.call-start = ((), (), s32[]{:S(2)}) async-start(), calls=%async_computation.17 | async-start | bytes 3317760 | tf_op jit(solution)/shard_map/reduce_scatter | solution.py:504
  240.4 20.7 %collective-permute-start.24 = (bf16[160,1152]{1,0:T(8,128)(2,1)}, bf16[160,1152]{1,0:T(8,128)(2,1)}, u32[]{:S(2)}, u32[]{:S(2)}) collective-permute-start(bf16[160,1152]{1,0:T(8,128)(2,1)} %get-tuple-element.182), channel_id=1, source_target_pairs={{0,8},{8,0},{16,24},{24,16},{1,9},{9,1},{17,25},{25,17},{2,10},{10... | collective-permute-start | bytes 1105928 | tf_op jit(solution)/shard_map/ppermute | solution.py:331
  244.1 36.7 %collective-permute-start.25 = (bf16[160,1152]{1,0:T(8,128)(2,1)}, bf16[160,1152]{1,0:T(8,128)(2,1)}, u32[]{:S(2)}, u32[]{:S(2)}) collective-permute-start(bf16[160,1152]{1,0:T(8,128)(2,1)} %get-tuple-element.180), channel_id=1, source_target_pairs={{0,16},{8,24},{16,0},{24,8},{1,17},{9,25},{17,1},{25,9},{2,18},{10... | collective-permute-start | bytes 1105928 | tf_op jit(solution)/shard_map/ppermute | solution.py:331
  245.2 35.6 %collective-permute-start.26 = (bf16[160,1152]{1,0:T(8,128)(2,1)}, bf16[160,1152]{1,0:T(8,128)(2,1)}, u32[]{:S(2)}, u32[]{:S(2)}) collective-permute-start(bf16[160,1152]{1,0:T(8,128)(2,1)} %get-tuple-element.181), channel_id=1, source_target_pairs={{0,24},{8,16},{16,8},{24,0},{1,25},{9,17},{17,9},{25,1},{2,26},{10... | collective-permute-start | bytes 1105928 | tf_op jit(solution)/shard_map/ppermute | solution.py:331
  283.4 23.5 %collective-permute-start.36 = (bf16[160,288]{1,0:T(8,128)(2,1)S(1)}, bf16[160,288]{1,0:T(8,128)(2,1)S(1)}, u32[]{:S(2)}, u32[]{:S(2)}) collective-permute-start(bf16[160,288]{1,0:T(8,128)(2,1)S(1)} %get-tuple-element.204), channel_id=1, source_target_pairs={{0,8},{8,0},{16,24},{24,16},{1,9},{9,1},{17,25},{25,17},{2,10},{10... | collective-permute-start | bytes 276488 | tf_op jit(solution)/shard_map/ppermute | solution.py:331
  283.5 23.4 %collective-permute-start.37 = (bf16[160,288]{1,0:T(8,128)(2,1)S(1)}, bf16[160,288]{1,0:T(8,128)(2,1)S(1)}, u32[]{:S(2)}, u32[]{:S(2)}) collective-permute-start(bf16[160,288]{1,0:T(8,128)(2,1)S(1)} %get-tuple-element.203), channel_id=1, source_target_pairs={{0,16},{8,24},{16,0},{24,8},{1,17},{9,25},{17,1},{25,9},{2,18},{10... | collective-permute-start | bytes 276488 | tf_op jit(solution)/shard_map/ppermute | solution.py:331
  285.5 21.2 %collective-permute-start.31 = (bf16[160,1152]{1,0:T(8,128)(2,1)S(1)}, bf16[160,1152]{1,0:T(8,128)(2,1)S(1)}, u32[]{:S(2)}, u32[]{:S(2)}) collective-permute-start(bf16[160,1152]{1,0:T(8,128)(2,1)S(1)} %copy-done.17), channel_id=1, source_target_pairs={{0,16},{8,24},{16,0},{24,8},{1,17},{9,25},{17,1},{25,9},{2,18},{10... | collective-permute-start | bytes 1105928 | tf_op jit(solution)/shard_map/ppermute | solution.py:331
  287.5 19.2 %collective-permute-start.32 = (bf16[160,1152]{1,0:T(8,128)(2,1)S(1)}, bf16[160,1152]{1,0:T(8,128)(2,1)S(1)}, u32[]{:S(2)}, u32[]{:S(2)}) collective-permute-start(bf16[160,1152]{1,0:T(8,128)(2,1)S(1)} %copy-done.17), channel_id=1, source_target_pairs={{0,24},{8,16},{16,8},{24,0},{1,25},{9,17},{17,9},{25,1},{2,26},{10... | collective-permute-start | bytes 1105928 | tf_op jit(solution)/shard_map/ppermute | solution.py:331
  337.4 49.3 %reduce-scatter.13.cloned.1.call-start = ((), (), s32[]{:S(2)}) async-start(), calls=%async_computation.18 | async-start | bytes 1492992
  354.0 31.4 %all-to-all-start.6 = ((f32[32,8,128]{2,1,0:T(8,128)}), f32[32,8,128]{2,1,0:T(8,128)S(1)}, u32[]{:S(2)}, u32[]{:S(2)}) async-start(f32[32,8,128]{2,1,0:T(8,128)} %bitcast.71), calls=%async_computation.9 | async-start | bytes 262144 | tf_op jit(solution)/shard_map/all_to_all | solution.py:555
  (77 other events, 839.5 us)
Sparse Core Ops, SparseCore 0:
  9.7 27.8 all-gather.5
  65.2 40.6 all-gather.7
  108.1 33.5 all-gather.9
  154.8 32.9 all-gather.11
  191.3 35.7 reduce-scatter.8
  229.2 45.3 reduce-scatter.6
  283.4 35.5 reduce-scatter.10
  352.9 33.6 reduce-scatter.12

commit v16 on v15

--- a/solution.py
+++ b/solution.py
@@ -33,15 +33,21 @@
     return passed, jnp.sum(incoming * standardized, axis=0), jnp.sum(incoming, axis=0)
 
 
-def segment_of(lengths, places):
-    running = jnp.zeros((), jnp.int32)
+def segment_of(lengths_ref, places):
+    running = jnp.int32(0)
     passed = jnp.zeros(places.shape, jnp.int32)
-    for slot in range(lengths.shape[1]):
-        running = running + lengths[0, slot]
+    for slot in range(lengths_ref.shape[1]):
+        running = running + lengths_ref[0, slot]
         passed = passed + (running <= places).astype(jnp.int32)
     return passed
 
 
+def same_item(lengths_ref, rows, columns, first_row):
+    of_rows = first_row + lax.broadcasted_iota(jnp.int32, (rows, 1), 0)
+    of_columns = lax.broadcasted_iota(jnp.int32, (1, columns), 1)
+    return segment_of(lengths_ref, of_rows) == segment_of(lengths_ref, of_columns)
+
+
 def dot(left, right):
     return jnp.dot(left, right, preferred_element_type=F32)
 
@@ -58,8 +64,11 @@
     return jnp.concatenate([part[:, :HEAD_DIM] for part in parts], axis=1)
 
 
-def attend_kernel(heads, scale, q_ref, k_ref, v_ref, seg_q_ref, seg_k_ref, out_ref, low_ref, lse_ref):
-    allowed = seg_q_ref[...] == seg_k_ref[...]
+def attend_kernel(
+    heads, scale, q_ref, k_ref, v_ref, lengths_ref, out_ref, low_ref, lse_ref
+):
+    step = q_ref.shape[0]
+    allowed = same_item(lengths_ref, step, k_ref.shape[0], pl.program_id(0) * step)
     lane = lax.broadcasted_iota(jnp.int32, (q_ref.shape[0], WIDE), 1)
     logs = jnp.zeros((q_ref.shape[0], WIDE), F32)
     outs = []
@@ -77,7 +86,7 @@
     low_ref[...] = side_by_side(outs).astype(BF16)
 
 
-def attend(triple, segments, heads, scale):
+def attend(triple, lengths, heads, scale):
     rows = triple.shape[0]
     wide = heads * WIDE
     step = 256 if rows % 256 == 0 else rows
@@ -88,8 +97,7 @@
             pl.BlockSpec((step, wide), lambda i: (i, 0)),
             pl.BlockSpec((rows, wide), lambda i: (0, 1)),
             pl.BlockSpec((rows, wide), lambda i: (0, 2)),
-            pl.BlockSpec((step, 1), lambda i: (i, 0)),
-            pl.BlockSpec((1, rows), lambda i: (0, 0)),
+            pl.BlockSpec(memory_space=pltpu.SMEM),
         ],
         out_specs=[
             pl.BlockSpec((step, wide), lambda i: (i, 0)),
@@ -107,11 +115,11 @@
             bytes_accessed=10 * rows * wide,
             transcendentals=heads * rows * rows,
         ),
-    )(triple, triple, triple, segments.reshape(rows, 1), segments.reshape(1, rows))
+    )(triple, triple, triple, lengths)
 
 
 def attend_back_kernel(
-    heads, scale, q_ref, k_ref, v_ref, out_grad_ref, out_ref, lse_ref, seg_q_ref, seg_k_ref,
+    heads, scale, q_ref, k_ref, v_ref, out_grad_ref, out_ref, lse_ref, lengths_ref,
     dq_ref, dkv_ref, sum_ref, grad_ref, delta_ref,
 ):
     step = pl.program_id(0)
@@ -133,7 +141,8 @@
             )
             delta_ref[h : h + 1, :] = delta[:1]
 
-    allowed = seg_k_ref[...] == seg_q_ref[...]
+    block, rows = k_ref.shape[0], q_ref.shape[0]
+    allowed = same_item(lengths_ref, block, rows, step * block)
     key_grads, value_grads = [], []
     for h in range(heads):
         at = slice(h * WIDE, (h + 1) * WIDE)
@@ -154,7 +163,7 @@
         ).astype(BF16)
 
 
-def attend_back(triple, out_grad, out, lse, segments, heads, scale):
+def attend_back(triple, out_grad, out, lse, lengths, heads, scale):
     rows = triple.shape[0]
     wide = heads * WIDE
     step = 256 if rows % 256 == 0 else rows
@@ -171,8 +180,7 @@
             whole,
             whole,
             row,
-            pl.BlockSpec((1, rows), lambda i: (0, 0)),
-            pl.BlockSpec((step, 1), lambda i: (i, 0)),
+            pl.BlockSpec(memory_space=pltpu.SMEM),
         ],
         out_specs=[
             pl.BlockSpec((rows, heads * HEAD_DIM), lambda i: (0, 0)),
@@ -193,10 +201,7 @@
             bytes_accessed=14 * rows * wide,
             transcendentals=heads * rows * rows,
         ),
-    )(
-        triple, triple, triple, out_grad, out, lse,
-        segments.reshape(1, rows), segments.reshape(rows, 1),
-    )
+    )(triple, triple, triple, out_grad, out, lse, lengths)
 
 
 def by_group_kernel(x_ref, w_ref, out_ref):
@@ -393,7 +398,6 @@
     row = ((block % nd) ^ dp_at) * part + (block // nd) * small + row
     order = (row == lax.broadcasted_iota(jnp.int32, (features, features), 1)).astype(BF16)
     qkv_out = qkv_w.reshape(small, 3, ns, head_cols).transpose(2, 0, 1, 3).reshape(ns, small, wide)
-    segments = segment_of(item_lengths, jnp.arange(row_len, dtype=jnp.int32))
     up_slices = jnp.swapaxes(fc1_w.reshape(small, nd, hidden_part), 0, 1)
     up_slices = jnp.concatenate(
         [index(up_slices, dp_at)] + [swap(index(up_slices, dp_at ^ k), k) for k in range(1, nd)],
@@ -417,19 +421,18 @@
     normed_one, qkv_mine, own_proj = after((normed_one, qkv_mine, proj_w))
     normed_one_row = lax.all_gather(normed_one, "seq", axis=0, tiled=True)
 
-    qkv_mine, order = after((qkv_mine, order))
     qkv_mine = lax.all_gather(qkv_mine, "dp", axis=0, tiled=True)
     qkv_mine, own_proj = after((qkv_mine, own_proj))
     proj_rows = lax.all_gather(own_proj, "seq", axis=0, tiled=True)
     half = part // 2
     own_half = lax.dynamic_slice_in_dim(proj_rows, core * half, half, 0)
     proj_halves = [swap(own_half, k) for k in range(1, nd)]
-    normed_one_row, qkv_mine, qkv_wide, segments, proj_rows = after(
-        (normed_one_row, qkv_mine, widen(qkv_mine), segments, proj_rows)
+    normed_one_row, qkv_mine, qkv_wide, proj_rows = after(
+        (normed_one_row, qkv_mine, widen(qkv_mine), proj_rows)
     )
     up_part = lax.all_gather(up_slices, "seq", axis=0, tiled=True)
     triple = dot(normed_one_row, qkv_wide).astype(BF16)
-    attended, attended_low, lse = attend(triple, segments, heads, scale)
+    attended, attended_low, lse = attend(triple, item_lengths, heads, scale)
 
     def heads_to_tokens(v):
         v = seq_exchange(v.reshape(ns, local, head_cols))
@@ -449,9 +452,7 @@
         w_proj = lax.dynamic_update_slice_in_dim(w_proj, there, (place + 1 - core) * half, 0)
     grad_out_rows = gather_rows(grad_out)
     attended_low = heads_to_tokens(attended_low)
-    attended_low, grad_out_rows, w_proj, order = after(
-        (attended_low, grad_out_rows, w_proj, order)
-    )
+    attended_low, grad_out_rows, w_proj = after((attended_low, grad_out_rows, w_proj))
     own_down, attended_low, up_part = after((fc2_w, attended_low, up_part))
     down_part = lax.all_gather(own_down, "seq", axis=0, tiled=True)
     second = first + dot(attended_low, w_proj) + b_proj
@@ -460,7 +461,7 @@
 
     normed_two_rows = gather_rows(normed_two)
     up_part = inner(order, up_part).astype(BF16)
-    normed_two_rows, up_part, order = after((normed_two_rows, up_part, order))
+    normed_two_rows, up_part = after((normed_two_rows, up_part))
     hidden, slope = gelu_of_matmul(normed_two_rows, up_part, up_bias)
 
     fc2_terms = inner(hidden, grad_out_rows).astype(BF16)
@@ -491,7 +492,7 @@
         (attended_grad, down_blocks[0], second_late, attended_slices)
     )
     triple_grad = jnp.concatenate(
-        attend_back(triple, attended_grad, attended, lse, segments, heads, scale), axis=1
+        attend_back(triple, attended_grad, attended, lse, item_lengths, heads, scale), axis=1
     )
     one_back = times_transposed(triple_grad, qkv_mine).astype(BF16)
     output = second + down_sums[:local] + b_down

time: 402 us -> 394 us (0.980)
  other arithmetic: 36.4 us -> 28.1 us
    ppermute x42, waiting for transfers between devices: 60.5 us -> 52.2 us  [swap(): return lax.ppermute(v, 'dp', [(i, i ^ k) for i in range(nd)])]
    unnamed x86 -> x106, local copies, waits for them, and re-layouts: 8.16 us -> 9.89 us
  transfers between devices with their start and end apart: 61 -> 61, of which waited for: 17 -> 19; matrix products, arithmetic and copies ran while one was open for 32% -> 31% of each run, Pallas kernels for 10% -> 10%
where the time goes in v16:
time: 394 us; the launch traced here: 387 us
  starting transfers between devices  81.1 us (21%)
  waiting for transfers between devices  79.9 us (20%)
  local copies, waits for them, and re-layouts  58.8 us (15%)
  matrix products  50.6 us (13%)
  Pallas kernels  39.9 us (10%)
  blocking collectives  33.1 us (8%)
  other arithmetic  28.1 us (7%)
  between operations  15.7 us (4%)
    ppermute x42, waiting for transfers between devices, swap(): return lax.ppermute(v, 'dp', [(i, i ^ k) for i in range(nd)])  52.2 us
    ppermute x42, starting transfers between devices, swap(): return lax.ppermute(v, 'dp', [(i, i ^ k) for i in range(nd)])  51.9 us
    dot_general x6, matrix products, inner(): lax.dot_general(left, right, (((0,), (0,)), ((), ())), preferred_element_...  26.6 us
    all_gather x1, blocking collectives, on_device(): proj_rows = lax.all_gather(own_proj, 'seq', axis=0, tiled=True)  19.8 us
    all_to_all x4, waiting for transfers between devices, seq_exchange(): return lax.all_to_all(v, 'seq', 0, 0, tiled=True)  17.8 us
    dot_general x4, matrix products, dot(): return jnp.dot(left, right, preferred_element_type=F32)  17.8 us
    all_to_all x4, starting transfers between devices, seq_exchange(): return lax.all_to_all(v, 'seq', 0, 0, tiled=True)  15.4 us
    pallas_call x1, Pallas kernels, attend_back(): pl.pallas_call(partial(attend_back_kernel, heads, scale), grid=(rows // s...  14.1 us
  transfers between devices with their start and end apart: 61, of which 19 were waited for; matrix products, arithmetic and copies ran while one was open for 31% of the time, Pallas kernels for 10%

profile of v16, /device:TPU:0, one launch (start us, length us, event | category | flops | bytes accessed | tf_op | source)
XLA Modules:
  0.0 387.0 jit_solution(5447901891188997923)
XLA Ops:
  19.6 4.0 %all-to-all-start = ((bf16[32,8,128]{2,1,0:T(8,128)(2,1)}), bf16[32,8,128]{2,1,0:T(8,128)(2,1)S(1)}, u32[]{:S(2)}, u32[]{:S(2)}) async-start(bf16[32,8,128]{2,1,0:T(8,128)(2,1)} %broadcast_in_dim.15), calls=%async_computation | async-start | bytes 131072 | tf_op jit(solution)/shard_map/all_to_all | solution.py:381
  37.2 4.3 %fusion.60 = (bf16[640,1152]{1,0:T(8,128)(2,1)S(1)}, f32[640,1152]{1,0:T(8,128)}) fusion(bf16[640,576]{1,0:T(8,128)(2,1)S(1)} %pad_maximum_fusion.7, bf16[576,1152]{1,0:T(8,128)(2,1)} %all-gather.6.cloned.1.call-done), kind=kOutput, calls=%fused_computation.167 | convolution fusion | flops 850083840 | bytes 6488064 | tf_op jit(solution)/shard_map/dot_general | solution.py:52
  53.1 8.3 %collective-permute-done.7 = bf16[160,1152]{1,0:T(8,128)(2,1)S(1)} collective-permute-done((bf16[160,1152]{1,0:T(8,128)(2,1)S(1)}, bf16[160,1152]{1,0:T(8,128)(2,1)S(1)}, u32[]{:S(2)}, u32[]{:S(2)}) %collective-permute-start.7) | collective-permute-done | bytes 368672 | tf_op jit(solution)/shard_map/ppermute | solution.py:336
  65.0 13.3 %all_gather.20 = bf16[1152,432]{1,0:T(8,128)(2,1)S(1)} all-gather(bf16[288,432]{1,0:T(8,128)(2,1)S(1)} %reshape.194), channel_id=1, replica_groups=mesh['dp'=4,'seq'=8] {'dp'}, dimensions={0}, use_global_device_ids=true | all-gather | bytes 1244160 | tf_op jit(solution)/shard_map/all_gather | solution.py:424
  78.2 19.8 %all-gather = bf16[8,36,1152]{2,1,0:T(8,128)(2,1)} all-gather(bf16[1,36,1152]{2,1,0:T(8,128)(2,1)S(1)} %bitcast.172), channel_id=1, replica_groups=mesh['dp'=4,'seq'=8] {'seq'}, dimensions={0}, use_global_device_ids=true | all-gather | bytes 746496 | tf_op jit(solution)/shard_map/all_gather | solution.py:426
  107.7 5.1 %convolution_convert_fusion.4.q_ref.k_ref.v_ref = bf16[1280,768]{1,0:T(8,128)(2,1)S(1)} fusion(bf16[1280,1152]{1,0:T(8,128)(2,1)} %all-gather.8.cloned.1.call-done, bf16[1152,768]{0,1:T(8,128)(2,1)} %bitcast.152), kind=kOutput, calls=%fused_computation.22 | convolution fusion | flops 2265907200 | bytes 6684672 | tf_op jit(solution)/shard_map/dot_general | solution.py:52
  112.9 8.4 %shard_map.288 = (f32[1280,256]{1,0:T(8,128)S(1)}, bf16[1280,144]{1,0:T(8,128)(2,1)S(1)}, f32[8,1280]{1,0:T(8,128)S(1)}) custom-call(bf16[1280,768]{1,0:T(8,128)(2,1)S(1)} %convolution_convert_fusion.4.q_ref.k_ref.v_ref, bf16[1280,768]{1,0:T(8,128)(2,1)S(1)} %convolution_convert_fusion.4.q_ref.k_ref.v_ref, ...), custom_call_target="tpu_custom_call" | custom-call | flops 3355443200 | bytes 3276800 | tf_op jit(solution)/shard_map/pallas_call | solution.py:93
  146.3 5.6 %all-to-all-done.2 = bf16[8,160,144]{1,2,0:T(8,128)(2,1)S(1)} async-done(((bf16[8,160,144]{1,2,0:T(8,128)(2,1)}), bf16[8,160,144]{1,2,0:T(8,128)(2,1)S(1)}, u32[]{:S(2)}, u32[]{:S(2)}) %all-to-all-start.2) | async-done | bytes 368672 | tf_op jit(solution)/shard_map/all_to_all | solution.py:360
  160.1 4.6 %convolution_convert_fusion.3.up_ref = bf16[1152,1152]{1,0:T(8,128)(2,1)S(1)} fusion(bf16[1152,1152]{1,0:T(8,128)(2,1)S(1)} %copy-done.49, s32[1152]{0:T(1024)S(1)} %get-tuple-element.237, s32[1152]{0:T(1024)S(1)} %get-tuple-element.238, s32[]{:T(128)S(6)} %axis_index.23, s32[1152]{0:T(1024)S(1)} %get-tuple-element.236, s32[1152]{0:T(1024)S(1)} %get-tuple-element.239, ...), kind=kOutput, calls=%fused_computation.11 | convolution fusion | flops 3094806528 | bytes 5329156 | tf_op jit(solution)/shard_map/dot_general | solution.py:56
  168.1 8.2 %collective-permute-done.19 = bf16[160,1152]{1,0:T(8,128)(2,1)S(1)} collective-permute-done((bf16[160,1152]{1,0:T(8,128)(2,1)S(1)}, bf16[160,1152]{1,0:T(8,128)(2,1)S(1)}, u32[]{:S(2)}, u32[]{:S(2)}) %collective-permute-start.19) | collective-permute-done | bytes 368672 | tf_op jit(solution)/shard_map/ppermute | solution.py:336
  176.4 5.6 %shard_map.289 = (bf16[640,1152]{1,0:T(8,128)(2,1)S(1)}, f32[640,1152]{1,0:T(8,128)S(1)}) custom-call(bf16[640,1152]{1,0:T(8,128)(2,1)S(1)} %pad_maximum_fusion.1.x_ref, bf16[1152,1152]{1,0:T(8,128)(2,1)S(1)} %convolution_convert_fusion.3.up_ref, f32[1,1152]{1,0:T(1,128)S(1)} %reshape_reshape.6.bias_ref), custom_call_target="tpu_custom_call" | custom-call | flops 1698693120 | bytes 8552448 | tf_op jit(solution)/shard_map/pallas_call | solution.py:255
  183.7 4.0 %convolution_convert_fusion.2 = bf16[1152,1152]{1,0:T(8,128)(2,1)} fusion(bf16[640,1152]{1,0:T(8,128)(2,1)S(1)} %get-tuple-element.124, bf16[640,1152]{1,0:T(8,128)(2,1)S(1)} %copy-done.26), kind=kOutput, calls=%fused_computation.10 | convolution fusion | flops 1700020224 | bytes 5603328 | tf_op jit(solution)/shard_map/dot_general | solution.py:56
  188.0 8.2 %shard_map.290 = (bf16[640,1152]{1,0:T(8,128)(2,1)}, f32[1,1152]{1,0:T(1,128)S(1)}, f32[160,1152]{1,0:T(8,128)S(1)}, bf16[160,1152]{1,0:T(8,128)(2,1)S(1)}, bf16...) custom-call(bf16[640,1152]{1,0:T(8,128)(2,1)} %pad_maximum_fusion.grad_ref, bf16[1152,1152]{1,0:T(8,128)(2,1)} %copy-done.2, ...), custom_call_target="tpu_custom_call" | custom-call | flops 3397386240 | bytes 12681216 | tf_op jit(solution)/shard_map/pallas_call | solution.py:293
  199.7 9.8 %convolution_convert_fusion.1 = bf16[1152,1152]{1,0:T(8,128)(2,1)} fusion(bf16[640,1152]{1,0:T(8,128)(2,1)} %get-tuple-element.120, bf16[640,1152]{1,0:T(8,128)(2,1)S(1)} %pad_maximum_fusion.1.x_ref, s32[1152]{0:T(1024)S(1)} %get-tuple-element.237, s32[1152]{0:T(1024)S(1)} %copy-done.36, s32[]{:T(128)S(6)} %axis_index.23, s32[1152]{0:T(1024)S(1)} %get-tuple-element.236, ...), kind=kOutput, calls=%fused_computation.9 | convolution fusion | flops 3435282432 | bytes 5624068 | tf_op jit(solution)/shard_map/dot_general | solution.py:56
  209.6 5.2 %collective-permute-done.22 = bf16[160,1152]{1,0:T(8,128)(2,1)} collective-permute-done((bf16[160,1152]{1,0:T(8,128)(2,1)S(1)}, bf16[160,1152]{1,0:T(8,128)(2,1)}, u32[]{:S(2)}, u32[]{:S(2)}) %collective-permute-start.22) | collective-permute-done | bytes 368672 | tf_op jit(solution)/shard_map/ppermute | solution.py:336
  223.6 4.2 %all-to-all-start.3 = ((bf16[8,160,144]{1,2,0:T(8,128)(2,1)}), bf16[8,160,144]{1,2,0:T(8,128)(2,1)}, u32[]{:S(2)}, u32[]{:S(2)}) async-start(bf16[8,160,144]{1,2,0:T(8,128)(2,1)} %copy.61), calls=%async_computation.3 | async-start | bytes 1179648 | tf_op jit(solution)/shard_map/all_to_all | solution.py:360
  227.9 5.7 %fusion.62 = (bf16[640,1152]{1,0:T(8,128)(2,1)S(1)}, f32[640,1152]{1,0:T(8,128)}) fusion(bf16[640,1152]{1,0:T(8,128)(2,1)S(1)} %copy-done.4, bf16[1152,1152]{1,0:T(8,128)(2,1)} %all-gather.12.cloned.1.call-done.down_ref), kind=kOutput, calls=%fused_computation.169 | convolution fusion | flops 1699430400 | bytes 8552448 | tf_op jit(solution)/shard_map/dot_general | solution.py:52
  241.3 10.0 %all-to-all-done.3 = bf16[8,160,144]{1,2,0:T(8,128)(2,1)} async-done(((bf16[8,160,144]{1,2,0:T(8,128)(2,1)}), bf16[8,160,144]{1,2,0:T(8,128)(2,1)}, u32[]{:S(2)}, u32[]{:S(2)}) %all-to-all-start.3) | async-done | bytes 368672 | tf_op jit(solution)/shard_map/all_to_all | solution.py:360
  256.1 14.1 %shard_map.292 = (bf16[1280,144]{1,0:T(8,128)(2,1)S(1)}, bf16[1280,288]{1,0:T(8,128)(2,1)S(1)}) custom-call(bf16[1280,768]{1,0:T(8,128)(2,1)S(1)} %copy-done.6, bf16[1280,768]{1,0:T(8,128)(2,1)S(1)} %copy-done.6, bf16[1280,768]{1,0:T(8,128)(2,1)S(1)} %copy-done.6, bf16[1280,256]{1,0:T(8,128)(2,1)S(1)} %pad.18.out_grad_ref, f32[1280,256]{1,0:T(8,128)S(1)} %copy-done.8, ...), custom_call_target="tpu_custom_call" | custom-call | flops 8388608000 | bytes 4587520 | tf_op jit(solution)/shard_map/pallas_call | solution.py:173
  282.8 3.9 %fusion.63 = f32[1152,432]{1,0:T(8,128)S(1)} fusion(bf16[1280,1152]{1,0:T(8,128)(2,1)} %all-gather.8.cloned.1.call-done, bf16[1280,432]{1,0:T(8,128)(2,1)} %copy-done.27), kind=kOutput, calls=%fused_computation.170 | convolution fusion | flops 1274019840 | bytes 6045696 | tf_op jit(solution)/shard_map/dot_general | solution.py:56
  293.0 7.1 %collective-permute-done.31 = bf16[160,1152]{1,0:T(8,128)(2,1)S(1)} collective-permute-done((bf16[160,1152]{1,0:T(8,128)(2,1)S(1)}, bf16[160,1152]{1,0:T(8,128)(2,1)S(1)}, u32[]{:S(2)}, u32[]{:S(2)}) %collective-permute-start.31) | collective-permute-done | bytes 368672 | tf_op jit(solution)/shard_map/ppermute | solution.py:336
  311.2 4.9 %all-to-all-start.5 = ((bf16[4,36,1152]{2,1,0:T(8,128)(2,1)}), bf16[4,36,1152]{2,1,0:T(8,128)(2,1)S(1)}, u32[]{:S(2)}, u32[]{:S(2)}) async-start(bf16[4,36,1152]{2,1,0:T(8,128)(2,1)} %fusion.27), calls=%async_computation.8 | async-start | bytes 737280 | tf_op jit(solution)/shard_map/all_to_all | solution.py:370
  327.1 4.2 %all-to-all-start.4 = ((bf16[8,36,432]{2,1,0:T(8,128)(2,1)}), bf16[8,36,432]{2,1,0:T(8,128)(2,1)}, u32[]{:S(2)}, u32[]{:S(2)}) async-start(bf16[8,36,432]{2,1,0:T(8,128)(2,1)} %reshape.202), calls=%async_computation.7 | async-start | bytes 655360 | tf_op jit(solution)/shard_map/all_to_all | solution.py:360
  366.3 6.8 %collective-permute-done.41 = bf16[160,576]{0,1:T(8,128)(2,1)} collective-permute-done((bf16[160,576]{0,1:T(8,128)(2,1)}, bf16[160,576]{0,1:T(8,128)(2,1)}, u32[]{:S(2)}, u32[]{:S(2)}) %collective-permute-start.41) | collective-permute-done | bytes 184352 | tf_op jit(solution)/shard_map/ppermute | solution.py:336
  (353 shorter events, 196.2 us)
Async XLA Ops:
  7.2 30.0 %all-gather.6.cloned.1.call-start = ((), (), s32[]{:S(2)}) async-start(), calls=%async_computation.11 | async-start | bytes 1492992 | tf_op jit(solution)/shard_map/all_gather | solution.py:373
  9.7 22.1 %collective-permute-start = (bf16[160,576]{1,0:T(8,128)(2,1)S(1)}, bf16[160,576]{1,0:T(8,128)(2,1)S(1)}, u32[]{:S(2)}, u32[]{:S(2)}) collective-permute-start(bf16[160,576]{1,0:T(8,128)(2,1)S(1)} %get-tuple-element.186), channel_id=1, source_target_pairs={{0,8},{8,0},{16,24},{24,16},{1,9},{9,1},{17,25},{25,17},{2,10},{10... | collective-permute-start | bytes 552968 | tf_op jit(solution)/shard_map/ppermute | solution.py:336
  12.8 19.1 %collective-permute-start.1 = (bf16[160,576]{1,0:T(8,128)(2,1)S(1)}, bf16[160,576]{1,0:T(8,128)(2,1)S(1)}, u32[]{:S(2)}, u32[]{:S(2)}) collective-permute-start(bf16[160,576]{1,0:T(8,128)(2,1)S(1)} %get-tuple-element.185), channel_id=1, source_target_pairs={{0,16},{8,24},{16,0},{24,8},{1,17},{9,25},{17,1},{25,9},{2,18},{10... | collective-permute-start | bytes 552968 | tf_op jit(solution)/shard_map/ppermute | solution.py:336
  49.8 57.9 %all-gather.8.cloned.1.call-start = ((), (), s32[]{:S(2)}) async-start(), calls=%async_computation.12 | async-start | bytes 3317760 | tf_op jit(solution)/shard_map/all_gather | solution.py:422
  64.2 88.0 %all-gather.10.cloned.1.call-start = ((), (), s32[]{:S(2)}) async-start(), calls=%async_computation.13 | async-start | bytes 2985984 | tf_op jit(solution)/shard_map/all_gather | solution.py:433
  100.0 22.3 %collective-permute-start.10 = (bf16[144,1152]{1,0:T(8,128)(2,1)}, bf16[144,1152]{1,0:T(8,128)(2,1)}, u32[]{:S(2)}, u32[]{:S(2)}) collective-permute-start(bf16[144,1152]{1,0:T(8,128)(2,1)} %constant_dynamic-slice_fusion.5), channel_id=1, source_target_pairs={{0,16},{8,24},{16,0},{24,8},{1,17},{9,25},{17,1},{25,9},{2,18},{10... | collective-permute-start | bytes 995336 | tf_op jit(solution)/shard_map/ppermute | solution.py:336
  101.1 21.2 %collective-permute-start.11 = (bf16[144,1152]{1,0:T(8,128)(2,1)}, bf16[144,1152]{1,0:T(8,128)(2,1)}, u32[]{:S(2)}, u32[]{:S(2)}) collective-permute-start(bf16[144,1152]{1,0:T(8,128)(2,1)} %constant_dynamic-slice_fusion.5), channel_id=1, source_target_pairs={{0,24},{8,16},{16,8},{24,0},{1,25},{9,17},{17,9},{25,1},{2,26},{10... | collective-permute-start | bytes 995336 | tf_op jit(solution)/shard_map/ppermute | solution.py:336
  102.6 19.7 %collective-permute-start.9 = (bf16[144,1152]{1,0:T(8,128)(2,1)}, bf16[144,1152]{1,0:T(8,128)(2,1)}, u32[]{:S(2)}, u32[]{:S(2)}) collective-permute-start(bf16[144,1152]{1,0:T(8,128)(2,1)} %constant_dynamic-slice_fusion.5), channel_id=1, source_target_pairs={{0,8},{8,0},{16,24},{24,16},{1,9},{9,1},{17,25},{25,17},{2,10},{10... | collective-permute-start | bytes 995336 | tf_op jit(solution)/shard_map/ppermute | solution.py:336
  122.3 21.5 %collective-permute-start.12 = (bf16[160,1152]{1,0:T(8,128)(2,1)S(1)}, bf16[160,1152]{1,0:T(8,128)(2,1)}, u32[]{:S(2)}, u32[]{:S(2)}) collective-permute-start(bf16[160,1152]{1,0:T(8,128)(2,1)S(1)} %bitcast.153), channel_id=1, source_target_pairs={{0,8},{8,0},{16,24},{24,16},{1,9},{9,1},{17,25},{25,17},{2,10},{10... | collective-permute-start | bytes 1105928 | tf_op jit(solution)/shard_map/ppermute | solution.py:336
  123.5 20.4 %collective-permute-start.13 = (bf16[160,1152]{1,0:T(8,128)(2,1)S(1)}, bf16[160,1152]{1,0:T(8,128)(2,1)}, u32[]{:S(2)}, u32[]{:S(2)}) collective-permute-start(bf16[160,1152]{1,0:T(8,128)(2,1)S(1)} %bitcast.154), channel_id=1, source_target_pairs={{0,16},{8,24},{16,0},{24,8},{1,17},{9,25},{17,1},{25,9},{2,18},{10... | collective-permute-start | bytes 1105928 | tf_op jit(solution)/shard_map/ppermute | solution.py:336
  124.4 19.4 %collective-permute-start.14 = (bf16[160,1152]{1,0:T(8,128)(2,1)S(1)}, bf16[160,1152]{1,0:T(8,128)(2,1)}, u32[]{:S(2)}, u32[]{:S(2)}) collective-permute-start(bf16[160,1152]{1,0:T(8,128)(2,1)S(1)} %bitcast.155), channel_id=1, source_target_pairs={{0,24},{8,16},{16,8},{24,0},{1,25},{9,17},{17,9},{25,1},{2,26},{10... | collective-permute-start | bytes 1105928 | tf_op jit(solution)/shard_map/ppermute | solution.py:336
  127.6 24.3 %all-to-all-start.2 = ((bf16[8,160,144]{1,2,0:T(8,128)(2,1)}), bf16[8,160,144]{1,2,0:T(8,128)(2,1)S(1)}, u32[]{:S(2)}, u32[]{:S(2)}) async-start(bf16[8,160,144]{1,2,0:T(8,128)(2,1)} %copy.59), calls=%async_computation.2 | async-start | bytes 1179648 | tf_op jit(solution)/shard_map/all_to_all | solution.py:360
  131.1 56.8 %all-gather.12.cloned.1.call-start = ((), (), s32[]{:S(2)}) async-start(), calls=%async_computation.14 | async-start | bytes 2985984 | tf_op jit(solution)/shard_map/all_gather | solution.py:457
  152.2 125.6 %reduce-scatter.9.cloned.1.call-start = ((), (), s32[]{:S(2)}) async-start(), calls=%async_computation.16 | async-start | bytes 2985984 | tf_op jit(solution)/shard_map/reduce_scatter | solution.py:468
  187.7 90.1 %reduce-scatter.7.cloned.1.call-start = ((), (), s32[]{:S(2)}) async-start(), calls=%async_computation.15 | async-start | bytes 2985984 | tf_op jit(solution)/shard_map/reduce_scatter | solution.py:485
  223.6 27.7 %all-to-all-start.3 = ((bf16[8,160,144]{1,2,0:T(8,128)(2,1)}), bf16[8,160,144]{1,2,0:T(8,128)(2,1)}, u32[]{:S(2)}, u32[]{:S(2)}) async-start(bf16[8,160,144]{1,2,0:T(8,128)(2,1)} %copy.61), calls=%async_computation.3 | async-start | bytes 1179648 | tf_op jit(solution)/shard_map/all_to_all | solution.py:360
  227.8 88.3 %reduce-scatter.11.cloned.1.call-start = ((), (), s32[]{:S(2)}) async-start(), calls=%async_computation.17 | async-start | bytes 3317760 | tf_op jit(solution)/shard_map/reduce_scatter | solution.py:505
  238.6 36.9 %collective-permute-start.25 = (bf16[160,1152]{1,0:T(8,128)(2,1)}, bf16[160,1152]{1,0:T(8,128)(2,1)S(1)}, u32[]{:S(2)}, u32[]{:S(2)}) collective-permute-start(bf16[160,1152]{1,0:T(8,128)(2,1)} %get-tuple-element.170), channel_id=1, source_target_pairs={{0,16},{8,24},{16,0},{24,8},{1,17},{9,25},{17,1},{25,9},{2,18},{10... | collective-permute-start | bytes 1105928 | tf_op jit(solution)/shard_map/ppermute | solution.py:336
  239.5 35.9 %collective-permute-start.26 = (bf16[160,1152]{1,0:T(8,128)(2,1)}, bf16[160,1152]{1,0:T(8,128)(2,1)}, u32[]{:S(2)}, u32[]{:S(2)}) collective-permute-start(bf16[160,1152]{1,0:T(8,128)(2,1)} %get-tuple-element.171), channel_id=1, source_target_pairs={{0,24},{8,16},{16,8},{24,0},{1,25},{9,17},{17,9},{25,1},{2,26},{10... | collective-permute-start | bytes 1105928 | tf_op jit(solution)/shard_map/ppermute | solution.py:336
  277.9 22.3 %collective-permute-start.36 = (bf16[160,288]{1,0:T(8,128)(2,1)S(1)}, bf16[160,288]{1,0:T(8,128)(2,1)S(1)}, u32[]{:S(2)}, u32[]{:S(2)}) collective-permute-start(bf16[160,288]{1,0:T(8,128)(2,1)S(1)} %get-tuple-element.194), channel_id=1, source_target_pairs={{0,8},{8,0},{16,24},{24,16},{1,9},{9,1},{17,25},{25,17},{2,10},{10... | collective-permute-start | bytes 276488 | tf_op jit(solution)/shard_map/ppermute | solution.py:336
  278.3 21.9 %collective-permute-start.37 = (bf16[160,288]{1,0:T(8,128)(2,1)S(1)}, bf16[160,288]{1,0:T(8,128)(2,1)S(1)}, u32[]{:S(2)}, u32[]{:S(2)}) collective-permute-start(bf16[160,288]{1,0:T(8,128)(2,1)S(1)} %get-tuple-element.193), channel_id=1, source_target_pairs={{0,16},{8,24},{16,0},{24,8},{1,17},{9,25},{17,1},{25,9},{2,18},{10... | collective-permute-start | bytes 276488 | tf_op jit(solution)/shard_map/ppermute | solution.py:336
  280.4 19.7 %collective-permute-start.31 = (bf16[160,1152]{1,0:T(8,128)(2,1)S(1)}, bf16[160,1152]{1,0:T(8,128)(2,1)S(1)}, u32[]{:S(2)}, u32[]{:S(2)}) collective-permute-start(bf16[160,1152]{1,0:T(8,128)(2,1)S(1)} %copy-done.19), channel_id=1, source_target_pairs={{0,16},{8,24},{16,0},{24,8},{1,17},{9,25},{17,1},{25,9},{2,18},{10... | collective-permute-start | bytes 1105928 | tf_op jit(solution)/shard_map/ppermute | solution.py:336
  331.2 47.0 %reduce-scatter.13.cloned.1.call-start = ((), (), s32[]{:S(2)}) async-start(), calls=%async_computation.18 | async-start | bytes 1492992
  346.1 30.9 %all-to-all-start.6 = ((f32[32,8,128]{2,1,0:T(8,128)}), f32[32,8,128]{2,1,0:T(8,128)S(1)}, u32[]{:S(2)}, u32[]{:S(2)}) async-start(f32[32,8,128]{2,1,0:T(8,128)} %bitcast.66), calls=%async_computation.9 | async-start | bytes 262144 | tf_op jit(solution)/shard_map/all_to_all | solution.py:556
  (87 other events, 981.7 us)
Sparse Core Ops, SparseCore 0:
  9.7 27.5 all-gather.5
  64.3 41.1 all-gather.7
  107.7 36.9 all-gather.9
  152.3 32.3 all-gather.11
  187.8 36.4 reduce-scatter.8
  226.5 43.5 reduce-scatter.6
  277.9 36.7 reduce-scatter.10
  345.0 32.8 reduce-scatter.12

commit v17 on v16

--- a/solution.py
+++ b/solution.py
@@ -129,10 +129,9 @@
         sum_ref[...] = jnp.zeros_like(sum_ref)
         ones = jnp.ones((8, WIDE), F32)
         for h in range(heads):
-            grad = out_grad_ref[...]
-            if h > 0:
-                grad = pltpu.roll(grad.astype(F32), 2 * WIDE - HEAD_DIM, 1).astype(BF16)
-            grad = grad[:, :WIDE]
+            grad = out_grad_ref[:, h * HEAD_DIM : (h + 1) * HEAD_DIM]
+            gap = jnp.zeros((grad.shape[0], WIDE - HEAD_DIM), BF16)
+            grad = jnp.concatenate([grad, gap], axis=1)
             at = slice(h * WIDE, (h + 1) * WIDE)
             grad_ref[:, at] = grad
             delta = lax.dot_general(
@@ -168,7 +167,6 @@
     wide = heads * WIDE
     step = 256 if rows % 256 == 0 else rows
     whole = pl.BlockSpec((rows, wide), lambda i: (0, 0))
-    out_grad = jnp.pad(out_grad, ((0, 0), (0, wide - out_grad.shape[1])))
     row = pl.BlockSpec((8, rows), lambda i: (0, 0))
     return pl.pallas_call(
         partial(attend_back_kernel, heads, scale),
@@ -177,7 +175,7 @@
             whole,
             pl.BlockSpec((step, wide), lambda i: (i, 1)),
             pl.BlockSpec((step, wide), lambda i: (i, 2)),
-            whole,
+            pl.BlockSpec((rows, heads * HEAD_DIM), lambda i: (0, 0)),
             whole,
             row,
             pl.BlockSpec(memory_space=pltpu.SMEM),
@@ -422,13 +420,14 @@
     normed_one_row = lax.all_gather(normed_one, "seq", axis=0, tiled=True)
 
     qkv_mine = lax.all_gather(qkv_mine, "dp", axis=0, tiled=True)
-    qkv_mine, own_proj = after((qkv_mine, own_proj))
+    qkv_mine, own_proj, grad_out = after((qkv_mine, own_proj, cotangent[0]))
+    grad_out_rows = gather_rows(grad_out)
     proj_rows = lax.all_gather(own_proj, "seq", axis=0, tiled=True)
     half = part // 2
     own_half = lax.dynamic_slice_in_dim(proj_rows, core * half, half, 0)
     proj_halves = [swap(own_half, k) for k in range(1, nd)]
-    normed_one_row, qkv_mine, qkv_wide, proj_rows = after(
-        (normed_one_row, qkv_mine, widen(qkv_mine), proj_rows)
+    normed_one_row, qkv_mine, qkv_wide, proj_rows, grad_out_rows = after(
+        (normed_one_row, qkv_mine, widen(qkv_mine), proj_rows, grad_out_rows)
     )
     up_part = lax.all_gather(up_slices, "seq", axis=0, tiled=True)
     triple = dot(normed_one_row, qkv_wide).astype(BF16)
@@ -438,9 +437,7 @@
         v = seq_exchange(v.reshape(ns, local, head_cols))
         return jnp.swapaxes(v, 0, 1).reshape(local, features)
 
-    attended_low, grad_out, proj_halves, proj_rows = after(
-        (attended_low, cotangent[0], proj_halves, proj_rows)
-    )
+    attended_low, proj_halves, proj_rows = after((attended_low, proj_halves, proj_rows))
     w_proj = lax.dynamic_update_slice_in_dim(
         jnp.zeros((features, features), BF16), proj_rows, dp_at * part, 0
     )
@@ -450,7 +447,6 @@
         there = other_core(here)
         w_proj = lax.dynamic_update_slice_in_dim(w_proj, here, (place + core) * half, 0)
         w_proj = lax.dynamic_update_slice_in_dim(w_proj, there, (place + 1 - core) * half, 0)
-    grad_out_rows = gather_rows(grad_out)
     attended_low = heads_to_tokens(attended_low)
     attended_low, grad_out_rows, w_proj = after((attended_low, grad_out_rows, w_proj))
     own_down, attended_low, up_part = after((fc2_w, attended_low, up_part))
@@ -495,13 +491,13 @@
         attend_back(triple, attended_grad, attended, lse, item_lengths, heads, scale), axis=1
     )
     one_back = times_transposed(triple_grad, qkv_mine).astype(BF16)
+    one_back, triple_late, down_blocks, second_late, fc1_terms, fc2_w_grad = after(
+        (one_back, triple_grad, down_blocks, second_late, fc1_terms, fc2_w_grad)
+    )
     output = second + down_sums[:local] + b_down
     for block in down_blocks:
         output = output + block.astype(F32)
     output = output.astype(BF16)
-    one_back, triple_late, output, second_late, fc1_terms, fc2_w_grad = after(
-        (one_back, triple_grad, output, second_late, fc1_terms, fc2_w_grad)
-    )
     normed_one_grad = lax.psum_scatter(one_back, "seq", scatter_dimension=0, tiled=True)
     second_rows = gather_rows(second_late)
     qkv_terms = inner(normed_one_row, triple_late).reshape(nd, part, wide)
@@ -525,9 +521,7 @@
     first_low_rows = gather_rows(first_low)
     proj_w_grad = chip_sums(proj_sums)
     qkv_w_grad = seq_exchange(qkv_sum)
-    first_low_rows, first_grad, qkv_w_grad, proj_w_grad = after(
-        (first_low_rows, first_grad, qkv_w_grad, proj_w_grad)
-    )
+    first_low_rows, first_grad, proj_w_grad = after((first_low_rows, first_grad, proj_w_grad))
     skip_terms = inner(joined_here, first_low_rows).astype(BF16)
     skip_w_grad = lax.psum_scatter(skip_terms, "seq", scatter_dimension=0, tiled=True).astype(F32)
     skip_terms, first_low_rows, first_grad, fc1_terms, qkv_w_grad = after(

time: 394 us -> 392 us (level)
  local copies, waits for them, and re-layouts: 58.8 us -> 53 us
    ppermute x42, waiting for transfers between devices: 52.2 us -> 56.5 us  [swap(): return lax.ppermute(v, 'dp', [(i, i ^ k) for i in range(nd)])]
  transfers between devices with their start and end apart: 61 -> 61, of which waited for: 19 -> 18; matrix products, arithmetic and copies ran while one was open for 31% -> 30% of each run, Pallas kernels for 10% -> 10%
where the time goes in v17:
time: 392 us; the launch traced here: 386 us
  starting transfers between devices  83.4 us (21%)
  waiting for transfers between devices  83.1 us (21%)
  local copies, waits for them, and re-layouts  53 us (14%)
  matrix products  50.3 us (13%)
  Pallas kernels  39.8 us (10%)
  blocking collectives  33.2 us (8%)
  other arithmetic  27.1 us (7%)
  between operations  15.7 us (4%)
    ppermute x42, waiting for transfers between devices, swap(): return lax.ppermute(v, 'dp', [(i, i ^ k) for i in range(nd)])  56.5 us
    ppermute x42, starting transfers between devices, swap(): return lax.ppermute(v, 'dp', [(i, i ^ k) for i in range(nd)])  51.7 us
    dot_general x6, matrix products, inner(): lax.dot_general(left, right, (((0,), (0,)), ((), ())), preferred_element_...  26.2 us
    all_gather x1, blocking collectives, on_device(): proj_rows = lax.all_gather(own_proj, 'seq', axis=0, tiled=True)  19.9 us
    dot_general x4, matrix products, dot(): return jnp.dot(left, right, preferred_element_type=F32)  18 us
    all_to_all x4, waiting for transfers between devices, seq_exchange(): return lax.all_to_all(v, 'seq', 0, 0, tiled=True)  18 us
    all_to_all x4, starting transfers between devices, seq_exchange(): return lax.all_to_all(v, 'seq', 0, 0, tiled=True)  16.2 us
    pallas_call x1, Pallas kernels, attend_back(): pl.pallas_call(partial(attend_back_kernel, heads, scale), grid=(rows // s...  14.1 us
  transfers between devices with their start and end apart: 61, of which 18 were waited for; matrix products, arithmetic and copies ran while one was open for 30% of the time, Pallas kernels for 10%

profile of v17, /device:TPU:0, one launch (start us, length us, event | category | flops | bytes accessed | tf_op | source)
XLA Modules:
  0.0 385.6 jit_solution(4516366622862516699)
XLA Ops:
  19.6 4.0 %all-to-all-start = ((bf16[32,8,128]{2,1,0:T(8,128)(2,1)}), bf16[32,8,128]{2,1,0:T(8,128)(2,1)S(1)}, u32[]{:S(2)}, u32[]{:S(2)}) async-start(bf16[32,8,128]{2,1,0:T(8,128)(2,1)} %broadcast_in_dim.15), calls=%async_computation | async-start | bytes 131072 | tf_op jit(solution)/shard_map/all_to_all | solution.py:379
  37.2 4.3 %fusion.61 = (bf16[640,1152]{1,0:T(8,128)(2,1)S(1)}, f32[640,1152]{1,0:T(8,128)}) fusion(bf16[640,576]{1,0:T(8,128)(2,1)S(1)} %pad_maximum_fusion.7, bf16[576,1152]{1,0:T(8,128)(2,1)} %all-gather.6.cloned.1.call-done), kind=kOutput, calls=%fused_computation.168 | convolution fusion | flops 850083840 | bytes 6488064 | tf_op jit(solution)/shard_map/dot_general | solution.py:52
  53.1 8.3 %collective-permute-done.7 = bf16[160,1152]{1,0:T(8,128)(2,1)S(1)} collective-permute-done((bf16[160,1152]{1,0:T(8,128)(2,1)S(1)}, bf16[160,1152]{1,0:T(8,128)(2,1)S(1)}, u32[]{:S(2)}, u32[]{:S(2)}) %collective-permute-start.7) | collective-permute-done | bytes 368672 | tf_op jit(solution)/shard_map/ppermute | solution.py:334
  65.0 13.3 %all_gather.20 = bf16[1152,432]{1,0:T(8,128)(2,1)S(1)} all-gather(bf16[288,432]{1,0:T(8,128)(2,1)S(1)} %reshape.194), channel_id=1, replica_groups=mesh['dp'=4,'seq'=8] {'dp'}, dimensions={0}, use_global_device_ids=true | all-gather | bytes 1244160 | tf_op jit(solution)/shard_map/all_gather | solution.py:422
  81.8 19.9 %all-gather = bf16[8,36,1152]{2,1,0:T(8,128)(2,1)} all-gather(bf16[1,36,1152]{2,1,0:T(8,128)(2,1)S(1)} %bitcast.172), channel_id=1, replica_groups=mesh['dp'=4,'seq'=8] {'seq'}, dimensions={0}, use_global_device_ids=true | all-gather | bytes 746496 | tf_op jit(solution)/shard_map/all_gather | solution.py:425
  113.9 5.3 %convolution_convert_fusion.4.q_ref.k_ref.v_ref = bf16[1280,768]{1,0:T(8,128)(2,1)S(1)} fusion(bf16[1280,1152]{1,0:T(8,128)(2,1)} %all-gather.8.cloned.1.call-done, bf16[1152,768]{0,1:T(8,128)(2,1)} %bitcast.153), kind=kOutput, calls=%fused_computation.22 | convolution fusion | flops 2265907200 | bytes 6684672 | tf_op jit(solution)/shard_map/dot_general | solution.py:52
  119.2 8.4 %shard_map.288 = (f32[1280,256]{1,0:T(8,128)S(1)}, bf16[1280,144]{1,0:T(8,128)(2,1)S(1)}, f32[8,1280]{1,0:T(8,128)S(1)}) custom-call(bf16[1280,768]{1,0:T(8,128)(2,1)S(1)} %convolution_convert_fusion.4.q_ref.k_ref.v_ref, bf16[1280,768]{1,0:T(8,128)(2,1)S(1)} %convolution_convert_fusion.4.q_ref.k_ref.v_ref, ...), custom_call_target="tpu_custom_call" | custom-call | flops 3355443200 | bytes 3276800 | tf_op jit(solution)/shard_map/pallas_call | solution.py:93
  146.1 5.8 %all-to-all-done.2 = bf16[8,160,144]{1,2,0:T(8,128)(2,1)S(1)} async-done(((bf16[8,160,144]{1,2,0:T(8,128)(2,1)}), bf16[8,160,144]{1,2,0:T(8,128)(2,1)S(1)}, u32[]{:S(2)}, u32[]{:S(2)}) %all-to-all-start.2) | async-done | bytes 368672 | tf_op jit(solution)/shard_map/all_to_all | solution.py:358
  160.2 4.6 %convolution_convert_fusion.3.up_ref = bf16[1152,1152]{1,0:T(8,128)(2,1)S(1)} fusion(bf16[1152,1152]{1,0:T(8,128)(2,1)S(1)} %copy-done.49, s32[1152]{0:T(1024)S(1)} %get-tuple-element.241, s32[1152]{0:T(1024)S(1)} %get-tuple-element.242, s32[]{:T(128)S(6)} %axis_index.23, s32[1152]{0:T(1024)S(1)} %get-tuple-element.240, s32[1152]{0:T(1024)S(1)} %get-tuple-element.243, ...), kind=kOutput, calls=%fused_computation.11 | convolution fusion | flops 3094806528 | bytes 5329156 | tf_op jit(solution)/shard_map/dot_general | solution.py:56
  168.1 8.1 %collective-permute-done.19 = bf16[160,1152]{1,0:T(8,128)(2,1)S(1)} collective-permute-done((bf16[160,1152]{1,0:T(8,128)(2,1)S(1)}, bf16[160,1152]{1,0:T(8,128)(2,1)S(1)}, u32[]{:S(2)}, u32[]{:S(2)}) %collective-permute-start.19) | collective-permute-done | bytes 368672 | tf_op jit(solution)/shard_map/ppermute | solution.py:334
  176.3 5.6 %shard_map.289 = (bf16[640,1152]{1,0:T(8,128)(2,1)S(1)}, f32[640,1152]{1,0:T(8,128)S(1)}) custom-call(bf16[640,1152]{1,0:T(8,128)(2,1)S(1)} %pad_maximum_fusion.1.x_ref, bf16[1152,1152]{1,0:T(8,128)(2,1)S(1)} %convolution_convert_fusion.3.up_ref, f32[1,1152]{1,0:T(1,128)S(1)} %reshape_reshape.6.bias_ref), custom_call_target="tpu_custom_call" | custom-call | flops 1698693120 | bytes 8552448 | tf_op jit(solution)/shard_map/pallas_call | solution.py:253
  187.9 8.2 %shard_map.290 = (bf16[640,1152]{1,0:T(8,128)(2,1)}, f32[1,1152]{1,0:T(1,128)S(1)}, f32[160,1152]{1,0:T(8,128)S(1)}, bf16[160,1152]{1,0:T(8,128)(2,1)S(1)}, bf16...) custom-call(bf16[640,1152]{1,0:T(8,128)(2,1)} %pad_maximum_fusion.grad_ref, bf16[1152,1152]{1,0:T(8,128)(2,1)} %copy-done.2, ...), custom_call_target="tpu_custom_call" | custom-call | flops 3397386240 | bytes 12681216 | tf_op jit(solution)/shard_map/pallas_call | solution.py:291
  199.6 9.8 %convolution_convert_fusion.1 = bf16[1152,1152]{1,0:T(8,128)(2,1)} fusion(bf16[640,1152]{1,0:T(8,128)(2,1)} %get-tuple-element.123, bf16[640,1152]{1,0:T(8,128)(2,1)S(1)} %pad_maximum_fusion.1.x_ref, s32[1152]{0:T(1024)S(1)} %get-tuple-element.241, s32[1152]{0:T(1024)S(1)} %copy-done.36, s32[]{:T(128)S(6)} %axis_index.23, s32[1152]{0:T(1024)S(1)} %get-tuple-element.240, ...), kind=kOutput, calls=%fused_computation.9 | convolution fusion | flops 3435282432 | bytes 5624068 | tf_op jit(solution)/shard_map/dot_general | solution.py:56
  209.5 5.5 %collective-permute-done.22 = bf16[160,1152]{1,0:T(8,128)(2,1)} collective-permute-done((bf16[160,1152]{1,0:T(8,128)(2,1)S(1)}, bf16[160,1152]{1,0:T(8,128)(2,1)}, u32[]{:S(2)}, u32[]{:S(2)}) %collective-permute-start.22) | collective-permute-done | bytes 368672 | tf_op jit(solution)/shard_map/ppermute | solution.py:334
  223.8 4.2 %all-to-all-start.3 = ((bf16[8,160,144]{1,2,0:T(8,128)(2,1)}), bf16[8,160,144]{1,2,0:T(8,128)(2,1)}, u32[]{:S(2)}, u32[]{:S(2)}) async-start(bf16[8,160,144]{1,2,0:T(8,128)(2,1)} %copy.61), calls=%async_computation.3 | async-start | bytes 1179648 | tf_op jit(solution)/shard_map/all_to_all | solution.py:358
  228.1 5.6 %fusion.63 = (bf16[640,1152]{1,0:T(8,128)(2,1)S(1)}, f32[640,1152]{1,0:T(8,128)}) fusion(bf16[640,1152]{1,0:T(8,128)(2,1)S(1)} %copy-done.4, bf16[1152,1152]{1,0:T(8,128)(2,1)} %all-gather.12.cloned.1.call-done.down_ref), kind=kOutput, calls=%fused_computation.170 | convolution fusion | flops 1699430400 | bytes 8552448 | tf_op jit(solution)/shard_map/dot_general | solution.py:52
  239.5 12.1 %all-to-all-done.3 = bf16[8,160,144]{1,2,0:T(8,128)(2,1)} async-done(((bf16[8,160,144]{1,2,0:T(8,128)(2,1)}), bf16[8,160,144]{1,2,0:T(8,128)(2,1)}, u32[]{:S(2)}, u32[]{:S(2)}) %all-to-all-start.3) | async-done | bytes 368672 | tf_op jit(solution)/shard_map/all_to_all | solution.py:358
  254.7 14.1 %shard_map.292 = (bf16[1280,144]{1,0:T(8,128)(2,1)S(1)}, bf16[1280,288]{1,0:T(8,128)(2,1)S(1)}) custom-call(bf16[1280,768]{1,0:T(8,128)(2,1)S(1)} %copy-done.6, bf16[1280,768]{1,0:T(8,128)(2,1)S(1)} %copy-done.6, bf16[1280,768]{1,0:T(8,128)(2,1)S(1)} %copy-done.6, bf16[1280,144]{1,0:T(8,128)(2,1)S(1)} %bitcast.145, f32[1280,256]{1,0:T(8,128)S(1)} %copy-done.8, ...), custom_call_target="tpu_custom_call" | custom-call | flops 8388608000 | bytes 4587520 | tf_op jit(solution)/shard_map/pallas_call | solution.py:171
  289.9 6.9 %collective-permute-done.34 = bf16[160,1152]{1,0:T(8,128)(2,1)S(1)} collective-permute-done((bf16[160,1152]{1,0:T(8,128)(2,1)S(1)}, bf16[160,1152]{1,0:T(8,128)(2,1)S(1)}, u32[]{:S(2)}, u32[]{:S(2)}) %collective-permute-start.34) | collective-permute-done | bytes 368672 | tf_op jit(solution)/shard_map/ppermute | solution.py:334
  309.0 4.9 %all-to-all-start.4 = ((bf16[4,36,1152]{2,1,0:T(8,128)(2,1)}), bf16[4,36,1152]{2,1,0:T(8,128)(2,1)S(1)}, u32[]{:S(2)}, u32[]{:S(2)}) async-start(bf16[4,36,1152]{2,1,0:T(8,128)(2,1)} %fusion.27), calls=%async_computation.7 | async-start | bytes 737280 | tf_op jit(solution)/shard_map/all_to_all | solution.py:368
  324.7 5.0 %all-to-all-start.5 = ((bf16[8,36,432]{2,1,0:T(8,128)(2,1)}), bf16[8,36,432]{2,1,0:T(8,128)(2,1)}, u32[]{:S(2)}, u32[]{:S(2)}) async-start(bf16[8,36,432]{2,1,0:T(8,128)(2,1)} %reshape.202), calls=%async_computation.8 | async-start | bytes 655360 | tf_op jit(solution)/shard_map/all_to_all | solution.py:358
  330.9 4.7 %collective-permute-done.28 = bf16[160,1152]{1,0:T(8,128)(2,1)S(1)} collective-permute-done((bf16[160,1152]{1,0:T(8,128)(2,1)S(1)}, bf16[160,1152]{1,0:T(8,128)(2,1)S(1)}, u32[]{:S(2)}, u32[]{:S(2)}) %collective-permute-start.28) | collective-permute-done | bytes 368672 | tf_op jit(solution)/shard_map/ppermute | solution.py:334
  342.7 4.7 %all-to-all-start.6 = ((f32[32,8,128]{2,1,0:T(8,128)}), f32[32,8,128]{2,1,0:T(8,128)S(1)}, u32[]{:S(2)}, u32[]{:S(2)}) async-start(f32[32,8,128]{2,1,0:T(8,128)} %bitcast.66), calls=%async_computation.9 | async-start | bytes 262144 | tf_op jit(solution)/shard_map/all_to_all | solution.py:550
  364.9 6.8 %collective-permute-done.41 = bf16[160,576]{0,1:T(8,128)(2,1)} collective-permute-done((bf16[160,576]{0,1:T(8,128)(2,1)}, bf16[160,576]{0,1:T(8,128)(2,1)}, u32[]{:S(2)}, u32[]{:S(2)}) %collective-permute-start.41) | collective-permute-done | bytes 184352 | tf_op jit(solution)/shard_map/ppermute | solution.py:334
  (352 shorter events, 189.8 us)
Async XLA Ops:
  7.2 30.0 %all-gather.6.cloned.1.call-start = ((), (), s32[]{:S(2)}) async-start(), calls=%async_computation.11 | async-start | bytes 1492992 | tf_op jit(solution)/shard_map/all_gather | solution.py:371
  9.7 22.1 %collective-permute-start = (bf16[160,576]{1,0:T(8,128)(2,1)S(1)}, bf16[160,576]{1,0:T(8,128)(2,1)S(1)}, u32[]{:S(2)}, u32[]{:S(2)}) collective-permute-start(bf16[160,576]{1,0:T(8,128)(2,1)S(1)} %get-tuple-element.190), channel_id=1, source_target_pairs={{0,8},{8,0},{16,24},{24,16},{1,9},{9,1},{17,25},{25,17},{2,10},{10... | collective-permute-start | bytes 552968 | tf_op jit(solution)/shard_map/ppermute | solution.py:334
  12.8 19.1 %collective-permute-start.1 = (bf16[160,576]{1,0:T(8,128)(2,1)S(1)}, bf16[160,576]{1,0:T(8,128)(2,1)S(1)}, u32[]{:S(2)}, u32[]{:S(2)}) collective-permute-start(bf16[160,576]{1,0:T(8,128)(2,1)S(1)} %get-tuple-element.189), channel_id=1, source_target_pairs={{0,16},{8,24},{16,0},{24,8},{1,17},{9,25},{17,1},{25,9},{2,18},{10... | collective-permute-start | bytes 552968 | tf_op jit(solution)/shard_map/ppermute | solution.py:334
  49.8 64.1 %all-gather.8.cloned.1.call-start = ((), (), s32[]{:S(2)}) async-start(), calls=%async_computation.12 | async-start | bytes 3317760 | tf_op jit(solution)/shard_map/all_gather | solution.py:420
  64.2 88.0 %all-gather.10.cloned.1.call-start = ((), (), s32[]{:S(2)}) async-start(), calls=%async_computation.13 | async-start | bytes 2985984 | tf_op jit(solution)/shard_map/all_gather | solution.py:432
  78.2 31.6 %collective-permute-start.10 = (bf16[160,1152]{1,0:T(8,128)(2,1)S(1)}, bf16[160,1152]{1,0:T(8,128)(2,1)}, u32[]{:S(2)}, u32[]{:S(2)}) collective-permute-start(bf16[160,1152]{1,0:T(8,128)(2,1)S(1)} %bitcast.154), channel_id=1, source_target_pairs={{0,16},{8,24},{16,0},{24,8},{1,17},{9,25},{17,1},{25,9},{2,18},{10... | collective-permute-start | bytes 1105928 | tf_op jit(solution)/shard_map/ppermute | solution.py:334
  79.3 32.1 %collective-permute-start.11 = (bf16[160,1152]{1,0:T(8,128)(2,1)S(1)}, bf16[160,1152]{1,0:T(8,128)(2,1)}, u32[]{:S(2)}, u32[]{:S(2)}) collective-permute-start(bf16[160,1152]{1,0:T(8,128)(2,1)S(1)} %bitcast.155), channel_id=1, source_target_pairs={{0,24},{8,16},{16,8},{24,0},{1,25},{9,17},{17,9},{25,1},{2,26},{10... | collective-permute-start | bytes 1105928 | tf_op jit(solution)/shard_map/ppermute | solution.py:334
  80.8 30.6 %collective-permute-start.9 = (bf16[160,1152]{1,0:T(8,128)(2,1)S(1)}, bf16[160,1152]{1,0:T(8,128)(2,1)}, u32[]{:S(2)}, u32[]{:S(2)}) collective-permute-start(bf16[160,1152]{1,0:T(8,128)(2,1)S(1)} %bitcast.156), channel_id=1, source_target_pairs={{0,8},{8,0},{16,24},{24,16},{1,9},{9,1},{17,25},{25,17},{2,10},{10... | collective-permute-start | bytes 1105928 | tf_op jit(solution)/shard_map/ppermute | solution.py:334
  103.7 24.9 %collective-permute-start.12 = (bf16[144,1152]{1,0:T(8,128)(2,1)}, bf16[144,1152]{1,0:T(8,128)(2,1)}, u32[]{:S(2)}, u32[]{:S(2)}) collective-permute-start(bf16[144,1152]{1,0:T(8,128)(2,1)} %constant_dynamic-slice_fusion.5), channel_id=1, source_target_pairs={{0,8},{8,0},{16,24},{24,16},{1,9},{9,1},{17,25},{25,17},{2,10},{10... | collective-permute-start | bytes 995336 | tf_op jit(solution)/shard_map/ppermute | solution.py:334
  104.6 24.0 %collective-permute-start.13 = (bf16[144,1152]{1,0:T(8,128)(2,1)}, bf16[144,1152]{1,0:T(8,128)(2,1)}, u32[]{:S(2)}, u32[]{:S(2)}) collective-permute-start(bf16[144,1152]{1,0:T(8,128)(2,1)} %constant_dynamic-slice_fusion.5), channel_id=1, source_target_pairs={{0,16},{8,24},{16,0},{24,8},{1,17},{9,25},{17,1},{25,9},{2,18},{10... | collective-permute-start | bytes 995336 | tf_op jit(solution)/shard_map/ppermute | solution.py:334
  130.5 21.4 %all-to-all-start.2 = ((bf16[8,160,144]{1,2,0:T(8,128)(2,1)}), bf16[8,160,144]{1,2,0:T(8,128)(2,1)S(1)}, u32[]{:S(2)}, u32[]{:S(2)}) async-start(bf16[8,160,144]{1,2,0:T(8,128)(2,1)} %copy.59), calls=%async_computation.2 | async-start | bytes 1179648 | tf_op jit(solution)/shard_map/all_to_all | solution.py:358
  134.0 53.8 %all-gather.12.cloned.1.call-start = ((), (), s32[]{:S(2)}) async-start(), calls=%async_computation.14 | async-start | bytes 2985984 | tf_op jit(solution)/shard_map/all_gather | solution.py:453
  152.2 121.5 %reduce-scatter.9.cloned.1.call-start = ((), (), s32[]{:S(2)}) async-start(), calls=%async_computation.16 | async-start | bytes 2985984 | tf_op jit(solution)/shard_map/reduce_scatter | solution.py:464
  187.6 86.2 %reduce-scatter.7.cloned.1.call-start = ((), (), s32[]{:S(2)}) async-start(), calls=%async_computation.15 | async-start | bytes 2985984 | tf_op jit(solution)/shard_map/reduce_scatter | solution.py:481
  223.8 27.9 %all-to-all-start.3 = ((bf16[8,160,144]{1,2,0:T(8,128)(2,1)}), bf16[8,160,144]{1,2,0:T(8,128)(2,1)}, u32[]{:S(2)}, u32[]{:S(2)}) async-start(bf16[8,160,144]{1,2,0:T(8,128)(2,1)} %copy.61), calls=%async_computation.3 | async-start | bytes 1179648 | tf_op jit(solution)/shard_map/all_to_all | solution.py:358
  228.0 85.8 %reduce-scatter.11.cloned.1.call-start = ((), (), s32[]{:S(2)}) async-start(), calls=%async_computation.17 | async-start | bytes 3317760 | tf_op jit(solution)/shard_map/reduce_scatter | solution.py:501
  236.4 37.3 %collective-permute-start.25 = (bf16[160,1152]{1,0:T(8,128)(2,1)}, bf16[160,1152]{1,0:T(8,128)(2,1)S(1)}, u32[]{:S(2)}, u32[]{:S(2)}) collective-permute-start(bf16[160,1152]{1,0:T(8,128)(2,1)} %get-tuple-element.175), channel_id=1, source_target_pairs={{0,16},{8,24},{16,0},{24,8},{1,17},{9,25},{17,1},{25,9},{2,18},{10... | collective-permute-start | bytes 1105928 | tf_op jit(solution)/shard_map/ppermute | solution.py:334
  237.8 35.9 %collective-permute-start.26 = (bf16[160,1152]{1,0:T(8,128)(2,1)}, bf16[160,1152]{1,0:T(8,128)(2,1)}, u32[]{:S(2)}, u32[]{:S(2)}) collective-permute-start(bf16[160,1152]{1,0:T(8,128)(2,1)} %get-tuple-element.174), channel_id=1, source_target_pairs={{0,24},{8,16},{16,8},{24,0},{1,25},{9,17},{17,9},{25,1},{2,26},{10... | collective-permute-start | bytes 1105928 | tf_op jit(solution)/shard_map/ppermute | solution.py:334
  274.8 22.1 %collective-permute-start.30 = (bf16[160,288]{1,0:T(8,128)(2,1)S(1)}, bf16[160,288]{1,0:T(8,128)(2,1)S(1)}, u32[]{:S(2)}, u32[]{:S(2)}) collective-permute-start(bf16[160,288]{1,0:T(8,128)(2,1)S(1)} %get-tuple-element.198), channel_id=1, source_target_pairs={{0,8},{8,0},{16,24},{24,16},{1,9},{9,1},{17,25},{25,17},{2,10},{10... | collective-permute-start | bytes 276488 | tf_op jit(solution)/shard_map/ppermute | solution.py:334
  274.8 22.0 %collective-permute-start.31 = (bf16[160,288]{1,0:T(8,128)(2,1)S(1)}, bf16[160,288]{1,0:T(8,128)(2,1)S(1)}, u32[]{:S(2)}, u32[]{:S(2)}) collective-permute-start(bf16[160,288]{1,0:T(8,128)(2,1)S(1)} %get-tuple-element.197), channel_id=1, source_target_pairs={{0,16},{8,24},{16,0},{24,8},{1,17},{9,25},{17,1},{25,9},{2,18},{10... | collective-permute-start | bytes 276488 | tf_op jit(solution)/shard_map/ppermute | solution.py:334
  276.9 19.9 %collective-permute-start.34 = (bf16[160,1152]{1,0:T(8,128)(2,1)S(1)}, bf16[160,1152]{1,0:T(8,128)(2,1)S(1)}, u32[]{:S(2)}, u32[]{:S(2)}) collective-permute-start(bf16[160,1152]{1,0:T(8,128)(2,1)S(1)} %copy-done.20), channel_id=1, source_target_pairs={{0,16},{8,24},{16,0},{24,8},{1,17},{9,25},{17,1},{25,9},{2,18},{10... | collective-permute-start | bytes 1105928 | tf_op jit(solution)/shard_map/ppermute | solution.py:334
  318.6 19.1 %collective-permute-start.29 = (bf16[160,1152]{1,0:T(8,128)(2,1)S(1)}, bf16[160,1152]{1,0:T(8,128)(2,1)}, u32[]{:S(2)}, u32[]{:S(2)}) collective-permute-start(bf16[160,1152]{1,0:T(8,128)(2,1)S(1)} %get-tuple-element.168), channel_id=1, source_target_pairs={{0,24},{8,16},{16,8},{24,0},{1,25},{9,17},{17,9},{25,1},{2,26},{10... | collective-permute-start | bytes 1105928 | tf_op jit(solution)/shard_map/ppermute | solution.py:334
  329.7 47.2 %reduce-scatter.13.cloned.1.call-start = ((), (), s32[]{:S(2)}) async-start(), calls=%async_computation.18 | async-start | bytes 1492992
  342.7 32.9 %all-to-all-start.6 = ((f32[32,8,128]{2,1,0:T(8,128)}), f32[32,8,128]{2,1,0:T(8,128)S(1)}, u32[]{:S(2)}, u32[]{:S(2)}) async-start(f32[32,8,128]{2,1,0:T(8,128)} %bitcast.66), calls=%async_computation.9 | async-start | bytes 262144 | tf_op jit(solution)/shard_map/all_to_all | solution.py:550
  (87 other events, 997.7 us)
Sparse Core Ops, SparseCore 0:
  9.7 27.5 all-gather.5
  64.3 41.0 all-gather.7
  107.6 33.9 all-gather.9
  152.3 32.9 all-gather.11
  187.7 36.5 reduce-scatter.8
  226.5 43.6 reduce-scatter.6
  273.9 36.5 reduce-scatter.10
  341.6 34.5 reduce-scatter.12

commit v18 on v17

--- a/solution.py
+++ b/solution.py
@@ -420,14 +420,13 @@
     normed_one_row = lax.all_gather(normed_one, "seq", axis=0, tiled=True)
 
     qkv_mine = lax.all_gather(qkv_mine, "dp", axis=0, tiled=True)
-    qkv_mine, own_proj, grad_out = after((qkv_mine, own_proj, cotangent[0]))
-    grad_out_rows = gather_rows(grad_out)
+    qkv_mine, own_proj = after((qkv_mine, own_proj))
     proj_rows = lax.all_gather(own_proj, "seq", axis=0, tiled=True)
     half = part // 2
     own_half = lax.dynamic_slice_in_dim(proj_rows, core * half, half, 0)
     proj_halves = [swap(own_half, k) for k in range(1, nd)]
-    normed_one_row, qkv_mine, qkv_wide, proj_rows, grad_out_rows = after(
-        (normed_one_row, qkv_mine, widen(qkv_mine), proj_rows, grad_out_rows)
+    normed_one_row, qkv_mine, qkv_wide, proj_rows = after(
+        (normed_one_row, qkv_mine, widen(qkv_mine), proj_rows)
     )
     up_part = lax.all_gather(up_slices, "seq", axis=0, tiled=True)
     triple = dot(normed_one_row, qkv_wide).astype(BF16)
@@ -437,7 +436,9 @@
         v = seq_exchange(v.reshape(ns, local, head_cols))
         return jnp.swapaxes(v, 0, 1).reshape(local, features)
 
-    attended_low, proj_halves, proj_rows = after((attended_low, proj_halves, proj_rows))
+    attended_low, grad_out, proj_halves, proj_rows = after(
+        (attended_low, cotangent[0], proj_halves, proj_rows)
+    )
     w_proj = lax.dynamic_update_slice_in_dim(
         jnp.zeros((features, features), BF16), proj_rows, dp_at * part, 0
     )
@@ -447,6 +448,7 @@
         there = other_core(here)
         w_proj = lax.dynamic_update_slice_in_dim(w_proj, here, (place + core) * half, 0)
         w_proj = lax.dynamic_update_slice_in_dim(w_proj, there, (place + 1 - core) * half, 0)
+    grad_out_rows = gather_rows(grad_out)
     attended_low = heads_to_tokens(attended_low)
     attended_low, grad_out_rows, w_proj = after((attended_low, grad_out_rows, w_proj))
     own_down, attended_low, up_part = after((fc2_w, attended_low, up_part))

time: 392 us -> 392 us (level)
  no operation moved by 1% of the time
where the time goes in v18:
time: 392 us; the launch traced here: 385 us
  starting transfers between devices  84.1 us (21%)
  waiting for transfers between devices  81.7 us (21%)
  local copies, waits for them, and re-layouts  53.7 us (14%)
  matrix products  50.1 us (13%)
  Pallas kernels  39.8 us (10%)
  blocking collectives  33.1 us (8%)
  other arithmetic  27.1 us (7%)
  between operations  15.7 us (4%)
    ppermute x42, waiting for transfers between devices, swap(): return lax.ppermute(v, 'dp', [(i, i ^ k) for i in range(nd)])  55.2 us
    ppermute x42, starting transfers between devices, swap(): return lax.ppermute(v, 'dp', [(i, i ^ k) for i in range(nd)])  52 us
    dot_general x6, matrix products, inner(): lax.dot_general(left, right, (((0,), (0,)), ((), ())), preferred_element_...  26.2 us
    all_gather x1, blocking collectives, on_device(): proj_rows = lax.all_gather(own_proj, 'seq', axis=0, tiled=True)  19.8 us
    dot_general x4, matrix products, dot(): return jnp.dot(left, right, preferred_element_type=F32)  17.7 us
    all_to_all x4, waiting for transfers between devices, seq_exchange(): return lax.all_to_all(v, 'seq', 0, 0, tiled=True)  17.7 us
    all_to_all x4, starting transfers between devices, seq_exchange(): return lax.all_to_all(v, 'seq', 0, 0, tiled=True)  16.2 us
    pallas_call x1, Pallas kernels, attend_back(): pl.pallas_call(partial(attend_back_kernel, heads, scale), grid=(rows // s...  14.1 us
  transfers between devices with their start and end apart: 61, of which 18 were waited for; matrix products, arithmetic and copies ran while one was open for 30% of the time, Pallas kernels for 10%

profile of v18, /device:TPU:0, one launch (start us, length us, event | category | flops | bytes accessed | tf_op | source)
XLA Modules:
  0.0 385.3 jit_solution(14832233713682912500)
XLA Ops:
  19.6 4.0 %all-to-all-start = ((bf16[32,8,128]{2,1,0:T(8,128)(2,1)}), bf16[32,8,128]{2,1,0:T(8,128)(2,1)S(1)}, u32[]{:S(2)}, u32[]{:S(2)}) async-start(bf16[32,8,128]{2,1,0:T(8,128)(2,1)} %broadcast_in_dim.15), calls=%async_computation | async-start | bytes 131072 | tf_op jit(solution)/shard_map/all_to_all | solution.py:379
  37.2 4.3 %fusion.61 = (bf16[640,1152]{1,0:T(8,128)(2,1)S(1)}, f32[640,1152]{1,0:T(8,128)}) fusion(bf16[640,576]{1,0:T(8,128)(2,1)S(1)} %pad_maximum_fusion.7, bf16[576,1152]{1,0:T(8,128)(2,1)} %all-gather.6.cloned.1.call-done), kind=kOutput, calls=%fused_computation.168 | convolution fusion | flops 850083840 | bytes 6488064 | tf_op jit(solution)/shard_map/dot_general | solution.py:52
  53.1 8.3 %collective-permute-done.7 = bf16[160,1152]{1,0:T(8,128)(2,1)S(1)} collective-permute-done((bf16[160,1152]{1,0:T(8,128)(2,1)S(1)}, bf16[160,1152]{1,0:T(8,128)(2,1)S(1)}, u32[]{:S(2)}, u32[]{:S(2)}) %collective-permute-start.7) | collective-permute-done | bytes 368672 | tf_op jit(solution)/shard_map/ppermute | solution.py:334
  65.0 13.3 %all_gather.20 = bf16[1152,432]{1,0:T(8,128)(2,1)S(1)} all-gather(bf16[288,432]{1,0:T(8,128)(2,1)S(1)} %reshape.194), channel_id=1, replica_groups=mesh['dp'=4,'seq'=8] {'dp'}, dimensions={0}, use_global_device_ids=true | all-gather | bytes 1244160 | tf_op jit(solution)/shard_map/all_gather | solution.py:422
  78.2 19.8 %all-gather = bf16[8,36,1152]{2,1,0:T(8,128)(2,1)} all-gather(bf16[1,36,1152]{2,1,0:T(8,128)(2,1)S(1)} %bitcast.172), channel_id=1, replica_groups=mesh['dp'=4,'seq'=8] {'seq'}, dimensions={0}, use_global_device_ids=true | all-gather | bytes 746496 | tf_op jit(solution)/shard_map/all_gather | solution.py:424
  107.7 5.1 %convolution_convert_fusion.4.q_ref.k_ref.v_ref = bf16[1280,768]{1,0:T(8,128)(2,1)S(1)} fusion(bf16[1280,1152]{1,0:T(8,128)(2,1)} %all-gather.8.cloned.1.call-done, bf16[1152,768]{0,1:T(8,128)(2,1)} %bitcast.153), kind=kOutput, calls=%fused_computation.22 | convolution fusion | flops 2265907200 | bytes 6684672 | tf_op jit(solution)/shard_map/dot_general | solution.py:52
  112.9 8.4 %shard_map.288 = (f32[1280,256]{1,0:T(8,128)S(1)}, bf16[1280,144]{1,0:T(8,128)(2,1)S(1)}, f32[8,1280]{1,0:T(8,128)S(1)}) custom-call(bf16[1280,768]{1,0:T(8,128)(2,1)S(1)} %convolution_convert_fusion.4.q_ref.k_ref.v_ref, bf16[1280,768]{1,0:T(8,128)(2,1)S(1)} %convolution_convert_fusion.4.q_ref.k_ref.v_ref, ...), custom_call_target="tpu_custom_call" | custom-call | flops 3355443200 | bytes 3276800 | tf_op jit(solution)/shard_map/pallas_call | solution.py:93
  146.1 5.8 %all-to-all-done.2 = bf16[8,160,144]{1,2,0:T(8,128)(2,1)S(1)} async-done(((bf16[8,160,144]{1,2,0:T(8,128)(2,1)}), bf16[8,160,144]{1,2,0:T(8,128)(2,1)S(1)}, u32[]{:S(2)}, u32[]{:S(2)}) %all-to-all-start.2) | async-done | bytes 368672 | tf_op jit(solution)/shard_map/all_to_all | solution.py:358
  160.1 4.6 %convolution_convert_fusion.3.up_ref = bf16[1152,1152]{1,0:T(8,128)(2,1)S(1)} fusion(bf16[1152,1152]{1,0:T(8,128)(2,1)S(1)} %copy-done.49, s32[1152]{0:T(1024)S(1)} %get-tuple-element.239, s32[1152]{0:T(1024)S(1)} %get-tuple-element.240, s32[]{:T(128)S(6)} %axis_index.23, s32[1152]{0:T(1024)S(1)} %get-tuple-element.238, s32[1152]{0:T(1024)S(1)} %get-tuple-element.241, ...), kind=kOutput, calls=%fused_computation.11 | convolution fusion | flops 3094806528 | bytes 5329156 | tf_op jit(solution)/shard_map/dot_general | solution.py:56
  168.1 8.2 %collective-permute-done.19 = bf16[160,1152]{1,0:T(8,128)(2,1)S(1)} collective-permute-done((bf16[160,1152]{1,0:T(8,128)(2,1)S(1)}, bf16[160,1152]{1,0:T(8,128)(2,1)S(1)}, u32[]{:S(2)}, u32[]{:S(2)}) %collective-permute-start.19) | collective-permute-done | bytes 368672 | tf_op jit(solution)/shard_map/ppermute | solution.py:334
  176.4 5.6 %shard_map.289 = (bf16[640,1152]{1,0:T(8,128)(2,1)S(1)}, f32[640,1152]{1,0:T(8,128)S(1)}) custom-call(bf16[640,1152]{1,0:T(8,128)(2,1)S(1)} %pad_maximum_fusion.1.x_ref, bf16[1152,1152]{1,0:T(8,128)(2,1)S(1)} %convolution_convert_fusion.3.up_ref, f32[1,1152]{1,0:T(1,128)S(1)} %reshape_reshape.6.bias_ref), custom_call_target="tpu_custom_call" | custom-call | flops 1698693120 | bytes 8552448 | tf_op jit(solution)/shard_map/pallas_call | solution.py:253
  188.0 8.2 %shard_map.290 = (bf16[640,1152]{1,0:T(8,128)(2,1)}, f32[1,1152]{1,0:T(1,128)S(1)}, f32[160,1152]{1,0:T(8,128)S(1)}, bf16[160,1152]{1,0:T(8,128)(2,1)S(1)}, bf16...) custom-call(bf16[640,1152]{1,0:T(8,128)(2,1)} %pad_maximum_fusion.grad_ref, bf16[1152,1152]{1,0:T(8,128)(2,1)} %copy-done.2, ...), custom_call_target="tpu_custom_call" | custom-call | flops 3397386240 | bytes 12681216 | tf_op jit(solution)/shard_map/pallas_call | solution.py:291
  199.7 9.8 %convolution_convert_fusion.1 = bf16[1152,1152]{1,0:T(8,128)(2,1)} fusion(bf16[640,1152]{1,0:T(8,128)(2,1)} %get-tuple-element.121, bf16[640,1152]{1,0:T(8,128)(2,1)S(1)} %pad_maximum_fusion.1.x_ref, s32[1152]{0:T(1024)S(1)} %get-tuple-element.239, s32[1152]{0:T(1024)S(1)} %copy-done.36, s32[]{:T(128)S(6)} %axis_index.23, s32[1152]{0:T(1024)S(1)} %get-tuple-element.238, ...), kind=kOutput, calls=%fused_computation.9 | convolution fusion | flops 3435282432 | bytes 5624068 | tf_op jit(solution)/shard_map/dot_general | solution.py:56
  209.6 5.2 %collective-permute-done.22 = bf16[160,1152]{1,0:T(8,128)(2,1)} collective-permute-done((bf16[160,1152]{1,0:T(8,128)(2,1)S(1)}, bf16[160,1152]{1,0:T(8,128)(2,1)}, u32[]{:S(2)}, u32[]{:S(2)}) %collective-permute-start.22) | collective-permute-done | bytes 368672 | tf_op jit(solution)/shard_map/ppermute | solution.py:334
  223.6 4.2 %all-to-all-start.3 = ((bf16[8,160,144]{1,2,0:T(8,128)(2,1)}), bf16[8,160,144]{1,2,0:T(8,128)(2,1)}, u32[]{:S(2)}, u32[]{:S(2)}) async-start(bf16[8,160,144]{1,2,0:T(8,128)(2,1)} %copy.61), calls=%async_computation.3 | async-start | bytes 1179648 | tf_op jit(solution)/shard_map/all_to_all | solution.py:358
  227.9 5.6 %fusion.63 = (bf16[640,1152]{1,0:T(8,128)(2,1)S(1)}, f32[640,1152]{1,0:T(8,128)}) fusion(bf16[640,1152]{1,0:T(8,128)(2,1)S(1)} %copy-done.4, bf16[1152,1152]{1,0:T(8,128)(2,1)} %all-gather.12.cloned.1.call-done.down_ref), kind=kOutput, calls=%fused_computation.170 | convolution fusion | flops 1699430400 | bytes 8552448 | tf_op jit(solution)/shard_map/dot_general | solution.py:52
  239.3 11.9 %all-to-all-done.3 = bf16[8,160,144]{1,2,0:T(8,128)(2,1)} async-done(((bf16[8,160,144]{1,2,0:T(8,128)(2,1)}), bf16[8,160,144]{1,2,0:T(8,128)(2,1)}, u32[]{:S(2)}, u32[]{:S(2)}) %all-to-all-start.3) | async-done | bytes 368672 | tf_op jit(solution)/shard_map/all_to_all | solution.py:358
  254.2 14.1 %shard_map.292 = (bf16[1280,144]{1,0:T(8,128)(2,1)S(1)}, bf16[1280,288]{1,0:T(8,128)(2,1)S(1)}) custom-call(bf16[1280,768]{1,0:T(8,128)(2,1)S(1)} %copy-done.6, bf16[1280,768]{1,0:T(8,128)(2,1)S(1)} %copy-done.6, bf16[1280,768]{1,0:T(8,128)(2,1)S(1)} %copy-done.6, bf16[1280,144]{1,0:T(8,128)(2,1)S(1)} %bitcast.145, f32[1280,256]{1,0:T(8,128)S(1)} %copy-done.8, ...), custom_call_target="tpu_custom_call" | custom-call | flops 8388608000 | bytes 4587520 | tf_op jit(solution)/shard_map/pallas_call | solution.py:171
  289.4 7.1 %collective-permute-done.34 = bf16[160,1152]{1,0:T(8,128)(2,1)S(1)} collective-permute-done((bf16[160,1152]{1,0:T(8,128)(2,1)S(1)}, bf16[160,1152]{1,0:T(8,128)(2,1)S(1)}, u32[]{:S(2)}, u32[]{:S(2)}) %collective-permute-start.34) | collective-permute-done | bytes 368672 | tf_op jit(solution)/shard_map/ppermute | solution.py:334
  308.7 4.9 %all-to-all-start.4 = ((bf16[4,36,1152]{2,1,0:T(8,128)(2,1)}), bf16[4,36,1152]{2,1,0:T(8,128)(2,1)S(1)}, u32[]{:S(2)}, u32[]{:S(2)}) async-start(bf16[4,36,1152]{2,1,0:T(8,128)(2,1)} %fusion.27), calls=%async_computation.7 | async-start | bytes 737280 | tf_op jit(solution)/shard_map/all_to_all | solution.py:368
  324.4 5.0 %all-to-all-start.5 = ((bf16[8,36,432]{2,1,0:T(8,128)(2,1)}), bf16[8,36,432]{2,1,0:T(8,128)(2,1)}, u32[]{:S(2)}, u32[]{:S(2)}) async-start(bf16[8,36,432]{2,1,0:T(8,128)(2,1)} %reshape.202), calls=%async_computation.8 | async-start | bytes 655360 | tf_op jit(solution)/shard_map/all_to_all | solution.py:358
  332.1 5.1 %collective-permute-done.29 = bf16[160,1152]{1,0:T(8,128)(2,1)} collective-permute-done((bf16[160,1152]{1,0:T(8,128)(2,1)S(1)}, bf16[160,1152]{1,0:T(8,128)(2,1)}, u32[]{:S(2)}, u32[]{:S(2)}) %collective-permute-start.29) | collective-permute-done | bytes 368672 | tf_op jit(solution)/shard_map/ppermute | solution.py:334
  342.2 4.9 %all-to-all-start.6 = ((f32[32,8,128]{2,1,0:T(8,128)}), f32[32,8,128]{2,1,0:T(8,128)S(1)}, u32[]{:S(2)}, u32[]{:S(2)}) async-start(f32[32,8,128]{2,1,0:T(8,128)} %bitcast.66), calls=%async_computation.9 | async-start | bytes 262144 | tf_op jit(solution)/shard_map/all_to_all | solution.py:552
  364.6 6.8 %collective-permute-done.41 = bf16[160,576]{0,1:T(8,128)(2,1)} collective-permute-done((bf16[160,576]{0,1:T(8,128)(2,1)}, bf16[160,576]{0,1:T(8,128)(2,1)}, u32[]{:S(2)}, u32[]{:S(2)}) %collective-permute-start.41) | collective-permute-done | bytes 184352 | tf_op jit(solution)/shard_map/ppermute | solution.py:334
  (352 shorter events, 189.5 us)
Async XLA Ops:
  7.2 30.0 %all-gather.6.cloned.1.call-start = ((), (), s32[]{:S(2)}) async-start(), calls=%async_computation.11 | async-start | bytes 1492992 | tf_op jit(solution)/shard_map/all_gather | solution.py:371
  9.7 22.1 %collective-permute-start = (bf16[160,576]{1,0:T(8,128)(2,1)S(1)}, bf16[160,576]{1,0:T(8,128)(2,1)S(1)}, u32[]{:S(2)}, u32[]{:S(2)}) collective-permute-start(bf16[160,576]{1,0:T(8,128)(2,1)S(1)} %get-tuple-element.188), channel_id=1, source_target_pairs={{0,8},{8,0},{16,24},{24,16},{1,9},{9,1},{17,25},{25,17},{2,10},{10... | collective-permute-start | bytes 552968 | tf_op jit(solution)/shard_map/ppermute | solution.py:334
  12.8 19.1 %collective-permute-start.1 = (bf16[160,576]{1,0:T(8,128)(2,1)S(1)}, bf16[160,576]{1,0:T(8,128)(2,1)S(1)}, u32[]{:S(2)}, u32[]{:S(2)}) collective-permute-start(bf16[160,576]{1,0:T(8,128)(2,1)S(1)} %get-tuple-element.187), channel_id=1, source_target_pairs={{0,16},{8,24},{16,0},{24,8},{1,17},{9,25},{17,1},{25,9},{2,18},{10... | collective-permute-start | bytes 552968 | tf_op jit(solution)/shard_map/ppermute | solution.py:334
  49.8 57.9 %all-gather.8.cloned.1.call-start = ((), (), s32[]{:S(2)}) async-start(), calls=%async_computation.12 | async-start | bytes 3317760 | tf_op jit(solution)/shard_map/all_gather | solution.py:420
  64.2 88.0 %all-gather.10.cloned.1.call-start = ((), (), s32[]{:S(2)}) async-start(), calls=%async_computation.13 | async-start | bytes 2985984 | tf_op jit(solution)/shard_map/all_gather | solution.py:431
  100.0 22.3 %collective-permute-start.10 = (bf16[144,1152]{1,0:T(8,128)(2,1)}, bf16[144,1152]{1,0:T(8,128)(2,1)}, u32[]{:S(2)}, u32[]{:S(2)}) collective-permute-start(bf16[144,1152]{1,0:T(8,128)(2,1)} %constant_dynamic-slice_fusion.5), channel_id=1, source_target_pairs={{0,16},{8,24},{16,0},{24,8},{1,17},{9,25},{17,1},{25,9},{2,18},{10... | collective-permute-start | bytes 995336 | tf_op jit(solution)/shard_map/ppermute | solution.py:334
  101.1 21.2 %collective-permute-start.11 = (bf16[144,1152]{1,0:T(8,128)(2,1)}, bf16[144,1152]{1,0:T(8,128)(2,1)}, u32[]{:S(2)}, u32[]{:S(2)}) collective-permute-start(bf16[144,1152]{1,0:T(8,128)(2,1)} %constant_dynamic-slice_fusion.5), channel_id=1, source_target_pairs={{0,24},{8,16},{16,8},{24,0},{1,25},{9,17},{17,9},{25,1},{2,26},{10... | collective-permute-start | bytes 995336 | tf_op jit(solution)/shard_map/ppermute | solution.py:334
  102.6 19.7 %collective-permute-start.9 = (bf16[144,1152]{1,0:T(8,128)(2,1)}, bf16[144,1152]{1,0:T(8,128)(2,1)}, u32[]{:S(2)}, u32[]{:S(2)}) collective-permute-start(bf16[144,1152]{1,0:T(8,128)(2,1)} %constant_dynamic-slice_fusion.5), channel_id=1, source_target_pairs={{0,8},{8,0},{16,24},{24,16},{1,9},{9,1},{17,25},{25,17},{2,10},{10... | collective-permute-start | bytes 995336 | tf_op jit(solution)/shard_map/ppermute | solution.py:334
  122.3 21.3 %collective-permute-start.12 = (bf16[160,1152]{1,0:T(8,128)(2,1)S(1)}, bf16[160,1152]{1,0:T(8,128)(2,1)}, u32[]{:S(2)}, u32[]{:S(2)}) collective-permute-start(bf16[160,1152]{1,0:T(8,128)(2,1)S(1)} %bitcast.154), channel_id=1, source_target_pairs={{0,8},{8,0},{16,24},{24,16},{1,9},{9,1},{17,25},{25,17},{2,10},{10... | collective-permute-start | bytes 1105928 | tf_op jit(solution)/shard_map/ppermute | solution.py:334
  123.5 20.2 %collective-permute-start.13 = (bf16[160,1152]{1,0:T(8,128)(2,1)S(1)}, bf16[160,1152]{1,0:T(8,128)(2,1)}, u32[]{:S(2)}, u32[]{:S(2)}) collective-permute-start(bf16[160,1152]{1,0:T(8,128)(2,1)S(1)} %bitcast.155), channel_id=1, source_target_pairs={{0,16},{8,24},{16,0},{24,8},{1,17},{9,25},{17,1},{25,9},{2,18},{10... | collective-permute-start | bytes 1105928 | tf_op jit(solution)/shard_map/ppermute | solution.py:334
  124.4 19.2 %collective-permute-start.14 = (bf16[160,1152]{1,0:T(8,128)(2,1)S(1)}, bf16[160,1152]{1,0:T(8,128)(2,1)}, u32[]{:S(2)}, u32[]{:S(2)}) collective-permute-start(bf16[160,1152]{1,0:T(8,128)(2,1)S(1)} %bitcast.156), channel_id=1, source_target_pairs={{0,24},{8,16},{16,8},{24,0},{1,25},{9,17},{17,9},{25,1},{2,26},{10... | collective-permute-start | bytes 1105928 | tf_op jit(solution)/shard_map/ppermute | solution.py:334
  127.6 24.3 %all-to-all-start.2 = ((bf16[8,160,144]{1,2,0:T(8,128)(2,1)}), bf16[8,160,144]{1,2,0:T(8,128)(2,1)S(1)}, u32[]{:S(2)}, u32[]{:S(2)}) async-start(bf16[8,160,144]{1,2,0:T(8,128)(2,1)} %copy.59), calls=%async_computation.2 | async-start | bytes 1179648 | tf_op jit(solution)/shard_map/all_to_all | solution.py:358
  131.1 56.8 %all-gather.12.cloned.1.call-start = ((), (), s32[]{:S(2)}) async-start(), calls=%async_computation.14 | async-start | bytes 2985984 | tf_op jit(solution)/shard_map/all_gather | solution.py:455
  152.2 121.0 %reduce-scatter.9.cloned.1.call-start = ((), (), s32[]{:S(2)}) async-start(), calls=%async_computation.16 | async-start | bytes 2985984 | tf_op jit(solution)/shard_map/reduce_scatter | solution.py:466
  187.7 85.6 %reduce-scatter.7.cloned.1.call-start = ((), (), s32[]{:S(2)}) async-start(), calls=%async_computation.15 | async-start | bytes 2985984 | tf_op jit(solution)/shard_map/reduce_scatter | solution.py:483
  223.6 27.6 %all-to-all-start.3 = ((bf16[8,160,144]{1,2,0:T(8,128)(2,1)}), bf16[8,160,144]{1,2,0:T(8,128)(2,1)}, u32[]{:S(2)}, u32[]{:S(2)}) async-start(bf16[8,160,144]{1,2,0:T(8,128)(2,1)} %copy.61), calls=%async_computation.3 | async-start | bytes 1179648 | tf_op jit(solution)/shard_map/all_to_all | solution.py:358
  227.8 85.7 %reduce-scatter.11.cloned.1.call-start = ((), (), s32[]{:S(2)}) async-start(), calls=%async_computation.17 | async-start | bytes 3317760 | tf_op jit(solution)/shard_map/reduce_scatter | solution.py:503
  236.6 36.7 %collective-permute-start.25 = (bf16[160,1152]{1,0:T(8,128)(2,1)}, bf16[160,1152]{1,0:T(8,128)(2,1)S(1)}, u32[]{:S(2)}, u32[]{:S(2)}) collective-permute-start(bf16[160,1152]{1,0:T(8,128)(2,1)} %get-tuple-element.173), channel_id=1, source_target_pairs={{0,16},{8,24},{16,0},{24,8},{1,17},{9,25},{17,1},{25,9},{2,18},{10... | collective-permute-start | bytes 1105928 | tf_op jit(solution)/shard_map/ppermute | solution.py:334
  237.5 35.7 %collective-permute-start.26 = (bf16[160,1152]{1,0:T(8,128)(2,1)}, bf16[160,1152]{1,0:T(8,128)(2,1)}, u32[]{:S(2)}, u32[]{:S(2)}) collective-permute-start(bf16[160,1152]{1,0:T(8,128)(2,1)} %get-tuple-element.172), channel_id=1, source_target_pairs={{0,24},{8,16},{16,8},{24,0},{1,25},{9,17},{17,9},{25,1},{2,26},{10... | collective-permute-start | bytes 1105928 | tf_op jit(solution)/shard_map/ppermute | solution.py:334
  274.3 22.3 %collective-permute-start.30 = (bf16[160,288]{1,0:T(8,128)(2,1)S(1)}, bf16[160,288]{1,0:T(8,128)(2,1)S(1)}, u32[]{:S(2)}, u32[]{:S(2)}) collective-permute-start(bf16[160,288]{1,0:T(8,128)(2,1)S(1)} %get-tuple-element.196), channel_id=1, source_target_pairs={{0,8},{8,0},{16,24},{24,16},{1,9},{9,1},{17,25},{25,17},{2,10},{10... | collective-permute-start | bytes 276488 | tf_op jit(solution)/shard_map/ppermute | solution.py:334
  274.7 21.9 %collective-permute-start.31 = (bf16[160,288]{1,0:T(8,128)(2,1)S(1)}, bf16[160,288]{1,0:T(8,128)(2,1)S(1)}, u32[]{:S(2)}, u32[]{:S(2)}) collective-permute-start(bf16[160,288]{1,0:T(8,128)(2,1)S(1)} %get-tuple-element.195), channel_id=1, source_target_pairs={{0,16},{8,24},{16,0},{24,8},{1,17},{9,25},{17,1},{25,9},{2,18},{10... | collective-permute-start | bytes 276488 | tf_op jit(solution)/shard_map/ppermute | solution.py:334
  276.8 19.7 %collective-permute-start.34 = (bf16[160,1152]{1,0:T(8,128)(2,1)S(1)}, bf16[160,1152]{1,0:T(8,128)(2,1)S(1)}, u32[]{:S(2)}, u32[]{:S(2)}) collective-permute-start(bf16[160,1152]{1,0:T(8,128)(2,1)S(1)} %copy-done.20), channel_id=1, source_target_pairs={{0,16},{8,24},{16,0},{24,8},{1,17},{9,25},{17,1},{25,9},{2,18},{10... | collective-permute-start | bytes 1105928 | tf_op jit(solution)/shard_map/ppermute | solution.py:334
  329.4 47.2 %reduce-scatter.13.cloned.1.call-start = ((), (), s32[]{:S(2)}) async-start(), calls=%async_computation.18 | async-start | bytes 1492992
  342.2 33.1 %all-to-all-start.6 = ((f32[32,8,128]{2,1,0:T(8,128)}), f32[32,8,128]{2,1,0:T(8,128)S(1)}, u32[]{:S(2)}, u32[]{:S(2)}) async-start(f32[32,8,128]{2,1,0:T(8,128)} %bitcast.66), calls=%async_computation.9 | async-start | bytes 262144 | tf_op jit(solution)/shard_map/all_to_all | solution.py:552
  (87 other events, 969.3 us)
Sparse Core Ops, SparseCore 0:
  9.7 27.5 all-gather.5
  64.3 41.1 all-gather.7
  107.7 36.9 all-gather.9
  152.3 32.3 all-gather.11
  187.8 36.4 reduce-scatter.8
  226.5 43.4 reduce-scatter.6
  273.4 36.6 reduce-scatter.10
  341.1 34.8 reduce-scatter.12

commit v19 on v17

--- a/solution.py
+++ b/solution.py
@@ -12,6 +12,7 @@
 HEAD_DIM = 72
 EPSILON = 1e-05
 NEGATIVE = -1e30
+LOG2_E = math.log2(math.e)
 WIDE = 128
 F32 = jnp.float32
 BF16 = jnp.bfloat16
@@ -74,14 +75,14 @@
     outs = []
     for h in range(heads):
         at = slice(h * WIDE, (h + 1) * WIDE)
-        logits = times_transposed(q_ref[:, at], k_ref[:, at]) * scale
+        logits = times_transposed(q_ref[:, at], k_ref[:, at]) * (scale * LOG2_E)
         logits = jnp.where(allowed, logits, NEGATIVE)
         top = jnp.max(logits, axis=1, keepdims=True)
-        weights = jnp.exp(logits - top)
+        weights = jnp.exp2(logits - top)
         total = jnp.sum(weights, axis=1, keepdims=True)
         outs.append(dot(weights.astype(BF16), v_ref[:, at]) / total)
         out_ref[:, at] = outs[h]
-        logs = jnp.where(lane == h, top + jnp.log(total), logs)
+        logs = jnp.where(lane == h, top + LOG2_E * jnp.log(total), logs)
     lse_ref[...] = jnp.transpose(logs)[:8]
     low_ref[...] = side_by_side(outs).astype(BF16)
 
@@ -146,19 +147,19 @@
     for h in range(heads):
         at = slice(h * WIDE, (h + 1) * WIDE)
         queries, keys, out_grad = q_ref[:, at], k_ref[:, at], grad_ref[:, at]
-        logits = times_transposed(keys, queries) * scale - lse_ref[h : h + 1, :]
-        probs = jnp.where(allowed, jnp.exp(logits), 0.0)
+        logits = times_transposed(keys, queries) * (scale * LOG2_E) - lse_ref[h : h + 1, :]
+        probs = jnp.where(allowed, jnp.exp2(logits), 0.0)
         prob_grad = times_transposed(v_ref[:, at], out_grad)
-        logit_grad = (probs * (prob_grad - delta_ref[h : h + 1, :]) * scale).astype(BF16)
+        logit_grad = (probs * (prob_grad - delta_ref[h : h + 1, :])).astype(BF16)
         value_grads.append(dot(probs.astype(BF16), out_grad))
-        key_grads.append(dot(logit_grad, queries))
+        key_grads.append(dot(logit_grad, queries) * scale)
         sum_ref[:, at] += inner(logit_grad, keys)
     dkv_ref[...] = side_by_side(key_grads + value_grads).astype(BF16)
 
     @pl.when(step == pl.num_programs(0) - 1)
     def _():
         dq_ref[...] = side_by_side(
-            [sum_ref[:, h * WIDE : (h + 1) * WIDE] for h in range(heads)]
+            [sum_ref[:, h * WIDE : (h + 1) * WIDE] * scale for h in range(heads)]
         ).astype(BF16)
 
 
@@ -411,6 +412,7 @@
     up_bias = lax.dynamic_slice_in_dim(vectors[:, 7 * small : own_size], dp_at * ns, ns, 0)
     up_bias = up_bias.reshape(hidden_part)
 
+    up_part = lax.all_gather(up_slices, "seq", axis=0, tiled=True)
     first_terms = dot(joined_here, skip_part)
     first = add_blocks(first_terms[:local], low_rows(first_terms)) + b_skip
     qkv_mine = seq_exchange(qkv_out).reshape(part, wide)
@@ -426,10 +428,9 @@
     half = part // 2
     own_half = lax.dynamic_slice_in_dim(proj_rows, core * half, half, 0)
     proj_halves = [swap(own_half, k) for k in range(1, nd)]
-    normed_one_row, qkv_mine, qkv_wide, proj_rows, grad_out_rows = after(
-        (normed_one_row, qkv_mine, widen(qkv_mine), proj_rows, grad_out_rows)
-    )
-    up_part = lax.all_gather(up_slices, "seq", axis=0, tiled=True)
+    normed_one_row, qkv_mine, qkv_wide, proj_rows, grad_out_rows, up_part = after(
+        (normed_one_row, qkv_mine, widen(qkv_mine), proj_rows, grad_out_rows, up_part)
+    )
     triple = dot(normed_one_row, qkv_wide).astype(BF16)
     attended, attended_low, lse = attend(triple, item_lengths, heads, scale)
 

time: 392 us -> 397 us (1.013)
  waiting for transfers between devices: 83.1 us -> 89.5 us
    all_to_all x4, waiting for transfers between devices: 18 us -> 22.2 us  [seq_exchange(): return lax.all_to_all(v, 'seq', 0, 0, tiled=True)]
  transfers between devices with their start and end apart: 61 -> 61, of which waited for: 18 -> 21; matrix products, arithmetic and copies ran while one was open for 30% -> 31% of each run, Pallas kernels for 10% -> 10%
where the time goes in v19:
time: 397 us; the launch traced here: 391 us
  waiting for transfers between devices  89.5 us (23%)
  starting transfers between devices  83 us (21%)
  local copies, waits for them, and re-layouts  53 us (13%)
  matrix products  50.1 us (13%)
  Pallas kernels  38.7 us (10%)
  blocking collectives  33.6 us (8%)
  other arithmetic  27.1 us (7%)
  between operations  15.7 us (4%)
    ppermute x42, waiting for transfers between devices, swap(): return lax.ppermute(v, 'dp', [(i, i ^ k) for i in range(nd)])  55.5 us
    ppermute x42, starting transfers between devices, swap(): return lax.ppermute(v, 'dp', [(i, i ^ k) for i in range(nd)])  52.2 us
    dot_general x6, matrix products, inner(): lax.dot_general(left, right, (((0,), (0,)), ((), ())), preferred_element_...  26.2 us
    all_to_all x4, waiting for transfers between devices, seq_exchange(): return lax.all_to_all(v, 'seq', 0, 0, tiled=True)  22.2 us
    all_gather x1, blocking collectives, on_device(): proj_rows = lax.all_gather(own_proj, 'seq', axis=0, tiled=True)  20 us
    dot_general x4, matrix products, dot(): return jnp.dot(left, right, preferred_element_type=F32)  17.7 us
    all_to_all x4, starting transfers between devices, seq_exchange(): return lax.all_to_all(v, 'seq', 0, 0, tiled=True)  15.4 us
    all_gather x1, blocking collectives, on_device(): qkv_mine = lax.all_gather(qkv_mine, 'dp', axis=0, tiled=True)  13.7 us
  transfers between devices with their start and end apart: 61, of which 21 were waited for; matrix products, arithmetic and copies ran while one was open for 31% of the time, Pallas kernels for 10%

profile of v19, /device:TPU:0, one launch (start us, length us, event | category | flops | bytes accessed | tf_op | source)
XLA Modules:
  0.0 390.7 jit_solution(4513915564974112380)
XLA Ops:
  37.3 4.3 %fusion.61 = (bf16[640,1152]{1,0:T(8,128)(2,1)S(1)}, f32[640,1152]{1,0:T(8,128)}) fusion(bf16[640,576]{1,0:T(8,128)(2,1)S(1)} %pad_maximum_fusion.7, bf16[576,1152]{1,0:T(8,128)(2,1)} %all-gather.6.cloned.1.call-done), kind=kOutput, calls=%fused_computation.168 | convolution fusion | flops 850083840 | bytes 6488064 | tf_op jit(solution)/shard_map/dot_general | solution.py:53
  53.1 8.3 %collective-permute-done.7 = bf16[160,1152]{1,0:T(8,128)(2,1)S(1)} collective-permute-done((bf16[160,1152]{1,0:T(8,128)(2,1)S(1)}, bf16[160,1152]{1,0:T(8,128)(2,1)S(1)}, u32[]{:S(2)}, u32[]{:S(2)}) %collective-permute-start.7) | collective-permute-done | bytes 368672 | tf_op jit(solution)/shard_map/ppermute | solution.py:335
  64.1 6.0 %all-to-all-done.1 = bf16[8,36,432]{2,1,0:T(8,128)(2,1)S(1)} async-done(((bf16[8,36,432]{2,1,0:T(8,128)(2,1)}), bf16[8,36,432]{2,1,0:T(8,128)(2,1)S(1)}, u32[]{:S(2)}, u32[]{:S(2)}) %all-to-all-start.1) | async-done | bytes 248864 | tf_op jit(solution)/shard_map/all_to_all | solution.py:359
  70.3 13.7 %all_gather.20 = bf16[1152,432]{1,0:T(8,128)(2,1)S(1)} all-gather(bf16[288,432]{1,0:T(8,128)(2,1)S(1)} %reshape.194), channel_id=1, replica_groups=mesh['dp'=4,'seq'=8] {'dp'}, dimensions={0}, use_global_device_ids=true | all-gather | bytes 1244160 | tf_op jit(solution)/shard_map/all_gather | solution.py:424
  87.6 20.0 %all-gather = bf16[8,36,1152]{2,1,0:T(8,128)(2,1)} all-gather(bf16[1,36,1152]{2,1,0:T(8,128)(2,1)S(1)} %bitcast.172), channel_id=1, replica_groups=mesh['dp'=4,'seq'=8] {'seq'}, dimensions={0}, use_global_device_ids=true | all-gather | bytes 746496 | tf_op jit(solution)/shard_map/all_gather | solution.py:427
  123.2 5.1 %convolution_convert_fusion.4.q_ref.k_ref.v_ref = bf16[1280,768]{1,0:T(8,128)(2,1)S(1)} fusion(bf16[1280,1152]{1,0:T(8,128)(2,1)} %all-gather.8.cloned.1.call-done, bf16[1152,768]{0,1:T(8,128)(2,1)} %bitcast.153), kind=kOutput, calls=%fused_computation.22 | convolution fusion | flops 2265907200 | bytes 6684672 | tf_op jit(solution)/shard_map/dot_general | solution.py:53
  128.3 8.3 %shard_map.288 = (f32[1280,256]{1,0:T(8,128)S(1)}, bf16[1280,144]{1,0:T(8,128)(2,1)S(1)}, f32[8,1280]{1,0:T(8,128)S(1)}) custom-call(bf16[1280,768]{1,0:T(8,128)(2,1)S(1)} %convolution_convert_fusion.4.q_ref.k_ref.v_ref, bf16[1280,768]{1,0:T(8,128)(2,1)S(1)} %convolution_convert_fusion.4.q_ref.k_ref.v_ref, ...), custom_call_target="tpu_custom_call" | custom-call | flops 3355443200 | bytes 3276800 | tf_op jit(solution)/shard_map/pallas_call | solution.py:94
  155.4 4.6 %all-to-all-done.2 = bf16[8,160,144]{1,2,0:T(8,128)(2,1)S(1)} async-done(((bf16[8,160,144]{1,2,0:T(8,128)(2,1)}), bf16[8,160,144]{1,2,0:T(8,128)(2,1)S(1)}, u32[]{:S(2)}, u32[]{:S(2)}) %all-to-all-start.2) | async-done | bytes 368672 | tf_op jit(solution)/shard_map/all_to_all | solution.py:359
  168.2 4.6 %convolution_convert_fusion.3.up_ref = bf16[1152,1152]{1,0:T(8,128)(2,1)S(1)} fusion(bf16[1152,1152]{1,0:T(8,128)(2,1)S(1)} %copy-done.49, s32[1152]{0:T(1024)S(1)} %get-tuple-element.243, s32[1152]{0:T(1024)S(1)} %get-tuple-element.244, s32[]{:T(128)S(6)} %axis_index.23, s32[1152]{0:T(1024)S(1)} %get-tuple-element.242, s32[1152]{0:T(1024)S(1)} %get-tuple-element.245, ...), kind=kOutput, calls=%fused_computation.11 | convolution fusion | flops 3094806528 | bytes 5329156 | tf_op jit(solution)/shard_map/dot_general | solution.py:57
  176.2 7.8 %collective-permute-done.19 = bf16[160,1152]{1,0:T(8,128)(2,1)S(1)} collective-permute-done((bf16[160,1152]{1,0:T(8,128)(2,1)S(1)}, bf16[160,1152]{1,0:T(8,128)(2,1)S(1)}, u32[]{:S(2)}, u32[]{:S(2)}) %collective-permute-start.19) | collective-permute-done | bytes 368672 | tf_op jit(solution)/shard_map/ppermute | solution.py:335
  184.1 5.6 %shard_map.289 = (bf16[640,1152]{1,0:T(8,128)(2,1)S(1)}, f32[640,1152]{1,0:T(8,128)S(1)}) custom-call(bf16[640,1152]{1,0:T(8,128)(2,1)S(1)} %pad_maximum_fusion.1.x_ref, bf16[1152,1152]{1,0:T(8,128)(2,1)S(1)} %convolution_convert_fusion.3.up_ref, f32[1,1152]{1,0:T(1,128)S(1)} %reshape_reshape.6.bias_ref), custom_call_target="tpu_custom_call" | custom-call | flops 1698693120 | bytes 8552448 | tf_op jit(solution)/shard_map/pallas_call | solution.py:254
  195.6 8.2 %shard_map.290 = (bf16[640,1152]{1,0:T(8,128)(2,1)}, f32[1,1152]{1,0:T(1,128)S(1)}, f32[160,1152]{1,0:T(8,128)S(1)}, bf16[160,1152]{1,0:T(8,128)(2,1)S(1)}, bf16...) custom-call(bf16[640,1152]{1,0:T(8,128)(2,1)} %pad_maximum_fusion.grad_ref, bf16[1152,1152]{1,0:T(8,128)(2,1)} %copy-done.2, ...), custom_call_target="tpu_custom_call" | custom-call | flops 3397386240 | bytes 12681216 | tf_op jit(solution)/shard_map/pallas_call | solution.py:292
  207.4 9.8 %convolution_convert_fusion.1 = bf16[1152,1152]{1,0:T(8,128)(2,1)} fusion(bf16[640,1152]{1,0:T(8,128)(2,1)} %get-tuple-element.125, bf16[640,1152]{1,0:T(8,128)(2,1)S(1)} %pad_maximum_fusion.1.x_ref, s32[1152]{0:T(1024)S(1)} %get-tuple-element.243, s32[1152]{0:T(1024)S(1)} %copy-done.36, s32[]{:T(128)S(6)} %axis_index.23, s32[1152]{0:T(1024)S(1)} %get-tuple-element.242, ...), kind=kOutput, calls=%fused_computation.9 | convolution fusion | flops 3435282432 | bytes 5624068 | tf_op jit(solution)/shard_map/dot_general | solution.py:57
  217.2 4.3 %collective-permute-done.22 = bf16[160,1152]{1,0:T(8,128)(2,1)} collective-permute-done((bf16[160,1152]{1,0:T(8,128)(2,1)S(1)}, bf16[160,1152]{1,0:T(8,128)(2,1)}, u32[]{:S(2)}, u32[]{:S(2)}) %collective-permute-start.22) | collective-permute-done | bytes 368672 | tf_op jit(solution)/shard_map/ppermute | solution.py:335
  230.3 4.2 %all-to-all-start.3 = ((bf16[8,160,144]{1,2,0:T(8,128)(2,1)}), bf16[8,160,144]{1,2,0:T(8,128)(2,1)}, u32[]{:S(2)}, u32[]{:S(2)}) async-start(bf16[8,160,144]{1,2,0:T(8,128)(2,1)} %copy.61), calls=%async_computation.3 | async-start | bytes 1179648 | tf_op jit(solution)/shard_map/all_to_all | solution.py:359
  234.6 5.6 %fusion.63 = (bf16[640,1152]{1,0:T(8,128)(2,1)S(1)}, f32[640,1152]{1,0:T(8,128)}) fusion(bf16[640,1152]{1,0:T(8,128)(2,1)S(1)} %copy-done.4, bf16[1152,1152]{1,0:T(8,128)(2,1)} %all-gather.12.cloned.1.call-done.down_ref), kind=kOutput, calls=%fused_computation.170 | convolution fusion | flops 1699430400 | bytes 8552448 | tf_op jit(solution)/shard_map/dot_general | solution.py:53
  246.1 11.5 %all-to-all-done.3 = bf16[8,160,144]{1,2,0:T(8,128)(2,1)} async-done(((bf16[8,160,144]{1,2,0:T(8,128)(2,1)}), bf16[8,160,144]{1,2,0:T(8,128)(2,1)}, u32[]{:S(2)}, u32[]{:S(2)}) %all-to-all-start.3) | async-done | bytes 368672 | tf_op jit(solution)/shard_map/all_to_all | solution.py:359
  260.6 12.9 %shard_map.292 = (bf16[1280,144]{1,0:T(8,128)(2,1)S(1)}, bf16[1280,288]{1,0:T(8,128)(2,1)S(1)}) custom-call(bf16[1280,768]{1,0:T(8,128)(2,1)S(1)} %copy-done.6, bf16[1280,768]{1,0:T(8,128)(2,1)S(1)} %copy-done.6, bf16[1280,768]{1,0:T(8,128)(2,1)S(1)} %copy-done.6, bf16[1280,144]{1,0:T(8,128)(2,1)S(1)} %bitcast.145, f32[1280,256]{1,0:T(8,128)S(1)} %copy-done.8, ...), custom_call_target="tpu_custom_call" | custom-call | flops 8388608000 | bytes 4587520 | tf_op jit(solution)/shard_map/pallas_call | solution.py:172
  294.6 7.8 %collective-permute-done.34 = bf16[160,1152]{1,0:T(8,128)(2,1)S(1)} collective-permute-done((bf16[160,1152]{1,0:T(8,128)(2,1)S(1)}, bf16[160,1152]{1,0:T(8,128)(2,1)S(1)}, u32[]{:S(2)}, u32[]{:S(2)}) %collective-permute-start.34) | collective-permute-done | bytes 368672 | tf_op jit(solution)/shard_map/ppermute | solution.py:335
  314.7 4.4 %all-to-all-start.4 = ((bf16[4,36,1152]{2,1,0:T(8,128)(2,1)}), bf16[4,36,1152]{2,1,0:T(8,128)(2,1)S(1)}, u32[]{:S(2)}, u32[]{:S(2)}) async-start(bf16[4,36,1152]{2,1,0:T(8,128)(2,1)} %fusion.27), calls=%async_computation.7 | async-start | bytes 737280 | tf_op jit(solution)/shard_map/all_to_all | solution.py:369
  330.0 4.2 %all-to-all-start.5 = ((bf16[8,36,432]{2,1,0:T(8,128)(2,1)}), bf16[8,36,432]{2,1,0:T(8,128)(2,1)}, u32[]{:S(2)}, u32[]{:S(2)}) async-start(bf16[8,36,432]{2,1,0:T(8,128)(2,1)} %reshape.202), calls=%async_computation.8 | async-start | bytes 655360 | tf_op jit(solution)/shard_map/all_to_all | solution.py:359
  335.4 5.9 %collective-permute-done.28 = bf16[160,1152]{1,0:T(8,128)(2,1)S(1)} collective-permute-done((bf16[160,1152]{1,0:T(8,128)(2,1)S(1)}, bf16[160,1152]{1,0:T(8,128)(2,1)S(1)}, u32[]{:S(2)}, u32[]{:S(2)}) %collective-permute-start.28) | collective-permute-done | bytes 368672 | tf_op jit(solution)/shard_map/ppermute | solution.py:335
  347.5 4.9 %all-to-all-start.6 = ((f32[32,8,128]{2,1,0:T(8,128)}), f32[32,8,128]{2,1,0:T(8,128)S(1)}, u32[]{:S(2)}, u32[]{:S(2)}) async-start(f32[32,8,128]{2,1,0:T(8,128)} %bitcast.66), calls=%async_computation.9 | async-start | bytes 262144 | tf_op jit(solution)/shard_map/all_to_all | solution.py:551
  370.0 6.8 %collective-permute-done.41 = bf16[160,576]{0,1:T(8,128)(2,1)} collective-permute-done((bf16[160,576]{0,1:T(8,128)(2,1)}, bf16[160,576]{0,1:T(8,128)(2,1)}, u32[]{:S(2)}, u32[]{:S(2)}) %collective-permute-start.41) | collective-permute-done | bytes 184352 | tf_op jit(solution)/shard_map/ppermute | solution.py:335
  (352 shorter events, 196.0 us)
Async XLA Ops:
  7.2 30.0 %all-gather.6.cloned.1.call-start = ((), (), s32[]{:S(2)}) async-start(), calls=%async_computation.11 | async-start | bytes 1492992 | tf_op jit(solution)/shard_map/all_gather | solution.py:372
  9.7 22.1 %collective-permute-start = (bf16[160,576]{1,0:T(8,128)(2,1)S(1)}, bf16[160,576]{1,0:T(8,128)(2,1)S(1)}, u32[]{:S(2)}, u32[]{:S(2)}) collective-permute-start(bf16[160,576]{1,0:T(8,128)(2,1)S(1)} %get-tuple-element.192), channel_id=1, source_target_pairs={{0,8},{8,0},{16,24},{24,16},{1,9},{9,1},{17,25},{25,17},{2,10},{10... | collective-permute-start | bytes 552968 | tf_op jit(solution)/shard_map/ppermute | solution.py:335
  23.6 96.1 %all-gather.10.cloned.1.call-start = ((), (), s32[]{:S(2)}) async-start(), calls=%async_computation.13 | async-start | bytes 2985984 | tf_op jit(solution)/shard_map/all_gather | solution.py:415
  46.4 23.7 %all-to-all-start.1 = ((bf16[8,36,432]{2,1,0:T(8,128)(2,1)}), bf16[8,36,432]{2,1,0:T(8,128)(2,1)S(1)}, u32[]{:S(2)}, u32[]{:S(2)}) async-start(bf16[8,36,432]{2,1,0:T(8,128)(2,1)} %copy.57), calls=%async_computation.1 | async-start | bytes 655360 | tf_op jit(solution)/shard_map/all_to_all | solution.py:359
  49.8 73.3 %all-gather.8.cloned.1.call-start = ((), (), s32[]{:S(2)}) async-start(), calls=%async_computation.12 | async-start | bytes 3317760 | tf_op jit(solution)/shard_map/all_gather | solution.py:422
  84.0 31.7 %collective-permute-start.10 = (bf16[160,1152]{1,0:T(8,128)(2,1)S(1)}, bf16[160,1152]{1,0:T(8,128)(2,1)}, u32[]{:S(2)}, u32[]{:S(2)}) collective-permute-start(bf16[160,1152]{1,0:T(8,128)(2,1)S(1)} %bitcast.154), channel_id=1, source_target_pairs={{0,16},{8,24},{16,0},{24,8},{1,17},{9,25},{17,1},{25,9},{2,18},{10... | collective-permute-start | bytes 1105928 | tf_op jit(solution)/shard_map/ppermute | solution.py:335
  85.1 32.1 %collective-permute-start.11 = (bf16[160,1152]{1,0:T(8,128)(2,1)S(1)}, bf16[160,1152]{1,0:T(8,128)(2,1)}, u32[]{:S(2)}, u32[]{:S(2)}) collective-permute-start(bf16[160,1152]{1,0:T(8,128)(2,1)S(1)} %bitcast.155), channel_id=1, source_target_pairs={{0,24},{8,16},{16,8},{24,0},{1,25},{9,17},{17,9},{25,1},{2,26},{10... | collective-permute-start | bytes 1105928 | tf_op jit(solution)/shard_map/ppermute | solution.py:335
  86.6 30.6 %collective-permute-start.9 = (bf16[160,1152]{1,0:T(8,128)(2,1)S(1)}, bf16[160,1152]{1,0:T(8,128)(2,1)}, u32[]{:S(2)}, u32[]{:S(2)}) collective-permute-start(bf16[160,1152]{1,0:T(8,128)(2,1)S(1)} %bitcast.156), channel_id=1, source_target_pairs={{0,8},{8,0},{16,24},{24,16},{1,9},{9,1},{17,25},{25,17},{2,10},{10... | collective-permute-start | bytes 1105928 | tf_op jit(solution)/shard_map/ppermute | solution.py:335
  109.5 28.2 %collective-permute-start.12 = (bf16[144,1152]{1,0:T(8,128)(2,1)}, bf16[144,1152]{1,0:T(8,128)(2,1)}, u32[]{:S(2)}, u32[]{:S(2)}) collective-permute-start(bf16[144,1152]{1,0:T(8,128)(2,1)} %constant_dynamic-slice_fusion.5), channel_id=1, source_target_pairs={{0,8},{8,0},{16,24},{24,16},{1,9},{9,1},{17,25},{25,17},{2,10},{10... | collective-permute-start | bytes 995336 | tf_op jit(solution)/shard_map/ppermute | solution.py:335
  111.0 26.7 %collective-permute-start.13 = (bf16[144,1152]{1,0:T(8,128)(2,1)}, bf16[144,1152]{1,0:T(8,128)(2,1)}, u32[]{:S(2)}, u32[]{:S(2)}) collective-permute-start(bf16[144,1152]{1,0:T(8,128)(2,1)} %constant_dynamic-slice_fusion.5), channel_id=1, source_target_pairs={{0,16},{8,24},{16,0},{24,8},{1,17},{9,25},{17,1},{25,9},{2,18},{10... | collective-permute-start | bytes 995336 | tf_op jit(solution)/shard_map/ppermute | solution.py:335
  115.7 22.1 %collective-permute-start.14 = (bf16[144,1152]{1,0:T(8,128)(2,1)}, bf16[144,1152]{1,0:T(8,128)(2,1)S(1)}, u32[]{:S(2)}, u32[]{:S(2)}) collective-permute-start(bf16[144,1152]{1,0:T(8,128)(2,1)} %constant_dynamic-slice_fusion.5), channel_id=1, source_target_pairs={{0,24},{8,16},{16,8},{24,0},{1,25},{9,17},{17,9},{25,1},{2,26},{10... | collective-permute-start | bytes 995336 | tf_op jit(solution)/shard_map/ppermute | solution.py:335
  139.7 20.2 %all-to-all-start.2 = ((bf16[8,160,144]{1,2,0:T(8,128)(2,1)}), bf16[8,160,144]{1,2,0:T(8,128)(2,1)S(1)}, u32[]{:S(2)}, u32[]{:S(2)}) async-start(bf16[8,160,144]{1,2,0:T(8,128)(2,1)} %copy.59), calls=%async_computation.2 | async-start | bytes 1179648 | tf_op jit(solution)/shard_map/all_to_all | solution.py:359
  143.3 52.3 %all-gather.12.cloned.1.call-start = ((), (), s32[]{:S(2)}) async-start(), calls=%async_computation.14 | async-start | bytes 2985984 | tf_op jit(solution)/shard_map/all_gather | solution.py:454
  160.2 118.2 %reduce-scatter.9.cloned.1.call-start = ((), (), s32[]{:S(2)}) async-start(), calls=%async_computation.16 | async-start | bytes 2985984 | tf_op jit(solution)/shard_map/reduce_scatter | solution.py:465
  195.3 83.2 %reduce-scatter.7.cloned.1.call-start = ((), (), s32[]{:S(2)}) async-start(), calls=%async_computation.15 | async-start | bytes 2985984 | tf_op jit(solution)/shard_map/reduce_scatter | solution.py:482
  230.3 27.3 %all-to-all-start.3 = ((bf16[8,160,144]{1,2,0:T(8,128)(2,1)}), bf16[8,160,144]{1,2,0:T(8,128)(2,1)}, u32[]{:S(2)}, u32[]{:S(2)}) async-start(bf16[8,160,144]{1,2,0:T(8,128)(2,1)} %copy.61), calls=%async_computation.3 | async-start | bytes 1179648 | tf_op jit(solution)/shard_map/all_to_all | solution.py:359
  234.5 84.5 %reduce-scatter.11.cloned.1.call-start = ((), (), s32[]{:S(2)}) async-start(), calls=%async_computation.17 | async-start | bytes 3317760 | tf_op jit(solution)/shard_map/reduce_scatter | solution.py:502
  243.8 34.7 %collective-permute-start.25 = (bf16[160,1152]{1,0:T(8,128)(2,1)}, bf16[160,1152]{1,0:T(8,128)(2,1)S(1)}, u32[]{:S(2)}, u32[]{:S(2)}) collective-permute-start(bf16[160,1152]{1,0:T(8,128)(2,1)} %get-tuple-element.177), channel_id=1, source_target_pairs={{0,16},{8,24},{16,0},{24,8},{1,17},{9,25},{17,1},{25,9},{2,18},{10... | collective-permute-start | bytes 1105928 | tf_op jit(solution)/shard_map/ppermute | solution.py:335
  244.3 34.1 %collective-permute-start.26 = (bf16[160,1152]{1,0:T(8,128)(2,1)}, bf16[160,1152]{1,0:T(8,128)(2,1)}, u32[]{:S(2)}, u32[]{:S(2)}) collective-permute-start(bf16[160,1152]{1,0:T(8,128)(2,1)} %get-tuple-element.176), channel_id=1, source_target_pairs={{0,24},{8,16},{16,8},{24,0},{1,25},{9,17},{17,9},{25,1},{2,26},{10... | collective-permute-start | bytes 1105928 | tf_op jit(solution)/shard_map/ppermute | solution.py:335
  279.5 23.1 %collective-permute-start.30 = (bf16[160,288]{1,0:T(8,128)(2,1)S(1)}, bf16[160,288]{1,0:T(8,128)(2,1)S(1)}, u32[]{:S(2)}, u32[]{:S(2)}) collective-permute-start(bf16[160,288]{1,0:T(8,128)(2,1)S(1)} %get-tuple-element.200), channel_id=1, source_target_pairs={{0,8},{8,0},{16,24},{24,16},{1,9},{9,1},{17,25},{25,17},{2,10},{10... | collective-permute-start | bytes 276488 | tf_op jit(solution)/shard_map/ppermute | solution.py:335
  280.8 21.8 %collective-permute-start.31 = (bf16[160,288]{1,0:T(8,128)(2,1)S(1)}, bf16[160,288]{1,0:T(8,128)(2,1)S(1)}, u32[]{:S(2)}, u32[]{:S(2)}) collective-permute-start(bf16[160,288]{1,0:T(8,128)(2,1)S(1)} %get-tuple-element.199), channel_id=1, source_target_pairs={{0,16},{8,24},{16,0},{24,8},{1,17},{9,25},{17,1},{25,9},{2,18},{10... | collective-permute-start | bytes 276488 | tf_op jit(solution)/shard_map/ppermute | solution.py:335
  282.8 19.7 %collective-permute-start.34 = (bf16[160,1152]{1,0:T(8,128)(2,1)S(1)}, bf16[160,1152]{1,0:T(8,128)(2,1)S(1)}, u32[]{:S(2)}, u32[]{:S(2)}) collective-permute-start(bf16[160,1152]{1,0:T(8,128)(2,1)S(1)} %copy-done.20), channel_id=1, source_target_pairs={{0,16},{8,24},{16,0},{24,8},{1,17},{9,25},{17,1},{25,9},{2,18},{10... | collective-permute-start | bytes 1105928 | tf_op jit(solution)/shard_map/ppermute | solution.py:335
  334.2 47.8 %reduce-scatter.13.cloned.1.call-start = ((), (), s32[]{:S(2)}) async-start(), calls=%async_computation.18 | async-start | bytes 1492992
  347.5 33.2 %all-to-all-start.6 = ((f32[32,8,128]{2,1,0:T(8,128)}), f32[32,8,128]{2,1,0:T(8,128)S(1)}, u32[]{:S(2)}, u32[]{:S(2)}) async-start(f32[32,8,128]{2,1,0:T(8,128)} %bitcast.66), calls=%async_computation.9 | async-start | bytes 262144 | tf_op jit(solution)/shard_map/all_to_all | solution.py:551
  (87 other events, 1015.1 us)
Sparse Core Ops, SparseCore 0:
  9.7 27.5 all-gather.5
  39.4 40.6 all-gather.9
  82.3 40.8 all-gather.7
  160.4 32.4 all-gather.11
  195.4 36.2 reduce-scatter.8
  233.9 42.6 reduce-scatter.6
  279.0 38.0 reduce-scatter.10
  346.4 34.9 reduce-scatter.12

commit v20 on v19

--- a/solution.py
+++ b/solution.py
@@ -412,7 +412,6 @@
     up_bias = lax.dynamic_slice_in_dim(vectors[:, 7 * small : own_size], dp_at * ns, ns, 0)
     up_bias = up_bias.reshape(hidden_part)
 
-    up_part = lax.all_gather(up_slices, "seq", axis=0, tiled=True)
     first_terms = dot(joined_here, skip_part)
     first = add_blocks(first_terms[:local], low_rows(first_terms)) + b_skip
     qkv_mine = seq_exchange(qkv_out).reshape(part, wide)
@@ -428,9 +427,10 @@
     half = part // 2
     own_half = lax.dynamic_slice_in_dim(proj_rows, core * half, half, 0)
     proj_halves = [swap(own_half, k) for k in range(1, nd)]
-    normed_one_row, qkv_mine, qkv_wide, proj_rows, grad_out_rows, up_part = after(
-        (normed_one_row, qkv_mine, widen(qkv_mine), proj_rows, grad_out_rows, up_part)
-    )
+    normed_one_row, qkv_mine, qkv_wide, proj_rows, grad_out_rows = after(
+        (normed_one_row, qkv_mine, widen(qkv_mine), proj_rows, grad_out_rows)
+    )
+    up_part = lax.all_gather(up_slices, "seq", axis=0, tiled=True)
     triple = dot(normed_one_row, qkv_wide).astype(BF16)
     attended, attended_low, lse = attend(triple, item_lengths, heads, scale)
 

time: 397 us -> 391 us (0.985)
  waiting for transfers between devices: 89.5 us -> 83.2 us
    all_to_all x4, waiting for transfers between devices: 22.2 us -> 18 us  [seq_exchange(): return lax.all_to_all(v, 'seq', 0, 0, tiled=True)]
  transfers between devices with their start and end apart: 61 -> 61, of which waited for: 21 -> 18; matrix products, arithmetic and copies ran while one was open for 31% -> 30% of each run, Pallas kernels for 10% -> 10%
where the time goes in v20:
time: 391 us; the launch traced here: 385 us
  starting transfers between devices  83.4 us (21%)
  waiting for transfers between devices  83.2 us (21%)
  local copies, waits for them, and re-layouts  53 us (14%)
  matrix products  50.3 us (13%)
  Pallas kernels  38.7 us (10%)
  blocking collectives  33.2 us (8%)
  other arithmetic  27.1 us (7%)
  between operations  15.7 us (4%)
    ppermute x42, waiting for transfers between devices, swap(): return lax.ppermute(v, 'dp', [(i, i ^ k) for i in range(nd)])  56.5 us
    ppermute x42, starting transfers between devices, swap(): return lax.ppermute(v, 'dp', [(i, i ^ k) for i in range(nd)])  51.6 us
    dot_general x6, matrix products, inner(): lax.dot_general(left, right, (((0,), (0,)), ((), ())), preferred_element_...  26.2 us
    all_gather x1, blocking collectives, on_device(): proj_rows = lax.all_gather(own_proj, 'seq', axis=0, tiled=True)  19.9 us
    all_to_all x4, waiting for transfers between devices, seq_exchange(): return lax.all_to_all(v, 'seq', 0, 0, tiled=True)  18 us
    dot_general x4, matrix products, dot(): return jnp.dot(left, right, preferred_element_type=F32)  18 us
    all_to_all x4, starting transfers between devices, seq_exchange(): return lax.all_to_all(v, 'seq', 0, 0, tiled=True)  16.2 us
    all_gather x1, blocking collectives, on_device(): qkv_mine = lax.all_gather(qkv_mine, 'dp', axis=0, tiled=True)  13.3 us
  transfers between devices with their start and end apart: 61, of which 18 were waited for; matrix products, arithmetic and copies ran while one was open for 30% of the time, Pallas kernels for 10%

profile of v20, /device:TPU:0, one launch (start us, length us, event | category | flops | bytes accessed | tf_op | source)
XLA Modules:
  0.0 384.5 jit_solution(477061989180812826)
XLA Ops:
  19.6 4.0 %all-to-all-start = ((bf16[32,8,128]{2,1,0:T(8,128)(2,1)}), bf16[32,8,128]{2,1,0:T(8,128)(2,1)S(1)}, u32[]{:S(2)}, u32[]{:S(2)}) async-start(bf16[32,8,128]{2,1,0:T(8,128)(2,1)} %broadcast_in_dim.15), calls=%async_computation | async-start | bytes 131072 | tf_op jit(solution)/shard_map/all_to_all | solution.py:380
  37.2 4.3 %fusion.61 = (bf16[640,1152]{1,0:T(8,128)(2,1)S(1)}, f32[640,1152]{1,0:T(8,128)}) fusion(bf16[640,576]{1,0:T(8,128)(2,1)S(1)} %pad_maximum_fusion.7, bf16[576,1152]{1,0:T(8,128)(2,1)} %all-gather.6.cloned.1.call-done), kind=kOutput, calls=%fused_computation.168 | convolution fusion | flops 850083840 | bytes 6488064 | tf_op jit(solution)/shard_map/dot_general | solution.py:53
  53.1 8.3 %collective-permute-done.7 = bf16[160,1152]{1,0:T(8,128)(2,1)S(1)} collective-permute-done((bf16[160,1152]{1,0:T(8,128)(2,1)S(1)}, bf16[160,1152]{1,0:T(8,128)(2,1)S(1)}, u32[]{:S(2)}, u32[]{:S(2)}) %collective-permute-start.7) | collective-permute-done | bytes 368672 | tf_op jit(solution)/shard_map/ppermute | solution.py:335
  65.0 13.3 %all_gather.20 = bf16[1152,432]{1,0:T(8,128)(2,1)S(1)} all-gather(bf16[288,432]{1,0:T(8,128)(2,1)S(1)} %reshape.194), channel_id=1, replica_groups=mesh['dp'=4,'seq'=8] {'dp'}, dimensions={0}, use_global_device_ids=true | all-gather | bytes 1244160 | tf_op jit(solution)/shard_map/all_gather | solution.py:423
  81.8 19.9 %all-gather = bf16[8,36,1152]{2,1,0:T(8,128)(2,1)} all-gather(bf16[1,36,1152]{2,1,0:T(8,128)(2,1)S(1)} %bitcast.172), channel_id=1, replica_groups=mesh['dp'=4,'seq'=8] {'seq'}, dimensions={0}, use_global_device_ids=true | all-gather | bytes 746496 | tf_op jit(solution)/shard_map/all_gather | solution.py:426
  113.9 5.3 %convolution_convert_fusion.4.q_ref.k_ref.v_ref = bf16[1280,768]{1,0:T(8,128)(2,1)S(1)} fusion(bf16[1280,1152]{1,0:T(8,128)(2,1)} %all-gather.8.cloned.1.call-done, bf16[1152,768]{0,1:T(8,128)(2,1)} %bitcast.153), kind=kOutput, calls=%fused_computation.22 | convolution fusion | flops 2265907200 | bytes 6684672 | tf_op jit(solution)/shard_map/dot_general | solution.py:53
  119.2 8.3 %shard_map.288 = (f32[1280,256]{1,0:T(8,128)S(1)}, bf16[1280,144]{1,0:T(8,128)(2,1)S(1)}, f32[8,1280]{1,0:T(8,128)S(1)}) custom-call(bf16[1280,768]{1,0:T(8,128)(2,1)S(1)} %convolution_convert_fusion.4.q_ref.k_ref.v_ref, bf16[1280,768]{1,0:T(8,128)(2,1)S(1)} %convolution_convert_fusion.4.q_ref.k_ref.v_ref, ...), custom_call_target="tpu_custom_call" | custom-call | flops 3355443200 | bytes 3276800 | tf_op jit(solution)/shard_map/pallas_call | solution.py:94
  146.1 5.8 %all-to-all-done.2 = bf16[8,160,144]{1,2,0:T(8,128)(2,1)S(1)} async-done(((bf16[8,160,144]{1,2,0:T(8,128)(2,1)}), bf16[8,160,144]{1,2,0:T(8,128)(2,1)S(1)}, u32[]{:S(2)}, u32[]{:S(2)}) %all-to-all-start.2) | async-done | bytes 368672 | tf_op jit(solution)/shard_map/all_to_all | solution.py:359
  160.2 4.6 %convolution_convert_fusion.3.up_ref = bf16[1152,1152]{1,0:T(8,128)(2,1)S(1)} fusion(bf16[1152,1152]{1,0:T(8,128)(2,1)S(1)} %copy-done.49, s32[1152]{0:T(1024)S(1)} %get-tuple-element.241, s32[1152]{0:T(1024)S(1)} %get-tuple-element.242, s32[]{:T(128)S(6)} %axis_index.23, s32[1152]{0:T(1024)S(1)} %get-tuple-element.240, s32[1152]{0:T(1024)S(1)} %get-tuple-element.243, ...), kind=kOutput, calls=%fused_computation.11 | convolution fusion | flops 3094806528 | bytes 5329156 | tf_op jit(solution)/shard_map/dot_general | solution.py:57
  168.1 8.1 %collective-permute-done.19 = bf16[160,1152]{1,0:T(8,128)(2,1)S(1)} collective-permute-done((bf16[160,1152]{1,0:T(8,128)(2,1)S(1)}, bf16[160,1152]{1,0:T(8,128)(2,1)S(1)}, u32[]{:S(2)}, u32[]{:S(2)}) %collective-permute-start.19) | collective-permute-done | bytes 368672 | tf_op jit(solution)/shard_map/ppermute | solution.py:335
  176.3 5.6 %shard_map.289 = (bf16[640,1152]{1,0:T(8,128)(2,1)S(1)}, f32[640,1152]{1,0:T(8,128)S(1)}) custom-call(bf16[640,1152]{1,0:T(8,128)(2,1)S(1)} %pad_maximum_fusion.1.x_ref, bf16[1152,1152]{1,0:T(8,128)(2,1)S(1)} %convolution_convert_fusion.3.up_ref, f32[1,1152]{1,0:T(1,128)S(1)} %reshape_reshape.6.bias_ref), custom_call_target="tpu_custom_call" | custom-call | flops 1698693120 | bytes 8552448 | tf_op jit(solution)/shard_map/pallas_call | solution.py:254
  187.9 8.2 %shard_map.290 = (bf16[640,1152]{1,0:T(8,128)(2,1)}, f32[1,1152]{1,0:T(1,128)S(1)}, f32[160,1152]{1,0:T(8,128)S(1)}, bf16[160,1152]{1,0:T(8,128)(2,1)S(1)}, bf16...) custom-call(bf16[640,1152]{1,0:T(8,128)(2,1)} %pad_maximum_fusion.grad_ref, bf16[1152,1152]{1,0:T(8,128)(2,1)} %copy-done.2, ...), custom_call_target="tpu_custom_call" | custom-call | flops 3397386240 | bytes 12681216 | tf_op jit(solution)/shard_map/pallas_call | solution.py:292
  199.6 9.8 %convolution_convert_fusion.1 = bf16[1152,1152]{1,0:T(8,128)(2,1)} fusion(bf16[640,1152]{1,0:T(8,128)(2,1)} %get-tuple-element.123, bf16[640,1152]{1,0:T(8,128)(2,1)S(1)} %pad_maximum_fusion.1.x_ref, s32[1152]{0:T(1024)S(1)} %get-tuple-element.241, s32[1152]{0:T(1024)S(1)} %copy-done.36, s32[]{:T(128)S(6)} %axis_index.23, s32[1152]{0:T(1024)S(1)} %get-tuple-element.240, ...), kind=kOutput, calls=%fused_computation.9 | convolution fusion | flops 3435282432 | bytes 5624068 | tf_op jit(solution)/shard_map/dot_general | solution.py:57
  209.5 5.6 %collective-permute-done.22 = bf16[160,1152]{1,0:T(8,128)(2,1)} collective-permute-done((bf16[160,1152]{1,0:T(8,128)(2,1)S(1)}, bf16[160,1152]{1,0:T(8,128)(2,1)}, u32[]{:S(2)}, u32[]{:S(2)}) %collective-permute-start.22) | collective-permute-done | bytes 368672 | tf_op jit(solution)/shard_map/ppermute | solution.py:335
  223.8 4.2 %all-to-all-start.3 = ((bf16[8,160,144]{1,2,0:T(8,128)(2,1)}), bf16[8,160,144]{1,2,0:T(8,128)(2,1)}, u32[]{:S(2)}, u32[]{:S(2)}) async-start(bf16[8,160,144]{1,2,0:T(8,128)(2,1)} %copy.61), calls=%async_computation.3 | async-start | bytes 1179648 | tf_op jit(solution)/shard_map/all_to_all | solution.py:359
  228.1 5.6 %fusion.63 = (bf16[640,1152]{1,0:T(8,128)(2,1)S(1)}, f32[640,1152]{1,0:T(8,128)}) fusion(bf16[640,1152]{1,0:T(8,128)(2,1)S(1)} %copy-done.4, bf16[1152,1152]{1,0:T(8,128)(2,1)} %all-gather.12.cloned.1.call-done.down_ref), kind=kOutput, calls=%fused_computation.170 | convolution fusion | flops 1699430400 | bytes 8552448 | tf_op jit(solution)/shard_map/dot_general | solution.py:53
  239.6 12.2 %all-to-all-done.3 = bf16[8,160,144]{1,2,0:T(8,128)(2,1)} async-done(((bf16[8,160,144]{1,2,0:T(8,128)(2,1)}), bf16[8,160,144]{1,2,0:T(8,128)(2,1)}, u32[]{:S(2)}, u32[]{:S(2)}) %all-to-all-start.3) | async-done | bytes 368672 | tf_op jit(solution)/shard_map/all_to_all | solution.py:359
  254.7 12.9 %shard_map.292 = (bf16[1280,144]{1,0:T(8,128)(2,1)S(1)}, bf16[1280,288]{1,0:T(8,128)(2,1)S(1)}) custom-call(bf16[1280,768]{1,0:T(8,128)(2,1)S(1)} %copy-done.6, bf16[1280,768]{1,0:T(8,128)(2,1)S(1)} %copy-done.6, bf16[1280,768]{1,0:T(8,128)(2,1)S(1)} %copy-done.6, bf16[1280,144]{1,0:T(8,128)(2,1)S(1)} %bitcast.145, f32[1280,256]{1,0:T(8,128)S(1)} %copy-done.8, ...), custom_call_target="tpu_custom_call" | custom-call | flops 8388608000 | bytes 4587520 | tf_op jit(solution)/shard_map/pallas_call | solution.py:172
  288.7 6.9 %collective-permute-done.34 = bf16[160,1152]{1,0:T(8,128)(2,1)S(1)} collective-permute-done((bf16[160,1152]{1,0:T(8,128)(2,1)S(1)}, bf16[160,1152]{1,0:T(8,128)(2,1)S(1)}, u32[]{:S(2)}, u32[]{:S(2)}) %collective-permute-start.34) | collective-permute-done | bytes 368672 | tf_op jit(solution)/shard_map/ppermute | solution.py:335
  307.8 4.9 %all-to-all-start.4 = ((bf16[4,36,1152]{2,1,0:T(8,128)(2,1)}), bf16[4,36,1152]{2,1,0:T(8,128)(2,1)S(1)}, u32[]{:S(2)}, u32[]{:S(2)}) async-start(bf16[4,36,1152]{2,1,0:T(8,128)(2,1)} %fusion.27), calls=%async_computation.7 | async-start | bytes 737280 | tf_op jit(solution)/shard_map/all_to_all | solution.py:369
  323.5 5.0 %all-to-all-start.5 = ((bf16[8,36,432]{2,1,0:T(8,128)(2,1)}), bf16[8,36,432]{2,1,0:T(8,128)(2,1)}, u32[]{:S(2)}, u32[]{:S(2)}) async-start(bf16[8,36,432]{2,1,0:T(8,128)(2,1)} %reshape.202), calls=%async_computation.8 | async-start | bytes 655360 | tf_op jit(solution)/shard_map/all_to_all | solution.py:359
  329.8 4.7 %collective-permute-done.28 = bf16[160,1152]{1,0:T(8,128)(2,1)S(1)} collective-permute-done((bf16[160,1152]{1,0:T(8,128)(2,1)S(1)}, bf16[160,1152]{1,0:T(8,128)(2,1)S(1)}, u32[]{:S(2)}, u32[]{:S(2)}) %collective-permute-start.28) | collective-permute-done | bytes 368672 | tf_op jit(solution)/shard_map/ppermute | solution.py:335
  341.5 4.7 %all-to-all-start.6 = ((f32[32,8,128]{2,1,0:T(8,128)}), f32[32,8,128]{2,1,0:T(8,128)S(1)}, u32[]{:S(2)}, u32[]{:S(2)}) async-start(f32[32,8,128]{2,1,0:T(8,128)} %bitcast.66), calls=%async_computation.9 | async-start | bytes 262144 | tf_op jit(solution)/shard_map/all_to_all | solution.py:551
  363.8 6.8 %collective-permute-done.41 = bf16[160,576]{0,1:T(8,128)(2,1)} collective-permute-done((bf16[160,576]{0,1:T(8,128)(2,1)}, bf16[160,576]{0,1:T(8,128)(2,1)}, u32[]{:S(2)}, u32[]{:S(2)}) %collective-permute-start.41) | collective-permute-done | bytes 184352 | tf_op jit(solution)/shard_map/ppermute | solution.py:335
  (352 shorter events, 189.7 us)
Async XLA Ops:
  7.2 30.0 %all-gather.6.cloned.1.call-start = ((), (), s32[]{:S(2)}) async-start(), calls=%async_computation.11 | async-start | bytes 1492992 | tf_op jit(solution)/shard_map/all_gather | solution.py:372
  9.7 22.1 %collective-permute-start = (bf16[160,576]{1,0:T(8,128)(2,1)S(1)}, bf16[160,576]{1,0:T(8,128)(2,1)S(1)}, u32[]{:S(2)}, u32[]{:S(2)}) collective-permute-start(bf16[160,576]{1,0:T(8,128)(2,1)S(1)} %get-tuple-element.190), channel_id=1, source_target_pairs={{0,8},{8,0},{16,24},{24,16},{1,9},{9,1},{17,25},{25,17},{2,10},{10... | collective-permute-start | bytes 552968 | tf_op jit(solution)/shard_map/ppermute | solution.py:335
  12.8 19.1 %collective-permute-start.1 = (bf16[160,576]{1,0:T(8,128)(2,1)S(1)}, bf16[160,576]{1,0:T(8,128)(2,1)S(1)}, u32[]{:S(2)}, u32[]{:S(2)}) collective-permute-start(bf16[160,576]{1,0:T(8,128)(2,1)S(1)} %get-tuple-element.189), channel_id=1, source_target_pairs={{0,16},{8,24},{16,0},{24,8},{1,17},{9,25},{17,1},{25,9},{2,18},{10... | collective-permute-start | bytes 552968 | tf_op jit(solution)/shard_map/ppermute | solution.py:335
  49.8 64.1 %all-gather.8.cloned.1.call-start = ((), (), s32[]{:S(2)}) async-start(), calls=%async_computation.12 | async-start | bytes 3317760 | tf_op jit(solution)/shard_map/all_gather | solution.py:421
  64.2 88.0 %all-gather.10.cloned.1.call-start = ((), (), s32[]{:S(2)}) async-start(), calls=%async_computation.13 | async-start | bytes 2985984 | tf_op jit(solution)/shard_map/all_gather | solution.py:433
  78.2 31.6 %collective-permute-start.10 = (bf16[160,1152]{1,0:T(8,128)(2,1)S(1)}, bf16[160,1152]{1,0:T(8,128)(2,1)}, u32[]{:S(2)}, u32[]{:S(2)}) collective-permute-start(bf16[160,1152]{1,0:T(8,128)(2,1)S(1)} %bitcast.154), channel_id=1, source_target_pairs={{0,16},{8,24},{16,0},{24,8},{1,17},{9,25},{17,1},{25,9},{2,18},{10... | collective-permute-start | bytes 1105928 | tf_op jit(solution)/shard_map/ppermute | solution.py:335
  79.3 32.1 %collective-permute-start.11 = (bf16[160,1152]{1,0:T(8,128)(2,1)S(1)}, bf16[160,1152]{1,0:T(8,128)(2,1)}, u32[]{:S(2)}, u32[]{:S(2)}) collective-permute-start(bf16[160,1152]{1,0:T(8,128)(2,1)S(1)} %bitcast.155), channel_id=1, source_target_pairs={{0,24},{8,16},{16,8},{24,0},{1,25},{9,17},{17,9},{25,1},{2,26},{10... | collective-permute-start | bytes 1105928 | tf_op jit(solution)/shard_map/ppermute | solution.py:335
  80.8 30.6 %collective-permute-start.9 = (bf16[160,1152]{1,0:T(8,128)(2,1)S(1)}, bf16[160,1152]{1,0:T(8,128)(2,1)}, u32[]{:S(2)}, u32[]{:S(2)}) collective-permute-start(bf16[160,1152]{1,0:T(8,128)(2,1)S(1)} %bitcast.156), channel_id=1, source_target_pairs={{0,8},{8,0},{16,24},{24,16},{1,9},{9,1},{17,25},{25,17},{2,10},{10... | collective-permute-start | bytes 1105928 | tf_op jit(solution)/shard_map/ppermute | solution.py:335
  103.7 24.9 %collective-permute-start.12 = (bf16[144,1152]{1,0:T(8,128)(2,1)}, bf16[144,1152]{1,0:T(8,128)(2,1)}, u32[]{:S(2)}, u32[]{:S(2)}) collective-permute-start(bf16[144,1152]{1,0:T(8,128)(2,1)} %constant_dynamic-slice_fusion.5), channel_id=1, source_target_pairs={{0,8},{8,0},{16,24},{24,16},{1,9},{9,1},{17,25},{25,17},{2,10},{10... | collective-permute-start | bytes 995336 | tf_op jit(solution)/shard_map/ppermute | solution.py:335
  104.6 24.0 %collective-permute-start.13 = (bf16[144,1152]{1,0:T(8,128)(2,1)}, bf16[144,1152]{1,0:T(8,128)(2,1)}, u32[]{:S(2)}, u32[]{:S(2)}) collective-permute-start(bf16[144,1152]{1,0:T(8,128)(2,1)} %constant_dynamic-slice_fusion.5), channel_id=1, source_target_pairs={{0,16},{8,24},{16,0},{24,8},{1,17},{9,25},{17,1},{25,9},{2,18},{10... | collective-permute-start | bytes 995336 | tf_op jit(solution)/shard_map/ppermute | solution.py:335
  130.5 21.5 %all-to-all-start.2 = ((bf16[8,160,144]{1,2,0:T(8,128)(2,1)}), bf16[8,160,144]{1,2,0:T(8,128)(2,1)S(1)}, u32[]{:S(2)}, u32[]{:S(2)}) async-start(bf16[8,160,144]{1,2,0:T(8,128)(2,1)} %copy.59), calls=%async_computation.2 | async-start | bytes 1179648 | tf_op jit(solution)/shard_map/all_to_all | solution.py:359
  134.0 53.9 %all-gather.12.cloned.1.call-start = ((), (), s32[]{:S(2)}) async-start(), calls=%async_computation.14 | async-start | bytes 2985984 | tf_op jit(solution)/shard_map/all_gather | solution.py:454
  152.2 120.4 %reduce-scatter.9.cloned.1.call-start = ((), (), s32[]{:S(2)}) async-start(), calls=%async_computation.16 | async-start | bytes 2985984 | tf_op jit(solution)/shard_map/reduce_scatter | solution.py:465
  187.6 85.0 %reduce-scatter.7.cloned.1.call-start = ((), (), s32[]{:S(2)}) async-start(), calls=%async_computation.15 | async-start | bytes 2985984 | tf_op jit(solution)/shard_map/reduce_scatter | solution.py:482
  223.8 27.9 %all-to-all-start.3 = ((bf16[8,160,144]{1,2,0:T(8,128)(2,1)}), bf16[8,160,144]{1,2,0:T(8,128)(2,1)}, u32[]{:S(2)}, u32[]{:S(2)}) async-start(bf16[8,160,144]{1,2,0:T(8,128)(2,1)} %copy.61), calls=%async_computation.3 | async-start | bytes 1179648 | tf_op jit(solution)/shard_map/all_to_all | solution.py:359
  228.0 84.7 %reduce-scatter.11.cloned.1.call-start = ((), (), s32[]{:S(2)}) async-start(), calls=%async_computation.17 | async-start | bytes 3317760 | tf_op jit(solution)/shard_map/reduce_scatter | solution.py:502
  236.4 36.2 %collective-permute-start.25 = (bf16[160,1152]{1,0:T(8,128)(2,1)}, bf16[160,1152]{1,0:T(8,128)(2,1)S(1)}, u32[]{:S(2)}, u32[]{:S(2)}) collective-permute-start(bf16[160,1152]{1,0:T(8,128)(2,1)} %get-tuple-element.175), channel_id=1, source_target_pairs={{0,16},{8,24},{16,0},{24,8},{1,17},{9,25},{17,1},{25,9},{2,18},{10... | collective-permute-start | bytes 1105928 | tf_op jit(solution)/shard_map/ppermute | solution.py:335
  237.8 34.8 %collective-permute-start.26 = (bf16[160,1152]{1,0:T(8,128)(2,1)}, bf16[160,1152]{1,0:T(8,128)(2,1)}, u32[]{:S(2)}, u32[]{:S(2)}) collective-permute-start(bf16[160,1152]{1,0:T(8,128)(2,1)} %get-tuple-element.174), channel_id=1, source_target_pairs={{0,24},{8,16},{16,8},{24,0},{1,25},{9,17},{17,9},{25,1},{2,26},{10... | collective-permute-start | bytes 1105928 | tf_op jit(solution)/shard_map/ppermute | solution.py:335
  273.7 22.1 %collective-permute-start.30 = (bf16[160,288]{1,0:T(8,128)(2,1)S(1)}, bf16[160,288]{1,0:T(8,128)(2,1)S(1)}, u32[]{:S(2)}, u32[]{:S(2)}) collective-permute-start(bf16[160,288]{1,0:T(8,128)(2,1)S(1)} %get-tuple-element.198), channel_id=1, source_target_pairs={{0,8},{8,0},{16,24},{24,16},{1,9},{9,1},{17,25},{25,17},{2,10},{10... | collective-permute-start | bytes 276488 | tf_op jit(solution)/shard_map/ppermute | solution.py:335
  273.7 22.0 %collective-permute-start.31 = (bf16[160,288]{1,0:T(8,128)(2,1)S(1)}, bf16[160,288]{1,0:T(8,128)(2,1)S(1)}, u32[]{:S(2)}, u32[]{:S(2)}) collective-permute-start(bf16[160,288]{1,0:T(8,128)(2,1)S(1)} %get-tuple-element.197), channel_id=1, source_target_pairs={{0,16},{8,24},{16,0},{24,8},{1,17},{9,25},{17,1},{25,9},{2,18},{10... | collective-permute-start | bytes 276488 | tf_op jit(solution)/shard_map/ppermute | solution.py:335
  275.8 19.9 %collective-permute-start.34 = (bf16[160,1152]{1,0:T(8,128)(2,1)S(1)}, bf16[160,1152]{1,0:T(8,128)(2,1)S(1)}, u32[]{:S(2)}, u32[]{:S(2)}) collective-permute-start(bf16[160,1152]{1,0:T(8,128)(2,1)S(1)} %copy-done.20), channel_id=1, source_target_pairs={{0,16},{8,24},{16,0},{24,8},{1,17},{9,25},{17,1},{25,9},{2,18},{10... | collective-permute-start | bytes 1105928 | tf_op jit(solution)/shard_map/ppermute | solution.py:335
  317.5 19.0 %collective-permute-start.29 = (bf16[160,1152]{1,0:T(8,128)(2,1)S(1)}, bf16[160,1152]{1,0:T(8,128)(2,1)}, u32[]{:S(2)}, u32[]{:S(2)}) collective-permute-start(bf16[160,1152]{1,0:T(8,128)(2,1)S(1)} %get-tuple-element.168), channel_id=1, source_target_pairs={{0,24},{8,16},{16,8},{24,0},{1,25},{9,17},{17,9},{25,1},{2,26},{10... | collective-permute-start | bytes 1105928 | tf_op jit(solution)/shard_map/ppermute | solution.py:335
  328.6 47.2 %reduce-scatter.13.cloned.1.call-start = ((), (), s32[]{:S(2)}) async-start(), calls=%async_computation.18 | async-start | bytes 1492992
  341.5 32.9 %all-to-all-start.6 = ((f32[32,8,128]{2,1,0:T(8,128)}), f32[32,8,128]{2,1,0:T(8,128)S(1)}, u32[]{:S(2)}, u32[]{:S(2)}) async-start(f32[32,8,128]{2,1,0:T(8,128)} %bitcast.66), calls=%async_computation.9 | async-start | bytes 262144 | tf_op jit(solution)/shard_map/all_to_all | solution.py:551
  (87 other events, 997.8 us)
Sparse Core Ops, SparseCore 0:
  9.7 27.5 all-gather.5
  64.3 41.0 all-gather.7
  107.6 33.9 all-gather.9
  152.3 32.9 all-gather.11
  187.7 36.5 reduce-scatter.8
  226.4 43.7 reduce-scatter.6
  272.8 37.4 reduce-scatter.10
  340.4 34.5 reduce-scatter.12

commit v21 on v20

--- a/solution.py
+++ b/solution.py
@@ -422,13 +422,13 @@
 
     qkv_mine = lax.all_gather(qkv_mine, "dp", axis=0, tiled=True)
     qkv_mine, own_proj, grad_out = after((qkv_mine, own_proj, cotangent[0]))
-    grad_out_rows = gather_rows(grad_out)
+    grad_blocks = [grad_out] + [swap(grad_out, k) for k in range(1, nd)]
     proj_rows = lax.all_gather(own_proj, "seq", axis=0, tiled=True)
     half = part // 2
     own_half = lax.dynamic_slice_in_dim(proj_rows, core * half, half, 0)
     proj_halves = [swap(own_half, k) for k in range(1, nd)]
-    normed_one_row, qkv_mine, qkv_wide, proj_rows, grad_out_rows = after(
-        (normed_one_row, qkv_mine, widen(qkv_mine), proj_rows, grad_out_rows)
+    normed_one_row, qkv_mine, qkv_wide, proj_rows, grad_blocks = after(
+        (normed_one_row, qkv_mine, widen(qkv_mine), proj_rows, grad_blocks)
     )
     up_part = lax.all_gather(up_slices, "seq", axis=0, tiled=True)
     triple = dot(normed_one_row, qkv_wide).astype(BF16)
@@ -438,7 +438,10 @@
         v = seq_exchange(v.reshape(ns, local, head_cols))
         return jnp.swapaxes(v, 0, 1).reshape(local, features)
 
-    attended_low, proj_halves, proj_rows = after((attended_low, proj_halves, proj_rows))
+    attended_low, proj_halves, proj_rows, grad_blocks = after(
+        (attended_low, proj_halves, proj_rows, grad_blocks)
+    )
+    grad_out_rows = jnp.concatenate(grad_blocks, axis=0)
     w_proj = lax.dynamic_update_slice_in_dim(
         jnp.zeros((features, features), BF16), proj_rows, dp_at * part, 0
     )

time: 391 us -> 391 us (level)
    unnamed x106 -> x108, local copies, waits for them, and re-layouts: 9.23 us -> 9.24 us
  transfers between devices with their start and end apart: 61 -> 61, of which waited for: 18 -> 19; matrix products, arithmetic and copies ran while one was open for 30% -> 30% of each run, Pallas kernels for 10% -> 10%
where the time goes in v21:
time: 391 us; the launch traced here: 384 us
  starting transfers between devices  83.8 us (21%)
  waiting for transfers between devices  81.7 us (21%)
  local copies, waits for them, and re-layouts  54 us (14%)
  matrix products  50.3 us (13%)
  Pallas kernels  38.7 us (10%)
  blocking collectives  33.2 us (8%)
  other arithmetic  27.1 us (7%)
  between operations  15.7 us (4%)
    ppermute x42, waiting for transfers between devices, swap(): return lax.ppermute(v, 'dp', [(i, i ^ k) for i in range(nd)])  56 us
    ppermute x42, starting transfers between devices, swap(): return lax.ppermute(v, 'dp', [(i, i ^ k) for i in range(nd)])  51.8 us
    dot_general x6, matrix products, inner(): lax.dot_general(left, right, (((0,), (0,)), ((), ())), preferred_element_...  26.2 us
    all_gather x1, blocking collectives, on_device(): proj_rows = lax.all_gather(own_proj, 'seq', axis=0, tiled=True)  19.9 us
    dot_general x4, matrix products, dot(): return jnp.dot(left, right, preferred_element_type=F32)  17.8 us
    all_to_all x4, waiting for transfers between devices, seq_exchange(): return lax.all_to_all(v, 'seq', 0, 0, tiled=True)  16.8 us
    all_to_all x4, starting transfers between devices, seq_exchange(): return lax.all_to_all(v, 'seq', 0, 0, tiled=True)  16.3 us
    all_gather x1, blocking collectives, on_device(): qkv_mine = lax.all_gather(qkv_mine, 'dp', axis=0, tiled=True)  13.3 us
  transfers between devices with their start and end apart: 61, of which 19 were waited for; matrix products, arithmetic and copies ran while one was open for 30% of the time, Pallas kernels for 10%

profile of v21, /device:TPU:0, one launch (start us, length us, event | category | flops | bytes accessed | tf_op | source)
XLA Modules:
  0.0 384.4 jit_solution(8422871612584531532)
XLA Ops:
  37.2 4.3 %fusion.61 = (bf16[640,1152]{1,0:T(8,128)(2,1)S(1)}, f32[640,1152]{1,0:T(8,128)}) fusion(bf16[640,576]{1,0:T(8,128)(2,1)S(1)} %pad_maximum_fusion.7, bf16[576,1152]{1,0:T(8,128)(2,1)} %all-gather.6.cloned.1.call-done), kind=kOutput, calls=%fused_computation.168 | convolution fusion | flops 850083840 | bytes 6488064 | tf_op jit(solution)/shard_map/dot_general | solution.py:53
  53.1 8.3 %collective-permute-done.7 = bf16[160,1152]{1,0:T(8,128)(2,1)S(1)} collective-permute-done((bf16[160,1152]{1,0:T(8,128)(2,1)S(1)}, bf16[160,1152]{1,0:T(8,128)(2,1)S(1)}, u32[]{:S(2)}, u32[]{:S(2)}) %collective-permute-start.7) | collective-permute-done | bytes 368672 | tf_op jit(solution)/shard_map/ppermute | solution.py:335
  65.0 13.3 %all_gather.20 = bf16[1152,432]{1,0:T(8,128)(2,1)S(1)} all-gather(bf16[288,432]{1,0:T(8,128)(2,1)S(1)} %reshape.194), channel_id=1, replica_groups=mesh['dp'=4,'seq'=8] {'dp'}, dimensions={0}, use_global_device_ids=true | all-gather | bytes 1244160 | tf_op jit(solution)/shard_map/all_gather | solution.py:423
  81.8 19.9 %all-gather = bf16[8,36,1152]{2,1,0:T(8,128)(2,1)} all-gather(bf16[1,36,1152]{2,1,0:T(8,128)(2,1)S(1)} %bitcast.172), channel_id=1, replica_groups=mesh['dp'=4,'seq'=8] {'seq'}, dimensions={0}, use_global_device_ids=true | all-gather | bytes 746496 | tf_op jit(solution)/shard_map/all_gather | solution.py:426
  111.4 5.2 %convolution_convert_fusion.4.q_ref.k_ref.v_ref = bf16[1280,768]{1,0:T(8,128)(2,1)S(1)} fusion(bf16[1280,1152]{1,0:T(8,128)(2,1)} %all-gather.8.cloned.1.call-done, bf16[1152,768]{0,1:T(8,128)(2,1)} %bitcast.153), kind=kOutput, calls=%fused_computation.22 | convolution fusion | flops 2265907200 | bytes 6684672 | tf_op jit(solution)/shard_map/dot_general | solution.py:53
  116.7 8.3 %shard_map.288 = (f32[1280,256]{1,0:T(8,128)S(1)}, bf16[1280,144]{1,0:T(8,128)(2,1)S(1)}, f32[8,1280]{1,0:T(8,128)S(1)}) custom-call(bf16[1280,768]{1,0:T(8,128)(2,1)S(1)} %convolution_convert_fusion.4.q_ref.k_ref.v_ref, bf16[1280,768]{1,0:T(8,128)(2,1)S(1)} %convolution_convert_fusion.4.q_ref.k_ref.v_ref, ...), custom_call_target="tpu_custom_call" | custom-call | flops 3355443200 | bytes 3276800 | tf_op jit(solution)/shard_map/pallas_call | solution.py:94
  147.1 4.8 %all-to-all-done.2 = bf16[8,160,144]{1,2,0:T(8,128)(2,1)S(1)} async-done(((bf16[8,160,144]{1,2,0:T(8,128)(2,1)}), bf16[8,160,144]{1,2,0:T(8,128)(2,1)S(1)}, u32[]{:S(2)}, u32[]{:S(2)}) %all-to-all-start.2) | async-done | bytes 368672 | tf_op jit(solution)/shard_map/all_to_all | solution.py:359
  160.1 4.6 %convolution_convert_fusion.3.up_ref = bf16[1152,1152]{1,0:T(8,128)(2,1)S(1)} fusion(bf16[1152,1152]{1,0:T(8,128)(2,1)S(1)} %copy-done.50, s32[1152]{0:T(1024)S(1)} %get-tuple-element.255, s32[1152]{0:T(1024)S(1)} %get-tuple-element.256, s32[]{:T(128)S(6)} %axis_index.23, s32[1152]{0:T(1024)S(1)} %get-tuple-element.254, s32[1152]{0:T(1024)S(1)} %get-tuple-element.257, ...), kind=kOutput, calls=%fused_computation.11 | convolution fusion | flops 3094806528 | bytes 5329156 | tf_op jit(solution)/shard_map/dot_general | solution.py:57
  168.1 8.2 %collective-permute-done.19 = bf16[160,1152]{1,0:T(8,128)(2,1)S(1)} collective-permute-done((bf16[160,1152]{1,0:T(8,128)(2,1)S(1)}, bf16[160,1152]{1,0:T(8,128)(2,1)S(1)}, u32[]{:S(2)}, u32[]{:S(2)}) %collective-permute-start.19) | collective-permute-done | bytes 368672 | tf_op jit(solution)/shard_map/ppermute | solution.py:335
  176.5 5.6 %shard_map.289 = (bf16[640,1152]{1,0:T(8,128)(2,1)S(1)}, f32[640,1152]{1,0:T(8,128)S(1)}) custom-call(bf16[640,1152]{1,0:T(8,128)(2,1)S(1)} %pad_maximum_fusion.1.x_ref, bf16[1152,1152]{1,0:T(8,128)(2,1)S(1)} %convolution_convert_fusion.3.up_ref, f32[1,1152]{1,0:T(1,128)S(1)} %reshape_reshape.6.bias_ref), custom_call_target="tpu_custom_call" | custom-call | flops 1698693120 | bytes 8552448 | tf_op jit(solution)/shard_map/pallas_call | solution.py:254
  183.7 4.0 %convolution_convert_fusion.2 = bf16[1152,1152]{1,0:T(8,128)(2,1)} fusion(bf16[640,1152]{1,0:T(8,128)(2,1)S(1)} %get-tuple-element.140, bf16[640,1152]{1,0:T(8,128)(2,1)S(1)} %copy-done.28), kind=kOutput, calls=%fused_computation.10 | convolution fusion | flops 1700020224 | bytes 5603328 | tf_op jit(solution)/shard_map/dot_general | solution.py:57
  188.0 8.2 %shard_map.290 = (bf16[640,1152]{1,0:T(8,128)(2,1)}, f32[1,1152]{1,0:T(1,128)S(1)}, f32[160,1152]{1,0:T(8,128)S(1)}, bf16[160,1152]{1,0:T(8,128)(2,1)S(1)}, bf16...) custom-call(bf16[640,1152]{1,0:T(8,128)(2,1)} %pad_maximum_fusion.grad_ref, bf16[1152,1152]{1,0:T(8,128)(2,1)} %copy-done.2, ...), custom_call_target="tpu_custom_call" | custom-call | flops 3397386240 | bytes 12681216 | tf_op jit(solution)/shard_map/pallas_call | solution.py:292
  199.8 9.8 %convolution_convert_fusion.1 = bf16[1152,1152]{1,0:T(8,128)(2,1)} fusion(bf16[640,1152]{1,0:T(8,128)(2,1)} %get-tuple-element.137, bf16[640,1152]{1,0:T(8,128)(2,1)S(1)} %pad_maximum_fusion.1.x_ref, s32[1152]{0:T(1024)S(1)} %get-tuple-element.255, s32[1152]{0:T(1024)S(1)} %copy-done.37, s32[]{:T(128)S(6)} %axis_index.23, s32[1152]{0:T(1024)S(1)} %get-tuple-element.254, ...), kind=kOutput, calls=%fused_computation.9 | convolution fusion | flops 3435282432 | bytes 5624068 | tf_op jit(solution)/shard_map/dot_general | solution.py:57
  209.6 5.3 %collective-permute-done.22 = bf16[160,1152]{1,0:T(8,128)(2,1)} collective-permute-done((bf16[160,1152]{1,0:T(8,128)(2,1)S(1)}, bf16[160,1152]{1,0:T(8,128)(2,1)}, u32[]{:S(2)}, u32[]{:S(2)}) %collective-permute-start.22) | collective-permute-done | bytes 368672 | tf_op jit(solution)/shard_map/ppermute | solution.py:335
  223.7 4.2 %all-to-all-start.3 = ((bf16[8,160,144]{1,2,0:T(8,128)(2,1)}), bf16[8,160,144]{1,2,0:T(8,128)(2,1)}, u32[]{:S(2)}, u32[]{:S(2)}) async-start(bf16[8,160,144]{1,2,0:T(8,128)(2,1)} %copy.61), calls=%async_computation.3 | async-start | bytes 1179648 | tf_op jit(solution)/shard_map/all_to_all | solution.py:359
  228.0 5.6 %fusion.63 = (bf16[640,1152]{1,0:T(8,128)(2,1)S(1)}, f32[640,1152]{1,0:T(8,128)}) fusion(bf16[640,1152]{1,0:T(8,128)(2,1)S(1)} %copy-done.4, bf16[1152,1152]{1,0:T(8,128)(2,1)} %all-gather.12.cloned.1.call-done.down_ref), kind=kOutput, calls=%fused_computation.170 | convolution fusion | flops 1699430400 | bytes 8552448 | tf_op jit(solution)/shard_map/dot_general | solution.py:53
  239.4 12.0 %all-to-all-done.3 = bf16[8,160,144]{1,2,0:T(8,128)(2,1)} async-done(((bf16[8,160,144]{1,2,0:T(8,128)(2,1)}), bf16[8,160,144]{1,2,0:T(8,128)(2,1)}, u32[]{:S(2)}, u32[]{:S(2)}) %all-to-all-start.3) | async-done | bytes 368672 | tf_op jit(solution)/shard_map/all_to_all | solution.py:359
  254.4 12.9 %shard_map.292 = (bf16[1280,144]{1,0:T(8,128)(2,1)S(1)}, bf16[1280,288]{1,0:T(8,128)(2,1)S(1)}) custom-call(bf16[1280,768]{1,0:T(8,128)(2,1)S(1)} %copy-done.6, bf16[1280,768]{1,0:T(8,128)(2,1)S(1)} %copy-done.6, bf16[1280,768]{1,0:T(8,128)(2,1)S(1)} %copy-done.6, bf16[1280,144]{1,0:T(8,128)(2,1)S(1)} %bitcast.145, f32[1280,256]{1,0:T(8,128)S(1)} %copy-done.8, ...), custom_call_target="tpu_custom_call" | custom-call | flops 8388608000 | bytes 4587520 | tf_op jit(solution)/shard_map/pallas_call | solution.py:172
  288.4 7.1 %collective-permute-done.34 = bf16[160,1152]{1,0:T(8,128)(2,1)S(1)} collective-permute-done((bf16[160,1152]{1,0:T(8,128)(2,1)S(1)}, bf16[160,1152]{1,0:T(8,128)(2,1)S(1)}, u32[]{:S(2)}, u32[]{:S(2)}) %collective-permute-start.34) | collective-permute-done | bytes 368672 | tf_op jit(solution)/shard_map/ppermute | solution.py:335
  307.7 4.9 %all-to-all-start.4 = ((bf16[4,36,1152]{2,1,0:T(8,128)(2,1)}), bf16[4,36,1152]{2,1,0:T(8,128)(2,1)S(1)}, u32[]{:S(2)}, u32[]{:S(2)}) async-start(bf16[4,36,1152]{2,1,0:T(8,128)(2,1)} %fusion.27), calls=%async_computation.7 | async-start | bytes 737280 | tf_op jit(solution)/shard_map/all_to_all | solution.py:369
  323.4 5.0 %all-to-all-start.5 = ((bf16[8,36,432]{2,1,0:T(8,128)(2,1)}), bf16[8,36,432]{2,1,0:T(8,128)(2,1)}, u32[]{:S(2)}, u32[]{:S(2)}) async-start(bf16[8,36,432]{2,1,0:T(8,128)(2,1)} %reshape.202), calls=%async_computation.8 | async-start | bytes 655360 | tf_op jit(solution)/shard_map/all_to_all | solution.py:359
  329.7 4.7 %collective-permute-done.28 = bf16[160,1152]{1,0:T(8,128)(2,1)S(1)} collective-permute-done((bf16[160,1152]{1,0:T(8,128)(2,1)S(1)}, bf16[160,1152]{1,0:T(8,128)(2,1)S(1)}, u32[]{:S(2)}, u32[]{:S(2)}) %collective-permute-start.28) | collective-permute-done | bytes 368672 | tf_op jit(solution)/shard_map/ppermute | solution.py:335
  341.3 4.8 %all-to-all-start.6 = ((f32[32,8,128]{2,1,0:T(8,128)}), f32[32,8,128]{2,1,0:T(8,128)S(1)}, u32[]{:S(2)}, u32[]{:S(2)}) async-start(f32[32,8,128]{2,1,0:T(8,128)} %bitcast.66), calls=%async_computation.9 | async-start | bytes 262144 | tf_op jit(solution)/shard_map/all_to_all | solution.py:554
  363.7 6.8 %collective-permute-done.41 = bf16[160,576]{0,1:T(8,128)(2,1)} collective-permute-done((bf16[160,576]{0,1:T(8,128)(2,1)}, bf16[160,576]{0,1:T(8,128)(2,1)}, u32[]{:S(2)}, u32[]{:S(2)}) %collective-permute-start.41) | collective-permute-done | bytes 184352 | tf_op jit(solution)/shard_map/ppermute | solution.py:335
  (354 shorter events, 190.8 us)
Async XLA Ops:
  7.2 30.0 %all-gather.6.cloned.1.call-start = ((), (), s32[]{:S(2)}) async-start(), calls=%async_computation.11 | async-start | bytes 1492992 | tf_op jit(solution)/shard_map/all_gather | solution.py:372
  9.7 22.1 %collective-permute-start = (bf16[160,576]{1,0:T(8,128)(2,1)S(1)}, bf16[160,576]{1,0:T(8,128)(2,1)S(1)}, u32[]{:S(2)}, u32[]{:S(2)}) collective-permute-start(bf16[160,576]{1,0:T(8,128)(2,1)S(1)} %get-tuple-element.204), channel_id=1, source_target_pairs={{0,8},{8,0},{16,24},{24,16},{1,9},{9,1},{17,25},{25,17},{2,10},{10... | collective-permute-start | bytes 552968 | tf_op jit(solution)/shard_map/ppermute | solution.py:335
  12.8 19.1 %collective-permute-start.1 = (bf16[160,576]{1,0:T(8,128)(2,1)S(1)}, bf16[160,576]{1,0:T(8,128)(2,1)S(1)}, u32[]{:S(2)}, u32[]{:S(2)}) collective-permute-start(bf16[160,576]{1,0:T(8,128)(2,1)S(1)} %get-tuple-element.203), channel_id=1, source_target_pairs={{0,16},{8,24},{16,0},{24,8},{1,17},{9,25},{17,1},{25,9},{2,18},{10... | collective-permute-start | bytes 552968 | tf_op jit(solution)/shard_map/ppermute | solution.py:335
  49.8 61.6 %all-gather.8.cloned.1.call-start = ((), (), s32[]{:S(2)}) async-start(), calls=%async_computation.12 | async-start | bytes 3317760 | tf_op jit(solution)/shard_map/all_gather | solution.py:421
  64.2 88.0 %all-gather.10.cloned.1.call-start = ((), (), s32[]{:S(2)}) async-start(), calls=%async_computation.13 | async-start | bytes 2985984 | tf_op jit(solution)/shard_map/all_gather | solution.py:433
  78.2 31.6 %collective-permute-start.10 = (bf16[160,1152]{1,0:T(8,128)(2,1)S(1)}, bf16[160,1152]{1,0:T(8,128)(2,1)}, u32[]{:S(2)}, u32[]{:S(2)}) collective-permute-start(bf16[160,1152]{1,0:T(8,128)(2,1)S(1)} %bitcast.154), channel_id=1, source_target_pairs={{0,16},{8,24},{16,0},{24,8},{1,17},{9,25},{17,1},{25,9},{2,18},{10... | collective-permute-start | bytes 1105928 | tf_op jit(solution)/shard_map/ppermute | solution.py:335
  79.3 32.1 %collective-permute-start.11 = (bf16[160,1152]{1,0:T(8,128)(2,1)S(1)}, bf16[160,1152]{1,0:T(8,128)(2,1)}, u32[]{:S(2)}, u32[]{:S(2)}) collective-permute-start(bf16[160,1152]{1,0:T(8,128)(2,1)S(1)} %bitcast.155), channel_id=1, source_target_pairs={{0,24},{8,16},{16,8},{24,0},{1,25},{9,17},{17,9},{25,1},{2,26},{10... | collective-permute-start | bytes 1105928 | tf_op jit(solution)/shard_map/ppermute | solution.py:335
  80.8 30.6 %collective-permute-start.9 = (bf16[160,1152]{1,0:T(8,128)(2,1)S(1)}, bf16[160,1152]{1,0:T(8,128)(2,1)}, u32[]{:S(2)}, u32[]{:S(2)}) collective-permute-start(bf16[160,1152]{1,0:T(8,128)(2,1)S(1)} %bitcast.156), channel_id=1, source_target_pairs={{0,8},{8,0},{16,24},{24,16},{1,9},{9,1},{17,25},{25,17},{2,10},{10... | collective-permute-start | bytes 1105928 | tf_op jit(solution)/shard_map/ppermute | solution.py:335
  103.7 22.4 %collective-permute-start.12 = (bf16[144,1152]{1,0:T(8,128)(2,1)}, bf16[144,1152]{1,0:T(8,128)(2,1)}, u32[]{:S(2)}, u32[]{:S(2)}) collective-permute-start(bf16[144,1152]{1,0:T(8,128)(2,1)} %constant_dynamic-slice_fusion.5), channel_id=1, source_target_pairs={{0,8},{8,0},{16,24},{24,16},{1,9},{9,1},{17,25},{25,17},{2,10},{10... | collective-permute-start | bytes 995336 | tf_op jit(solution)/shard_map/ppermute | solution.py:335
  104.6 21.5 %collective-permute-start.13 = (bf16[144,1152]{1,0:T(8,128)(2,1)}, bf16[144,1152]{1,0:T(8,128)(2,1)}, u32[]{:S(2)}, u32[]{:S(2)}) collective-permute-start(bf16[144,1152]{1,0:T(8,128)(2,1)} %constant_dynamic-slice_fusion.5), channel_id=1, source_target_pairs={{0,16},{8,24},{16,0},{24,8},{1,17},{9,25},{17,1},{25,9},{2,18},{10... | collective-permute-start | bytes 995336 | tf_op jit(solution)/shard_map/ppermute | solution.py:335
  127.9 24.0 %all-to-all-start.2 = ((bf16[8,160,144]{1,2,0:T(8,128)(2,1)}), bf16[8,160,144]{1,2,0:T(8,128)(2,1)S(1)}, u32[]{:S(2)}, u32[]{:S(2)}) async-start(bf16[8,160,144]{1,2,0:T(8,128)(2,1)} %copy.59), calls=%async_computation.2 | async-start | bytes 1179648 | tf_op jit(solution)/shard_map/all_to_all | solution.py:359
  131.6 56.4 %all-gather.12.cloned.1.call-start = ((), (), s32[]{:S(2)}) async-start(), calls=%async_computation.14 | async-start | bytes 2985984 | tf_op jit(solution)/shard_map/all_gather | solution.py:457
  152.2 120.1 %reduce-scatter.9.cloned.1.call-start = ((), (), s32[]{:S(2)}) async-start(), calls=%async_computation.16 | async-start | bytes 2985984 | tf_op jit(solution)/shard_map/reduce_scatter | solution.py:468
  187.7 84.6 %reduce-scatter.7.cloned.1.call-start = ((), (), s32[]{:S(2)}) async-start(), calls=%async_computation.15 | async-start | bytes 2985984 | tf_op jit(solution)/shard_map/reduce_scatter | solution.py:485
  223.7 27.7 %all-to-all-start.3 = ((bf16[8,160,144]{1,2,0:T(8,128)(2,1)}), bf16[8,160,144]{1,2,0:T(8,128)(2,1)}, u32[]{:S(2)}, u32[]{:S(2)}) async-start(bf16[8,160,144]{1,2,0:T(8,128)(2,1)} %copy.61), calls=%async_computation.3 | async-start | bytes 1179648 | tf_op jit(solution)/shard_map/all_to_all | solution.py:359
  227.9 84.7 %reduce-scatter.11.cloned.1.call-start = ((), (), s32[]{:S(2)}) async-start(), calls=%async_computation.17 | async-start | bytes 3317760 | tf_op jit(solution)/shard_map/reduce_scatter | solution.py:505
  236.7 35.5 %collective-permute-start.25 = (bf16[160,1152]{1,0:T(8,128)(2,1)}, bf16[160,1152]{1,0:T(8,128)(2,1)S(1)}, u32[]{:S(2)}, u32[]{:S(2)}) collective-permute-start(bf16[160,1152]{1,0:T(8,128)(2,1)} %get-tuple-element.189), channel_id=1, source_target_pairs={{0,16},{8,24},{16,0},{24,8},{1,17},{9,25},{17,1},{25,9},{2,18},{10... | collective-permute-start | bytes 1105928 | tf_op jit(solution)/shard_map/ppermute | solution.py:335
  237.7 34.6 %collective-permute-start.26 = (bf16[160,1152]{1,0:T(8,128)(2,1)}, bf16[160,1152]{1,0:T(8,128)(2,1)}, u32[]{:S(2)}, u32[]{:S(2)}) collective-permute-start(bf16[160,1152]{1,0:T(8,128)(2,1)} %get-tuple-element.188), channel_id=1, source_target_pairs={{0,24},{8,16},{16,8},{24,0},{1,25},{9,17},{17,9},{25,1},{2,26},{10... | collective-permute-start | bytes 1105928 | tf_op jit(solution)/shard_map/ppermute | solution.py:335
  273.3 22.3 %collective-permute-start.30 = (bf16[160,288]{1,0:T(8,128)(2,1)S(1)}, bf16[160,288]{1,0:T(8,128)(2,1)S(1)}, u32[]{:S(2)}, u32[]{:S(2)}) collective-permute-start(bf16[160,288]{1,0:T(8,128)(2,1)S(1)} %get-tuple-element.212), channel_id=1, source_target_pairs={{0,8},{8,0},{16,24},{24,16},{1,9},{9,1},{17,25},{25,17},{2,10},{10... | collective-permute-start | bytes 276488 | tf_op jit(solution)/shard_map/ppermute | solution.py:335
  273.8 21.8 %collective-permute-start.31 = (bf16[160,288]{1,0:T(8,128)(2,1)S(1)}, bf16[160,288]{1,0:T(8,128)(2,1)S(1)}, u32[]{:S(2)}, u32[]{:S(2)}) collective-permute-start(bf16[160,288]{1,0:T(8,128)(2,1)S(1)} %get-tuple-element.211), channel_id=1, source_target_pairs={{0,16},{8,24},{16,0},{24,8},{1,17},{9,25},{17,1},{25,9},{2,18},{10... | collective-permute-start | bytes 276488 | tf_op jit(solution)/shard_map/ppermute | solution.py:335
  275.8 19.7 %collective-permute-start.34 = (bf16[160,1152]{1,0:T(8,128)(2,1)S(1)}, bf16[160,1152]{1,0:T(8,128)(2,1)S(1)}, u32[]{:S(2)}, u32[]{:S(2)}) collective-permute-start(bf16[160,1152]{1,0:T(8,128)(2,1)S(1)} %copy-done.20), channel_id=1, source_target_pairs={{0,16},{8,24},{16,0},{24,8},{1,17},{9,25},{17,1},{25,9},{2,18},{10... | collective-permute-start | bytes 1105928 | tf_op jit(solution)/shard_map/ppermute | solution.py:335
  317.4 18.9 %collective-permute-start.29 = (bf16[160,1152]{1,0:T(8,128)(2,1)S(1)}, bf16[160,1152]{1,0:T(8,128)(2,1)}, u32[]{:S(2)}, u32[]{:S(2)}) collective-permute-start(bf16[160,1152]{1,0:T(8,128)(2,1)S(1)} %get-tuple-element.182), channel_id=1, source_target_pairs={{0,24},{8,16},{16,8},{24,0},{1,25},{9,17},{17,9},{25,1},{2,26},{10... | collective-permute-start | bytes 1105928 | tf_op jit(solution)/shard_map/ppermute | solution.py:335
  328.4 47.2 %reduce-scatter.13.cloned.1.call-start = ((), (), s32[]{:S(2)}) async-start(), calls=%async_computation.18 | async-start | bytes 1492992
  341.3 33.1 %all-to-all-start.6 = ((f32[32,8,128]{2,1,0:T(8,128)}), f32[32,8,128]{2,1,0:T(8,128)S(1)}, u32[]{:S(2)}, u32[]{:S(2)}) async-start(f32[32,8,128]{2,1,0:T(8,128)} %bitcast.66), calls=%async_computation.9 | async-start | bytes 262144 | tf_op jit(solution)/shard_map/all_to_all | solution.py:554
  (88 other events, 1011.9 us)
Sparse Core Ops, SparseCore 0:
  9.7 27.5 all-gather.5
  64.3 41.0 all-gather.7
  107.6 36.3 all-gather.9
  152.3 32.3 all-gather.11
  187.9 36.5 reduce-scatter.8
  226.6 43.3 reduce-scatter.6
  272.5 37.6 reduce-scatter.10
  340.2 34.8 reduce-scatter.12
